TPU v7x, 256 devices: a whole 4x4x8 slice. The times are simulated.
256 devices in a mesh: gx: 4 (over y), gy: 8 (over x, core), gz: 8 (over z).
Axes of the slice: x: 4, y: 4, z: 8, core: 2. Of those that a mesh axis runs over, the one named last changes fastest.
Arguments:
- activation: bfloat16 [2, 16, 64, 64, 128], P(None, 'gx', 'gy', 'gz'), may hold values from -6 to 6
- w_in: bfloat16 [3456, 256], replicated, may hold values from -0.109375 to 0.109375
- w_up: bfloat16 [2048, 128], replicated, may hold values from -0.375 to 0.375
- w_out: bfloat16 [6912, 128], replicated, may hold values from -0.078125 to 0.078125
- cotangent: bfloat16 [2, 16, 64, 64, 128], P(None, 'gx', 'gy', 'gz'), may hold values from -6 to 6
Outputs:
- output: bfloat16 [2, 16, 64, 64, 128], P(None, 'gx', 'gy', 'gz')
- d_activation: bfloat16 [2, 16, 64, 64, 128], P(None, 'gx', 'gy', 'gz')
- clipped: float32 [2031616], P(('gx', 'gy', 'gz'))
All inputs are finite; a program needn't handle non-finite values.
Results may differ from a plain program's by a relative error of at most 0.0024.
Values may be sent and summed in bfloat16 or wider, within the bound.
No kernel may reach another device: no remote copies, remote signals or barrier semaphores. Data moves between devices by JAX's collectives and lax.ppermute only.
A program may use at most 128 MiB of HBM per device.

v0:
```python
import itertools

import jax
import jax.numpy as jnp
import numpy as np
from jax import lax
from jax.experimental import pallas as pl
from jax.experimental.pallas import tpu as pltpu
from jax.sharding import Mesh, PartitionSpec as P

F32 = jnp.float32
BF16 = jnp.bfloat16
PARAMS = 2031616
CELLS = ("gx", ("x", "core"), "gz")


def traded_faces(arrays, axis, dim):
    count = lax.axis_size(axis)
    even = lax.axis_index(axis) % 2 == 0
    first_pairs = [(i, i ^ 1) for i in range(count)]
    second_pairs = [(i, j) for i in range(count) for j in [((i + 1) ^ 1) - 1] if 0 <= j < count]

    def face(last):
        parts = []
        for array in arrays:
            at = array.shape[dim] - 1 if last else 0
            parts.append(lax.slice_in_dim(array, at, at + 1, axis=dim).reshape(-1, 128))
        return jnp.concatenate(parts, axis=0)

    lasts, firsts = face(True), face(False)
    one = lax.ppermute(jnp.where(even, lasts, firsts), axis, first_pairs)
    two = lax.ppermute(jnp.where(even, firsts, lasts), axis, second_pairs)
    lows, highs = jnp.where(even, two, one), jnp.where(even, one, two)
    faces, at = [], 0
    for array in arrays:
        shape = array.shape[:dim] + (1,) + array.shape[dim + 1 :]
        rows = array.size // array.shape[dim] // 128
        faces.append((lows[at : at + rows].reshape(shape), highs[at : at + rows].reshape(shape)))
        at += rows
    return faces


def joined_faces(arrays, faces, dim):
    return [jnp.concatenate([low, array, high], axis=dim) for array, (low, high) in zip(arrays, faces)]


def extended(arrays, axes=CELLS):
    for dim, axis in enumerate(axes):
        arrays = joined_faces(arrays, traded_faces(arrays, axis, dim + 1), dim + 1)
    return arrays


def conv_forward(padded, weight):
    kernel = weight.reshape(3, 3, 3, padded.shape[4], -1)
    return lax.conv_general_dilated(
        padded, kernel, (1, 1, 1), "VALID",
        dimension_numbers=("NXYZC", "XYZIO", "NXYZC"), preferred_element_type=F32,
    )


def conv_transpose(padded, weight):
    kernel = weight.reshape(3, 3, 3, -1, padded.shape[4])[::-1, ::-1, ::-1]
    return lax.conv_general_dilated(
        padded, kernel, (1, 1, 1), "VALID",
        dimension_numbers=("NXYZC", "XYZOI", "NXYZC"), preferred_element_type=F32,
    )


def pool_half(volume):
    samples, size_x, size_y, size_z, chans = volume.shape
    blocks = volume.astype(F32).reshape(samples, size_x // 2, 2, size_y // 2, 2, size_z // 2, 2, chans)
    return jnp.mean(blocks, axis=(2, 4, 6))


def spread(volume):
    samples, size_x, size_y, size_z, chans = volume.shape
    wide = jnp.broadcast_to(
        volume[:, :, None, :, None, :, None, :], (samples, size_x, 2, size_y, 2, size_z, 2, chans)
    )
    return wide.reshape(samples, 2 * size_x, 2 * size_y, 2 * size_z, chans)


def up_conv(bottom, w_up):
    samples, size_x, size_y, size_z, wide = bottom.shape
    kernel = w_up.reshape(2, 2, 2, wide, -1)
    result = jnp.einsum("sijkc,abeco->siajbkeo", bottom, kernel, preferred_element_type=F32)
    return result.reshape(samples, 2 * size_x, 2 * size_y, 2 * size_z, -1)


def _select_pooled():
    sel = np.zeros((9, 2, 4, 4, 4, 288), np.float32)
    for dy in range(3):
        for dz in range(3):
            for s, x, y, z in itertools.product(range(2), range(4), range(4), range(4)):
                line, k = (s * 4 + x) * 6 + y + dy, z + dz - 1
                source = 192 + line if k < 0 else 240 + line if k > 3 else line * 4 + k
                sel[3 * dy + dz, s, x, y, z, source] = 1
    return sel.reshape(1152, 288)


def _fine_from_blocks():
    perm = np.zeros((512, 512), np.float32)
    for s, x, y, z in itertools.product(range(2), range(4), range(8), range(8)):
        fine = ((s * 4 + x) * 8 + y) * 8 + z
        part = (x % 2) * 4 + (y % 2) * 2 + z % 2
        perm[fine, part * 64 + ((s * 2 + x // 2) * 4 + y // 2) * 4 + z // 2] = 1
    return perm


def _dot(a, b, contract=((1,), (0,))):
    return lax.dot_general(a, b, (contract, ((), ())), preferred_element_type=F32)


def _gradients_kernel(
    core_ref, act_ref, cot_ref, cot_low_ref, cot_high_ref, pool_ref, sel_ref, perm_ref, perm_t_ref,
    w_in_hbm, w_back_hbm, w_up_hbm,
    keep_hbm, send_hbm, bottom_ref, slope_ref, d_act_ref,
    w_in, w_back, w_up, lines, shifted, pooled, spaced, sums, sem_in, sem_out,
):
    loads = [
        pltpu.make_async_copy(source, target, sem_in.at[i])
        for i, (source, target) in enumerate(((w_in_hbm, w_in), (w_up_hbm, w_up), (w_back_hbm, w_back)))
    ]
    for load in loads:
        load.start()
    core = core_ref[0]
    side = (core, 1 - core)

    def put(row, value, stride=1):
        done, count = 0, value.shape[0]
        while done < count:
            first = row + stride * done
            block = first // 496
            here = min(count - done, -((first - 496 * (block + 1)) // stride))
            where = pl.ds(first % 496, here) if stride == 1 else pl.ds(first % 496, here, stride)
            sums[side[block % 2], block // 2, where, :] = value[done : done + here]
            done += here

    def ship(index, first, last):
        copies = [
            pltpu.make_async_copy(sums.at[i, pl.ds(first, last - first)], hbm.at[pl.ds(first, last - first)], sem_out.at[index, i])
            for i, hbm in enumerate((keep_hbm, send_hbm))
        ]
        for copy in copies:
            copy.start()
        return copies

    picked = _dot(sel_ref[...], pool_ref[...])
    for u in range(9):
        pooled[:, :, :, u * 128 : (u + 1) * 128] = picked[u * 128 : (u + 1) * 128].reshape(2, 4, 16, 128).astype(BF16)
    loads[0].wait()
    before = jnp.zeros((64, 256), F32)
    for dx in range(3):
        before += _dot(pooled[:, dx : dx + 2].reshape(64, 1152), w_in[dx * 1152 : (dx + 1) * 1152, :])
    squash = 1.0 / (1.0 + jnp.exp(-before))
    bottom32 = (before * squash).astype(BF16).astype(F32)
    bottom = bottom32.astype(BF16)
    bottom_ref[...] = bottom
    loads[1].wait()
    parts = [_dot(bottom, w_up[p * 256 : (p + 1) * 256, :]).astype(BF16) for p in range(8)]
    upward = _dot(perm_ref[...], jnp.concatenate(parts, axis=0))

    lines[:, 8:16, :] = cot_ref[...].astype(F32).reshape(120, 8, 128)
    lines[:, 7:8, :] = cot_low_ref[...].astype(F32)[:, None, :]
    lines[:, 16:17, :] = cot_high_ref[...].astype(F32)[:, None, :]
    for dz in range(3):
        window = lines[:, 7 + dz : 15 + dz, :].reshape(2, 6, 10, 8, 128)
        for dy in range(3):
            u = 3 * dy + dz
            shifted[:, :, :, u * 128 : (u + 1) * 128] = window[:, :, dy : dy + 8].reshape(2, 6, 64, 128).astype(BF16)

    loads[2].wait()
    d_joined = jnp.zeros((512, 256), F32)
    for dx in range(3):
        d_joined += _dot(shifted[:, dx : dx + 4].reshape(512, 1152), w_back[dx * 1152 : (dx + 1) * 1152, :])
    d_act_ref[...] = d_joined[:, :128]

    joined_t = jnp.concatenate([act_ref[...].astype(F32).T, upward.T], axis=0).astype(BF16)
    for dx in range(3):
        grad = _dot(joined_t, shifted[:, dx : dx + 4].reshape(512, 1152))
        for u in range(9):
            put(8960 + (26 - 9 * dx - u) * 256, grad[:, u * 128 : (u + 1) * 128])
    copies = ship(0, 10, 16)

    blocks = _dot(perm_t_ref[...], d_joined[:, 128:].astype(BF16)).astype(BF16)
    d_bottom = jnp.zeros((64, 256), F32)
    for p in range(8):
        d_bottom += _dot(blocks[p * 64 : (p + 1) * 64], w_up[p * 256 : (p + 1) * 256, :], ((1,), (1,)))
    bottom_t = bottom32.T.astype(BF16)
    for p in range(8):
        put(6912 + p * 256, _dot(bottom_t, blocks[p * 64 : (p + 1) * 64]))
    slope = (d_bottom * squash * (1.0 + before * (1.0 - squash))).astype(BF16)
    slope_ref[...] = slope

    spaced[...] = jnp.zeros((128, 768), BF16)
    for s in range(2):
        for dx in range(3):
            spaced[s * 64 + dx * 16 : s * 64 + dx * 16 + 32, dx * 256 : (dx + 1) * 256] = slope[s * 32 : (s + 1) * 32]
    for u in range(9):
        picked_t = picked[u * 128 : (u + 1) * 128].T.astype(BF16)
        grad = _dot(picked_t, spaced[...])
        for dx in range(3):
            for h in range(2):
                put((9 * dx + u) * 256 + h, grad[:, dx * 256 + h * 128 : dx * 256 + (h + 1) * 128], 2)
    copies += ship(1, 0, 10)
    for copy in copies:
        copy.wait()


def gradients(core, act, cot, cot_low, cot_high, pool, w_in, w_back, w_up):
    shape = jax.ShapeDtypeStruct
    vmem, hbm = pl.BlockSpec(memory_space=pltpu.VMEM), pl.BlockSpec(memory_space=pl.ANY)
    return pl.pallas_call(
        _gradients_kernel,
        out_shape=(
            shape((16, 496, 128), F32), shape((16, 496, 128), F32),
            shape((64, 256), BF16), shape((64, 256), BF16), shape((512, 128), F32),
        ),
        in_specs=[pl.BlockSpec(memory_space=pltpu.SMEM)] + [vmem] * 8 + [hbm] * 3,
        out_specs=(hbm, hbm, vmem, vmem, vmem),
        scratch_shapes=[
            pltpu.VMEM((3456, 256), BF16), pltpu.VMEM((3456, 256), BF16), pltpu.VMEM((2048, 128), BF16),
            pltpu.VMEM((120, 24, 128), F32), pltpu.VMEM((2, 6, 64, 1152), BF16),
            pltpu.VMEM((2, 4, 16, 1152), BF16), pltpu.VMEM((128, 768), BF16),
            pltpu.VMEM((2, 16, 496, 128), F32),
            pltpu.SemaphoreType.DMA((3,)), pltpu.SemaphoreType.DMA((2, 2)),
        ],
        compiler_params=pltpu.CompilerParams(vmem_limit_bytes=48 * 1024 * 1024),
        cost_estimate=pl.CostEstimate(flops=2_500_000_000, bytes_accessed=16_000_000, transcendentals=16384),
    )(
        core, act, cot, cot_low, cot_high, pool,
        jnp.asarray(_select_pooled(), BF16), jnp.asarray(_fine_from_blocks(), BF16), jnp.asarray(_fine_from_blocks().T, BF16),
        w_in, w_back, w_up,
    )


def at(array, index, axis):
    return lax.dynamic_index_in_dim(array, index, axis, keepdims=False)


def turned(array, axis, shift):
    count = lax.axis_size(axis)
    return lax.ppermute(array, axis, [(i, (i + shift) % count) for i in range(count)])


def paired(array, axis, bit):
    count = lax.axis_size(axis)
    return lax.ppermute(array, axis, [(i, i ^ bit) for i in range(count)])


def scattered_sum(keep, send):
    gx, x, gz = (lax.axis_index(a) for a in ("gx", "x", "gz"))
    blocks = (keep + paired(send, "core", 1)).reshape(4, 4, 496, 128)
    one, two = blocks[:, :, :248], blocks[:, :, 248:]
    got_one, got_two = [], []
    for s in (2, 1, 3):
        got_one.append(turned(at(one, (gx + s) % 4, 0).astype(BF16), "gx", s))
        got_two.append(turned(at(two, (x + s) % 4, 1).astype(BF16), "x", s))
    one = at(one, gx, 0) + sum(g.astype(F32) for g in got_one)
    two = at(two, x, 1) + sum(g.astype(F32) for g in got_two)
    got_one, got_two = [], []
    for s in (2, 1, 3):
        got_one.append(turned(at(one, (x + s) % 4, 0), "x", s))
        got_two.append(turned(at(two, (gx + s) % 4, 0), "gx", s))
    one = at(one, x, 0) + sum(got_one)
    two = at(two, gx, 0) + sum(got_two)
    mine = jnp.concatenate([one, two], axis=0).reshape(2, 2, 2, 62, 128)
    for bit in (1, 2, 4):
        half = (gz // bit) % 2
        axis = mine.ndim - 3
        mine = at(mine, half, axis) + paired(at(mine, 1 - half, axis), "gz", bit)
    return mine


def summed_everywhere(value):
    for axis, bits in (("core", (1,)), ("gx", (1, 2)), ("x", (1, 2)), ("gz", (1, 2, 4))):
        for bit in bits:
            value = value + paired(value, axis, bit)
    return value


def local(activation, w_in, w_up, w_out, cotangent):
    pooled = pool_half(activation).astype(BF16)
    arrays = extended([activation, cotangent, pooled], CELLS[:2])
    faces = traded_faces(arrays, "gz", 3)
    active_pad = jnp.concatenate([faces[0][0], arrays[0], faces[0][1]], axis=3)
    cot_low, cot_high = (face.reshape(120, 128) for face in faces[1])
    pool_rows = jnp.concatenate([p.reshape(-1, 128) for p in (arrays[2], *faces[2])], axis=0)
    w_back = w_out.reshape(27, 256, 128)[::-1].transpose(0, 2, 1).reshape(3456, 256)

    core = lax.axis_index("core").astype(jnp.int32)[None]
    keep, send, bottom, d_before, d_direct = gradients(
        core, activation.reshape(512, 128), arrays[1].reshape(960, 128), cot_low, cot_high,
        pool_rows, w_in, w_back, w_up,
    )
    mine = scattered_sum(keep, send)
    total = jnp.sum(summed_everywhere(jnp.sum(mine * mine, axis=0, keepdims=True)))
    factor = jnp.minimum(1.0, jnp.sqrt(PARAMS / (total + 1e-06)))
    clipped = (mine * factor).reshape(-1)

    bottom_pad, slope_pad = extended([bottom.reshape(2, 2, 4, 4, 256), d_before.reshape(2, 2, 4, 4, 256)])
    upward_pad = up_conv(bottom_pad, w_up).astype(BF16)[:, 1:-1, 1:-1, 1:-1]
    output = conv_forward(jnp.concatenate([active_pad, upward_pad], axis=4), w_out).astype(BF16)
    d_pooled = conv_transpose(slope_pad, w_in)
    d_activation = (d_direct.reshape(activation.shape) + spread(d_pooled) * 0.125).astype(BF16)
    return (output, d_activation, clipped)


def solution(mesh):
    gx, gy, gz = mesh.devices.shape
    split = Mesh(mesh.devices.reshape(gx, gy // 2, 2, gz), ("gx", "x", "core", "gz"))
    cells = P(None, "gx", ("x", "core"), "gz", None)
    return jax.shard_map(
        local, mesh=split, in_specs=(cells, P(), P(), P(), cells),
        out_specs=(cells, cells, P(("gx", "x", "core", "gz"))), check_vma=False,
    )
```

profile of v0, /device:TPU:32, one launch (start us, length us, event | category | flops | bytes accessed | tf_op | source)
XLA Modules:
  0.0 159.4 jit_solution(599497330018602437)
XLA Ops:
  4.2 4.5 %collective-permute-start.1 = (bf16[288,128]{1,0:T(8,128)(2,1)S(1)}, bf16[288,128]{1,0:T(8,128)(2,1)S(1)}, u32[]{:S(2)}, u32[]{:S(2)}) collective-permute-start(bf16[288,128]{1,0:T(8,128)(2,1)S(1)} %get-tuple-element.53), channel_id=1, source_target_pairs={{0,64},{64,0},{128,192},{192,128},{1,65},{65,1},{129,193},{193,129... | collective-permute-start | bytes 221192 | tf_op jit(solution)/shard_map/ppermute | solution.py:31
  8.7 2.3 %collective-permute-done.1 = bf16[288,128]{1,0:T(8,128)(2,1)S(1)} collective-permute-done((bf16[288,128]{1,0:T(8,128)(2,1)S(1)}, bf16[288,128]{1,0:T(8,128)(2,1)S(1)}, u32[]{:S(2)}, u32[]{:S(2)}) %collective-permute-start.1) | collective-permute-done | bytes 73760 | tf_op jit(solution)/shard_map/ppermute | solution.py:31
  12.4 2.9 %collective-permute-start.3 = (bf16[224,128]{1,0:T(8,128)(2,1)S(1)}, bf16[224,128]{1,0:T(8,128)(2,1)S(1)}, u32[]{:S(2)}, u32[]{:S(2)}) collective-permute-start(bf16[224,128]{1,0:T(8,128)(2,1)S(1)} %get-tuple-element.61), channel_id=1, source_target_pairs={{0,8},{8,0},{16,24},{24,16},{32,40},{40,32},{48,56},{56,48},{1,9},... | collective-permute-start | bytes 172040 | tf_op jit(solution)/shard_map/ppermute | solution.py:31
  18.5 5.6 %collective-permute-start.4 = (bf16[288,128]{1,0:T(8,128)(2,1)}, bf16[288,128]{1,0:T(8,128)(2,1)}, u32[]{:S(2)}, u32[]{:S(2)}) collective-permute-start(bf16[288,128]{1,0:T(8,128)(2,1)} %get-tuple-element.49), channel_id=1, source_target_pairs={{1,2},{2,1},{3,4},{4,3},{5,6},{6,5},{9,10},{10,9},{11,12},{12,11},... | collective-permute-start | bytes 221192 | tf_op jit(solution)/shard_map/ppermute | solution.py:32
  24.2 2.2 %copy.98 = bf16[27,256,128]{1,2,0:T(8,128)(2,1)} copy(bf16[27,256,128]{2,1,0:T(8,128)(2,1)S(1)} %bitcast.146) | data formatting | bytes 3538944 | tf_op jit(solution)/shard_map/reshape | solution.py:289
  26.4 3.0 %rev.4 = bf16[27,256,128]{1,2,0:T(8,128)(2,1)} reverse(bf16[27,256,128]{1,2,0:T(8,128)(2,1)} %copy.98), dimensions={0} | reverse | bytes 3538944 | tf_op jit(solution)/shard_map/rev | solution.py:289
  31.1 1.2 copy-done.3
  33.3 8.1 %shard_map.103 = (f32[16,496,128]{2,1,0:T(8,128)}, f32[16,496,128]{2,1,0:T(8,128)}, bf16[64,256]{1,0:T(8,128)(2,1)S(1)}, bf16[64,256]{1,0:T(8,128)(2,1)S(1)}, f32[512,128]{1,0:T(8,128)S(1)}) custom-call(s32[1]{0:T(128)} %bitcast.29.core_ref, bf16[512,128]{1,0:T(8,128)(2,1)S(1)} %bitcast.140, bf16[960,128]{1,0:T(8,128)(2,1)S(1)} %bitcast.141, ...), custom_call_target="tpu_custom_call" | custom-call | flops 2500000000 | bytes 16000000 | tf_op jit(solution)/shard_map/pallas_call | solution.py:213
  42.0 2.1 %collective-permute-start.7 = (bf16[128,128]{1,0:T(8,128)(2,1)S(1)}, bf16[128,128]{1,0:T(8,128)(2,1)S(1)}, u32[]{:S(2)}, u32[]{:S(2)}) collective-permute-start(bf16[128,128]{1,0:T(8,128)(2,1)S(1)} %get-tuple-element.86), channel_id=1, source_target_pairs={{0,64},{64,0},{128,192},{192,128},{1,65},{65,1},{129,193},{193,129... | collective-permute-start | bytes 98312 | tf_op jit(solution)/shard_map/ppermute | solution.py:31
  44.8 1.2 collective-permute-done.7
  47.2 4.0 %collective-permute-start.9 = (bf16[128,128]{1,0:T(8,128)(2,1)S(1)}, bf16[128,128]{1,0:T(8,128)(2,1)S(1)}, u32[]{:S(2)}, u32[]{:S(2)}) collective-permute-start(bf16[128,128]{1,0:T(8,128)(2,1)S(1)} %get-tuple-element.79), channel_id=1, source_target_pairs={{0,8},{8,0},{16,24},{24,16},{32,40},{40,32},{48,56},{56,48},{1,9},... | collective-permute-start | bytes 98312 | tf_op jit(solution)/shard_map/ppermute | solution.py:31
  53.3 3.8 %add.217 = f32[16,496,128]{2,1,0:T(8,128)S(1)} add(f32[16,496,128]{2,1,0:T(8,128)} %get-tuple-element.11, f32[16,496,128]{2,1,0:T(8,128)} %collective-permute-done.12) | non-fusion elementwise | flops 1015808 | bytes 12189696 | tf_op jit(solution)/shard_map/add | solution.py:253
  57.1 1.6 %fusion.37 = (f32[4,4,248,128]{3,2,1,0:T(8,128)}, f32[4,4,248,128]{3,2,1,0:T(8,128)S(1)}) fusion(f32[4,4,496,128]{3,2,1,0:T(8,128)S(1)} %bitcast.145), kind=kLoop, calls=%fused_computation.147 | loop fusion | bytes 8126464 | tf_op jit(solution)/shard_map/slice | solution.py:254
  58.8 1.3 copy-done.6
  61.0 2.9 %collective-permute-start.21 = (bf16[4,248,128]{2,1,0:T(8,128)(2,1)}, bf16[4,248,128]{2,1,0:T(8,128)(2,1)S(1)}, u32[]{:S(2)}, u32[]{:S(2)}) collective-permute-start(bf16[4,248,128]{2,1,0:T(8,128)(2,1)} %get-tuple-element.32), channel_id=1, source_target_pairs={{0,48},{16,0},{32,16},{48,32},{1,49},{17,1},{33,17},{49,33},{2,50}... | collective-permute-start | bytes 761864 | tf_op jit(solution)/shard_map/ppermute | solution.py:243
  63.9 2.3 %collective-permute-start.19 = (bf16[4,248,128]{2,1,0:T(8,128)(2,1)S(1)}, bf16[4,248,128]{2,1,0:T(8,128)(2,1)}, u32[]{:S(2)}, u32[]{:S(2)}) collective-permute-start(bf16[4,248,128]{2,1,0:T(8,128)(2,1)S(1)} %get-tuple-element.31), channel_id=1, source_target_pairs={{0,32},{16,48},{32,0},{48,16},{1,33},{17,49},{33,1},{49,17},{2,34}... | collective-permute-start | bytes 761864 | tf_op jit(solution)/shard_map/ppermute | solution.py:243
  68.6 1.5 fusion.10
  70.1 1.1 collective-permute-start.15
  71.2 2.8 %collective-permute-start.14 = (bf16[4,248,128]{2,1,0:T(8,128)(2,1)S(1)}, bf16[4,248,128]{2,1,0:T(8,128)(2,1)S(1)}, u32[]{:S(2)}, u32[]{:S(2)}) collective-permute-start(bf16[4,248,128]{2,1,0:T(8,128)(2,1)S(1)} %get-tuple-element.30), channel_id=1, source_target_pairs={{0,64},{64,128},{128,192},{192,0},{1,65},{65,129},{129,193},{193,1... | collective-permute-start | bytes 761864 | tf_op jit(solution)/shard_map/ppermute | solution.py:243
  74.4 2.1 %collective-permute-start.13 = (bf16[4,248,128]{2,1,0:T(8,128)(2,1)S(1)}, bf16[4,248,128]{2,1,0:T(8,128)(2,1)S(1)}, u32[]{:S(2)}, u32[]{:S(2)}) collective-permute-start(bf16[4,248,128]{2,1,0:T(8,128)(2,1)S(1)} %get-tuple-element.28), channel_id=1, source_target_pairs={{0,128},{64,192},{128,0},{192,64},{1,129},{65,193},{129,1},{193,65... | collective-permute-start | bytes 761864 | tf_op jit(solution)/shard_map/ppermute | solution.py:243
  76.4 1.4 collective-permute-done.19
  77.8 1.3 bitcast_add_fusion
  80.2 4.5 %collective-permute-start.22 = (f32[248,128]{1,0:T(8,128)S(1)}, f32[248,128]{1,0:T(8,128)S(1)}, u32[]{:S(2)}, u32[]{:S(2)}) collective-permute-start(f32[248,128]{1,0:T(8,128)S(1)} %get-tuple-element.39), channel_id=1, source_target_pairs={{0,128},{64,192},{128,0},{192,64},{1,129},{65,193},{129,1},{193,65... | collective-permute-start | bytes 380936 | tf_op jit(solution)/shard_map/ppermute | solution.py:243
  84.8 4.1 %collective-permute-done.13 = bf16[4,248,128]{2,1,0:T(8,128)(2,1)S(1)} collective-permute-done((bf16[4,248,128]{2,1,0:T(8,128)(2,1)S(1)}, bf16[4,248,128]{2,1,0:T(8,128)(2,1)S(1)}, u32[]{:S(2)}, u32[]{:S(2)}) %collective-permute-start.13) | collective-permute-done | bytes 253984 | tf_op jit(solution)/shard_map/ppermute | solution.py:243
  88.9 1.1 bitcast_add_fusion.1
  90.1 1.2 collective-permute-start.18
  91.3 2.1 %collective-permute-start.16 = (f32[248,128]{1,0:T(8,128)S(1)}, f32[248,128]{1,0:T(8,128)S(1)}, u32[]{:S(2)}, u32[]{:S(2)}) collective-permute-start(f32[248,128]{1,0:T(8,128)S(1)} %get-tuple-element.36), channel_id=1, source_target_pairs={{0,32},{16,48},{32,0},{48,16},{1,33},{17,49},{33,1},{49,17},{2,34}... | collective-permute-start | bytes 380936 | tf_op jit(solution)/shard_map/ppermute | solution.py:243
  93.5 1.6 collective-permute-done.18
  95.1 2.6 %collective-permute-done.16 = f32[248,128]{1,0:T(8,128)S(1)} collective-permute-done((f32[248,128]{1,0:T(8,128)S(1)}, f32[248,128]{1,0:T(8,128)S(1)}, u32[]{:S(2)}, u32[]{:S(2)}) %collective-permute-start.16) | collective-permute-done | bytes 127008 | tf_op jit(solution)/shard_map/ppermute | solution.py:243
  97.8 1.8 %collective-permute-done.17 = f32[248,128]{1,0:T(8,128)S(1)} collective-permute-done((f32[248,128]{1,0:T(8,128)S(1)}, f32[248,128]{1,0:T(8,128)S(1)}, u32[]{:S(2)}, u32[]{:S(2)}) %collective-permute-start.17) | collective-permute-done | bytes 127008 | tf_op jit(solution)/shard_map/ppermute | solution.py:243
  100.0 4.8 %collective-permute-done.25 = f32[2,2,62,128]{3,2,1,0:T(8,128)S(1)} collective-permute-done((f32[2,2,62,128]{3,2,1,0:T(8,128)S(1)}, f32[2,2,62,128]{3,2,1,0:T(8,128)S(1)}, u32[]{:S(2)}, u32[]{:S(2)}) %collective-permute-start.25) | collective-permute-done | bytes 127008 | tf_op jit(solution)/shard_map/ppermute | solution.py:248
  104.8 3.7 %collective-permute-start.26 = (f32[2,62,128]{2,1,0:T(8,128)S(1)}, f32[2,62,128]{2,1,0:T(8,128)S(1)}, u32[]{:S(2)}, u32[]{:S(2)}) collective-permute-start(f32[2,62,128]{2,1,0:T(8,128)S(1)} %dynamic-slice_bitcast_fusion.7), channel_id=1, source_target_pairs={{0,2},{1,3},{2,0},{3,1},{4,6},{5,7},{6,4},{7,5},{8,10},{9,11},{10,... | collective-permute-start | bytes 190472 | tf_op jit(solution)/shard_map/ppermute | solution.py:248
  108.5 2.2 %collective-permute-done.26 = f32[2,62,128]{2,1,0:T(8,128)S(1)} collective-permute-done((f32[2,62,128]{2,1,0:T(8,128)S(1)}, f32[2,62,128]{2,1,0:T(8,128)S(1)}, u32[]{:S(2)}, u32[]{:S(2)}) %collective-permute-start.26) | collective-permute-done | bytes 63520 | tf_op jit(solution)/shard_map/ppermute | solution.py:248
  110.8 4.2 %collective-permute-start.27 = (f32[62,128]{1,0:T(8,128)S(1)}, f32[62,128]{1,0:T(8,128)S(1)}, u32[]{:S(2)}, u32[]{:S(2)}) collective-permute-start(f32[62,128]{1,0:T(8,128)S(1)} %dynamic-slice_bitcast_fusion.8), channel_id=1, source_target_pairs={{0,4},{1,5},{2,6},{3,7},{4,0},{5,1},{6,2},{7,3},{8,12},{9,13},{10,... | collective-permute-start | bytes 95240 | tf_op jit(solution)/shard_map/ppermute | solution.py:248
  115.0 3.9 %collective-permute-done.27 = f32[62,128]{1,0:T(8,128)S(1)} collective-permute-done((f32[62,128]{1,0:T(8,128)S(1)}, f32[62,128]{1,0:T(8,128)S(1)}, u32[]{:S(2)}, u32[]{:S(2)}) %collective-permute-start.27) | collective-permute-done | bytes 31776 | tf_op jit(solution)/shard_map/ppermute | solution.py:248
  119.1 3.4 %collective-permute-start.10 = (bf16[192,128]{1,0:T(8,128)(2,1)S(1)}, bf16[192,128]{1,0:T(8,128)(2,1)S(1)}, u32[]{:S(2)}, u32[]{:S(2)}) collective-permute-start(bf16[192,128]{1,0:T(8,128)(2,1)S(1)} %get-tuple-element.64), channel_id=1, source_target_pairs={{1,2},{2,1},{3,4},{4,3},{5,6},{6,5},{9,10},{10,9},{11,12},{12,11},... | collective-permute-start | bytes 147464 | tf_op jit(solution)/shard_map/ppermute | solution.py:32
  122.8 2.3 %collective-permute-done.10 = bf16[192,128]{1,0:T(8,128)(2,1)S(1)} collective-permute-done((bf16[192,128]{1,0:T(8,128)(2,1)S(1)}, bf16[192,128]{1,0:T(8,128)(2,1)S(1)}, u32[]{:S(2)}, u32[]{:S(2)}) %collective-permute-start.10) | collective-permute-done | bytes 49184 | tf_op jit(solution)/shard_map/ppermute | solution.py:32
  125.1 1.5 collective-permute-done.11
  126.7 1.6 collective-permute-start.30
  128.2 3.6 %collective-permute-done.30 = f32[1,128]{1,0:T(1,128)S(1)} collective-permute-done((f32[1,128]{1,0:T(1,128)S(1)}, f32[1,128]{1,0:T(1,128)S(1)}, u32[]{:S(2)}, u32[]{:S(2)}) %collective-permute-start.30) | collective-permute-done | bytes 544 | tf_op jit(solution)/shard_map/ppermute | solution.py:248
  132.2 3.2 %collective-permute-done.31 = f32[1,128]{1,0:T(1,128)S(1)} collective-permute-done((f32[1,128]{1,0:T(1,128)S(1)}, f32[1,128]{1,0:T(1,128)S(1)}, u32[]{:S(2)}, u32[]{:S(2)}) %collective-permute-start.31) | collective-permute-done | bytes 544 | tf_op jit(solution)/shard_map/ppermute | solution.py:248
  135.3 1.7 %collective-permute-start.32 = (f32[1,128]{1,0:T(1,128)S(1)}, f32[1,128]{1,0:T(1,128)S(1)}, u32[]{:S(2)}, u32[]{:S(2)}) collective-permute-start(f32[1,128]{1,0:T(1,128)S(1)} %add.264), channel_id=1, source_target_pairs={{0,32},{16,48},{32,0},{48,16},{1,33},{17,49},{33,1},{49,17},{2,34}... | collective-permute-start | bytes 1544 | tf_op jit(solution)/shard_map/ppermute | solution.py:248
  138.5 1.9 %collective-permute-done.32 = f32[1,128]{1,0:T(1,128)S(1)} collective-permute-done((f32[1,128]{1,0:T(1,128)S(1)}, f32[1,128]{1,0:T(1,128)S(1)}, u32[]{:S(2)}, u32[]{:S(2)}) %collective-permute-start.32) | collective-permute-done | bytes 544 | tf_op jit(solution)/shard_map/ppermute | solution.py:248
  140.4 1.4 collective-permute-start.33
  141.8 3.4 %convolution_convert_fusion.1 = bf16[2,4,8,8,128]{4,0,3,2,1:T(2,128)(2,1)S(1)} fusion(bf16[3,3,3,256,128]{4,3,2,1,0:T(8,128)(2,1)S(1)} %bitcast.147, bf16[2,6,10,10,128]{4,0,3,2,1:T(2,128)(2,1)S(1)} %copy.122, bf16[2,6,10,1,128]{4,0,3,2,1:T(2,128)(2,1)S(1)} %copy-done.24, bf16[2,6,1,8,128]{4,0,3,2,1:T(2,128)(2,1)S(1)} %copy-done.14, ...), kind=kOutput, calls=%fused_computation.2 | convolution fusion | flops 909721600 | bytes 2514944 | tf_op jit(solution)/shard_map/conv_general_dilated | solution.py:55
  145.4 3.1 %collective-permute-start.34 = (f32[1,128]{1,0:T(1,128)S(1)}, f32[1,128]{1,0:T(1,128)S(1)}, u32[]{:S(2)}, u32[]{:S(2)}) collective-permute-start(f32[1,128]{1,0:T(1,128)S(1)} %add.266), channel_id=1, source_target_pairs={{0,2},{1,3},{2,0},{3,1},{4,6},{5,7},{6,4},{7,5},{8,10},{9,11},{10,... | collective-permute-start | bytes 1544 | tf_op jit(solution)/shard_map/ppermute | solution.py:248
  150.0 4.2 %collective-permute-start.35 = (f32[1,128]{1,0:T(1,128)S(1)}, f32[1,128]{1,0:T(1,128)S(1)}, u32[]{:S(2)}, u32[]{:S(2)}) collective-permute-start(f32[1,128]{1,0:T(1,128)S(1)} %add.267), channel_id=1, source_target_pairs={{0,4},{1,5},{2,6},{3,7},{4,0},{5,1},{6,2},{7,3},{8,12},{9,13},{10,... | collective-permute-start | bytes 1544 | tf_op jit(solution)/shard_map/ppermute | solution.py:248
  155.7 1.8 %collective-permute-done.35 = f32[1,128]{1,0:T(1,128)S(1)} collective-permute-done((f32[1,128]{1,0:T(1,128)S(1)}, f32[1,128]{1,0:T(1,128)S(1)}, u32[]{:S(2)}, u32[]{:S(2)}) %collective-permute-start.35) | collective-permute-done | bytes 544 | tf_op jit(solution)/shard_map/ppermute | solution.py:248
  (254 shorter events, 26.3 us)
Async XLA Ops:
  0.6 10.5 %copy-start = (bf16[2,4,8,8,128]{4,3,2,1,0:T(8,128)(2,1)S(1)}, bf16[2,4,8,8,128]{4,3,2,1,0:T(8,128)(2,1)}, u32[]{:S(2)}) copy-start(bf16[2,4,8,8,128]{4,3,2,1,0:T(8,128)(2,1)} %param.8) | copy-start | bytes 393220
  0.6 10.9 %copy-start.9 = (bf16[2,4,8,8,128]{4,3,2,1,0:T(8,128)(2,1)S(1)}, bf16[2,4,8,8,128]{4,3,2,1,0:T(8,128)(2,1)}, u32[]{:S(2)}) copy-start(bf16[2,4,8,8,128]{4,3,2,1,0:T(8,128)(2,1)} %param.12) | copy-start | bytes 393220
  3.5 5.2 %collective-permute-start = (bf16[288,128]{1,0:T(8,128)(2,1)S(1)}, bf16[288,128]{1,0:T(8,128)(2,1)S(1)}, u32[]{:S(2)}, u32[]{:S(2)}) collective-permute-start(bf16[288,128]{1,0:T(8,128)(2,1)S(1)} %get-tuple-element.52), channel_id=1, source_target_pairs={{64,128},{128,64},{65,129},{129,65},{66,130},{130,66},{67,131},{13... | collective-permute-start | bytes 221192 | tf_op jit(solution)/shard_map/ppermute | solution.py:32
  4.2 6.8 %collective-permute-start.1 = (bf16[288,128]{1,0:T(8,128)(2,1)S(1)}, bf16[288,128]{1,0:T(8,128)(2,1)S(1)}, u32[]{:S(2)}, u32[]{:S(2)}) collective-permute-start(bf16[288,128]{1,0:T(8,128)(2,1)S(1)} %get-tuple-element.53), channel_id=1, source_target_pairs={{0,64},{64,0},{128,192},{192,128},{1,65},{65,1},{129,193},{193,129... | collective-permute-start | bytes 221192 | tf_op jit(solution)/shard_map/ppermute | solution.py:31
  11.4 7.0 %copy-start.10 = (bf16[2,6,8,8,128]{4,0,3,2,1:T(2,128)(2,1)}, bf16[2,6,8,8,128]{4,0,3,2,1:T(2,128)(2,1)S(1)}, u32[]{:S(2)}) copy-start(bf16[2,6,8,8,128]{4,0,3,2,1:T(2,128)(2,1)S(1)} %constant_dynamic-update-slice_fusion) | copy-start | bytes 589828
  11.5 12.7 %copy-start.7 = (bf16[6912,128]{1,0:T(8,128)(2,1)S(1)}, bf16[6912,128]{1,0:T(8,128)(2,1)}, u32[]{:S(2)}) copy-start(bf16[6912,128]{1,0:T(8,128)(2,1)} %param.11) | copy-start | bytes 5308420
  11.6 3.7 %collective-permute-start.2 = (bf16[224,128]{1,0:T(8,128)(2,1)S(1)}, bf16[224,128]{1,0:T(8,128)(2,1)S(1)}, u32[]{:S(2)}, u32[]{:S(2)}) collective-permute-start(bf16[224,128]{1,0:T(8,128)(2,1)S(1)} %get-tuple-element.60), channel_id=1, source_target_pairs={{8,16},{16,8},{24,32},{32,24},{40,48},{48,40},{9,17},{17,9},{25,33... | collective-permute-start | bytes 172040 | tf_op jit(solution)/shard_map/ppermute | solution.py:32
  12.4 3.8 %collective-permute-start.3 = (bf16[224,128]{1,0:T(8,128)(2,1)S(1)}, bf16[224,128]{1,0:T(8,128)(2,1)S(1)}, u32[]{:S(2)}, u32[]{:S(2)}) collective-permute-start(bf16[224,128]{1,0:T(8,128)(2,1)S(1)} %get-tuple-element.61), channel_id=1, source_target_pairs={{0,8},{8,0},{16,24},{24,16},{32,40},{40,32},{48,56},{56,48},{1,9},... | collective-permute-start | bytes 172040 | tf_op jit(solution)/shard_map/ppermute | solution.py:31
  18.4 11.0 %collective-permute-start.5 = (bf16[288,128]{1,0:T(8,128)(2,1)}, bf16[288,128]{1,0:T(8,128)(2,1)S(1)}, u32[]{:S(2)}, u32[]{:S(2)}) collective-permute-start(bf16[288,128]{1,0:T(8,128)(2,1)} %get-tuple-element.48), channel_id=1, source_target_pairs={{0,1},{1,0},{2,3},{3,2},{4,5},{5,4},{6,7},{7,6},{8,9},{9,8},{10,11... | collective-permute-start | bytes 221192 | tf_op jit(solution)/shard_map/ppermute | solution.py:31
  18.5 10.9 %collective-permute-start.4 = (bf16[288,128]{1,0:T(8,128)(2,1)}, bf16[288,128]{1,0:T(8,128)(2,1)}, u32[]{:S(2)}, u32[]{:S(2)}) collective-permute-start(bf16[288,128]{1,0:T(8,128)(2,1)} %get-tuple-element.49), channel_id=1, source_target_pairs={{1,2},{2,1},{3,4},{4,3},{5,6},{6,5},{9,10},{10,9},{11,12},{12,11},... | collective-permute-start | bytes 221192 | tf_op jit(solution)/shard_map/ppermute | solution.py:32
  26.4 4.6 %copy-start.1 = (bf16[3456,256]{1,0:T(8,128)(2,1)S(1)}, bf16[3456,256]{1,0:T(8,128)(2,1)}, u32[]{:S(2)}) copy-start(bf16[3456,256]{1,0:T(8,128)(2,1)} %w_in_hbm.1) | copy-start | bytes 5308420
  26.4 4.6 %copy-start.2 = (bf16[2048,128]{1,0:T(8,128)(2,1)S(1)}, bf16[2048,128]{1,0:T(8,128)(2,1)}, u32[]{:S(2)}) copy-start(bf16[2048,128]{1,0:T(8,128)(2,1)} %w_up_hbm.1) | copy-start | bytes 1572868
  26.4 4.6 %copy-start.4 = (bf16[512,512]{1,0:T(8,128)(2,1)S(1)}, bf16[512,512]{1,0:T(8,128)(2,1)}, u32[]{:S(2)}) copy-start(bf16[512,512]{1,0:T(8,128)(2,1)} %constant.207.clone.perm_ref) | copy-start | bytes 1572868
  41.4 10.5 %copy-start.12 = (bf16[120,128]{1,0:T(8,128)(2,1)S(1)}, bf16[120,128]{1,0:T(8,128)(2,1)}, u32[]{:S(2)}) copy-start(bf16[120,128]{1,0:T(8,128)(2,1)} %get-tuple-element.68) | copy-start | bytes 92164
  41.6 11.7 %collective-permute-start.12 = (f32[16,496,128]{2,1,0:T(8,128)}, f32[16,496,128]{2,1,0:T(8,128)}, u32[]{:S(2)}, u32[]{:S(2)}) collective-permute-start(f32[16,496,128]{2,1,0:T(8,128)} %get-tuple-element.12), channel_id=1, source_target_pairs={{0,8},{8,0},{1,9},{9,1},{2,10},{10,2},{3,11},{11,3},{4,12},{12,4},... | collective-permute-start | bytes 12189704 | tf_op jit(solution)/shard_map/ppermute | solution.py:248
  42.0 4.0 %collective-permute-start.7 = (bf16[128,128]{1,0:T(8,128)(2,1)S(1)}, bf16[128,128]{1,0:T(8,128)(2,1)S(1)}, u32[]{:S(2)}, u32[]{:S(2)}) collective-permute-start(bf16[128,128]{1,0:T(8,128)(2,1)S(1)} %get-tuple-element.86), channel_id=1, source_target_pairs={{0,64},{64,0},{128,192},{192,128},{1,65},{65,1},{129,193},{193,129... | collective-permute-start | bytes 98312 | tf_op jit(solution)/shard_map/ppermute | solution.py:31
  44.1 1.9 %collective-permute-start.6 = (bf16[128,128]{1,0:T(8,128)(2,1)S(1)}, bf16[128,128]{1,0:T(8,128)(2,1)S(1)}, u32[]{:S(2)}, u32[]{:S(2)}) collective-permute-start(bf16[128,128]{1,0:T(8,128)(2,1)S(1)} %get-tuple-element.87), channel_id=1, source_target_pairs={{64,128},{128,64},{65,129},{129,65},{66,130},{130,66},{67,131},{13... | collective-permute-start | bytes 98312 | tf_op jit(solution)/shard_map/ppermute | solution.py:32
  46.6 6.0 %collective-permute-start.8 = (bf16[128,128]{1,0:T(8,128)(2,1)S(1)}, bf16[128,128]{1,0:T(8,128)(2,1)S(1)}, u32[]{:S(2)}, u32[]{:S(2)}) collective-permute-start(bf16[128,128]{1,0:T(8,128)(2,1)S(1)} %get-tuple-element.78), channel_id=1, source_target_pairs={{8,16},{16,8},{24,32},{32,24},{40,48},{48,40},{9,17},{17,9},{25,33... | collective-permute-start | bytes 98312 | tf_op jit(solution)/shard_map/ppermute | solution.py:32
  47.2 5.3 %collective-permute-start.9 = (bf16[128,128]{1,0:T(8,128)(2,1)S(1)}, bf16[128,128]{1,0:T(8,128)(2,1)S(1)}, u32[]{:S(2)}, u32[]{:S(2)}) collective-permute-start(bf16[128,128]{1,0:T(8,128)(2,1)S(1)} %get-tuple-element.79), channel_id=1, source_target_pairs={{0,8},{8,0},{16,24},{24,16},{32,40},{40,32},{48,56},{56,48},{1,9},... | collective-permute-start | bytes 98312 | tf_op jit(solution)/shard_map/ppermute | solution.py:31
  61.0 13.3 %collective-permute-start.21 = (bf16[4,248,128]{2,1,0:T(8,128)(2,1)}, bf16[4,248,128]{2,1,0:T(8,128)(2,1)S(1)}, u32[]{:S(2)}, u32[]{:S(2)}) collective-permute-start(bf16[4,248,128]{2,1,0:T(8,128)(2,1)} %get-tuple-element.32), channel_id=1, source_target_pairs={{0,48},{16,0},{32,16},{48,32},{1,49},{17,1},{33,17},{49,33},{2,50}... | collective-permute-start | bytes 761864 | tf_op jit(solution)/shard_map/ppermute | solution.py:243
  63.9 12.5 %collective-permute-start.20 = (bf16[4,248,128]{2,1,0:T(8,128)(2,1)}, bf16[4,248,128]{2,1,0:T(8,128)(2,1)S(1)}, u32[]{:S(2)}, u32[]{:S(2)}) collective-permute-start(bf16[4,248,128]{2,1,0:T(8,128)(2,1)} %get-tuple-element.33), channel_id=1, source_target_pairs={{0,16},{16,32},{32,48},{48,0},{1,17},{17,33},{33,49},{49,1},{2,18}... | collective-permute-start | bytes 761864 | tf_op jit(solution)/shard_map/ppermute | solution.py:243
  63.9 13.9 %collective-permute-start.19 = (bf16[4,248,128]{2,1,0:T(8,128)(2,1)S(1)}, bf16[4,248,128]{2,1,0:T(8,128)(2,1)}, u32[]{:S(2)}, u32[]{:S(2)}) collective-permute-start(bf16[4,248,128]{2,1,0:T(8,128)(2,1)S(1)} %get-tuple-element.31), channel_id=1, source_target_pairs={{0,32},{16,48},{32,0},{48,16},{1,33},{17,49},{33,1},{49,17},{2,34}... | collective-permute-start | bytes 761864 | tf_op jit(solution)/shard_map/ppermute | solution.py:243
  70.1 14.7 %collective-permute-start.15 = (bf16[4,248,128]{2,1,0:T(8,128)(2,1)S(1)}, bf16[4,248,128]{2,1,0:T(8,128)(2,1)S(1)}, u32[]{:S(2)}, u32[]{:S(2)}) collective-permute-start(bf16[4,248,128]{2,1,0:T(8,128)(2,1)S(1)} %get-tuple-element.29), channel_id=1, source_target_pairs={{0,192},{64,0},{128,64},{192,128},{1,193},{65,1},{129,65},{193,129... | collective-permute-start | bytes 761864 | tf_op jit(solution)/shard_map/ppermute | solution.py:243
  71.2 13.6 %collective-permute-start.14 = (bf16[4,248,128]{2,1,0:T(8,128)(2,1)S(1)}, bf16[4,248,128]{2,1,0:T(8,128)(2,1)S(1)}, u32[]{:S(2)}, u32[]{:S(2)}) collective-permute-start(bf16[4,248,128]{2,1,0:T(8,128)(2,1)S(1)} %get-tuple-element.30), channel_id=1, source_target_pairs={{0,64},{64,128},{128,192},{192,0},{1,65},{65,129},{129,193},{193,1... | collective-permute-start | bytes 761864 | tf_op jit(solution)/shard_map/ppermute | solution.py:243
  74.4 14.6 %collective-permute-start.13 = (bf16[4,248,128]{2,1,0:T(8,128)(2,1)S(1)}, bf16[4,248,128]{2,1,0:T(8,128)(2,1)S(1)}, u32[]{:S(2)}, u32[]{:S(2)}) collective-permute-start(bf16[4,248,128]{2,1,0:T(8,128)(2,1)S(1)} %get-tuple-element.28), channel_id=1, source_target_pairs={{0,128},{64,192},{128,0},{192,64},{1,129},{65,193},{129,1},{193,65... | collective-permute-start | bytes 761864 | tf_op jit(solution)/shard_map/ppermute | solution.py:243
  79.1 14.4 %collective-permute-start.24 = (f32[248,128]{1,0:T(8,128)S(1)}, f32[248,128]{1,0:T(8,128)S(1)}, u32[]{:S(2)}, u32[]{:S(2)}) collective-permute-start(f32[248,128]{1,0:T(8,128)S(1)} %get-tuple-element.38), channel_id=1, source_target_pairs={{0,192},{64,0},{128,64},{192,128},{1,193},{65,1},{129,65},{193,129... | collective-permute-start | bytes 380936 | tf_op jit(solution)/shard_map/ppermute | solution.py:243
  80.2 13.2 %collective-permute-start.22 = (f32[248,128]{1,0:T(8,128)S(1)}, f32[248,128]{1,0:T(8,128)S(1)}, u32[]{:S(2)}, u32[]{:S(2)}) collective-permute-start(f32[248,128]{1,0:T(8,128)S(1)} %get-tuple-element.39), channel_id=1, source_target_pairs={{0,128},{64,192},{128,0},{192,64},{1,129},{65,193},{129,1},{193,65... | collective-permute-start | bytes 380936 | tf_op jit(solution)/shard_map/ppermute | solution.py:243
  84.8 8.7 %collective-permute-start.23 = (f32[248,128]{1,0:T(8,128)S(1)}, f32[248,128]{1,0:T(8,128)S(1)}, u32[]{:S(2)}, u32[]{:S(2)}) collective-permute-start(f32[248,128]{1,0:T(8,128)S(1)} %get-tuple-element.37), channel_id=1, source_target_pairs={{0,64},{64,128},{128,192},{192,0},{1,65},{65,129},{129,193},{193,1... | collective-permute-start | bytes 380936 | tf_op jit(solution)/shard_map/ppermute | solution.py:243
  90.1 5.0 %collective-permute-start.18 = (f32[248,128]{1,0:T(8,128)S(1)}, f32[248,128]{1,0:T(8,128)S(1)}, u32[]{:S(2)}, u32[]{:S(2)}) collective-permute-start(f32[248,128]{1,0:T(8,128)S(1)} %get-tuple-element.35), channel_id=1, source_target_pairs={{0,48},{16,0},{32,16},{48,32},{1,49},{17,1},{33,17},{49,33},{2,50}... | collective-permute-start | bytes 380936 | tf_op jit(solution)/shard_map/ppermute | solution.py:243
  91.3 6.4 %collective-permute-start.16 = (f32[248,128]{1,0:T(8,128)S(1)}, f32[248,128]{1,0:T(8,128)S(1)}, u32[]{:S(2)}, u32[]{:S(2)}) collective-permute-start(f32[248,128]{1,0:T(8,128)S(1)} %get-tuple-element.36), channel_id=1, source_target_pairs={{0,32},{16,48},{32,0},{48,16},{1,33},{17,49},{33,1},{49,17},{2,34}... | collective-permute-start | bytes 380936 | tf_op jit(solution)/shard_map/ppermute | solution.py:243
  93.5 6.1 %collective-permute-start.17 = (f32[248,128]{1,0:T(8,128)S(1)}, f32[248,128]{1,0:T(8,128)S(1)}, u32[]{:S(2)}, u32[]{:S(2)}) collective-permute-start(f32[248,128]{1,0:T(8,128)S(1)} %get-tuple-element.34), channel_id=1, source_target_pairs={{0,16},{16,32},{32,48},{48,0},{1,17},{17,33},{33,49},{49,1},{2,18}... | collective-permute-start | bytes 380936 | tf_op jit(solution)/shard_map/ppermute | solution.py:243
  99.6 37.4 %copy-start.19 = (bf16[2,4,1,4,256]{4,3,2,1,0:T(4,128)(2,1)S(1)}, bf16[2,4,1,4,256]{4,3,2,1,0:T(4,128)(2,1)}, u32[]{:S(2)}) copy-start(bf16[2,4,1,4,256]{4,3,2,1,0:T(4,128)(2,1)} %copy-done.18) | copy-start | bytes 49156
  99.6 37.4 %copy-start.23 = (bf16[2,4,1,4,256]{4,3,2,1,0:T(4,128)(2,1)S(1)}, bf16[2,4,1,4,256]{4,3,2,1,0:T(4,128)(2,1)}, u32[]{:S(2)}) copy-start(bf16[2,4,1,4,256]{4,3,2,1,0:T(4,128)(2,1)} %copy-done.22) | copy-start | bytes 49156
  99.7 5.1 %collective-permute-start.25 = (f32[2,2,62,128]{3,2,1,0:T(8,128)S(1)}, f32[2,2,62,128]{3,2,1,0:T(8,128)S(1)}, u32[]{:S(2)}, u32[]{:S(2)}) collective-permute-start(f32[2,2,62,128]{3,2,1,0:T(8,128)S(1)} %dynamic-slice_bitcast_fusion), channel_id=1, source_target_pairs={{0,1},{1,0},{2,3},{3,2},{4,5},{5,4},{6,7},{7,6},{8,9},{9,8},{10,11... | collective-permute-start | bytes 380936 | tf_op jit(solution)/shard_map/ppermute | solution.py:248
  104.8 5.9 %collective-permute-start.26 = (f32[2,62,128]{2,1,0:T(8,128)S(1)}, f32[2,62,128]{2,1,0:T(8,128)S(1)}, u32[]{:S(2)}, u32[]{:S(2)}) collective-permute-start(f32[2,62,128]{2,1,0:T(8,128)S(1)} %dynamic-slice_bitcast_fusion.7), channel_id=1, source_target_pairs={{0,2},{1,3},{2,0},{3,1},{4,6},{5,7},{6,4},{7,5},{8,10},{9,11},{10,... | collective-permute-start | bytes 190472 | tf_op jit(solution)/shard_map/ppermute | solution.py:248
  110.8 8.1 %collective-permute-start.27 = (f32[62,128]{1,0:T(8,128)S(1)}, f32[62,128]{1,0:T(8,128)S(1)}, u32[]{:S(2)}, u32[]{:S(2)}) collective-permute-start(f32[62,128]{1,0:T(8,128)S(1)} %dynamic-slice_bitcast_fusion.8), channel_id=1, source_target_pairs={{0,4},{1,5},{2,6},{3,7},{4,0},{5,1},{6,2},{7,3},{8,12},{9,13},{10,... | collective-permute-start | bytes 95240 | tf_op jit(solution)/shard_map/ppermute | solution.py:248
  118.9 3.6 %collective-permute-start.28 = (f32[1,128]{1,0:T(1,128)S(1)}, f32[1,128]{1,0:T(1,128)S(1)}, u32[]{:S(2)}, u32[]{:S(2)}) collective-permute-start(f32[1,128]{1,0:T(1,128)S(1)} %bitcast.178), channel_id=1, source_target_pairs={{0,8},{8,0},{1,9},{9,1},{2,10},{10,2},{3,11},{11,3},{4,12},{12,4},... | collective-permute-start | bytes 1544 | tf_op jit(solution)/shard_map/ppermute | solution.py:248
  119.1 6.0 %collective-permute-start.10 = (bf16[192,128]{1,0:T(8,128)(2,1)S(1)}, bf16[192,128]{1,0:T(8,128)(2,1)S(1)}, u32[]{:S(2)}, u32[]{:S(2)}) collective-permute-start(bf16[192,128]{1,0:T(8,128)(2,1)S(1)} %get-tuple-element.64), channel_id=1, source_target_pairs={{1,2},{2,1},{3,4},{4,3},{5,6},{6,5},{9,10},{10,9},{11,12},{12,11},... | collective-permute-start | bytes 147464 | tf_op jit(solution)/shard_map/ppermute | solution.py:32
  122.4 4.2 %collective-permute-start.11 = (bf16[192,128]{1,0:T(8,128)(2,1)S(1)}, bf16[192,128]{1,0:T(8,128)(2,1)S(1)}, u32[]{:S(2)}, u32[]{:S(2)}) collective-permute-start(bf16[192,128]{1,0:T(8,128)(2,1)S(1)} %get-tuple-element.65), channel_id=1, source_target_pairs={{0,1},{1,0},{2,3},{3,2},{4,5},{5,4},{6,7},{7,6},{8,9},{9,8},{10,11... | collective-permute-start | bytes 147464 | tf_op jit(solution)/shard_map/ppermute | solution.py:31
  122.6 4.1 %collective-permute-start.29 = (f32[1,128]{1,0:T(1,128)S(1)}, f32[1,128]{1,0:T(1,128)S(1)}, u32[]{:S(2)}, u32[]{:S(2)}) collective-permute-start(f32[1,128]{1,0:T(1,128)S(1)} %bitcast_add_fusion.7), channel_id=1, source_target_pairs={{0,64},{64,0},{128,192},{192,128},{1,65},{65,1},{129,193},{193,129... | collective-permute-start | bytes 1544 | tf_op jit(solution)/shard_map/ppermute | solution.py:248
  126.7 5.1 %collective-permute-start.30 = (f32[1,128]{1,0:T(1,128)S(1)}, f32[1,128]{1,0:T(1,128)S(1)}, u32[]{:S(2)}, u32[]{:S(2)}) collective-permute-start(f32[1,128]{1,0:T(1,128)S(1)} %add.262), channel_id=1, source_target_pairs={{0,128},{64,192},{128,0},{192,64},{1,129},{65,193},{129,1},{193,65... | collective-permute-start | bytes 1544 | tf_op jit(solution)/shard_map/ppermute | solution.py:248
  131.8 3.5 %collective-permute-start.31 = (f32[1,128]{1,0:T(1,128)S(1)}, f32[1,128]{1,0:T(1,128)S(1)}, u32[]{:S(2)}, u32[]{:S(2)}) collective-permute-start(f32[1,128]{1,0:T(1,128)S(1)} %add.263), channel_id=1, source_target_pairs={{0,16},{16,0},{32,48},{48,32},{1,17},{17,1},{33,49},{49,33},{2,18}... | collective-permute-start | bytes 1544 | tf_op jit(solution)/shard_map/ppermute | solution.py:248
  135.3 5.0 %collective-permute-start.32 = (f32[1,128]{1,0:T(1,128)S(1)}, f32[1,128]{1,0:T(1,128)S(1)}, u32[]{:S(2)}, u32[]{:S(2)}) collective-permute-start(f32[1,128]{1,0:T(1,128)S(1)} %add.264), channel_id=1, source_target_pairs={{0,32},{16,48},{32,0},{48,16},{1,33},{17,49},{33,1},{49,17},{2,34}... | collective-permute-start | bytes 1544 | tf_op jit(solution)/shard_map/ppermute | solution.py:248
  140.4 4.9 %collective-permute-start.33 = (f32[1,128]{1,0:T(1,128)S(1)}, f32[1,128]{1,0:T(1,128)S(1)}, u32[]{:S(2)}, u32[]{:S(2)}) collective-permute-start(f32[1,128]{1,0:T(1,128)S(1)} %add.265), channel_id=1, source_target_pairs={{0,1},{1,0},{2,3},{3,2},{4,5},{5,4},{6,7},{7,6},{8,9},{9,8},{10,11... | collective-permute-start | bytes 1544 | tf_op jit(solution)/shard_map/ppermute | solution.py:248
  141.8 6.7 %copy-start.17 = (bf16[2,4,1,4,256]{4,0,3,2,1:T(2,128)(2,1)S(1)}, bf16[2,4,1,4,256]{4,0,3,2,1:T(2,128)(2,1)}, u32[]{:S(2)}) copy-start(bf16[2,4,1,4,256]{4,0,3,2,1:T(2,128)(2,1)} %copy.105) | copy-start | bytes 49156
  141.8 6.7 %copy-start.21 = (bf16[2,4,1,4,256]{4,0,3,2,1:T(2,128)(2,1)S(1)}, bf16[2,4,1,4,256]{4,0,3,2,1:T(2,128)(2,1)}, u32[]{:S(2)}) copy-start(bf16[2,4,1,4,256]{4,0,3,2,1:T(2,128)(2,1)} %copy-done.20) | copy-start | bytes 49156
  145.4 4.7 %collective-permute-start.34 = (f32[1,128]{1,0:T(1,128)S(1)}, f32[1,128]{1,0:T(1,128)S(1)}, u32[]{:S(2)}, u32[]{:S(2)}) collective-permute-start(f32[1,128]{1,0:T(1,128)S(1)} %add.266), channel_id=1, source_target_pairs={{0,2},{1,3},{2,0},{3,1},{4,6},{5,7},{6,4},{7,5},{8,10},{9,11},{10,... | collective-permute-start | bytes 1544 | tf_op jit(solution)/shard_map/ppermute | solution.py:248
  150.0 7.4 %collective-permute-start.35 = (f32[1,128]{1,0:T(1,128)S(1)}, f32[1,128]{1,0:T(1,128)S(1)}, u32[]{:S(2)}, u32[]{:S(2)}) collective-permute-start(f32[1,128]{1,0:T(1,128)S(1)} %add.267), channel_id=1, source_target_pairs={{0,4},{1,5},{2,6},{3,7},{4,0},{5,1},{6,2},{7,3},{8,12},{9,13},{10,... | collective-permute-start | bytes 1544 | tf_op jit(solution)/shard_map/ppermute | solution.py:248
  (14 other events, 39.5 us)
where the time goes:
time: 160 us; the launch traced here: 159 us
  starting transfers between devices  66.7 us (42%)
  waiting for transfers between devices  42.3 us (26%)
  local copies, waits for them, and re-layouts  22.6 us (14%)
  other arithmetic  12.3 us (8%)
  Pallas kernels  8.12 us (5%)
  matrix products  4.66 us (3%)
  between operations  2.74 us (2%)
    ppermute x12, waiting for transfers between devices, paired(): return lax.ppermute(array, axis, [(i, i ^ bit) for i in range(count)])  22.1 us
    ppermute x12, starting transfers between devices, paired(): return lax.ppermute(array, axis, [(i, i ^ bit) for i in range(count)])  21 us
    ppermute x12, starting transfers between devices, turned(): lax.ppermute(array, axis, [(i, (i + shift) % count) for i in range(count)])  20.2 us
    ppermute x6, starting transfers between devices, traded_faces(): one = lax.ppermute(jnp.where(even, lasts, firsts), axis, first_pairs)  13.7 us
    ppermute x12, waiting for transfers between devices, turned(): lax.ppermute(array, axis, [(i, (i + shift) % count) for i in range(count)])  11.9 us
    ppermute x6, starting transfers between devices, traded_faces(): two = lax.ppermute(jnp.where(even, firsts, lasts), axis, second_pairs)  11.8 us
    pallas_call x1, Pallas kernels, gradients(): pl.pallas_call(_gradients_kernel, out_shape=(shape((16, 496, 128), F32),...  8.12 us
    ppermute x6, waiting for transfers between devices, traded_faces(): one = lax.ppermute(jnp.where(even, lasts, firsts), axis, first_pairs)  5.99 us
  transfers between devices with their start and end apart: 36, of which 19 were waited for; matrix products, arithmetic and copies ran while one was open for 13% of the time, Pallas kernels for 0%

commit v1 on v0

v1 whole, which is shorter than its diff:
```python
import itertools

import jax
import jax.numpy as jnp
import numpy as np
from jax import lax
from jax.experimental import pallas as pl
from jax.experimental.pallas import tpu as pltpu
from jax.sharding import Mesh, PartitionSpec as P

F32 = jnp.float32
BF16 = jnp.bfloat16
PARAMS = 2031616


def conv_forward(padded, weight):
    kernel = weight.reshape(3, 3, 3, padded.shape[4], -1)
    return lax.conv_general_dilated(
        padded, kernel, (1, 1, 1), "VALID",
        dimension_numbers=("NXYZC", "XYZIO", "NXYZC"), preferred_element_type=F32,
    )


def conv_transpose(padded, weight):
    kernel = weight.reshape(3, 3, 3, -1, padded.shape[4])[::-1, ::-1, ::-1]
    return lax.conv_general_dilated(
        padded, kernel, (1, 1, 1), "VALID",
        dimension_numbers=("NXYZC", "XYZOI", "NXYZC"), preferred_element_type=F32,
    )


def spread(volume):
    samples, size_x, size_y, size_z, chans = volume.shape
    wide = jnp.broadcast_to(
        volume[:, :, None, :, None, :, None, :], (samples, size_x, 2, size_y, 2, size_z, 2, chans)
    )
    return wide.reshape(samples, 2 * size_x, 2 * size_y, 2 * size_z, chans)


def up_conv(bottom, w_up):
    samples, size_x, size_y, size_z, wide = bottom.shape
    kernel = w_up.reshape(2, 2, 2, wide, -1)
    result = jnp.einsum("sijkc,abeco->siajbkeo", bottom, kernel, preferred_element_type=F32)
    return result.reshape(samples, 2 * size_x, 2 * size_y, 2 * size_z, -1)


def _select_pooled():
    sel = np.zeros((9, 4, 4, 48), np.float32)
    for dy, dz, y, z in itertools.product(range(3), range(3), range(4), range(4)):
        line, k = y + dy, z + dz - 1
        sel[3 * dy + dz, y, z, 24 + line if k < 0 else 32 + line if k > 3 else line * 4 + k] = 1
    return sel.reshape(144, 48)


def _fine_from_blocks():
    perm = np.zeros((128, 128), np.float32)
    for a, y, z in itertools.product(range(2), range(8), range(8)):
        perm[(a * 8 + y) * 8 + z, (a * 4 + (y % 2) * 2 + z % 2) * 16 + (y // 2) * 4 + z // 2] = 1
    return perm


def _picks(sources, width):
    picks = np.zeros((len(sources), width), np.float32)
    picks[np.arange(len(sources)), sources] = 1
    return picks


def _at_y(s, x, y, z):
    line = s * 2 + x
    return 64 + line * 4 + z if y < 0 else 80 + line * 4 + z if y > 3 else (line * 4 + y) * 4 + z


def _at_x(s, x, y, z):
    line = s * 6 + y + 1
    return 96 + line * 4 + z if x < 0 else 144 + line * 4 + z if x > 1 else _at_y(s, x, y, z)


def _at_z(s, x, y, z):
    line = (s * 4 + x + 1) * 6 + y + 1
    return 192 + line if z < 0 else 240 + line if z > 3 else _at_x(s, x, y, z)


def _pool_of():
    pool = np.zeros((16, 128), np.float32)
    for a, y, z in itertools.product(range(2), range(8), range(8)):
        pool[(y // 2) * 4 + z // 2, (a * 8 + y) * 8 + z] = 0.125
    return pool


S2, X2, Y4, Z4 = range(2), range(2), range(4), range(4)
X4, Y6, Z6 = range(-1, 3), range(-1, 5), range(-1, 5)
Y_FACES = _picks([_at_y(s, x, y, z) for y in (0, 3) for s in S2 for x in X2 for z in Z4], 64)
X_FACES = _picks([_at_y(s, x, y, z) for x in (0, 1) for s in S2 for y in Y6 for z in Z4], 96)
Z_FACES = _picks([_at_x(s, x, y, z) for z in (0, 3) for s in S2 for x in X4 for y in Y6], 192)
POOL_OF = _pool_of()
POOL_Y_FACES = _picks([p * 16 + y * 4 + z for y in (0, 3) for p in range(8) for z in Z4], 128)
POOL_GROW_Y = _picks(
    [128 + p * 4 + z if y < 0 else 160 + p * 4 + z if y > 3 else p * 16 + y * 4 + z for p in range(8) for y in Y6 for z in Z4], 192
)
POOL_Z_FACES = _picks([(p * 6 + y) * 4 + z if y < 6 else 192 for z in (0, 3) for p in range(8) for y in range(8)], 193)[:, :192]
PADDED = _picks([_at_z(s, x, y, z) for s in S2 for x in X4 for y in Y6 for z in Z6], 288)


def _dot(a, b, contract=((1,), (0,))):
    return lax.dot_general(a, b, (contract, ((), ())), preferred_element_type=F32)


def _flag(condition):
    return jnp.where(condition, 1.0, 0.0)


def _wide(rows, count):
    return jnp.concatenate([rows[i * count : (i + 1) * count] for i in range(4)], axis=1)


def _call(kernel, outs, *args, scratch=()):
    vmem = pl.BlockSpec(memory_space=pltpu.VMEM)
    return pl.pallas_call(
        kernel,
        out_shape=tuple(jax.ShapeDtypeStruct(shape, kind) for shape, kind in outs),
        in_specs=[pl.BlockSpec(memory_space=pltpu.SMEM)] + [vmem] * (len(args) - 1),
        out_specs=(vmem,) * len(outs),
        scratch_shapes=[pltpu.VMEM(shape, F32) for shape in scratch],
        compiler_params=pltpu.CompilerParams(vmem_limit_bytes=24 * 1024 * 1024),
        cost_estimate=pl.CostEstimate(flops=1_000_000, bytes_accessed=4_000_000, transcendentals=0),
    )(*args)


def _sides(place_index, here, there):
    even = _flag(place_index % 2 == 0)
    here, there = here[...].astype(F32), there[...].astype(F32)
    return there * even + here * (1.0 - even), here * even + there * (1.0 - even)


def _pack(place_index, first, last, here_ref, there_ref):
    even = _flag(place_index % 2 == 0)
    here_ref[...] = (last * even + first * (1.0 - even)).astype(BF16)
    there_ref[...] = (first * even + last * (1.0 - even)).astype(BF16)


def _pool_kernel(place_ref, pool_of_ref, act_ref, cot_ref, pooled_ref, here_ref, there_ref):
    planes = [_dot(pool_of_ref[...], act_ref[g * 128 : (g + 1) * 128, :]) for g in range(4)]
    pooled = jnp.concatenate(planes, axis=0).astype(BF16)
    pooled_ref[...] = pooled

    def face(x):
        fine = [ref[s * 256 + x * 192 : s * 256 + x * 192 + 64, :] for ref in (act_ref, cot_ref) for s in range(2)]
        return jnp.concatenate(fine + [pooled[s * 32 + x * 16 : s * 32 + x * 16 + 16] for s in range(2)], axis=0).astype(F32)

    _pack(place_ref[0], face(0), face(1), here_ref, there_ref)


def _grow_x_kernel(
    place_ref, pool_faces_ref, act_ref, cot_ref, pooled_ref, got_here, got_there,
    act_out, cot_out, pooled_out, here_ref, there_ref,
):
    low, high = _sides(place_ref[0], got_here, got_there)
    firsts, lasts = [], []
    for i, (ref, out) in enumerate(((act_ref, act_out), (cot_ref, cot_out))):
        fine = ref[...].astype(F32)
        parts = []
        for s in range(2):
            at_face = slice(i * 128 + s * 64, i * 128 + s * 64 + 64)
            parts += [low[at_face], fine[s * 256 : (s + 1) * 256], high[at_face]]
        grown = jnp.concatenate(parts, axis=0)
        out[...] = grown
        firsts += [grown[p * 64 : p * 64 + 8] for p in range(12)]
        lasts += [grown[p * 64 + 56 : p * 64 + 64] for p in range(12)]
    pooled = pooled_ref[...].astype(F32)
    parts = []
    for s in range(2):
        at_face = slice(256 + s * 16, 272 + s * 16)
        parts += [low[at_face], pooled[s * 32 : (s + 1) * 32], high[at_face]]
    grown = jnp.concatenate(parts, axis=0).astype(BF16)
    pooled_out[...] = grown
    faces = _dot(pool_faces_ref[...], grown)
    first = jnp.concatenate(firsts + [faces[0:32]], axis=0)
    last = jnp.concatenate(lasts + [faces[32:64]], axis=0)
    _pack(place_ref[2], first, last, here_ref, there_ref)


def _grow_y_kernel(
    place_ref, pool_grow_ref, pool_faces_ref, act_ref, cot_ref, pooled_ref, got_here, got_there,
    act_out, cot_out, pooled_out, here_ref, there_ref,
):
    low, high = _sides(place_ref[2], got_here, got_there)
    firsts, lasts = [], []
    for i, (ref, out) in enumerate(((act_ref, act_out), (cot_ref, cot_out))):
        for p in range(12):
            at_face = slice(i * 96 + p * 8, i * 96 + p * 8 + 8)
            out[p * 80 : p * 80 + 8, :] = low[at_face]
            out[p * 80 + 8 : p * 80 + 72, :] = ref[p * 64 : (p + 1) * 64, :]
            out[p * 80 + 72 : p * 80 + 80, :] = high[at_face]
        firsts.append(out[pl.ds(0, 120, 8), :])
        lasts.append(out[pl.ds(7, 120, 8), :])
    rows = jnp.concatenate([pooled_ref[...], low[192:224].astype(BF16), high[192:224].astype(BF16)], axis=0)
    grown = _dot(pool_grow_ref[...], rows)
    pooled_out[...] = grown
    faces = _dot(pool_faces_ref[...], grown.astype(BF16))
    first = jnp.concatenate(firsts + [faces[0:64]], axis=0)
    last = jnp.concatenate(lasts + [faces[64:128]], axis=0)
    _pack(place_ref[3], first, last, here_ref, there_ref)


def _grow_z_kernel(place_ref, act_ref, got_here, got_there, out_ref, lines):
    low, high = _sides(place_ref[3], got_here, got_there)
    lines[:, 8:16, :] = act_ref[...].reshape(120, 8, 128)
    lines[:, 7:8, :] = low[0:120][:, None, :]
    lines[:, 16:17, :] = high[0:120][:, None, :]
    out_ref[...] = lines[:, 7:17, :].astype(BF16)


def traded(here, there, axis):
    count = lax.axis_size(axis)
    first_pairs = [(i, i ^ 1) for i in range(count)]
    second_pairs = [(i, j) for i in range(count) for j in [((i + 1) ^ 1) - 1] if 0 <= j < count]
    return lax.ppermute(here, axis, first_pairs), lax.ppermute(there, axis, second_pairs)


def extended(place, act, cot):
    rows, f32_rows = lambda n: ((n, 128), BF16), lambda n: ((n, 128), F32)
    pooled, *faces = _call(_pool_kernel, (rows(64), rows(288), rows(288)), place, jnp.asarray(POOL_OF, BF16), act, cot)
    outs = (f32_rows(768), f32_rows(768), rows(128), rows(224), rows(224))
    act, cot, pooled, *faces = _call(
        _grow_x_kernel, outs, place, jnp.asarray(POOL_Y_FACES, BF16), act, cot, pooled, *traded(*faces, "gx")
    )
    outs = (f32_rows(960), f32_rows(960), f32_rows(192), rows(304), rows(304))
    act, cot, pooled, *faces = _call(
        _grow_y_kernel, outs, place, jnp.asarray(POOL_GROW_Y, BF16), jnp.asarray(POOL_Z_FACES, BF16),
        act, cot, pooled, *traded(*faces, ("x", "core")),
    )
    return act, cot, pooled, traded(*faces, "gz")


def _gradients_kernel(
    place_ref, act_ref, cot_ref, pool_ref, got_here, got_there, sel_ref, perm_ref, perm_t_ref, y_faces_ref,
    w_in_hbm, w_back_hbm, w_up_hbm,
    keep_ref, send_ref, coarse_ref, d_act_ref,
    w_in, w_back, w_up, lines, shifted, pooled, spaced, sums, sem_in, sem_out,
):
    loads = [
        pltpu.make_async_copy(source, target, sem_in.at[i])
        for i, (source, target) in enumerate(((w_in_hbm, w_in), (w_up_hbm, w_up), (w_back_hbm, w_back)))
    ]
    for load in loads:
        load.start()
    core = place_ref[2]
    side = (core, 1 - core)

    def put(row, value, stride=1):
        done, count = 0, value.shape[0]
        while done < count:
            first = row + stride * done
            block = first // 496
            here = min(count - done, -((first - 496 * (block + 1)) // stride))
            start = block // 2 * 496 + first % 496
            where = pl.ds(start, here) if stride == 1 else pl.ds(start, here, stride)
            sums[side[block % 2], where, :] = value[done : done + here]
            done += here

    def ship(index, first, last):
        copies = [
            pltpu.make_async_copy(sums.at[i, pl.ds(first, end - first)], target.at[pl.ds(first, end - first)], sem_out.at[index, i])
            for i, (target, end) in enumerate(((keep_ref, min(last, 7936)), (send_ref, last)))
            if end > first
        ]
        for copy in copies:
            copy.start()
        return copies

    low, high = _sides(place_ref[3], got_here, got_there)
    lines[:, 8:16, :] = cot_ref[...].reshape(120, 8, 128)
    lines[:, 7:8, :] = low[120:240][:, None, :]
    lines[:, 16:17, :] = high[120:240][:, None, :]
    for dz in range(3):
        window = lines[:, 7 + dz : 15 + dz, :].reshape(2, 6, 10, 8, 128)
        for dy in range(3):
            u = 8 - 3 * dy - dz
            shifted[:, :, :, u * 128 : (u + 1) * 128] = window[:, :, dy : dy + 8].reshape(2, 6, 64, 128).astype(BF16)

    for g in range(8):
        at_face = slice(240 + g * 8, 248 + g * 8)
        plane = [pool_ref[g * 24 : (g + 1) * 24, :], low[at_face], high[at_face], jnp.zeros((8, 128), F32)]
        picked = _dot(sel_ref[...], jnp.concatenate(plane, axis=0).astype(BF16))
        for u in range(9):
            pooled[g // 4, g % 4, :, u * 128 : (u + 1) * 128] = picked[u * 16 : (u + 1) * 16].astype(BF16)
    loads[0].wait()
    before = jnp.zeros((64, 256), F32)
    for dx in range(3):
        before += _dot(pooled[:, dx : dx + 2].reshape(64, 1152), w_in[dx * 1152 : (dx + 1) * 1152, :])
    squash = 1.0 / (1.0 + jnp.exp(-before))
    bottom32 = (before * squash).astype(BF16).astype(F32)
    bottom = bottom32.astype(BF16)
    loads[1].wait()
    parts = [_dot(bottom, w_up[p * 256 : (p + 1) * 256, :]).astype(BF16) for p in range(8)]
    upward = jnp.concatenate(
        [_dot(perm_ref[...], jnp.concatenate([p[g * 16 : (g + 1) * 16] for p in parts], axis=0)) for g in range(4)], axis=0
    )

    loads[2].wait()
    d_joined = jnp.zeros((512, 256), F32)
    for dx in range(3):
        d_joined += _dot(shifted[:, dx : dx + 4].reshape(512, 1152), w_back[(2 - dx) * 1152 : (3 - dx) * 1152, :])
    d_act_ref[...] = d_joined[:, :128]

    joined_t = jnp.concatenate([act_ref[...].astype(F32).T, upward.T], axis=0).astype(BF16)
    for dx in range(3):
        grad = _dot(joined_t, shifted[:, dx : dx + 4].reshape(512, 1152))
        for u in range(9):
            put(8960 + (18 - 9 * dx + u) * 256, grad[:, u * 128 : (u + 1) * 128])
    copies = ship(0, 4960, 7936)

    d_upward = d_joined[:, 128:].astype(BF16)
    planes = [_dot(perm_t_ref[...], d_upward[g * 128 : (g + 1) * 128]).astype(BF16) for g in range(4)]
    blocks = [jnp.concatenate([plane[p * 16 : (p + 1) * 16] for plane in planes], axis=0) for p in range(8)]
    d_bottom = jnp.zeros((64, 256), F32)
    for p in range(8):
        d_bottom += _dot(blocks[p], w_up[p * 256 : (p + 1) * 256, :], ((1,), (1,)))
    bottom_t = bottom32.T.astype(BF16)
    for p in range(8):
        put(6912 + p * 256, _dot(bottom_t, blocks[p]))
    slope = (d_bottom * squash * (1.0 + before * (1.0 - squash))).astype(BF16)
    coarse = jnp.concatenate([bottom, slope], axis=1)
    coarse_ref[...] = coarse
    faces = _dot(y_faces_ref[...], coarse)
    for lane in range(4):
        sums[1, 7936 + lane * 32 : 7968 + lane * 32, :] = faces[:, lane * 128 : (lane + 1) * 128]
    copies += ship(1, 7936, 8064)

    spaced[...] = jnp.zeros((128, 768), BF16)
    for s in range(2):
        for dx in range(3):
            spaced[s * 64 + dx * 16 : s * 64 + dx * 16 + 32, dx * 256 : (dx + 1) * 256] = slope[s * 32 : (s + 1) * 32]
    for u in range(9):
        picked_t = pooled[:, :, :, u * 128 : (u + 1) * 128].reshape(128, 128).astype(F32).T.astype(BF16)
        grad = _dot(picked_t, spaced[...])
        for dx in range(3):
            for h in range(2):
                put((9 * dx + u) * 256 + h, grad[:, dx * 256 + h * 128 : dx * 256 + (h + 1) * 128], 2)
    copies += ship(2, 0, 4960)
    for copy in copies:
        copy.wait()


def gradients(place, act, cot, pool, got_here, got_there, w_in, w_back, w_up):
    shape = jax.ShapeDtypeStruct
    vmem, hbm = pl.BlockSpec(memory_space=pltpu.VMEM), pl.BlockSpec(memory_space=pltpu.HBM)
    return pl.pallas_call(
        _gradients_kernel,
        out_shape=(
            shape((7936, 128), F32), shape((8064, 128), F32), shape((64, 512), BF16), shape((512, 128), F32),
        ),
        in_specs=[pl.BlockSpec(memory_space=pltpu.SMEM)] + [vmem] * 9 + [hbm] * 3,
        out_specs=(vmem,) * 4,
        scratch_shapes=[
            pltpu.VMEM((3456, 256), BF16), pltpu.VMEM((3456, 256), BF16), pltpu.VMEM((2048, 128), BF16),
            pltpu.VMEM((120, 24, 128), F32), pltpu.VMEM((2, 6, 64, 1152), BF16),
            pltpu.VMEM((2, 4, 16, 1152), BF16), pltpu.VMEM((128, 768), BF16),
            pltpu.VMEM((2, 8064, 128), F32),
            pltpu.SemaphoreType.DMA((3,)), pltpu.SemaphoreType.DMA((3, 2)),
        ],
        compiler_params=pltpu.CompilerParams(vmem_limit_bytes=36 * 1024 * 1024),
        cost_estimate=pl.CostEstimate(flops=2_500_000_000, bytes_accessed=16_000_000, transcendentals=16384),
    )(
        place, act, cot, pool, got_here, got_there,
        jnp.asarray(_select_pooled(), BF16), jnp.asarray(_fine_from_blocks(), BF16), jnp.asarray(_fine_from_blocks().T, BF16),
        jnp.asarray(Y_FACES, BF16), w_in, w_back, w_up,
    )


def at(array, index, axis):
    return lax.dynamic_index_in_dim(array, index, axis, keepdims=False)


def turned(array, axis, shift):
    count = lax.axis_size(axis)
    return lax.ppermute(array, axis, [(i, (i + shift) % count) for i in range(count)])


def paired(array, axis, bit):
    count = lax.axis_size(axis)
    return lax.ppermute(array, axis, [(i, i ^ bit) for i in range(count)])


def _split_kernel(place_ref, keep_ref, got_ref, one_ref, two_ref, faces_ref, *sends):
    for s in range(4):
        rows = [pl.multiple_of(((place_ref[0] + s) % 4 * 4 + j) * 496, 8) for j in range(4)]
        one = jnp.concatenate([keep_ref[pl.ds(r, 248), :] + got_ref[pl.ds(r, 248), :] for r in rows], axis=0)
        rows = [pl.multiple_of((j * 4 + (place_ref[1] + s) % 4) * 496 + 248, 8) for j in range(4)]
        two = jnp.concatenate([keep_ref[pl.ds(r, 248), :] + got_ref[pl.ds(r, 248), :] for r in rows], axis=0)
        if s == 0:
            one_ref[...] = one
            two_ref[...] = two
        else:
            sends[s - 1][...] = one.astype(BF16)
            sends[s + 2][0:992, :] = two.astype(BF16)
    faces = got_ref[7936:8064, :].astype(BF16)
    faces_ref[...] = faces
    for lane in range(4):
        sends[3][992 + lane * 16 : 1008 + lane * 16, :] = faces[lane * 32 + 16 : lane * 32 + 32]
        sends[5][992 + lane * 16 : 1008 + lane * 16, :] = faces[lane * 32 : lane * 32 + 16]


def _second_kernel(
    place_ref, coarse_ref, faces_ref, x_faces_ref, one_ref, one_1, one_2, one_3, two_ref, two_1, two_2, two_3,
    grown_ref, own_one, own_two, send_one_1, send_one_2, send_one_3, send_two_1, send_two_2, send_two_3, one, two,
):
    gx, x, core = place_ref[0], place_ref[1], place_ref[2]
    one[...] = one_ref[...] + (one_1[...].astype(F32) + one_2[...].astype(F32) + one_3[...].astype(F32))
    two[...] = two_ref[...] + (two_1[0:992, :].astype(F32) + two_2[...].astype(F32) + two_3[0:992, :].astype(F32))
    for s, (to_one, to_two) in enumerate(
        ((own_one, own_two), (send_one_1, send_two_1), (send_one_2, send_two_2), (send_one_3, send_two_3))
    ):
        to_one[...] = one[pl.ds(pl.multiple_of((x + s) % 4 * 248, 8), 248), :]
        to_two[0:248, :] = two[pl.ds(pl.multiple_of((gx + s) % 4 * 248, 8), 248), :]
    near = faces_ref[...].astype(F32)
    near_first = jnp.concatenate([near[i * 32 : i * 32 + 16] for i in range(4)], axis=0)
    near_last = jnp.concatenate([near[i * 32 + 16 : i * 32 + 32] for i in range(4)], axis=0)
    low = two_1[992:1056, :].astype(F32) * _flag((core == 0) & (x > 0)) + near_last * _flag(core == 1)
    high = two_3[992:1056, :].astype(F32) * _flag((core == 1) & (x < 3)) + near_first * _flag(core == 0)
    grown = jnp.concatenate([coarse_ref[...], _wide(low, 16).astype(BF16), _wide(high, 16).astype(BF16)], axis=0)
    grown_ref[...] = grown
    faces = _dot(x_faces_ref[...], grown)
    for lane in range(4):
        send_two_1[248 + lane * 48 : 296 + lane * 48, :] = faces[48:96, lane * 128 : (lane + 1) * 128]
        send_two_3[248 + lane * 48 : 296 + lane * 48, :] = faces[0:48, lane * 128 : (lane + 1) * 128]


def _third_kernel(
    place_ref, grown_ref, z_faces_ref, one_ref, one_1, one_2, one_3, two_ref, two_1, two_2, two_3,
    grown_out, keep_ref, send_ref, other_ref, rows, chunks,
):
    gx, gz = place_ref[0], place_ref[3]
    rows[0:248, :] = one_ref[...] + (one_1[...] + one_2[...] + one_3[...])
    rows[248:496, :] = two_ref[...] + (two_1[0:248, :] + two_2[...] + two_3[0:248, :])
    chunks[...] = jnp.zeros((2, 256, 128), F32)
    for r, q, p in itertools.product(range(2), repeat=3):
        chunk, place = 4 * r + 2 * q + p, ((q ^ r) * 2 + r) * 64
        chunks[p ^ r, place : place + 62, :] = rows[chunk * 62 : (chunk + 1) * 62, :]
    half = (gz + gz // 4) % 2
    keep_ref[...] = chunks[half]
    send_ref[0:256, :] = chunks[1 - half]
    low = _wide(two_1[248:440, :] * _flag(gx > 0), 48).astype(BF16)
    high = _wide(two_3[248:440, :] * _flag(gx < 3), 48).astype(BF16)
    grown = jnp.concatenate([grown_ref[...], low, high], axis=0)
    grown_out[...] = grown
    faces = _dot(z_faces_ref[...], grown)
    even = _flag(gz % 2 == 0)
    here = faces[48:96] * even + faces[0:48] * (1.0 - even)
    there = (faces[0:48] * even + faces[48:96] * (1.0 - even)).astype(BF16)
    for lane in range(4):
        send_ref[256 + lane * 48 : 304 + lane * 48, :] = here[:, lane * 128 : (lane + 1) * 128]
        other_ref[lane * 48 : (lane + 1) * 48, :] = there[:, lane * 128 : (lane + 1) * 128]


def _fourth_kernel(place_ref, grown_ref, padded_ref, keep_ref, got_ref, other_ref, bottom_ref, slope_ref, keep_out, send_out, both):
    gz = place_ref[3]
    mine = keep_ref[...] + got_ref[0:256, :]
    both[0] = mine[0:128]
    both[1] = mine[128:256]
    half = (gz // 2 + gz // 4) % 2
    keep_out[...] = both[half]
    send_out[...] = both[1 - half]
    even = _flag(gz % 2 == 0)
    here, there = got_ref[256:448, :], other_ref[...].astype(F32)
    low = _wide(there * even + here * (1.0 - even), 48).astype(BF16)
    high = _wide(here * even + there * (1.0 - even), 48).astype(BF16)
    padded = _dot(padded_ref[...], jnp.concatenate([grown_ref[...], low, high], axis=0)).astype(BF16)
    bottom_ref[...] = padded[:, 0:256]
    slope_ref[...] = padded[:, 256:512]


def scattered_sum(place, keep, send, coarse):
    gz = lax.axis_index("gz")
    half, quarter = ((992, 128), BF16), ((248, 128), F32)
    half_and_faces, quarter_and_faces = ((1056, 128), BF16), ((440, 128), F32)
    got = paired(send, "core", 1)
    outs = (((992, 128), F32),) * 2 + (((128, 128), BF16),) + (half,) * 3 + (half_and_faces, half, half_and_faces)
    one, two, faces, *sends = _call(_split_kernel, outs, place, keep, got)
    got_one = [turned(sends[s - 1], "gx", s) for s in (1, 2, 3)]
    got_two = [turned(sends[s + 2], "x", s) for s in (1, 2, 3)]
    outs = (((96, 512), BF16),) + (quarter,) * 5 + (quarter_and_faces, quarter, quarter_and_faces)
    grown, one, two, *sends = _call(
        _second_kernel, outs, place, coarse, faces, jnp.asarray(X_FACES, BF16), one, *got_one, two, *got_two,
        scratch=((992, 128), (992, 128)),
    )
    got_one = [turned(sends[s - 1], "x", s) for s in (1, 2, 3)]
    got_two = [turned(sends[s + 2], "gx", s) for s in (1, 2, 3)]
    outs = (((192, 512), BF16), ((256, 128), F32), ((448, 128), F32), ((192, 128), BF16))
    grown, keep, send, other = _call(
        _third_kernel, outs, place, grown, jnp.asarray(Z_FACES, BF16), one, *got_one, two, *got_two,
        scratch=((496, 128), (2, 256, 128)),
    )
    got = paired(send, "gz", 1)
    other = lax.ppermute(other, "gz", [(i, j) for i in range(8) for j in [((i + 1) ^ 1) - 1] if 0 <= j < 8])
    outs = (((288, 256), BF16),) * 2 + (((128, 128), F32),) * 2
    bottom_pad, slope_pad, keep, send = _call(
        _fourth_kernel, outs, place, grown, jnp.asarray(PADDED, BF16), keep, got, other, scratch=((2, 128, 128),)
    )
    mine = keep + paired(send, "gz", 2)
    mine = mine + paired(mine, "gz", 7)
    squares = jnp.sum(mine * mine, axis=0, keepdims=True)
    pads = [p.reshape(2, 4, 6, 6, 256) for p in (bottom_pad, slope_pad)]
    return at(mine.reshape(2, 64, 128), gz // 4, 0)[:62], squares, pads


def local(activation, w_in, w_up, w_out, cotangent):
    place = jnp.stack([lax.axis_index(a) for a in ("gx", "x", "core", "gz")]).astype(jnp.int32)
    own = activation.reshape(512, 128)
    act, cot, pooled, faces = extended(place, own, cotangent.reshape(512, 128))
    w_back = w_out.reshape(27, 256, 128).transpose(0, 2, 1).reshape(3456, 256)
    keep, send, coarse, d_direct = gradients(place, own, cot, pooled, *faces, w_in, w_back, w_up)
    mine, total, (bottom_pad, slope_pad) = scattered_sum(place, keep, send, coarse)

    def rounds(value, *others, axis, masks):
        for mask in masks:
            value = value + paired(value, axis, mask)
        return lax.optimization_barrier((value, *others))

    total, bottom_pad, act = rounds(total, bottom_pad, act, axis="core", masks=(1,))
    (active_pad,) = _call(_grow_z_kernel, (((120, 10, 128), BF16),), place, act, *faces, scratch=((120, 24, 128),))
    active_pad = active_pad.reshape(2, 6, 10, 10, 128)
    upward_pad = up_conv(bottom_pad, w_up).astype(BF16)[:, 1:-1, 1:-1, 1:-1]
    joined_pad = jnp.concatenate([active_pad, upward_pad], axis=4)
    total, joined_pad = rounds(total, joined_pad, axis="gx", masks=(1,))
    output = conv_forward(joined_pad, w_out).astype(BF16)
    total, output, slope_pad = rounds(total, output, slope_pad, axis="gx", masks=(3,))
    d_pooled = conv_transpose(slope_pad, w_in)
    d_activation = (d_direct.reshape(activation.shape) + spread(d_pooled) * 0.125).astype(BF16)
    total, d_activation = rounds(total, d_activation, axis="x", masks=(1,))
    (total,) = rounds(total, axis="x", masks=(3,))
    (total,) = rounds(total, axis="gz", masks=(1, 2))
    factor = jnp.minimum(1.0, jnp.sqrt(PARAMS / (jnp.sum(total) + 1e-06)))
    return (output, d_activation, (mine * factor).reshape(-1))


def solution(mesh):
    gx, gy, gz = mesh.devices.shape
    split = Mesh(mesh.devices.reshape(gx, gy // 2, 2, gz), ("gx", "x", "core", "gz"))
    cells = P(None, "gx", ("x", "core"), "gz", None)
    return jax.shard_map(
        local, mesh=split, in_specs=(cells, P(), P(), P(), cells),
        out_specs=(cells, cells, P(("gx", "x", "core", "gz"))), check_vma=False,
    )
```

time: 160 us -> 143 us (0.89)
  other arithmetic: 12.3 us -> 2.24 us
  local copies, waits for them, and re-layouts: 22.6 us -> 14.4 us
  Pallas kernels: 8.12 us -> 15.4 us
  waiting for transfers between devices: 42.3 us -> 39.2 us
  starting transfers between devices: 66.7 us -> 64.2 us
    ppermute x12, starting transfers between devices: 20.2 us -> 31 us  [turned(): lax.ppermute(array, axis, [(i, (i + shift) % count) for i in range(count)])]
    ppermute x12 -> x7, starting transfers between devices: 25.5 us -> 14.8 us  [the longest x1 6.02 us: scattered_sum(): lax.ppermute(other, 'gz', [(i, j) for i in range(8) for j in [(i + 1 ^ 1)...]
    pallas_call x1 -> x9, Pallas kernels: 8.12 us -> 15.4 us  [the longest x1 8.41 us: gradients(): pl.pallas_call(_gradients_kernel, out_shape=(shape((7936, 128), F32), sha...]
    add x14 -> x8, other arithmetic: 6.35 us -> 0.03 us  [the longest x7 0.02 us: rounds(): value = value + paired(value, axis, mask)]
    unnamed x70 -> x45, local copies, waits for them, and re-layouts: 5.37 us -> 10.8 us
    slice x43 -> x0, local copies, waits for them, and re-layouts: 5.31 us -> none  [the longest x25 2.39 us: face(): parts.append(lax.slice_in_dim(array, at, at + 1, axis=dim).reshape(-1, 128))]
    ppermute x12 -> x7, waiting for transfers between devices: 8.31 us -> 4.74 us  [the longest x3 2.67 us: traded(): lax.ppermute(here, axis, first_pairs)]
    ppermute x12 -> x11, waiting for transfers between devices: 22.1 us -> 25.2 us  [paired(): return lax.ppermute(array, axis, [(i, i ^ bit) for i in range(count)])]
  transfers between devices with their start and end apart: 36 -> 30, of which waited for: 19 -> 15; matrix products, arithmetic and copies ran while one was open for 13% -> 7% of each run, Pallas kernels for 0% -> 0%
where the time goes in v1:
time: 143 us; the launch traced here: 142 us
  starting transfers between devices  64.2 us (45%)
  waiting for transfers between devices  39.2 us (27%)
  Pallas kernels  15.4 us (11%)
  local copies, waits for them, and re-layouts  14.4 us (10%)
  matrix products  4.93 us (3%)
  other arithmetic  2.24 us (2%)
  between operations  1.8 us (1%)
    ppermute x12, starting transfers between devices, turned(): lax.ppermute(array, axis, [(i, (i + shift) % count) for i in range(count)])  31 us
    ppermute x11, waiting for transfers between devices, paired(): return lax.ppermute(array, axis, [(i, i ^ bit) for i in range(count)])  25.2 us
    ppermute x11, starting transfers between devices, paired(): return lax.ppermute(array, axis, [(i, i ^ bit) for i in range(count)])  18.4 us
    unnamed x45, local copies, waits for them, and re-layouts  10.8 us
    ppermute x12, waiting for transfers between devices, turned(): lax.ppermute(array, axis, [(i, (i + shift) % count) for i in range(count)])  9.27 us
    pallas_call x1, Pallas kernels, gradients(): pl.pallas_call(_gradients_kernel, out_shape=(shape((7936, 128), F32), sha...  8.41 us
    pallas_call x8, Pallas kernels, _call(): pl.pallas_call(kernel, out_shape=tuple((jax.ShapeDtypeStruct(shape, kind)...  6.98 us
    ppermute x1, starting transfers between devices, scattered_sum(): lax.ppermute(other, 'gz', [(i, j) for i in range(8) for j in [(i + 1 ^ 1)...  6.02 us
  transfers between devices with their start and end apart: 30, of which 15 were waited for; matrix products, arithmetic and copies ran while one was open for 7% of the time, Pallas kernels for 0%

profile of v1, /device:TPU:32, one launch (start us, length us, event | category | flops | bytes accessed | tf_op | source)
XLA Modules:
  0.0 142.1 jit_solution(350523703959847609)
XLA Ops:
  0.7 0.9 copy-done.1
  1.6 0.9 copy-done.3
  3.9 1.7 %collective-permute-start = (bf16[288,128]{1,0:T(8,128)(2,1)S(1)}, bf16[288,128]{1,0:T(8,128)(2,1)S(1)}, u32[]{:S(2)}, u32[]{:S(2)}) collective-permute-start(bf16[288,128]{1,0:T(8,128)(2,1)S(1)} %get-tuple-element.57), channel_id=1, source_target_pairs={{0,64},{64,0},{128,192},{192,128},{1,65},{65,1},{129,193},{193,129... | collective-permute-start | bytes 221192 | tf_op jit(solution)/shard_map/ppermute | solution.py:217
  6.2 2.1 %collective-permute-done.got_here = bf16[288,128]{1,0:T(8,128)(2,1)S(1)} collective-permute-done((bf16[288,128]{1,0:T(8,128)(2,1)S(1)}, bf16[288,128]{1,0:T(8,128)(2,1)S(1)}, u32[]{:S(2)}, u32[]{:S(2)}) %collective-permute-start) | collective-permute-done | bytes 73760 | tf_op jit(solution)/shard_map/ppermute | solution.py:217
  8.3 0.9 copy-done.2
  9.3 0.9 copy-done.4
  12.9 0.9 copy-done.7
  14.6 0.9 shard_map.177
  16.3 1.8 %collective-permute-start.4 = (bf16[304,128]{1,0:T(8,128)(2,1)S(1)}, bf16[304,128]{1,0:T(8,128)(2,1)S(1)}, u32[]{:S(2)}, u32[]{:S(2)}) collective-permute-start(bf16[304,128]{1,0:T(8,128)(2,1)S(1)} %get-tuple-element.66), channel_id=1, source_target_pairs={{0,1},{1,0},{2,3},{3,2},{4,5},{5,4},{6,7},{7,6},{8,9},{9,8},{10,11... | collective-permute-start | bytes 233480 | tf_op jit(solution)/shard_map/ppermute | solution.py:217
  18.2 3.9 %collective-permute-start.5 = (bf16[304,128]{1,0:T(8,128)(2,1)S(1)}, bf16[304,128]{1,0:T(8,128)(2,1)S(1)}, u32[]{:S(2)}, u32[]{:S(2)}) collective-permute-start(bf16[304,128]{1,0:T(8,128)(2,1)S(1)} %get-tuple-element.67), channel_id=1, source_target_pairs={{1,2},{2,1},{3,4},{4,3},{5,6},{6,5},{9,10},{10,9},{11,12},{12,11},... | collective-permute-start | bytes 233480 | tf_op jit(solution)/shard_map/ppermute | solution.py:217
  22.1 2.7 %copy.24 = bf16[27,256,128]{1,2,0:T(8,128)(2,1)S(1)} copy(bf16[27,256,128]{2,1,0:T(8,128)(2,1)} %bitcast.46) | data formatting | bytes 3538944 | tf_op jit(solution)/shard_map/reshape | solution.py:511
  24.9 1.5 %copy-done.13 = bf16[3456,256]{1,0:T(8,128)(2,1)S(1)} copy-done((bf16[3456,256]{1,0:T(8,128)(2,1)S(1)}, bf16[3456,256]{1,0:T(8,128)(2,1)}, u32[]{:S(2)}) %copy-start.13) | copy-done | bytes 1769496
  26.4 1.0 copy-done.16
  27.4 8.4 %shard_map.178 = (f32[7936,128]{1,0:T(8,128)S(1)}, f32[8064,128]{1,0:T(8,128)S(1)}, bf16[64,512]{1,0:T(8,128)(2,1)S(1)}, f32[512,128]{1,0:T(8,128)S(1)}) custom-call(s32[4]{0:T(128)S(1)} %pad_add_fusion.place_ref, bf16[512,128]{1,0:T(8,128)(2,1)S(1)} %bitcast.43, f32[960,128]{1,0:T(8,128)S(1)} %copy-done.16, f32[192,128]{1,0:T(8,128)S(1)} %get-tuple-element.65.pool_ref, ...), custom_call_target="tpu_custom_call" | custom-call | flops 2500000000 | bytes 16000000 | tf_op jit(solution)/shard_map/pallas_call | solution.py:348
  35.8 4.3 %collective-permute-start.6 = (f32[8064,128]{1,0:T(8,128)S(1)}, f32[8064,128]{1,0:T(8,128)S(1)}, u32[]{:S(2)}, u32[]{:S(2)}) collective-permute-start(f32[8064,128]{1,0:T(8,128)S(1)} %get-tuple-element.70), channel_id=1, source_target_pairs={{0,8},{8,0},{1,9},{9,1},{2,10},{10,2},{3,11},{11,3},{4,12},{12,4},... | collective-permute-start | bytes 12386312 | tf_op jit(solution)/shard_map/ppermute | solution.py:382
  40.1 6.7 %collective-permute-done.6.got_ref = f32[8064,128]{1,0:T(8,128)S(1)} collective-permute-done((f32[8064,128]{1,0:T(8,128)S(1)}, f32[8064,128]{1,0:T(8,128)S(1)}, u32[]{:S(2)}, u32[]{:S(2)}) %collective-permute-start.6) | collective-permute-done | bytes 4128800 | tf_op jit(solution)/shard_map/ppermute | solution.py:382
  46.8 1.2 shard_map.179
  48.0 4.4 %collective-permute-start.7 = (bf16[992,128]{1,0:T(8,128)(2,1)S(1)}, bf16[992,128]{1,0:T(8,128)(2,1)S(1)}, u32[]{:S(2)}, u32[]{:S(2)}) collective-permute-start(bf16[992,128]{1,0:T(8,128)(2,1)S(1)} %get-tuple-element.73), channel_id=1, source_target_pairs={{0,64},{64,128},{128,192},{192,0},{1,65},{65,129},{129,193},{193,1... | collective-permute-start | bytes 761864 | tf_op jit(solution)/shard_map/ppermute | solution.py:377
  52.4 1.9 %collective-permute-start.10 = (bf16[1056,128]{1,0:T(8,128)(2,1)S(1)}, bf16[1056,128]{1,0:T(8,128)(2,1)S(1)}, u32[]{:S(2)}, u32[]{:S(2)}) collective-permute-start(bf16[1056,128]{1,0:T(8,128)(2,1)S(1)} %get-tuple-element.77), channel_id=1, source_target_pairs={{0,16},{16,32},{32,48},{48,0},{1,17},{17,33},{33,49},{49,1},{2,18}... | collective-permute-start | bytes 811016 | tf_op jit(solution)/shard_map/ppermute | solution.py:377
  54.3 1.3 collective-permute-start.12
  55.6 2.2 %collective-permute-start.8 = (bf16[992,128]{1,0:T(8,128)(2,1)S(1)}, bf16[992,128]{1,0:T(8,128)(2,1)S(1)}, u32[]{:S(2)}, u32[]{:S(2)}) collective-permute-start(bf16[992,128]{1,0:T(8,128)(2,1)S(1)} %get-tuple-element.74), channel_id=1, source_target_pairs={{0,128},{64,192},{128,0},{192,64},{1,129},{65,193},{129,1},{193,65... | collective-permute-start | bytes 761864 | tf_op jit(solution)/shard_map/ppermute | solution.py:377
  57.8 2.5 %collective-permute-start.9 = (bf16[992,128]{1,0:T(8,128)(2,1)S(1)}, bf16[992,128]{1,0:T(8,128)(2,1)S(1)}, u32[]{:S(2)}, u32[]{:S(2)}) collective-permute-start(bf16[992,128]{1,0:T(8,128)(2,1)S(1)} %get-tuple-element.75), channel_id=1, source_target_pairs={{0,192},{64,0},{128,64},{192,128},{1,193},{65,1},{129,65},{193,129... | collective-permute-start | bytes 761864 | tf_op jit(solution)/shard_map/ppermute | solution.py:377
  60.3 2.3 %collective-permute-start.11 = (bf16[992,128]{1,0:T(8,128)(2,1)S(1)}, bf16[992,128]{1,0:T(8,128)(2,1)S(1)}, u32[]{:S(2)}, u32[]{:S(2)}) collective-permute-start(bf16[992,128]{1,0:T(8,128)(2,1)S(1)} %get-tuple-element.78), channel_id=1, source_target_pairs={{0,32},{16,48},{32,0},{48,16},{1,33},{17,49},{33,1},{49,17},{2,34}... | collective-permute-start | bytes 761864 | tf_op jit(solution)/shard_map/ppermute | solution.py:377
  62.6 4.0 %collective-permute-done.8.one_2 = bf16[992,128]{1,0:T(8,128)(2,1)S(1)} collective-permute-done((bf16[992,128]{1,0:T(8,128)(2,1)S(1)}, bf16[992,128]{1,0:T(8,128)(2,1)S(1)}, u32[]{:S(2)}, u32[]{:S(2)}) %collective-permute-start.8) | collective-permute-done | bytes 253984 | tf_op jit(solution)/shard_map/ppermute | solution.py:377
  66.5 2.4 %collective-permute-done.9.one_3 = bf16[992,128]{1,0:T(8,128)(2,1)S(1)} collective-permute-done((bf16[992,128]{1,0:T(8,128)(2,1)S(1)}, bf16[992,128]{1,0:T(8,128)(2,1)S(1)}, u32[]{:S(2)}, u32[]{:S(2)}) %collective-permute-start.9) | collective-permute-done | bytes 253984 | tf_op jit(solution)/shard_map/ppermute | solution.py:377
  69.0 1.1 shard_map.180
  70.1 1.0 collective-permute-start.13
  71.1 5.4 %collective-permute-start.16 = (f32[440,128]{1,0:T(8,128)S(1)}, f32[440,128]{1,0:T(8,128)S(1)}, u32[]{:S(2)}, u32[]{:S(2)}) collective-permute-start(f32[440,128]{1,0:T(8,128)S(1)} %get-tuple-element.86), channel_id=1, source_target_pairs={{0,64},{64,128},{128,192},{192,0},{1,65},{65,129},{129,193},{193,1... | collective-permute-start | bytes 675848 | tf_op jit(solution)/shard_map/ppermute | solution.py:377
  76.5 3.0 %collective-permute-start.14 = (f32[248,128]{1,0:T(8,128)S(1)}, f32[248,128]{1,0:T(8,128)S(1)}, u32[]{:S(2)}, u32[]{:S(2)}) collective-permute-start(f32[248,128]{1,0:T(8,128)S(1)} %get-tuple-element.83), channel_id=1, source_target_pairs={{0,32},{16,48},{32,0},{48,16},{1,33},{17,49},{33,1},{49,17},{2,34}... | collective-permute-start | bytes 380936 | tf_op jit(solution)/shard_map/ppermute | solution.py:377
  79.6 2.5 %collective-permute-start.15 = (f32[248,128]{1,0:T(8,128)S(1)}, f32[248,128]{1,0:T(8,128)S(1)}, u32[]{:S(2)}, u32[]{:S(2)}) collective-permute-start(f32[248,128]{1,0:T(8,128)S(1)} %get-tuple-element.84), channel_id=1, source_target_pairs={{0,48},{16,0},{32,16},{48,32},{1,49},{17,1},{33,17},{49,33},{2,50}... | collective-permute-start | bytes 380936 | tf_op jit(solution)/shard_map/ppermute | solution.py:377
  82.1 4.5 %collective-permute-start.17 = (f32[248,128]{1,0:T(8,128)S(1)}, f32[248,128]{1,0:T(8,128)S(1)}, u32[]{:S(2)}, u32[]{:S(2)}) collective-permute-start(f32[248,128]{1,0:T(8,128)S(1)} %get-tuple-element.87), channel_id=1, source_target_pairs={{0,128},{64,192},{128,0},{192,64},{1,129},{65,193},{129,1},{193,65... | collective-permute-start | bytes 380936 | tf_op jit(solution)/shard_map/ppermute | solution.py:377
  86.6 2.9 %collective-permute-done.17.two_2 = f32[248,128]{1,0:T(8,128)S(1)} collective-permute-done((f32[248,128]{1,0:T(8,128)S(1)}, f32[248,128]{1,0:T(8,128)S(1)}, u32[]{:S(2)}, u32[]{:S(2)}) %collective-permute-start.17) | collective-permute-done | bytes 127008 | tf_op jit(solution)/shard_map/ppermute | solution.py:377
  90.3 6.0 %collective-permute-start.20 = (bf16[192,128]{1,0:T(8,128)(2,1)S(1)}, bf16[192,128]{1,0:T(8,128)(2,1)S(1)}, u32[]{:S(2)}, u32[]{:S(2)}) collective-permute-start(bf16[192,128]{1,0:T(8,128)(2,1)S(1)} %get-tuple-element.92), channel_id=1, source_target_pairs={{1,2},{2,1},{3,4},{4,3},{5,6},{6,5},{9,10},{10,9},{11,12},{12,11},... | collective-permute-start | bytes 147464 | tf_op jit(solution)/shard_map/ppermute | solution.py:495
  96.4 2.1 %collective-permute-done.20.other_ref = bf16[192,128]{1,0:T(8,128)(2,1)S(1)} collective-permute-done((bf16[192,128]{1,0:T(8,128)(2,1)S(1)}, bf16[192,128]{1,0:T(8,128)(2,1)S(1)}, u32[]{:S(2)}, u32[]{:S(2)}) %collective-permute-start.20) | collective-permute-done | bytes 49184 | tf_op jit(solution)/shard_map/ppermute | solution.py:495
  98.4 0.9 shard_map.182
  99.3 2.8 %collective-permute-start.21 = (f32[128,128]{1,0:T(8,128)S(1)}, f32[128,128]{1,0:T(8,128)S(1)}, u32[]{:S(2)}, u32[]{:S(2)}) collective-permute-start(f32[128,128]{1,0:T(8,128)S(1)} %get-tuple-element.94), channel_id=1, source_target_pairs={{0,2},{1,3},{2,0},{3,1},{4,6},{5,7},{6,4},{7,5},{8,10},{9,11},{10,... | collective-permute-start | bytes 196616 | tf_op jit(solution)/shard_map/ppermute | solution.py:382
  102.1 2.6 %collective-permute-done.21 = f32[128,128]{1,0:T(8,128)S(1)} collective-permute-done((f32[128,128]{1,0:T(8,128)S(1)}, f32[128,128]{1,0:T(8,128)S(1)}, u32[]{:S(2)}, u32[]{:S(2)}) %collective-permute-start.21) | collective-permute-done | bytes 65568 | tf_op jit(solution)/shard_map/ppermute | solution.py:382
  104.7 3.8 %collective-permute-start.22 = (f32[128,128]{1,0:T(8,128)S(1)}, f32[128,128]{1,0:T(8,128)S(1)}, u32[]{:S(2)}, u32[]{:S(2)}) collective-permute-start(f32[128,128]{1,0:T(8,128)S(1)} %add.38), channel_id=1, source_target_pairs={{0,7},{1,6},{2,5},{3,4},{4,3},{5,2},{6,1},{7,0},{8,15},{9,14},{10,... | collective-permute-start | bytes 196616 | tf_op jit(solution)/shard_map/ppermute | solution.py:382
  108.5 3.6 %collective-permute-done.22 = f32[128,128]{1,0:T(8,128)S(1)} collective-permute-done((f32[128,128]{1,0:T(8,128)S(1)}, f32[128,128]{1,0:T(8,128)S(1)}, u32[]{:S(2)}, u32[]{:S(2)}) %collective-permute-start.22) | collective-permute-done | bytes 65568 | tf_op jit(solution)/shard_map/ppermute | solution.py:382
  112.3 1.0 collective-permute-done.23
  114.1 2.2 %collective-permute-start.24 = (f32[1,128]{1,0:T(1,128)S(1)}, f32[1,128]{1,0:T(1,128)S(1)}, u32[]{:S(2)}, u32[]{:S(2)}) collective-permute-start(f32[1,128]{1,0:T(1,128)S(1)} %bitcast_add_fusion), channel_id=1, source_target_pairs={{0,64},{64,0},{128,192},{192,128},{1,65},{65,1},{129,193},{193,129... | collective-permute-start | bytes 1544 | tf_op jit(solution)/shard_map/ppermute | solution.py:382
  117.9 2.2 %collective-permute-start.25 = (f32[1,128]{1,0:T(1,128)S(1)}, f32[1,128]{1,0:T(1,128)S(1)}, u32[]{:S(2)}, u32[]{:S(2)}) collective-permute-start(f32[1,128]{1,0:T(1,128)S(1)} %add.41), channel_id=1, source_target_pairs={{0,192},{64,128},{128,64},{192,0},{1,193},{65,129},{129,65},{193,1... | collective-permute-start | bytes 1544 | tf_op jit(solution)/shard_map/ppermute | solution.py:382
  120.0 3.8 %convolution_convert_fusion.1 = bf16[2,4,8,8,128]{4,0,3,2,1:T(2,128)(2,1)S(1)} fusion(bf16[3,3,3,256,128]{4,3,2,1,0:T(8,128)(2,1)S(1)} %bitcast.47, bf16[2,6,10,10,256]{4,1,3,2,0:T(8,128)(2,1)S(1)} %pad_maximum_fusion), kind=kOutput, calls=%fused_computation.2 | convolution fusion | flops 906035200 | bytes 2514944 | tf_op jit(solution)/shard_map/conv_general_dilated | solution.py:18
  125.5 1.9 %collective-permute-done.26 = f32[1,128]{1,0:T(1,128)S(1)} collective-permute-done((f32[1,128]{1,0:T(1,128)S(1)}, f32[1,128]{1,0:T(1,128)S(1)}, u32[]{:S(2)}, u32[]{:S(2)}) %collective-permute-start.26) | collective-permute-done | bytes 544 | tf_op jit(solution)/shard_map/ppermute | solution.py:382
  128.1 4.1 %collective-permute-done.27 = f32[1,128]{1,0:T(1,128)S(1)} collective-permute-done((f32[1,128]{1,0:T(1,128)S(1)}, f32[1,128]{1,0:T(1,128)S(1)}, u32[]{:S(2)}, u32[]{:S(2)}) %collective-permute-start.27) | collective-permute-done | bytes 544 | tf_op jit(solution)/shard_map/ppermute | solution.py:382
  132.2 3.5 %collective-permute-done.28 = f32[1,128]{1,0:T(1,128)S(1)} collective-permute-done((f32[1,128]{1,0:T(1,128)S(1)}, f32[1,128]{1,0:T(1,128)S(1)}, u32[]{:S(2)}, u32[]{:S(2)}) %collective-permute-start.28) | collective-permute-done | bytes 544 | tf_op jit(solution)/shard_map/ppermute | solution.py:382
  135.7 2.2 %collective-permute-start.29 = (f32[1,128]{1,0:T(1,128)S(1)}, f32[1,128]{1,0:T(1,128)S(1)}, u32[]{:S(2)}, u32[]{:S(2)}) collective-permute-start(f32[1,128]{1,0:T(1,128)S(1)} %add.47), channel_id=1, source_target_pairs={{0,2},{1,3},{2,0},{3,1},{4,6},{5,7},{6,4},{7,5},{8,10},{9,11},{10,... | collective-permute-start | bytes 1544 | tf_op jit(solution)/shard_map/ppermute | solution.py:382
  138.7 1.5 %collective-permute-done.29 = f32[1,128]{1,0:T(1,128)S(1)} collective-permute-done((f32[1,128]{1,0:T(1,128)S(1)}, f32[1,128]{1,0:T(1,128)S(1)}, u32[]{:S(2)}, u32[]{:S(2)}) %collective-permute-start.29) | collective-permute-done | bytes 544 | tf_op jit(solution)/shard_map/ppermute | solution.py:382
  (91 shorter events, 14.2 us)
Async XLA Ops:
  0.7 0.9 copy-start.1
  1.6 0.9 copy-start.3
  3.9 4.4 %collective-permute-start = (bf16[288,128]{1,0:T(8,128)(2,1)S(1)}, bf16[288,128]{1,0:T(8,128)(2,1)S(1)}, u32[]{:S(2)}, u32[]{:S(2)}) collective-permute-start(bf16[288,128]{1,0:T(8,128)(2,1)S(1)} %get-tuple-element.57), channel_id=1, source_target_pairs={{0,64},{64,0},{128,192},{192,128},{1,65},{65,1},{129,193},{193,129... | collective-permute-start | bytes 221192 | tf_op jit(solution)/shard_map/ppermute | solution.py:217
  5.6 2.8 %collective-permute-start.1 = (bf16[288,128]{1,0:T(8,128)(2,1)S(1)}, bf16[288,128]{1,0:T(8,128)(2,1)S(1)}, u32[]{:S(2)}, u32[]{:S(2)}) collective-permute-start(bf16[288,128]{1,0:T(8,128)(2,1)S(1)} %get-tuple-element.58), channel_id=1, source_target_pairs={{64,128},{128,64},{65,129},{129,65},{66,130},{130,66},{67,131},{13... | collective-permute-start | bytes 221192 | tf_op jit(solution)/shard_map/ppermute | solution.py:217
  8.3 0.9 copy-start.2
  9.2 0.9 copy-start.4
  11.6 1.3 collective-permute-start.2
  11.6 1.2 collective-permute-start.3
  12.9 0.9 copy-start.7
  16.3 8.5 %collective-permute-start.4 = (bf16[304,128]{1,0:T(8,128)(2,1)S(1)}, bf16[304,128]{1,0:T(8,128)(2,1)S(1)}, u32[]{:S(2)}, u32[]{:S(2)}) collective-permute-start(bf16[304,128]{1,0:T(8,128)(2,1)S(1)} %get-tuple-element.66), channel_id=1, source_target_pairs={{0,1},{1,0},{2,3},{3,2},{4,5},{5,4},{6,7},{7,6},{8,9},{9,8},{10,11... | collective-permute-start | bytes 233480 | tf_op jit(solution)/shard_map/ppermute | solution.py:217
  18.2 6.7 %collective-permute-start.5 = (bf16[304,128]{1,0:T(8,128)(2,1)S(1)}, bf16[304,128]{1,0:T(8,128)(2,1)S(1)}, u32[]{:S(2)}, u32[]{:S(2)}) collective-permute-start(bf16[304,128]{1,0:T(8,128)(2,1)S(1)} %get-tuple-element.67), channel_id=1, source_target_pairs={{1,2},{2,1},{3,4},{4,3},{5,6},{6,5},{9,10},{10,9},{11,12},{12,11},... | collective-permute-start | bytes 233480 | tf_op jit(solution)/shard_map/ppermute | solution.py:217
  22.1 2.8 %copy-start = (bf16[2048,128]{1,0:T(8,128)(2,1)S(1)}, bf16[2048,128]{1,0:T(8,128)(2,1)}, u32[]{:S(2)}) copy-start(bf16[2048,128]{1,0:T(8,128)(2,1)} %w_up_hbm.1) | copy-start | bytes 1572868
  22.1 2.8 %copy-start.5 = (bf16[2,4,8,8,128]{4,3,2,1,0:T(8,128)(2,1)S(1)}, bf16[2,4,8,8,128]{4,3,2,1,0:T(8,128)(2,1)}, u32[]{:S(2)}) copy-start(bf16[2,4,8,8,128]{4,3,2,1,0:T(8,128)(2,1)} %param.16) | copy-start | bytes 393220
  22.1 2.8 %copy-start.17 = (bf16[144,48]{1,0:T(8,128)(2,1)S(1)}, bf16[144,48]{1,0:T(8,128)(2,1)}, u32[]{:S(2)}) copy-start(bf16[144,48]{1,0:T(8,128)(2,1)} %constant.74.clone.sel_ref) | copy-start | bytes 41476
  22.1 2.8 %copy-start.18 = (bf16[128,128]{1,0:T(8,128)(2,1)S(1)}, bf16[128,128]{1,0:T(8,128)(2,1)}, u32[]{:S(2)}) copy-start(bf16[128,128]{1,0:T(8,128)(2,1)} %constant.76.clone.perm_t_ref) | copy-start | bytes 98308
  22.1 2.8 %copy-start.19 = (bf16[128,128]{1,0:T(8,128)(2,1)S(1)}, bf16[128,128]{1,0:T(8,128)(2,1)}, u32[]{:S(2)}) copy-start(bf16[128,128]{1,0:T(8,128)(2,1)} %constant.75.clone.perm_ref) | copy-start | bytes 98308
  22.1 2.8 %copy-start.20 = (bf16[32,64]{1,0:T(8,128)(2,1)S(1)}, bf16[32,64]{1,0:T(8,128)(2,1)}, u32[]{:S(2)}) copy-start(bf16[32,64]{1,0:T(8,128)(2,1)} %constant.77.clone.y_faces_ref) | copy-start | bytes 12292
  24.9 1.5 %copy-start.13 = (bf16[3456,256]{1,0:T(8,128)(2,1)S(1)}, bf16[3456,256]{1,0:T(8,128)(2,1)}, u32[]{:S(2)}) copy-start(bf16[3456,256]{1,0:T(8,128)(2,1)} %w_in_hbm.1) | copy-start | bytes 5308420
  26.4 1.0 copy-start.16
  35.8 11.0 %collective-permute-start.6 = (f32[8064,128]{1,0:T(8,128)S(1)}, f32[8064,128]{1,0:T(8,128)S(1)}, u32[]{:S(2)}, u32[]{:S(2)}) collective-permute-start(f32[8064,128]{1,0:T(8,128)S(1)} %get-tuple-element.70), channel_id=1, source_target_pairs={{0,8},{8,0},{1,9},{9,1},{2,10},{10,2},{3,11},{11,3},{4,12},{12,4},... | collective-permute-start | bytes 12386312 | tf_op jit(solution)/shard_map/ppermute | solution.py:382
  46.8 22.2 %copy-start.10 = (bf16[96,96]{1,0:T(8,128)(2,1)S(1)}, bf16[96,96]{1,0:T(8,128)(2,1)}, u32[]{:S(2)}) copy-start(bf16[96,96]{1,0:T(8,128)(2,1)} %constant.78.clone.x_faces_ref) | copy-start | bytes 55300
  48.0 41.5 %copy-start.9 = (bf16[96,192]{1,0:T(8,128)(2,1)S(1)}, bf16[96,192]{1,0:T(8,128)(2,1)}, u32[]{:S(2)}) copy-start(bf16[96,192]{1,0:T(8,128)(2,1)} %constant.79.clone.z_faces_ref) | copy-start | bytes 110596
  48.0 12.3 %collective-permute-start.7 = (bf16[992,128]{1,0:T(8,128)(2,1)S(1)}, bf16[992,128]{1,0:T(8,128)(2,1)S(1)}, u32[]{:S(2)}, u32[]{:S(2)}) collective-permute-start(bf16[992,128]{1,0:T(8,128)(2,1)S(1)} %get-tuple-element.73), channel_id=1, source_target_pairs={{0,64},{64,128},{128,192},{192,0},{1,65},{65,129},{129,193},{193,1... | collective-permute-start | bytes 761864 | tf_op jit(solution)/shard_map/ppermute | solution.py:377
  52.4 16.5 %collective-permute-start.10 = (bf16[1056,128]{1,0:T(8,128)(2,1)S(1)}, bf16[1056,128]{1,0:T(8,128)(2,1)S(1)}, u32[]{:S(2)}, u32[]{:S(2)}) collective-permute-start(bf16[1056,128]{1,0:T(8,128)(2,1)S(1)} %get-tuple-element.77), channel_id=1, source_target_pairs={{0,16},{16,32},{32,48},{48,0},{1,17},{17,33},{33,49},{49,1},{2,18}... | collective-permute-start | bytes 811016 | tf_op jit(solution)/shard_map/ppermute | solution.py:377
  54.3 14.6 %collective-permute-start.12 = (bf16[1056,128]{1,0:T(8,128)(2,1)S(1)}, bf16[1056,128]{1,0:T(8,128)(2,1)S(1)}, u32[]{:S(2)}, u32[]{:S(2)}) collective-permute-start(bf16[1056,128]{1,0:T(8,128)(2,1)S(1)} %get-tuple-element.79), channel_id=1, source_target_pairs={{0,48},{16,0},{32,16},{48,32},{1,49},{17,1},{33,17},{49,33},{2,50}... | collective-permute-start | bytes 811016 | tf_op jit(solution)/shard_map/ppermute | solution.py:377
  55.6 10.9 %collective-permute-start.8 = (bf16[992,128]{1,0:T(8,128)(2,1)S(1)}, bf16[992,128]{1,0:T(8,128)(2,1)S(1)}, u32[]{:S(2)}, u32[]{:S(2)}) collective-permute-start(bf16[992,128]{1,0:T(8,128)(2,1)S(1)} %get-tuple-element.74), channel_id=1, source_target_pairs={{0,128},{64,192},{128,0},{192,64},{1,129},{65,193},{129,1},{193,65... | collective-permute-start | bytes 761864 | tf_op jit(solution)/shard_map/ppermute | solution.py:377
  57.8 11.1 %collective-permute-start.9 = (bf16[992,128]{1,0:T(8,128)(2,1)S(1)}, bf16[992,128]{1,0:T(8,128)(2,1)S(1)}, u32[]{:S(2)}, u32[]{:S(2)}) collective-permute-start(bf16[992,128]{1,0:T(8,128)(2,1)S(1)} %get-tuple-element.75), channel_id=1, source_target_pairs={{0,192},{64,0},{128,64},{192,128},{1,193},{65,1},{129,65},{193,129... | collective-permute-start | bytes 761864 | tf_op jit(solution)/shard_map/ppermute | solution.py:377
  60.3 8.6 %collective-permute-start.11 = (bf16[992,128]{1,0:T(8,128)(2,1)S(1)}, bf16[992,128]{1,0:T(8,128)(2,1)S(1)}, u32[]{:S(2)}, u32[]{:S(2)}) collective-permute-start(bf16[992,128]{1,0:T(8,128)(2,1)S(1)} %get-tuple-element.78), channel_id=1, source_target_pairs={{0,32},{16,48},{32,0},{48,16},{1,33},{17,49},{33,1},{49,17},{2,34}... | collective-permute-start | bytes 761864 | tf_op jit(solution)/shard_map/ppermute | solution.py:377
  69.0 29.5 %copy-start.6 = (bf16[288,288]{1,0:T(8,128)(2,1)S(1)}, bf16[288,288]{1,0:T(8,128)(2,1)}, u32[]{:S(2)}) copy-start(bf16[288,288]{1,0:T(8,128)(2,1)} %constant.80.clone.padded_ref) | copy-start | bytes 497668
  70.1 12.0 %collective-permute-start.13 = (f32[248,128]{1,0:T(8,128)S(1)}, f32[248,128]{1,0:T(8,128)S(1)}, u32[]{:S(2)}, u32[]{:S(2)}) collective-permute-start(f32[248,128]{1,0:T(8,128)S(1)} %get-tuple-element.82), channel_id=1, source_target_pairs={{0,16},{16,32},{32,48},{48,0},{1,17},{17,33},{33,49},{49,1},{2,18}... | collective-permute-start | bytes 380936 | tf_op jit(solution)/shard_map/ppermute | solution.py:377
  71.1 18.4 %collective-permute-start.16 = (f32[440,128]{1,0:T(8,128)S(1)}, f32[440,128]{1,0:T(8,128)S(1)}, u32[]{:S(2)}, u32[]{:S(2)}) collective-permute-start(f32[440,128]{1,0:T(8,128)S(1)} %get-tuple-element.86), channel_id=1, source_target_pairs={{0,64},{64,128},{128,192},{192,0},{1,65},{65,129},{129,193},{193,1... | collective-permute-start | bytes 675848 | tf_op jit(solution)/shard_map/ppermute | solution.py:377
  76.5 13.0 %collective-permute-start.18 = (f32[440,128]{1,0:T(8,128)S(1)}, f32[440,128]{1,0:T(8,128)S(1)}, u32[]{:S(2)}, u32[]{:S(2)}) collective-permute-start(f32[440,128]{1,0:T(8,128)S(1)} %get-tuple-element.88), channel_id=1, source_target_pairs={{0,192},{64,0},{128,64},{192,128},{1,193},{65,1},{129,65},{193,129... | collective-permute-start | bytes 675848 | tf_op jit(solution)/shard_map/ppermute | solution.py:377
  76.5 10.1 %collective-permute-start.14 = (f32[248,128]{1,0:T(8,128)S(1)}, f32[248,128]{1,0:T(8,128)S(1)}, u32[]{:S(2)}, u32[]{:S(2)}) collective-permute-start(f32[248,128]{1,0:T(8,128)S(1)} %get-tuple-element.83), channel_id=1, source_target_pairs={{0,32},{16,48},{32,0},{48,16},{1,33},{17,49},{33,1},{49,17},{2,34}... | collective-permute-start | bytes 380936 | tf_op jit(solution)/shard_map/ppermute | solution.py:377
  79.6 7.0 %collective-permute-start.15 = (f32[248,128]{1,0:T(8,128)S(1)}, f32[248,128]{1,0:T(8,128)S(1)}, u32[]{:S(2)}, u32[]{:S(2)}) collective-permute-start(f32[248,128]{1,0:T(8,128)S(1)} %get-tuple-element.84), channel_id=1, source_target_pairs={{0,48},{16,0},{32,16},{48,32},{1,49},{17,1},{33,17},{49,33},{2,50}... | collective-permute-start | bytes 380936 | tf_op jit(solution)/shard_map/ppermute | solution.py:377
  82.1 7.4 %collective-permute-start.17 = (f32[248,128]{1,0:T(8,128)S(1)}, f32[248,128]{1,0:T(8,128)S(1)}, u32[]{:S(2)}, u32[]{:S(2)}) collective-permute-start(f32[248,128]{1,0:T(8,128)S(1)} %get-tuple-element.87), channel_id=1, source_target_pairs={{0,128},{64,192},{128,0},{192,64},{1,129},{65,193},{129,1},{193,65... | collective-permute-start | bytes 380936 | tf_op jit(solution)/shard_map/ppermute | solution.py:377
  90.2 8.2 %collective-permute-start.19 = (f32[448,128]{1,0:T(8,128)S(1)}, f32[448,128]{1,0:T(8,128)S(1)}, u32[]{:S(2)}, u32[]{:S(2)}) collective-permute-start(f32[448,128]{1,0:T(8,128)S(1)} %get-tuple-element.91), channel_id=1, source_target_pairs={{0,1},{1,0},{2,3},{3,2},{4,5},{5,4},{6,7},{7,6},{8,9},{9,8},{10,11... | collective-permute-start | bytes 688136 | tf_op jit(solution)/shard_map/ppermute | solution.py:382
  90.3 8.1 %collective-permute-start.20 = (bf16[192,128]{1,0:T(8,128)(2,1)S(1)}, bf16[192,128]{1,0:T(8,128)(2,1)S(1)}, u32[]{:S(2)}, u32[]{:S(2)}) collective-permute-start(bf16[192,128]{1,0:T(8,128)(2,1)S(1)} %get-tuple-element.92), channel_id=1, source_target_pairs={{1,2},{2,1},{3,4},{4,3},{5,6},{6,5},{9,10},{10,9},{11,12},{12,11},... | collective-permute-start | bytes 147464 | tf_op jit(solution)/shard_map/ppermute | solution.py:495
  99.3 5.3 %collective-permute-start.21 = (f32[128,128]{1,0:T(8,128)S(1)}, f32[128,128]{1,0:T(8,128)S(1)}, u32[]{:S(2)}, u32[]{:S(2)}) collective-permute-start(f32[128,128]{1,0:T(8,128)S(1)} %get-tuple-element.94), channel_id=1, source_target_pairs={{0,2},{1,3},{2,0},{3,1},{4,6},{5,7},{6,4},{7,5},{8,10},{9,11},{10,... | collective-permute-start | bytes 196616 | tf_op jit(solution)/shard_map/ppermute | solution.py:382
  104.7 7.4 %collective-permute-start.22 = (f32[128,128]{1,0:T(8,128)S(1)}, f32[128,128]{1,0:T(8,128)S(1)}, u32[]{:S(2)}, u32[]{:S(2)}) collective-permute-start(f32[128,128]{1,0:T(8,128)S(1)} %add.38), channel_id=1, source_target_pairs={{0,7},{1,6},{2,5},{3,4},{4,3},{5,2},{6,1},{7,0},{8,15},{9,14},{10,... | collective-permute-start | bytes 196616 | tf_op jit(solution)/shard_map/ppermute | solution.py:382
  112.1 1.2 collective-permute-start.23
  114.1 3.7 %collective-permute-start.24 = (f32[1,128]{1,0:T(1,128)S(1)}, f32[1,128]{1,0:T(1,128)S(1)}, u32[]{:S(2)}, u32[]{:S(2)}) collective-permute-start(f32[1,128]{1,0:T(1,128)S(1)} %bitcast_add_fusion), channel_id=1, source_target_pairs={{0,64},{64,0},{128,192},{192,128},{1,65},{65,1},{129,193},{193,129... | collective-permute-start | bytes 1544 | tf_op jit(solution)/shard_map/ppermute | solution.py:382
  116.7 3.3 %copy-start.21 = (bf16[6912,128]{1,0:T(8,128)(2,1)S(1)}, bf16[6912,128]{1,0:T(8,128)(2,1)}, u32[]{:S(2)}) copy-start(bf16[6912,128]{1,0:T(8,128)(2,1)} %param.19) | copy-start | bytes 5308420
  117.9 5.9 %collective-permute-start.25 = (f32[1,128]{1,0:T(1,128)S(1)}, f32[1,128]{1,0:T(1,128)S(1)}, u32[]{:S(2)}, u32[]{:S(2)}) collective-permute-start(f32[1,128]{1,0:T(1,128)S(1)} %add.41), channel_id=1, source_target_pairs={{0,192},{64,128},{128,64},{192,0},{1,193},{65,129},{129,65},{193,1... | collective-permute-start | bytes 1544 | tf_op jit(solution)/shard_map/ppermute | solution.py:382
  120.0 3.9 %copy-start.14 = (bf16[3456,256]{1,0:T(8,128)(2,1)S(1)}, bf16[3456,256]{1,0:T(8,128)(2,1)}, u32[]{:S(2)}) copy-start(bf16[3456,256]{1,0:T(8,128)(2,1)} %w_in_hbm.1) | copy-start | bytes 5308420
  123.8 3.6 %collective-permute-start.26 = (f32[1,128]{1,0:T(1,128)S(1)}, f32[1,128]{1,0:T(1,128)S(1)}, u32[]{:S(2)}, u32[]{:S(2)}) collective-permute-start(f32[1,128]{1,0:T(1,128)S(1)} %add.42), channel_id=1, source_target_pairs={{0,16},{16,0},{32,48},{48,32},{1,17},{17,1},{33,49},{49,33},{2,18}... | collective-permute-start | bytes 1544 | tf_op jit(solution)/shard_map/ppermute | solution.py:382
  127.4 4.8 %collective-permute-start.27 = (f32[1,128]{1,0:T(1,128)S(1)}, f32[1,128]{1,0:T(1,128)S(1)}, u32[]{:S(2)}, u32[]{:S(2)}) collective-permute-start(f32[1,128]{1,0:T(1,128)S(1)} %add.43), channel_id=1, source_target_pairs={{0,48},{16,32},{32,16},{48,0},{1,49},{17,33},{33,17},{49,1},{2,50}... | collective-permute-start | bytes 1544 | tf_op jit(solution)/shard_map/ppermute | solution.py:382
  132.2 3.5 %collective-permute-start.28 = (f32[1,128]{1,0:T(1,128)S(1)}, f32[1,128]{1,0:T(1,128)S(1)}, u32[]{:S(2)}, u32[]{:S(2)}) collective-permute-start(f32[1,128]{1,0:T(1,128)S(1)} %add.46), channel_id=1, source_target_pairs={{0,1},{1,0},{2,3},{3,2},{4,5},{5,4},{6,7},{7,6},{8,9},{9,8},{10,11... | collective-permute-start | bytes 1544 | tf_op jit(solution)/shard_map/ppermute | solution.py:382
  135.7 4.4 %collective-permute-start.29 = (f32[1,128]{1,0:T(1,128)S(1)}, f32[1,128]{1,0:T(1,128)S(1)}, u32[]{:S(2)}, u32[]{:S(2)}) collective-permute-start(f32[1,128]{1,0:T(1,128)S(1)} %add.47), channel_id=1, source_target_pairs={{0,2},{1,3},{2,0},{3,1},{4,6},{5,7},{6,4},{7,5},{8,10},{9,11},{10,... | collective-permute-start | bytes 1544 | tf_op jit(solution)/shard_map/ppermute | solution.py:382
  (4 other events, 3.0 us)

commit v2 on v1

--- a/solution.py
+++ b/solution.py
@@ -71,8 +71,10 @@
 
 
 def _at_x(s, x, y, z):
-    line = s * 6 + y + 1
-    return 96 + line * 4 + z if x < 0 else 144 + line * 4 + z if x > 1 else _at_y(s, x, y, z)
+    if 0 <= x <= 1:
+        return _at_y(s, x, y, z)
+    base = 96 if x < 0 else 144
+    return base + (s * 4 + y) * 4 + z if 0 <= y <= 3 else base + 32 + (s * 2 + int(y > 3)) * 4 + z
 
 
 def _at_z(s, x, y, z):
@@ -80,24 +82,11 @@
     return 192 + line if z < 0 else 240 + line if z > 3 else _at_x(s, x, y, z)
 
 
-def _pool_of():
-    pool = np.zeros((16, 128), np.float32)
-    for a, y, z in itertools.product(range(2), range(8), range(8)):
-        pool[(y // 2) * 4 + z // 2, (a * 8 + y) * 8 + z] = 0.125
-    return pool
-
-
 S2, X2, Y4, Z4 = range(2), range(2), range(4), range(4)
 X4, Y6, Z6 = range(-1, 3), range(-1, 5), range(-1, 5)
 Y_FACES = _picks([_at_y(s, x, y, z) for y in (0, 3) for s in S2 for x in X2 for z in Z4], 64)
-X_FACES = _picks([_at_y(s, x, y, z) for x in (0, 1) for s in S2 for y in Y6 for z in Z4], 96)
+X_EDGES = _picks([e * 16 + (s * 2 + x) * 4 + z for x in (0, 1) for s in S2 for e in range(2) for z in Z4], 32)
 Z_FACES = _picks([_at_x(s, x, y, z) for z in (0, 3) for s in S2 for x in X4 for y in Y6], 192)
-POOL_OF = _pool_of()
-POOL_Y_FACES = _picks([p * 16 + y * 4 + z for y in (0, 3) for p in range(8) for z in Z4], 128)
-POOL_GROW_Y = _picks(
-    [128 + p * 4 + z if y < 0 else 160 + p * 4 + z if y > 3 else p * 16 + y * 4 + z for p in range(8) for y in Y6 for z in Z4], 192
-)
-POOL_Z_FACES = _picks([(p * 6 + y) * 4 + z if y < 6 else 192 for z in (0, 3) for p in range(8) for y in range(8)], 193)[:, :192]
 PADDED = _picks([_at_z(s, x, y, z) for s in S2 for x in X4 for y in Y6 for z in Z6], 288)
 
 
@@ -138,8 +127,37 @@
     there_ref[...] = (first * even + last * (1.0 - even)).astype(BF16)
 
 
-def _pool_kernel(place_ref, pool_of_ref, act_ref, cot_ref, pooled_ref, here_ref, there_ref):
-    planes = [_dot(pool_of_ref[...], act_ref[g * 128 : (g + 1) * 128, :]) for g in range(4)]
+def _table(rows, columns, chosen, value=1.0):
+    row = lax.broadcasted_iota(jnp.int32, (rows, columns), 0)
+    column = lax.broadcasted_iota(jnp.int32, (rows, columns), 1)
+    return jnp.where(chosen(row, column), value, 0.0).astype(BF16)
+
+
+def _pool_of(r, c):
+    return (((c >> 4) & 3) == (r >> 2)) & (((c >> 1) & 3) == (r & 3))
+
+
+def _pool_y_faces(r, c):
+    return c == ((r >> 2) & 7) * 16 + (r >> 5) * 12 + (r & 3)
+
+
+def _pool_grow_y(r, c):
+    plane = (r * 2731) >> 16
+    y, z = (r - plane * 24) >> 2, r & 3
+    inside = plane * 16 + (y - 1) * 4 + z
+    return c == jnp.where(y == 0, 128 + plane * 4 + z, jnp.where(y == 5, 160 + plane * 4 + z, inside))
+
+
+def _pool_z_faces(r, c):
+    y = r & 7
+    return (c == (((r >> 3) & 7) * 6 + y) * 4 + (r >> 6) * 3) & (y < 6)
+
+
+def _pool_kernel(place_ref, act_ref, cot_ref, act_out, cot_out, pooled_ref, here_ref, there_ref):
+    act_out[...] = act_ref[...]
+    cot_out[...] = cot_ref[...]
+    pool_of = _table(16, 128, _pool_of, 0.125)
+    planes = [_dot(pool_of, act_ref[g * 128 : (g + 1) * 128, :]) for g in range(4)]
     pooled = jnp.concatenate(planes, axis=0).astype(BF16)
     pooled_ref[...] = pooled
 
@@ -151,7 +169,7 @@
 
 
 def _grow_x_kernel(
-    place_ref, pool_faces_ref, act_ref, cot_ref, pooled_ref, got_here, got_there,
+    place_ref, act_ref, cot_ref, pooled_ref, got_here, got_there,
     act_out, cot_out, pooled_out, here_ref, there_ref,
 ):
     low, high = _sides(place_ref[0], got_here, got_there)
@@ -173,19 +191,19 @@
         parts += [low[at_face], pooled[s * 32 : (s + 1) * 32], high[at_face]]
     grown = jnp.concatenate(parts, axis=0).astype(BF16)
     pooled_out[...] = grown
-    faces = _dot(pool_faces_ref[...], grown)
+    faces = _dot(_table(64, 128, _pool_y_faces), grown)
     first = jnp.concatenate(firsts + [faces[0:32]], axis=0)
     last = jnp.concatenate(lasts + [faces[32:64]], axis=0)
     _pack(place_ref[2], first, last, here_ref, there_ref)
 
 
 def _grow_y_kernel(
-    place_ref, pool_grow_ref, pool_faces_ref, act_ref, cot_ref, pooled_ref, got_here, got_there,
-    act_out, cot_out, pooled_out, here_ref, there_ref,
+    place_ref, act_ref, cot_ref, pooled_ref, got_here, got_there,
+    act_out, cot_out, pooled_out, here_ref, there_ref, act_lines,
 ):
     low, high = _sides(place_ref[2], got_here, got_there)
     firsts, lasts = [], []
-    for i, (ref, out) in enumerate(((act_ref, act_out), (cot_ref, cot_out))):
+    for i, (ref, out) in enumerate(((act_ref, act_lines), (cot_ref, cot_out))):
         for p in range(12):
             at_face = slice(i * 96 + p * 8, i * 96 + p * 8 + 8)
             out[p * 80 : p * 80 + 8, :] = low[at_face]
@@ -194,9 +212,10 @@
         firsts.append(out[pl.ds(0, 120, 8), :])
         lasts.append(out[pl.ds(7, 120, 8), :])
     rows = jnp.concatenate([pooled_ref[...], low[192:224].astype(BF16), high[192:224].astype(BF16)], axis=0)
-    grown = _dot(pool_grow_ref[...], rows)
+    act_out[...] = act_lines[...].astype(BF16)
+    grown = _dot(_table(192, 192, _pool_grow_y), rows)
     pooled_out[...] = grown
-    faces = _dot(pool_faces_ref[...], grown.astype(BF16))
+    faces = _dot(_table(128, 192, _pool_z_faces), grown.astype(BF16))
     first = jnp.concatenate(firsts + [faces[0:64]], axis=0)
     last = jnp.concatenate(lasts + [faces[64:128]], axis=0)
     _pack(place_ref[3], first, last, here_ref, there_ref)
@@ -204,7 +223,7 @@
 
 def _grow_z_kernel(place_ref, act_ref, got_here, got_there, out_ref, lines):
     low, high = _sides(place_ref[3], got_here, got_there)
-    lines[:, 8:16, :] = act_ref[...].reshape(120, 8, 128)
+    lines[:, 8:16, :] = act_ref[...].astype(F32).reshape(120, 8, 128)
     lines[:, 7:8, :] = low[0:120][:, None, :]
     lines[:, 16:17, :] = high[0:120][:, None, :]
     out_ref[...] = lines[:, 7:17, :].astype(BF16)
@@ -219,17 +238,14 @@
 
 def extended(place, act, cot):
     rows, f32_rows = lambda n: ((n, 128), BF16), lambda n: ((n, 128), F32)
-    pooled, *faces = _call(_pool_kernel, (rows(64), rows(288), rows(288)), place, jnp.asarray(POOL_OF, BF16), act, cot)
+    own, cot, pooled, *faces = _call(_pool_kernel, (rows(512), rows(512), rows(64), rows(288), rows(288)), place, act, cot)
     outs = (f32_rows(768), f32_rows(768), rows(128), rows(224), rows(224))
+    act, cot, pooled, *faces = _call(_grow_x_kernel, outs, place, own, cot, pooled, *traded(*faces, "gx"))
+    outs = (rows(960), f32_rows(960), f32_rows(192), rows(304), rows(304))
     act, cot, pooled, *faces = _call(
-        _grow_x_kernel, outs, place, jnp.asarray(POOL_Y_FACES, BF16), act, cot, pooled, *traded(*faces, "gx")
-    )
-    outs = (f32_rows(960), f32_rows(960), f32_rows(192), rows(304), rows(304))
-    act, cot, pooled, *faces = _call(
-        _grow_y_kernel, outs, place, jnp.asarray(POOL_GROW_Y, BF16), jnp.asarray(POOL_Z_FACES, BF16),
-        act, cot, pooled, *traded(*faces, ("x", "core")),
-    )
-    return act, cot, pooled, traded(*faces, "gz")
+        _grow_y_kernel, outs, place, act, cot, pooled, *traded(*faces, ("x", "core")), scratch=((960, 128),)
+    )
+    return own, act, cot, pooled, traded(*faces, "gz")
 
 
 def _gradients_kernel(
@@ -259,14 +275,10 @@
             done += here
 
     def ship(index, first, last):
-        copies = [
-            pltpu.make_async_copy(sums.at[i, pl.ds(first, end - first)], target.at[pl.ds(first, end - first)], sem_out.at[index, i])
-            for i, (target, end) in enumerate(((keep_ref, min(last, 7936)), (send_ref, last)))
-            if end > first
-        ]
-        for copy in copies:
-            copy.start()
-        return copies
+        copy = pltpu.make_async_copy(sums.at[0, pl.ds(first, last - first)], keep_ref.at[pl.ds(first, last - first)], sem_out.at[index])
+        copy.start()
+        send_ref[first:last, :] = sums[1, first:last, :].astype(BF16)
+        return copy
 
     low, high = _sides(place_ref[3], got_here, got_there)
     lines[:, 8:16, :] = cot_ref[...].reshape(120, 8, 128)
@@ -308,7 +320,7 @@
         grad = _dot(joined_t, shifted[:, dx : dx + 4].reshape(512, 1152))
         for u in range(9):
             put(8960 + (18 - 9 * dx + u) * 256, grad[:, u * 128 : (u + 1) * 128])
-    copies = ship(0, 4960, 7936)
+    copies = [ship(0, 4960, 7936)]
 
     d_upward = d_joined[:, 128:].astype(BF16)
     planes = [_dot(perm_t_ref[...], d_upward[g * 128 : (g + 1) * 128]).astype(BF16) for g in range(4)]
@@ -324,8 +336,7 @@
     coarse_ref[...] = coarse
     faces = _dot(y_faces_ref[...], coarse)
     for lane in range(4):
-        sums[1, 7936 + lane * 32 : 7968 + lane * 32, :] = faces[:, lane * 128 : (lane + 1) * 128]
-    copies += ship(1, 7936, 8064)
+        send_ref[7936 + lane * 32 : 7968 + lane * 32, :] = faces[:, lane * 128 : (lane + 1) * 128].astype(BF16)
 
     spaced[...] = jnp.zeros((128, 768), BF16)
     for s in range(2):
@@ -337,7 +348,7 @@
         for dx in range(3):
             for h in range(2):
                 put((9 * dx + u) * 256 + h, grad[:, dx * 256 + h * 128 : dx * 256 + (h + 1) * 128], 2)
-    copies += ship(2, 0, 4960)
+    copies.append(ship(1, 0, 4960))
     for copy in copies:
         copy.wait()
 
@@ -348,7 +359,7 @@
     return pl.pallas_call(
         _gradients_kernel,
         out_shape=(
-            shape((7936, 128), F32), shape((8064, 128), F32), shape((64, 512), BF16), shape((512, 128), F32),
+            shape((7936, 128), F32), shape((8064, 128), BF16), shape((64, 512), BF16), shape((512, 128), F32),
         ),
         in_specs=[pl.BlockSpec(memory_space=pltpu.SMEM)] + [vmem] * 9 + [hbm] * 3,
         out_specs=(vmem,) * 4,
@@ -356,10 +367,10 @@
             pltpu.VMEM((3456, 256), BF16), pltpu.VMEM((3456, 256), BF16), pltpu.VMEM((2048, 128), BF16),
             pltpu.VMEM((120, 24, 128), F32), pltpu.VMEM((2, 6, 64, 1152), BF16),
             pltpu.VMEM((2, 4, 16, 1152), BF16), pltpu.VMEM((128, 768), BF16),
-            pltpu.VMEM((2, 8064, 128), F32),
-            pltpu.SemaphoreType.DMA((3,)), pltpu.SemaphoreType.DMA((3, 2)),
+            pltpu.VMEM((2, 7936, 128), F32),
+            pltpu.SemaphoreType.DMA((3,)), pltpu.SemaphoreType.DMA((2,)),
         ],
-        compiler_params=pltpu.CompilerParams(vmem_limit_bytes=36 * 1024 * 1024),
+        compiler_params=pltpu.CompilerParams(vmem_limit_bytes=32 * 1024 * 1024),
         cost_estimate=pl.CostEstimate(flops=2_500_000_000, bytes_accessed=16_000_000, transcendentals=16384),
     )(
         place, act, cot, pool, got_here, got_there,
@@ -368,10 +379,6 @@
     )
 
 
-def at(array, index, axis):
-    return lax.dynamic_index_in_dim(array, index, axis, keepdims=False)
-
-
 def turned(array, axis, shift):
     count = lax.axis_size(axis)
     return lax.ppermute(array, axis, [(i, (i + shift) % count) for i in range(count)])
@@ -382,52 +389,57 @@
     return lax.ppermute(array, axis, [(i, i ^ bit) for i in range(count)])
 
 
-def _split_kernel(place_ref, keep_ref, got_ref, one_ref, two_ref, faces_ref, *sends):
+def _split_kernel(place_ref, keep_ref, got_ref, coarse_ref, one_ref, two_ref, faces_ref, *sends):
     for s in range(4):
-        rows = [pl.multiple_of(((place_ref[0] + s) % 4 * 4 + j) * 496, 8) for j in range(4)]
-        one = jnp.concatenate([keep_ref[pl.ds(r, 248), :] + got_ref[pl.ds(r, 248), :] for r in rows], axis=0)
-        rows = [pl.multiple_of((j * 4 + (place_ref[1] + s) % 4) * 496 + 248, 8) for j in range(4)]
-        two = jnp.concatenate([keep_ref[pl.ds(r, 248), :] + got_ref[pl.ds(r, 248), :] for r in rows], axis=0)
+        rows = [pl.multiple_of(((place_ref[0] + s) % 4 * 4 + j) * 496, 16) for j in range(4)]
+        one = jnp.concatenate([keep_ref[pl.ds(r, 248), :] + got_ref[pl.ds(r, 256), :].astype(F32)[:248] for r in rows], axis=0)
+        rows = [pl.multiple_of((j * 4 + (place_ref[1] + s) % 4) * 496 + 240, 16) for j in range(4)]
+        two = jnp.concatenate([keep_ref[pl.ds(r + 8, 248), :] + got_ref[pl.ds(r, 256), :].astype(F32)[8:] for r in rows], axis=0)
         if s == 0:
             one_ref[...] = one
             two_ref[...] = two
         else:
-            sends[s - 1][...] = one.astype(BF16)
+            sends[s - 1][0:992, :] = one.astype(BF16)
             sends[s + 2][0:992, :] = two.astype(BF16)
-    faces = got_ref[7936:8064, :].astype(BF16)
+    faces = got_ref[7936:8064, :]
     faces_ref[...] = faces
     for lane in range(4):
         sends[3][992 + lane * 16 : 1008 + lane * 16, :] = faces[lane * 32 + 16 : lane * 32 + 32]
         sends[5][992 + lane * 16 : 1008 + lane * 16, :] = faces[lane * 32 : lane * 32 + 16]
-
-
-def _second_kernel(
-    place_ref, coarse_ref, faces_ref, x_faces_ref, one_ref, one_1, one_2, one_3, two_ref, two_1, two_2, two_3,
-    grown_ref, own_one, own_two, send_one_1, send_one_2, send_one_3, send_two_1, send_two_2, send_two_3, one, two,
+        for s in range(2):
+            start, channels = 992 + lane * 32 + s * 16, slice(lane * 128, (lane + 1) * 128)
+            sends[0][start : start + 16, :] = coarse_ref[s * 32 + 16 : s * 32 + 32, channels]
+            sends[2][start : start + 16, :] = coarse_ref[s * 32 : s * 32 + 16, channels]
+
+
+def _second_one_kernel(place_ref, one_ref, got_1, got_2, got_3, own, send_1, send_2, send_3, one):
+    one[...] = one_ref[...] + (got_1[0:992, :].astype(F32) + got_2[...].astype(F32) + got_3[0:992, :].astype(F32))
+    for s, out in enumerate((own, send_1, send_2, send_3)):
+        out[...] = one[pl.ds(pl.multiple_of((place_ref[1] + s) % 4 * 248, 8), 248), :]
+
+
+def _second_two_kernel(
+    place_ref, faces_ref, x_edges_ref, two_ref, got_1, got_2, got_3, sides_ref, own, send_1, send_2, send_3, two
 ):
-    gx, x, core = place_ref[0], place_ref[1], place_ref[2]
-    one[...] = one_ref[...] + (one_1[...].astype(F32) + one_2[...].astype(F32) + one_3[...].astype(F32))
-    two[...] = two_ref[...] + (two_1[0:992, :].astype(F32) + two_2[...].astype(F32) + two_3[0:992, :].astype(F32))
-    for s, (to_one, to_two) in enumerate(
-        ((own_one, own_two), (send_one_1, send_two_1), (send_one_2, send_two_2), (send_one_3, send_two_3))
-    ):
-        to_one[...] = one[pl.ds(pl.multiple_of((x + s) % 4 * 248, 8), 248), :]
-        to_two[0:248, :] = two[pl.ds(pl.multiple_of((gx + s) % 4 * 248, 8), 248), :]
+    x, core = place_ref[1], place_ref[2]
+    two[...] = two_ref[...] + (got_1[0:992, :].astype(F32) + got_2[...].astype(F32) + got_3[0:992, :].astype(F32))
+    for s, out in enumerate((own, send_1, send_2, send_3)):
+        out[0:248, :] = two[pl.ds(pl.multiple_of((place_ref[0] + s) % 4 * 248, 8), 248), :]
     near = faces_ref[...].astype(F32)
     near_first = jnp.concatenate([near[i * 32 : i * 32 + 16] for i in range(4)], axis=0)
     near_last = jnp.concatenate([near[i * 32 + 16 : i * 32 + 32] for i in range(4)], axis=0)
-    low = two_1[992:1056, :].astype(F32) * _flag((core == 0) & (x > 0)) + near_last * _flag(core == 1)
-    high = two_3[992:1056, :].astype(F32) * _flag((core == 1) & (x < 3)) + near_first * _flag(core == 0)
-    grown = jnp.concatenate([coarse_ref[...], _wide(low, 16).astype(BF16), _wide(high, 16).astype(BF16)], axis=0)
-    grown_ref[...] = grown
-    faces = _dot(x_faces_ref[...], grown)
+    low = got_1[992:1056, :].astype(F32) * _flag((core == 0) & (x > 0)) + near_last * _flag(core == 1)
+    high = got_3[992:1056, :].astype(F32) * _flag((core == 1) & (x < 3)) + near_first * _flag(core == 0)
+    sides = jnp.concatenate([_wide(low, 16).astype(BF16), _wide(high, 16).astype(BF16)], axis=0)
+    sides_ref[...] = sides
+    edges = _dot(x_edges_ref[...], sides)
     for lane in range(4):
-        send_two_1[248 + lane * 48 : 296 + lane * 48, :] = faces[48:96, lane * 128 : (lane + 1) * 128]
-        send_two_3[248 + lane * 48 : 296 + lane * 48, :] = faces[0:48, lane * 128 : (lane + 1) * 128]
+        send_1[248 + lane * 16 : 264 + lane * 16, :] = edges[16:32, lane * 128 : (lane + 1) * 128]
+        send_3[248 + lane * 16 : 264 + lane * 16, :] = edges[0:16, lane * 128 : (lane + 1) * 128]
 
 
 def _third_kernel(
-    place_ref, grown_ref, z_faces_ref, one_ref, one_1, one_2, one_3, two_ref, two_1, two_2, two_3,
+    place_ref, coarse_ref, sides_ref, x_low, x_high, z_faces_ref, one_ref, one_1, one_2, one_3, two_ref, two_1, two_2, two_3,
     grown_out, keep_ref, send_ref, other_ref, rows, chunks,
 ):
     gx, gz = place_ref[0], place_ref[3]
@@ -440,9 +452,11 @@
     half = (gz + gz // 4) % 2
     keep_ref[...] = chunks[half]
     send_ref[0:256, :] = chunks[1 - half]
-    low = _wide(two_1[248:440, :] * _flag(gx > 0), 48).astype(BF16)
-    high = _wide(two_3[248:440, :] * _flag(gx < 3), 48).astype(BF16)
-    grown = jnp.concatenate([grown_ref[...], low, high], axis=0)
+    grown = [coarse_ref[...], sides_ref[...]]
+    for cells, edges, there in ((x_low, two_1, _flag(gx > 0)), (x_high, two_3, _flag(gx < 3))):
+        grown.append(_wide(cells[992:1120, :].astype(F32) * there, 32).astype(BF16))
+        grown.append(_wide(edges[248:312, :] * there, 16).astype(BF16))
+    grown = jnp.concatenate(grown, axis=0)
     grown_out[...] = grown
     faces = _dot(z_faces_ref[...], grown)
     even = _flag(gz % 2 == 0)
@@ -453,7 +467,7 @@
         other_ref[lane * 48 : (lane + 1) * 48, :] = there[:, lane * 128 : (lane + 1) * 128]
 
 
-def _fourth_kernel(place_ref, grown_ref, padded_ref, keep_ref, got_ref, other_ref, bottom_ref, slope_ref, keep_out, send_out, both):
+def _fourth_kernel(place_ref, keep_ref, got_ref, keep_out, send_out, both):
     gz = place_ref[3]
     mine = keep_ref[...] + got_ref[0:256, :]
     both[0] = mine[0:128]
@@ -461,7 +475,10 @@
     half = (gz // 2 + gz // 4) % 2
     keep_out[...] = both[half]
     send_out[...] = both[1 - half]
-    even = _flag(gz % 2 == 0)
+
+
+def _pad_kernel(place_ref, grown_ref, padded_ref, got_ref, other_ref, bottom_ref, slope_ref):
+    even = _flag(place_ref[3] % 2 == 0)
     here, there = got_ref[256:448, :], other_ref[...].astype(F32)
     low = _wide(there * even + here * (1.0 - even), 48).astype(BF16)
     high = _wide(here * even + there * (1.0 - even), 48).astype(BF16)
@@ -470,68 +487,72 @@
     slope_ref[...] = padded[:, 256:512]
 
 
+def _clip_kernel(place_ref, total_ref, both_ref, out_ref):
+    total = jnp.sum(total_ref[...], axis=1, keepdims=True)
+    factor = jnp.minimum(1.0, jnp.sqrt(PARAMS / (total + 1e-06)))
+    out_ref[...] = both_ref[pl.ds(pl.multiple_of(place_ref[3] // 4 * 64, 64), 62), :] * factor
+
+
 def scattered_sum(place, keep, send, coarse):
-    gz = lax.axis_index("gz")
-    half, quarter = ((992, 128), BF16), ((248, 128), F32)
-    half_and_faces, quarter_and_faces = ((1056, 128), BF16), ((440, 128), F32)
+    def f32_rows(n):
+        return ((n, 128), F32)
+
+    def rows(n):
+        return ((n, 128), BF16)
+
     got = paired(send, "core", 1)
-    outs = (((992, 128), F32),) * 2 + (((128, 128), BF16),) + (half,) * 3 + (half_and_faces, half, half_and_faces)
-    one, two, faces, *sends = _call(_split_kernel, outs, place, keep, got)
+    outs = (f32_rows(992), f32_rows(992), rows(128), rows(1120), rows(992), rows(1120), rows(1056), rows(992), rows(1056))
+    one, two, faces, *sends = _call(_split_kernel, outs, place, keep, got, coarse)
     got_one = [turned(sends[s - 1], "gx", s) for s in (1, 2, 3)]
     got_two = [turned(sends[s + 2], "x", s) for s in (1, 2, 3)]
-    outs = (((96, 512), BF16),) + (quarter,) * 5 + (quarter_and_faces, quarter, quarter_and_faces)
-    grown, one, two, *sends = _call(
-        _second_kernel, outs, place, coarse, faces, jnp.asarray(X_FACES, BF16), one, *got_one, two, *got_two,
-        scratch=((992, 128), (992, 128)),
-    )
-    got_one = [turned(sends[s - 1], "x", s) for s in (1, 2, 3)]
-    got_two = [turned(sends[s + 2], "gx", s) for s in (1, 2, 3)]
-    outs = (((192, 512), BF16), ((256, 128), F32), ((448, 128), F32), ((192, 128), BF16))
+    one, *sends_one = _call(_second_one_kernel, (f32_rows(248),) * 4, place, one, *got_one, scratch=((992, 128),))
+    x_low, x_high = got_one[0], got_one[2]
+    got_one = [turned(sends_one[s - 1], "x", s) for s in (1, 2, 3)]
+    outs = (((32, 512), BF16), f32_rows(248), f32_rows(312), f32_rows(248), f32_rows(312))
+    sides, two, *sends_two = _call(
+        _second_two_kernel, outs, place, faces, jnp.asarray(X_EDGES, BF16), two, *got_two, scratch=((992, 128),)
+    )
+    got_two = [turned(sends_two[s - 1], "gx", s) for s in (1, 2, 3)]
+    outs = (((192, 512), BF16), f32_rows(256), f32_rows(448), rows(192))
     grown, keep, send, other = _call(
-        _third_kernel, outs, place, grown, jnp.asarray(Z_FACES, BF16), one, *got_one, two, *got_two,
+        _third_kernel, outs, place, coarse, sides, x_low, x_high, jnp.asarray(Z_FACES, BF16), one, *got_one, two, *got_two,
         scratch=((496, 128), (2, 256, 128)),
     )
     got = paired(send, "gz", 1)
     other = lax.ppermute(other, "gz", [(i, j) for i in range(8) for j in [((i + 1) ^ 1) - 1] if 0 <= j < 8])
-    outs = (((288, 256), BF16),) * 2 + (((128, 128), F32),) * 2
-    bottom_pad, slope_pad, keep, send = _call(
-        _fourth_kernel, outs, place, grown, jnp.asarray(PADDED, BF16), keep, got, other, scratch=((2, 128, 128),)
-    )
-    mine = keep + paired(send, "gz", 2)
-    mine = mine + paired(mine, "gz", 7)
-    squares = jnp.sum(mine * mine, axis=0, keepdims=True)
-    pads = [p.reshape(2, 4, 6, 6, 256) for p in (bottom_pad, slope_pad)]
-    return at(mine.reshape(2, 64, 128), gz // 4, 0)[:62], squares, pads
+    keep, send = _call(_fourth_kernel, (f32_rows(128),) * 2, place, keep, got, scratch=((2, 128, 128),))
+    pads = _call(_pad_kernel, (((288, 256), BF16),) * 2, place, grown, jnp.asarray(PADDED, BF16), got, other)
+    return keep, send, [p.reshape(2, 4, 6, 6, 256) for p in pads]
 
 
 def local(activation, w_in, w_up, w_out, cotangent):
     place = jnp.stack([lax.axis_index(a) for a in ("gx", "x", "core", "gz")]).astype(jnp.int32)
-    own = activation.reshape(512, 128)
-    act, cot, pooled, faces = extended(place, own, cotangent.reshape(512, 128))
+    own, act, cot, pooled, faces = extended(place, activation.reshape(512, 128), cotangent.reshape(512, 128))
     w_back = w_out.reshape(27, 256, 128).transpose(0, 2, 1).reshape(3456, 256)
     keep, send, coarse, d_direct = gradients(place, own, cot, pooled, *faces, w_in, w_back, w_up)
-    mine, total, (bottom_pad, slope_pad) = scattered_sum(place, keep, send, coarse)
-
-    def rounds(value, *others, axis, masks):
-        for mask in masks:
-            value = value + paired(value, axis, mask)
-        return lax.optimization_barrier((value, *others))
-
-    total, bottom_pad, act = rounds(total, bottom_pad, act, axis="core", masks=(1,))
+    keep, send, (bottom_pad, slope_pad) = scattered_sum(place, keep, send, coarse)
+
     (active_pad,) = _call(_grow_z_kernel, (((120, 10, 128), BF16),), place, act, *faces, scratch=((120, 24, 128),))
-    active_pad = active_pad.reshape(2, 6, 10, 10, 128)
     upward_pad = up_conv(bottom_pad, w_up).astype(BF16)[:, 1:-1, 1:-1, 1:-1]
-    joined_pad = jnp.concatenate([active_pad, upward_pad], axis=4)
-    total, joined_pad = rounds(total, joined_pad, axis="gx", masks=(1,))
+    joined_pad = jnp.concatenate([active_pad.reshape(2, 6, 10, 10, 128), upward_pad], axis=4)
+    mine = keep + paired(send, "gz", 2)
+    mine, joined_pad, slope_pad = lax.optimization_barrier((mine, joined_pad, slope_pad))
+
     output = conv_forward(joined_pad, w_out).astype(BF16)
-    total, output, slope_pad = rounds(total, output, slope_pad, axis="gx", masks=(3,))
+    mine = mine + paired(mine, "gz", 7)
+    total = jnp.sum(mine * mine, axis=0, keepdims=True)
+    total = total + paired(total, "core", 1)
+    total, output, slope_pad = lax.optimization_barrier((total, output, slope_pad))
+
     d_pooled = conv_transpose(slope_pad, w_in)
     d_activation = (d_direct.reshape(activation.shape) + spread(d_pooled) * 0.125).astype(BF16)
-    total, d_activation = rounds(total, d_activation, axis="x", masks=(1,))
-    (total,) = rounds(total, axis="x", masks=(3,))
-    (total,) = rounds(total, axis="gz", masks=(1, 2))
-    factor = jnp.minimum(1.0, jnp.sqrt(PARAMS / (jnp.sum(total) + 1e-06)))
-    return (output, d_activation, (mine * factor).reshape(-1))
+    total = total + paired(total, "gx", 1)
+    total = total + paired(total, "gx", 3)
+    total, d_activation = lax.optimization_barrier((total, d_activation))
+    for axis, mask in (("x", 1), ("x", 3), ("gz", 1), ("gz", 2)):
+        total = total + paired(total, axis, mask)
+    (clipped,) = _call(_clip_kernel, (((62, 128), F32),), place, total, mine)
+    return (output, d_activation, clipped.reshape(-1))
 
 
 def solution(mesh):

time: 143 us -> 133 us (0.930)
  starting transfers between devices: 64.2 us -> 60.1 us
  local copies, waits for them, and re-layouts: 14.4 us -> 10.3 us
  waiting for transfers between devices: 39.2 us -> 36.2 us
    unnamed x45 -> x33, local copies, waits for them, and re-layouts: 10.8 us -> 5.83 us
    ppermute x12, starting transfers between devices: 31 us -> 28.6 us  [turned(): lax.ppermute(array, axis, [(i, (i + shift) % count) for i in range(count)])]
    pallas_call x8 -> x11, Pallas kernels: 6.98 us -> 9.17 us  [_call(): pl.pallas_call(kernel, out_shape=tuple((jax.ShapeDtypeStruct(shape, kind)...]
    ppermute x12, waiting for transfers between devices: 9.27 us -> 7.61 us  [turned(): lax.ppermute(array, axis, [(i, (i + shift) % count) for i in range(count)])]
    ppermute x11, starting transfers between devices: 18.4 us -> 16.7 us  [paired(): return lax.ppermute(array, axis, [(i, i ^ bit) for i in range(count)])]
    ppermute x1, waiting for transfers between devices: 2.05 us -> 0.41 us  [scattered_sum(): lax.ppermute(other, 'gz', [(i, j) for i in range(8) for j in [(i + 1 ^ 1)...]
  transfers between devices with their start and end apart: 30 -> 30, of which waited for: 15 -> 15; matrix products, arithmetic and copies ran while one was open for 7% -> 9% of each run, Pallas kernels for 0% -> 2%
where the time goes in v2:
time: 133 us; the launch traced here: 132 us
  starting transfers between devices  60.1 us (45%)
  waiting for transfers between devices  36.2 us (27%)
  Pallas kernels  16.7 us (13%)
  local copies, waits for them, and re-layouts  10.3 us (8%)
  matrix products  6.25 us (5%)
  other arithmetic  1.91 us (1%)
    ppermute x12, starting transfers between devices, turned(): lax.ppermute(array, axis, [(i, (i + shift) % count) for i in range(count)])  28.6 us
    ppermute x11, waiting for transfers between devices, paired(): return lax.ppermute(array, axis, [(i, i ^ bit) for i in range(count)])  25.5 us
    ppermute x11, starting transfers between devices, paired(): return lax.ppermute(array, axis, [(i, i ^ bit) for i in range(count)])  16.7 us
    pallas_call x11, Pallas kernels, _call(): pl.pallas_call(kernel, out_shape=tuple((jax.ShapeDtypeStruct(shape, kind)...  9.17 us
    ppermute x12, waiting for transfers between devices, turned(): lax.ppermute(array, axis, [(i, (i + shift) % count) for i in range(count)])  7.61 us
    pallas_call x1, Pallas kernels, gradients(): pl.pallas_call(_gradients_kernel, out_shape=(shape((7936, 128), F32), sha...  7.48 us
    ppermute x1, starting transfers between devices, scattered_sum(): lax.ppermute(other, 'gz', [(i, j) for i in range(8) for j in [(i + 1 ^ 1)...  6.03 us
    unnamed x33, local copies, waits for them, and re-layouts  5.83 us
  transfers between devices with their start and end apart: 30, of which 15 were waited for; matrix products, arithmetic and copies ran while one was open for 9% of the time, Pallas kernels for 2%

profile of v2, /device:TPU:32, one launch (start us, length us, event | category | flops | bytes accessed | tf_op | source)
XLA Modules:
  0.0 132.5 jit_solution(5650285478619865972)
XLA Ops:
  0.7 0.9 copy-done.2
  1.6 0.9 copy-done.3
  3.2 1.7 %collective-permute-start = (bf16[288,128]{1,0:T(8,128)(2,1)S(1)}, bf16[288,128]{1,0:T(8,128)(2,1)S(1)}, u32[]{:S(2)}, u32[]{:S(2)}) collective-permute-start(bf16[288,128]{1,0:T(8,128)(2,1)S(1)} %get-tuple-element.59), channel_id=1, source_target_pairs={{0,64},{64,0},{128,192},{192,128},{1,65},{65,1},{129,193},{193,129... | collective-permute-start | bytes 221192 | tf_op jit(solution)/shard_map/ppermute | solution.py:236
  5.6 2.1 %collective-permute-done.got_here = bf16[288,128]{1,0:T(8,128)(2,1)S(1)} collective-permute-done((bf16[288,128]{1,0:T(8,128)(2,1)S(1)}, bf16[288,128]{1,0:T(8,128)(2,1)S(1)}, u32[]{:S(2)}, u32[]{:S(2)}) %collective-permute-start) | collective-permute-done | bytes 73760 | tf_op jit(solution)/shard_map/ppermute | solution.py:236
  9.7 1.0 shard_map.141
  10.7 0.8 copy-done.8
  11.5 1.8 %collective-permute-start.4 = (bf16[304,128]{1,0:T(8,128)(2,1)S(1)}, bf16[304,128]{1,0:T(8,128)(2,1)S(1)}, u32[]{:S(2)}, u32[]{:S(2)}) collective-permute-start(bf16[304,128]{1,0:T(8,128)(2,1)S(1)} %get-tuple-element.68), channel_id=1, source_target_pairs={{0,1},{1,0},{2,3},{3,2},{4,5},{5,4},{6,7},{7,6},{8,9},{9,8},{10,11... | collective-permute-start | bytes 233480 | tf_op jit(solution)/shard_map/ppermute | solution.py:236
  13.3 3.9 %collective-permute-start.5 = (bf16[304,128]{1,0:T(8,128)(2,1)S(1)}, bf16[304,128]{1,0:T(8,128)(2,1)S(1)}, u32[]{:S(2)}, u32[]{:S(2)}) collective-permute-start(bf16[304,128]{1,0:T(8,128)(2,1)S(1)} %get-tuple-element.69), channel_id=1, source_target_pairs={{1,2},{2,1},{3,4},{4,3},{5,6},{6,5},{9,10},{10,9},{11,12},{12,11},... | collective-permute-start | bytes 233480 | tf_op jit(solution)/shard_map/ppermute | solution.py:236
  17.3 2.7 %copy.20 = bf16[27,256,128]{1,2,0:T(8,128)(2,1)S(1)} copy(bf16[27,256,128]{2,1,0:T(8,128)(2,1)} %bitcast.39) | data formatting | bytes 3538944 | tf_op jit(solution)/shard_map/reshape | solution.py:531
  20.0 1.5 %copy-done.6 = bf16[3456,256]{1,0:T(8,128)(2,1)S(1)} copy-done((bf16[3456,256]{1,0:T(8,128)(2,1)S(1)}, bf16[3456,256]{1,0:T(8,128)(2,1)}, u32[]{:S(2)}) %copy-start.6) | copy-done | bytes 1769496
  21.5 1.0 copy-done.9
  22.5 7.5 %shard_map.142 = (f32[7936,128]{1,0:T(8,128)S(1)}, bf16[8064,128]{1,0:T(8,128)(2,1)S(1)}, bf16[64,512]{1,0:T(8,128)(2,1)S(1)}, f32[512,128]{1,0:T(8,128)S(1)}) custom-call(s32[4]{0:T(128)S(1)} %pad_add_fusion.place_ref, bf16[512,128]{1,0:T(8,128)(2,1)S(1)} %get-tuple-element.56.act_ref, f32[960,128]{1,0:T(8,128)S(1)} %copy-done.9, ...), custom_call_target="tpu_custom_call" | custom-call | flops 2500000000 | bytes 16000000 | tf_op jit(solution)/shard_map/pallas_call | solution.py:359
  30.0 4.3 %collective-permute-start.6 = (bf16[8064,128]{1,0:T(8,128)(2,1)S(1)}, bf16[8064,128]{1,0:T(8,128)(2,1)S(1)}, u32[]{:S(2)}, u32[]{:S(2)}) collective-permute-start(bf16[8064,128]{1,0:T(8,128)(2,1)S(1)} %get-tuple-element.72), channel_id=1, source_target_pairs={{0,8},{8,0},{1,9},{9,1},{2,10},{10,2},{3,11},{11,3},{4,12},{12,4},... | collective-permute-start | bytes 6193160 | tf_op jit(solution)/shard_map/ppermute | solution.py:389
  34.3 3.7 %collective-permute-done.6.got_ref = bf16[8064,128]{1,0:T(8,128)(2,1)S(1)} collective-permute-done((bf16[8064,128]{1,0:T(8,128)(2,1)S(1)}, bf16[8064,128]{1,0:T(8,128)(2,1)S(1)}, u32[]{:S(2)}, u32[]{:S(2)}) %collective-permute-start.6) | collective-permute-done | bytes 2064416 | tf_op jit(solution)/shard_map/ppermute | solution.py:389
  38.1 1.0 shard_map.143
  39.1 3.6 %collective-permute-start.8 = (bf16[992,128]{1,0:T(8,128)(2,1)S(1)}, bf16[992,128]{1,0:T(8,128)(2,1)S(1)}, u32[]{:S(2)}, u32[]{:S(2)}) collective-permute-start(bf16[992,128]{1,0:T(8,128)(2,1)S(1)} %get-tuple-element.76), channel_id=1, source_target_pairs={{0,32},{16,48},{32,0},{48,16},{1,33},{17,49},{33,1},{49,17},{2,34}... | collective-permute-start | bytes 761864 | tf_op jit(solution)/shard_map/ppermute | solution.py:384
  43.2 2.6 %collective-permute-start.9 = (bf16[1056,128]{1,0:T(8,128)(2,1)S(1)}, bf16[1056,128]{1,0:T(8,128)(2,1)S(1)}, u32[]{:S(2)}, u32[]{:S(2)}) collective-permute-start(bf16[1056,128]{1,0:T(8,128)(2,1)S(1)} %get-tuple-element.77), channel_id=1, source_target_pairs={{0,48},{16,0},{32,16},{48,32},{1,49},{17,1},{33,17},{49,33},{2,50}... | collective-permute-start | bytes 811016 | tf_op jit(solution)/shard_map/ppermute | solution.py:384
  45.9 4.3 %collective-permute-start.10 = (bf16[1120,128]{1,0:T(8,128)(2,1)S(1)}, bf16[1120,128]{1,0:T(8,128)(2,1)S(1)}, u32[]{:S(2)}, u32[]{:S(2)}) collective-permute-start(bf16[1120,128]{1,0:T(8,128)(2,1)S(1)} %get-tuple-element.79), channel_id=1, source_target_pairs={{0,64},{64,128},{128,192},{192,0},{1,65},{65,129},{129,193},{193,1... | collective-permute-start | bytes 860168 | tf_op jit(solution)/shard_map/ppermute | solution.py:384
  50.2 5.8 %collective-permute-start.12 = (bf16[992,128]{1,0:T(8,128)(2,1)S(1)}, bf16[992,128]{1,0:T(8,128)(2,1)S(1)}, u32[]{:S(2)}, u32[]{:S(2)}) collective-permute-start(bf16[992,128]{1,0:T(8,128)(2,1)S(1)} %get-tuple-element.82), channel_id=1, source_target_pairs={{0,128},{64,192},{128,0},{192,64},{1,129},{65,193},{129,1},{193,65... | collective-permute-start | bytes 761864 | tf_op jit(solution)/shard_map/ppermute | solution.py:384
  56.0 0.9 shard_map.144
  56.9 5.5 %collective-permute-start.17 = (f32[248,128]{1,0:T(8,128)S(1)}, f32[248,128]{1,0:T(8,128)S(1)}, u32[]{:S(2)}, u32[]{:S(2)}) collective-permute-start(f32[248,128]{1,0:T(8,128)S(1)} %get-tuple-element.89), channel_id=1, source_target_pairs={{0,128},{64,192},{128,0},{192,64},{1,129},{65,193},{129,1},{193,65... | collective-permute-start | bytes 380936 | tf_op jit(solution)/shard_map/ppermute | solution.py:384
  62.4 2.4 %collective-permute-done.12.got_2 = bf16[992,128]{1,0:T(8,128)(2,1)S(1)} collective-permute-done((bf16[992,128]{1,0:T(8,128)(2,1)S(1)}, bf16[992,128]{1,0:T(8,128)(2,1)S(1)}, u32[]{:S(2)}, u32[]{:S(2)}) %collective-permute-start.12) | collective-permute-done | bytes 253984 | tf_op jit(solution)/shard_map/ppermute | solution.py:384
  64.9 2.8 %collective-permute-start.18 = (f32[312,128]{1,0:T(8,128)S(1)}, f32[312,128]{1,0:T(8,128)S(1)}, u32[]{:S(2)}, u32[]{:S(2)}) collective-permute-start(f32[312,128]{1,0:T(8,128)S(1)} %get-tuple-element.90), channel_id=1, source_target_pairs={{0,192},{64,0},{128,64},{192,128},{1,193},{65,1},{129,65},{193,129... | collective-permute-start | bytes 479240 | tf_op jit(solution)/shard_map/ppermute | solution.py:384
  67.7 0.8 shard_map.145
  68.5 2.1 %collective-permute-start.14 = (f32[248,128]{1,0:T(8,128)S(1)}, f32[248,128]{1,0:T(8,128)S(1)}, u32[]{:S(2)}, u32[]{:S(2)}) collective-permute-start(f32[248,128]{1,0:T(8,128)S(1)} %get-tuple-element.85), channel_id=1, source_target_pairs={{0,32},{16,48},{32,0},{48,16},{1,33},{17,49},{33,1},{49,17},{2,34}... | collective-permute-start | bytes 380936 | tf_op jit(solution)/shard_map/ppermute | solution.py:384
  70.6 1.1 collective-permute-start.15
  71.8 4.6 %collective-permute-done.13.one_1 = f32[248,128]{1,0:T(8,128)S(1)} collective-permute-done((f32[248,128]{1,0:T(8,128)S(1)}, f32[248,128]{1,0:T(8,128)S(1)}, u32[]{:S(2)}, u32[]{:S(2)}) %collective-permute-start.13) | collective-permute-done | bytes 127008 | tf_op jit(solution)/shard_map/ppermute | solution.py:384
  76.9 0.7 shard_map.146
  77.8 6.0 %collective-permute-start.21 = (bf16[192,128]{1,0:T(8,128)(2,1)S(1)}, bf16[192,128]{1,0:T(8,128)(2,1)S(1)}, u32[]{:S(2)}, u32[]{:S(2)}) collective-permute-start(bf16[192,128]{1,0:T(8,128)(2,1)S(1)} %get-tuple-element.97), channel_id=1, source_target_pairs={{1,2},{2,1},{3,4},{4,3},{5,6},{6,5},{9,10},{10,9},{11,12},{12,11},... | collective-permute-start | bytes 147464 | tf_op jit(solution)/shard_map/ppermute | solution.py:522
  83.8 0.7 shard_map.148
  84.6 0.9 copy.22
  85.9 0.9 shard_map.149
  88.4 2.8 %collective-permute-start.20 = (f32[128,128]{1,0:T(8,128)S(1)}, f32[128,128]{1,0:T(8,128)S(1)}, u32[]{:S(2)}, u32[]{:S(2)}) collective-permute-start(f32[128,128]{1,0:T(8,128)S(1)} %get-tuple-element.94), channel_id=1, source_target_pairs={{0,2},{1,3},{2,0},{3,1},{4,6},{5,7},{6,4},{7,5},{8,10},{9,11},{10,... | collective-permute-start | bytes 196616 | tf_op jit(solution)/shard_map/ppermute | solution.py:389
  91.2 1.1 pad_maximum_fusion
  92.3 1.4 %collective-permute-done.20 = f32[128,128]{1,0:T(8,128)S(1)} collective-permute-done((f32[128,128]{1,0:T(8,128)S(1)}, f32[128,128]{1,0:T(8,128)S(1)}, u32[]{:S(2)}, u32[]{:S(2)}) %collective-permute-start.20) | collective-permute-done | bytes 65568 | tf_op jit(solution)/shard_map/ppermute | solution.py:389
  93.7 3.9 %collective-permute-start.22 = (f32[128,128]{1,0:T(8,128)S(1)}, f32[128,128]{1,0:T(8,128)S(1)}, u32[]{:S(2)}, u32[]{:S(2)}) collective-permute-start(f32[128,128]{1,0:T(8,128)S(1)} %add.30), channel_id=1, source_target_pairs={{0,7},{1,6},{2,5},{3,4},{4,3},{5,2},{6,1},{7,0},{8,15},{9,14},{10,... | collective-permute-start | bytes 196616 | tf_op jit(solution)/shard_map/ppermute | solution.py:389
  97.6 3.5 %collective-permute-done.22 = f32[128,128]{1,0:T(8,128)S(1)} collective-permute-done((f32[128,128]{1,0:T(8,128)S(1)}, f32[128,128]{1,0:T(8,128)S(1)}, u32[]{:S(2)}, u32[]{:S(2)}) %collective-permute-start.22) | collective-permute-done | bytes 65568 | tf_op jit(solution)/shard_map/ppermute | solution.py:389
  101.5 5.1 %convolution_convert_fusion.1 = bf16[2,4,8,8,128]{4,0,3,2,1:T(2,128)(2,1)S(1)} fusion(bf16[3,3,3,256,128]{4,3,2,1,0:T(8,128)(2,1)S(1)} %bitcast.40, bf16[2,6,10,10,256]{4,1,3,2,0:T(8,128)(2,1)} %pad_maximum_fusion), kind=kOutput, calls=%fused_computation.2 | convolution fusion | flops 906035200 | bytes 2514944 | tf_op jit(solution)/shard_map/conv_general_dilated | solution.py:18
  106.7 0.8 convolution_multiply_fusion
  107.5 2.6 %collective-permute-done.24 = f32[1,128]{1,0:T(1,128)S(1)} collective-permute-done((f32[1,128]{1,0:T(1,128)S(1)}, f32[1,128]{1,0:T(1,128)S(1)}, u32[]{:S(2)}, u32[]{:S(2)}) %collective-permute-start.24) | collective-permute-done | bytes 544 | tf_op jit(solution)/shard_map/ppermute | solution.py:389
  111.0 4.0 %collective-permute-done.25 = f32[1,128]{1,0:T(1,128)S(1)} collective-permute-done((f32[1,128]{1,0:T(1,128)S(1)}, f32[1,128]{1,0:T(1,128)S(1)}, u32[]{:S(2)}, u32[]{:S(2)}) %collective-permute-start.25) | collective-permute-done | bytes 544 | tf_op jit(solution)/shard_map/ppermute | solution.py:389
  115.5 3.0 %collective-permute-done.26 = f32[1,128]{1,0:T(1,128)S(1)} collective-permute-done((f32[1,128]{1,0:T(1,128)S(1)}, f32[1,128]{1,0:T(1,128)S(1)}, u32[]{:S(2)}, u32[]{:S(2)}) %collective-permute-start.26) | collective-permute-done | bytes 544 | tf_op jit(solution)/shard_map/ppermute | solution.py:389
  118.5 2.5 %collective-permute-start.27 = (f32[1,128]{1,0:T(1,128)S(1)}, f32[1,128]{1,0:T(1,128)S(1)}, u32[]{:S(2)}, u32[]{:S(2)}) collective-permute-start(f32[1,128]{1,0:T(1,128)S(1)} %add.36), channel_id=1, source_target_pairs={{0,48},{16,32},{32,16},{48,0},{1,49},{17,33},{33,17},{49,1},{2,50}... | collective-permute-start | bytes 1544 | tf_op jit(solution)/shard_map/ppermute | solution.py:389
  121.0 2.3 %collective-permute-done.27 = f32[1,128]{1,0:T(1,128)S(1)} collective-permute-done((f32[1,128]{1,0:T(1,128)S(1)}, f32[1,128]{1,0:T(1,128)S(1)}, u32[]{:S(2)}, u32[]{:S(2)}) %collective-permute-start.27) | collective-permute-done | bytes 544 | tf_op jit(solution)/shard_map/ppermute | solution.py:389
  123.3 3.5 %collective-permute-done.28 = f32[1,128]{1,0:T(1,128)S(1)} collective-permute-done((f32[1,128]{1,0:T(1,128)S(1)}, f32[1,128]{1,0:T(1,128)S(1)}, u32[]{:S(2)}, u32[]{:S(2)}) %collective-permute-start.28) | collective-permute-done | bytes 544 | tf_op jit(solution)/shard_map/ppermute | solution.py:389
  126.8 2.3 %collective-permute-start.29 = (f32[1,128]{1,0:T(1,128)S(1)}, f32[1,128]{1,0:T(1,128)S(1)}, u32[]{:S(2)}, u32[]{:S(2)}) collective-permute-start(f32[1,128]{1,0:T(1,128)S(1)} %add.38), channel_id=1, source_target_pairs={{0,2},{1,3},{2,0},{3,1},{4,6},{5,7},{6,4},{7,5},{8,10},{9,11},{10,... | collective-permute-start | bytes 1544 | tf_op jit(solution)/shard_map/ppermute | solution.py:389
  129.7 1.5 %collective-permute-done.29 = f32[1,128]{1,0:T(1,128)S(1)} collective-permute-done((f32[1,128]{1,0:T(1,128)S(1)}, f32[1,128]{1,0:T(1,128)S(1)}, u32[]{:S(2)}, u32[]{:S(2)}) %collective-permute-start.29) | collective-permute-done | bytes 544 | tf_op jit(solution)/shard_map/ppermute | solution.py:389
  131.2 1.3 shard_map.150
  (80 shorter events, 9.5 us)
Async XLA Ops:
  0.7 0.9 copy-start.2
  1.6 0.9 copy-start.3
  3.2 4.4 %collective-permute-start = (bf16[288,128]{1,0:T(8,128)(2,1)S(1)}, bf16[288,128]{1,0:T(8,128)(2,1)S(1)}, u32[]{:S(2)}, u32[]{:S(2)}) collective-permute-start(bf16[288,128]{1,0:T(8,128)(2,1)S(1)} %get-tuple-element.59), channel_id=1, source_target_pairs={{0,64},{64,0},{128,192},{192,128},{1,65},{65,1},{129,193},{193,129... | collective-permute-start | bytes 221192 | tf_op jit(solution)/shard_map/ppermute | solution.py:236
  4.9 2.8 %collective-permute-start.1 = (bf16[288,128]{1,0:T(8,128)(2,1)S(1)}, bf16[288,128]{1,0:T(8,128)(2,1)S(1)}, u32[]{:S(2)}, u32[]{:S(2)}) collective-permute-start(bf16[288,128]{1,0:T(8,128)(2,1)S(1)} %get-tuple-element.60), channel_id=1, source_target_pairs={{64,128},{128,64},{65,129},{129,65},{66,130},{130,66},{67,131},{13... | collective-permute-start | bytes 221192 | tf_op jit(solution)/shard_map/ppermute | solution.py:236
  8.4 1.3 collective-permute-start.2
  8.5 1.2 collective-permute-start.3
  10.7 0.8 copy-start.8
  11.5 8.5 %collective-permute-start.4 = (bf16[304,128]{1,0:T(8,128)(2,1)S(1)}, bf16[304,128]{1,0:T(8,128)(2,1)S(1)}, u32[]{:S(2)}, u32[]{:S(2)}) collective-permute-start(bf16[304,128]{1,0:T(8,128)(2,1)S(1)} %get-tuple-element.68), channel_id=1, source_target_pairs={{0,1},{1,0},{2,3},{3,2},{4,5},{5,4},{6,7},{7,6},{8,9},{9,8},{10,11... | collective-permute-start | bytes 233480 | tf_op jit(solution)/shard_map/ppermute | solution.py:236
  13.3 6.7 %collective-permute-start.5 = (bf16[304,128]{1,0:T(8,128)(2,1)S(1)}, bf16[304,128]{1,0:T(8,128)(2,1)S(1)}, u32[]{:S(2)}, u32[]{:S(2)}) collective-permute-start(bf16[304,128]{1,0:T(8,128)(2,1)S(1)} %get-tuple-element.69), channel_id=1, source_target_pairs={{1,2},{2,1},{3,4},{4,3},{5,6},{6,5},{9,10},{10,9},{11,12},{12,11},... | collective-permute-start | bytes 233480 | tf_op jit(solution)/shard_map/ppermute | solution.py:236
  17.2 2.8 %copy-start = (bf16[2048,128]{1,0:T(8,128)(2,1)S(1)}, bf16[2048,128]{1,0:T(8,128)(2,1)}, u32[]{:S(2)}) copy-start(bf16[2048,128]{1,0:T(8,128)(2,1)} %w_up_hbm.1) | copy-start | bytes 1572868
  17.2 2.8 %copy-start.10 = (bf16[144,48]{1,0:T(8,128)(2,1)S(1)}, bf16[144,48]{1,0:T(8,128)(2,1)}, u32[]{:S(2)}) copy-start(bf16[144,48]{1,0:T(8,128)(2,1)} %constant.36.clone.sel_ref) | copy-start | bytes 41476
  17.2 2.8 %copy-start.11 = (bf16[128,128]{1,0:T(8,128)(2,1)S(1)}, bf16[128,128]{1,0:T(8,128)(2,1)}, u32[]{:S(2)}) copy-start(bf16[128,128]{1,0:T(8,128)(2,1)} %constant.37.clone.perm_ref) | copy-start | bytes 98308
  17.3 2.8 %copy-start.12 = (bf16[128,128]{1,0:T(8,128)(2,1)S(1)}, bf16[128,128]{1,0:T(8,128)(2,1)}, u32[]{:S(2)}) copy-start(bf16[128,128]{1,0:T(8,128)(2,1)} %constant.38.clone.perm_t_ref) | copy-start | bytes 98308
  17.3 2.8 %copy-start.13 = (bf16[32,64]{1,0:T(8,128)(2,1)S(1)}, bf16[32,64]{1,0:T(8,128)(2,1)}, u32[]{:S(2)}) copy-start(bf16[32,64]{1,0:T(8,128)(2,1)} %constant.39.clone.y_faces_ref) | copy-start | bytes 12292
  20.0 1.5 %copy-start.6 = (bf16[3456,256]{1,0:T(8,128)(2,1)S(1)}, bf16[3456,256]{1,0:T(8,128)(2,1)}, u32[]{:S(2)}) copy-start(bf16[3456,256]{1,0:T(8,128)(2,1)} %w_in_hbm.1) | copy-start | bytes 5308420
  21.5 1.0 copy-start.9
  30.0 8.0 %collective-permute-start.6 = (bf16[8064,128]{1,0:T(8,128)(2,1)S(1)}, bf16[8064,128]{1,0:T(8,128)(2,1)S(1)}, u32[]{:S(2)}, u32[]{:S(2)}) collective-permute-start(bf16[8064,128]{1,0:T(8,128)(2,1)S(1)} %get-tuple-element.72), channel_id=1, source_target_pairs={{0,8},{8,0},{1,9},{9,1},{2,10},{10,2},{3,11},{11,3},{4,12},{12,4},... | collective-permute-start | bytes 6193160 | tf_op jit(solution)/shard_map/ppermute | solution.py:389
  38.0 18.0 %copy-start.5 = (bf16[32,32]{1,0:T(8,128)(2,1)S(1)}, bf16[32,32]{1,0:T(8,128)(2,1)}, u32[]{:S(2)}) copy-start(bf16[32,32]{1,0:T(8,128)(2,1)} %constant.40.clone.x_edges_ref) | copy-start | bytes 6148
  39.0 37.9 %copy-start.4 = (bf16[96,192]{1,0:T(8,128)(2,1)S(1)}, bf16[96,192]{1,0:T(8,128)(2,1)}, u32[]{:S(2)}) copy-start(bf16[96,192]{1,0:T(8,128)(2,1)} %constant.41.clone.z_faces_ref) | copy-start | bytes 110596
  39.1 11.1 %collective-permute-start.8 = (bf16[992,128]{1,0:T(8,128)(2,1)S(1)}, bf16[992,128]{1,0:T(8,128)(2,1)S(1)}, u32[]{:S(2)}, u32[]{:S(2)}) collective-permute-start(bf16[992,128]{1,0:T(8,128)(2,1)S(1)} %get-tuple-element.76), channel_id=1, source_target_pairs={{0,32},{16,48},{32,0},{48,16},{1,33},{17,49},{33,1},{49,17},{2,34}... | collective-permute-start | bytes 761864 | tf_op jit(solution)/shard_map/ppermute | solution.py:384
  42.6 13.4 %collective-permute-start.7 = (bf16[1056,128]{1,0:T(8,128)(2,1)S(1)}, bf16[1056,128]{1,0:T(8,128)(2,1)S(1)}, u32[]{:S(2)}, u32[]{:S(2)}) collective-permute-start(bf16[1056,128]{1,0:T(8,128)(2,1)S(1)} %get-tuple-element.75), channel_id=1, source_target_pairs={{0,16},{16,32},{32,48},{48,0},{1,17},{17,33},{33,49},{49,1},{2,18}... | collective-permute-start | bytes 811016 | tf_op jit(solution)/shard_map/ppermute | solution.py:384
  43.2 12.8 %collective-permute-start.9 = (bf16[1056,128]{1,0:T(8,128)(2,1)S(1)}, bf16[1056,128]{1,0:T(8,128)(2,1)S(1)}, u32[]{:S(2)}, u32[]{:S(2)}) collective-permute-start(bf16[1056,128]{1,0:T(8,128)(2,1)S(1)} %get-tuple-element.77), channel_id=1, source_target_pairs={{0,48},{16,0},{32,16},{48,32},{1,49},{17,1},{33,17},{49,33},{2,50}... | collective-permute-start | bytes 811016 | tf_op jit(solution)/shard_map/ppermute | solution.py:384
  45.9 21.8 %collective-permute-start.10 = (bf16[1120,128]{1,0:T(8,128)(2,1)S(1)}, bf16[1120,128]{1,0:T(8,128)(2,1)S(1)}, u32[]{:S(2)}, u32[]{:S(2)}) collective-permute-start(bf16[1120,128]{1,0:T(8,128)(2,1)S(1)} %get-tuple-element.79), channel_id=1, source_target_pairs={{0,64},{64,128},{128,192},{192,0},{1,65},{65,129},{129,193},{193,1... | collective-permute-start | bytes 860168 | tf_op jit(solution)/shard_map/ppermute | solution.py:384
  50.2 17.5 %collective-permute-start.11 = (bf16[1120,128]{1,0:T(8,128)(2,1)S(1)}, bf16[1120,128]{1,0:T(8,128)(2,1)S(1)}, u32[]{:S(2)}, u32[]{:S(2)}) collective-permute-start(bf16[1120,128]{1,0:T(8,128)(2,1)S(1)} %get-tuple-element.80), channel_id=1, source_target_pairs={{0,192},{64,0},{128,64},{192,128},{1,193},{65,1},{129,65},{193,129... | collective-permute-start | bytes 860168 | tf_op jit(solution)/shard_map/ppermute | solution.py:384
  50.2 14.7 %collective-permute-start.12 = (bf16[992,128]{1,0:T(8,128)(2,1)S(1)}, bf16[992,128]{1,0:T(8,128)(2,1)S(1)}, u32[]{:S(2)}, u32[]{:S(2)}) collective-permute-start(bf16[992,128]{1,0:T(8,128)(2,1)S(1)} %get-tuple-element.82), channel_id=1, source_target_pairs={{0,128},{64,192},{128,0},{192,64},{1,129},{65,193},{129,1},{193,65... | collective-permute-start | bytes 761864 | tf_op jit(solution)/shard_map/ppermute | solution.py:384
  56.9 13.7 %collective-permute-start.17 = (f32[248,128]{1,0:T(8,128)S(1)}, f32[248,128]{1,0:T(8,128)S(1)}, u32[]{:S(2)}, u32[]{:S(2)}) collective-permute-start(f32[248,128]{1,0:T(8,128)S(1)} %get-tuple-element.89), channel_id=1, source_target_pairs={{0,128},{64,192},{128,0},{192,64},{1,129},{65,193},{129,1},{193,65... | collective-permute-start | bytes 380936 | tf_op jit(solution)/shard_map/ppermute | solution.py:384
  62.4 14.5 %collective-permute-start.16 = (f32[312,128]{1,0:T(8,128)S(1)}, f32[312,128]{1,0:T(8,128)S(1)}, u32[]{:S(2)}, u32[]{:S(2)}) collective-permute-start(f32[312,128]{1,0:T(8,128)S(1)} %get-tuple-element.88), channel_id=1, source_target_pairs={{0,64},{64,128},{128,192},{192,0},{1,65},{65,129},{129,193},{193,1... | collective-permute-start | bytes 479240 | tf_op jit(solution)/shard_map/ppermute | solution.py:384
  64.9 12.1 %collective-permute-start.18 = (f32[312,128]{1,0:T(8,128)S(1)}, f32[312,128]{1,0:T(8,128)S(1)}, u32[]{:S(2)}, u32[]{:S(2)}) collective-permute-start(f32[312,128]{1,0:T(8,128)S(1)} %get-tuple-element.90), channel_id=1, source_target_pairs={{0,192},{64,0},{128,64},{192,128},{1,193},{65,1},{129,65},{193,129... | collective-permute-start | bytes 479240 | tf_op jit(solution)/shard_map/ppermute | solution.py:384
  68.4 7.9 %collective-permute-start.13 = (f32[248,128]{1,0:T(8,128)S(1)}, f32[248,128]{1,0:T(8,128)S(1)}, u32[]{:S(2)}, u32[]{:S(2)}) collective-permute-start(f32[248,128]{1,0:T(8,128)S(1)} %get-tuple-element.84), channel_id=1, source_target_pairs={{0,16},{16,32},{32,48},{48,0},{1,17},{17,33},{33,49},{49,1},{2,18}... | collective-permute-start | bytes 380936 | tf_op jit(solution)/shard_map/ppermute | solution.py:384
  68.5 7.8 %collective-permute-start.14 = (f32[248,128]{1,0:T(8,128)S(1)}, f32[248,128]{1,0:T(8,128)S(1)}, u32[]{:S(2)}, u32[]{:S(2)}) collective-permute-start(f32[248,128]{1,0:T(8,128)S(1)} %get-tuple-element.85), channel_id=1, source_target_pairs={{0,32},{16,48},{32,0},{48,16},{1,33},{17,49},{33,1},{49,17},{2,34}... | collective-permute-start | bytes 380936 | tf_op jit(solution)/shard_map/ppermute | solution.py:384
  70.6 6.3 %collective-permute-start.15 = (f32[248,128]{1,0:T(8,128)S(1)}, f32[248,128]{1,0:T(8,128)S(1)}, u32[]{:S(2)}, u32[]{:S(2)}) collective-permute-start(f32[248,128]{1,0:T(8,128)S(1)} %get-tuple-element.86), channel_id=1, source_target_pairs={{0,48},{16,0},{32,16},{48,32},{1,49},{17,1},{33,17},{49,33},{2,50}... | collective-permute-start | bytes 380936 | tf_op jit(solution)/shard_map/ppermute | solution.py:384
  76.9 9.0 %copy-start.1 = (bf16[288,288]{1,0:T(8,128)(2,1)S(1)}, bf16[288,288]{1,0:T(8,128)(2,1)}, u32[]{:S(2)}) copy-start(bf16[288,288]{1,0:T(8,128)(2,1)} %constant.42.clone.padded_ref) | copy-start | bytes 497668
  77.7 8.2 %collective-permute-start.19 = (f32[448,128]{1,0:T(8,128)S(1)}, f32[448,128]{1,0:T(8,128)S(1)}, u32[]{:S(2)}, u32[]{:S(2)}) collective-permute-start(f32[448,128]{1,0:T(8,128)S(1)} %get-tuple-element.92), channel_id=1, source_target_pairs={{0,1},{1,0},{2,3},{3,2},{4,5},{5,4},{6,7},{7,6},{8,9},{9,8},{10,11... | collective-permute-start | bytes 688136 | tf_op jit(solution)/shard_map/ppermute | solution.py:389
  77.8 8.1 %collective-permute-start.21 = (bf16[192,128]{1,0:T(8,128)(2,1)S(1)}, bf16[192,128]{1,0:T(8,128)(2,1)S(1)}, u32[]{:S(2)}, u32[]{:S(2)}) collective-permute-start(bf16[192,128]{1,0:T(8,128)(2,1)S(1)} %get-tuple-element.97), channel_id=1, source_target_pairs={{1,2},{2,1},{3,4},{4,3},{5,6},{6,5},{9,10},{10,9},{11,12},{12,11},... | collective-permute-start | bytes 147464 | tf_op jit(solution)/shard_map/ppermute | solution.py:522
  86.8 4.4 %copy-start.15 = (bf16[2,6,10,10,128]{4,1,3,2,0:T(8,128)(2,1)S(1)}, bf16[2,6,10,10,128]{4,1,3,2,0:T(8,128)(2,1)}, u32[]{:S(2)}) copy-start(bf16[2,6,10,10,128]{4,1,3,2,0:T(8,128)(2,1)} %copy.22) | copy-start | bytes 921604
  87.7 13.7 %copy-start.14 = (bf16[6912,128]{1,0:T(8,128)(2,1)S(1)}, bf16[6912,128]{1,0:T(8,128)(2,1)}, u32[]{:S(2)}) copy-start(bf16[6912,128]{1,0:T(8,128)(2,1)} %param.15) | copy-start | bytes 5308420
  88.4 5.3 %collective-permute-start.20 = (f32[128,128]{1,0:T(8,128)S(1)}, f32[128,128]{1,0:T(8,128)S(1)}, u32[]{:S(2)}, u32[]{:S(2)}) collective-permute-start(f32[128,128]{1,0:T(8,128)S(1)} %get-tuple-element.94), channel_id=1, source_target_pairs={{0,2},{1,3},{2,0},{3,1},{4,6},{5,7},{6,4},{7,5},{8,10},{9,11},{10,... | collective-permute-start | bytes 196616 | tf_op jit(solution)/shard_map/ppermute | solution.py:389
  93.7 7.4 %collective-permute-start.22 = (f32[128,128]{1,0:T(8,128)S(1)}, f32[128,128]{1,0:T(8,128)S(1)}, u32[]{:S(2)}, u32[]{:S(2)}) collective-permute-start(f32[128,128]{1,0:T(8,128)S(1)} %add.30), channel_id=1, source_target_pairs={{0,7},{1,6},{2,5},{3,4},{4,3},{5,2},{6,1},{7,0},{8,15},{9,14},{10,... | collective-permute-start | bytes 196616 | tf_op jit(solution)/shard_map/ppermute | solution.py:389
  101.1 5.4 %collective-permute-start.23 = (f32[1,128]{1,0:T(1,128)S(1)}, f32[1,128]{1,0:T(1,128)S(1)}, u32[]{:S(2)}, u32[]{:S(2)}) collective-permute-start(f32[1,128]{1,0:T(1,128)S(1)} %bitcast.44), channel_id=1, source_target_pairs={{0,8},{8,0},{1,9},{9,1},{2,10},{10,2},{3,11},{11,3},{4,12},{12,4},... | collective-permute-start | bytes 1544 | tf_op jit(solution)/shard_map/ppermute | solution.py:389
  101.5 5.2 %copy-start.7 = (bf16[3456,256]{1,0:T(8,128)(2,1)S(1)}, bf16[3456,256]{1,0:T(8,128)(2,1)}, u32[]{:S(2)}) copy-start(bf16[3456,256]{1,0:T(8,128)(2,1)} %w_in_hbm.1) | copy-start | bytes 5308420
  106.6 3.6 %collective-permute-start.24 = (f32[1,128]{1,0:T(1,128)S(1)}, f32[1,128]{1,0:T(1,128)S(1)}, u32[]{:S(2)}, u32[]{:S(2)}) collective-permute-start(f32[1,128]{1,0:T(1,128)S(1)} %bitcast_add_fusion), channel_id=1, source_target_pairs={{0,64},{64,0},{128,192},{192,128},{1,65},{65,1},{129,193},{193,129... | collective-permute-start | bytes 1544 | tf_op jit(solution)/shard_map/ppermute | solution.py:389
  110.2 4.8 %collective-permute-start.25 = (f32[1,128]{1,0:T(1,128)S(1)}, f32[1,128]{1,0:T(1,128)S(1)}, u32[]{:S(2)}, u32[]{:S(2)}) collective-permute-start(f32[1,128]{1,0:T(1,128)S(1)} %add.33), channel_id=1, source_target_pairs={{0,192},{64,128},{128,64},{192,0},{1,193},{65,129},{129,65},{193,1... | collective-permute-start | bytes 1544 | tf_op jit(solution)/shard_map/ppermute | solution.py:389
  115.0 3.5 %collective-permute-start.26 = (f32[1,128]{1,0:T(1,128)S(1)}, f32[1,128]{1,0:T(1,128)S(1)}, u32[]{:S(2)}, u32[]{:S(2)}) collective-permute-start(f32[1,128]{1,0:T(1,128)S(1)} %add.34), channel_id=1, source_target_pairs={{0,16},{16,0},{32,48},{48,32},{1,17},{17,1},{33,49},{49,33},{2,18}... | collective-permute-start | bytes 1544 | tf_op jit(solution)/shard_map/ppermute | solution.py:389
  118.5 4.8 %collective-permute-start.27 = (f32[1,128]{1,0:T(1,128)S(1)}, f32[1,128]{1,0:T(1,128)S(1)}, u32[]{:S(2)}, u32[]{:S(2)}) collective-permute-start(f32[1,128]{1,0:T(1,128)S(1)} %add.36), channel_id=1, source_target_pairs={{0,48},{16,32},{32,16},{48,0},{1,49},{17,33},{33,17},{49,1},{2,50}... | collective-permute-start | bytes 1544 | tf_op jit(solution)/shard_map/ppermute | solution.py:389
  123.3 3.5 %collective-permute-start.28 = (f32[1,128]{1,0:T(1,128)S(1)}, f32[1,128]{1,0:T(1,128)S(1)}, u32[]{:S(2)}, u32[]{:S(2)}) collective-permute-start(f32[1,128]{1,0:T(1,128)S(1)} %add.37), channel_id=1, source_target_pairs={{0,1},{1,0},{2,3},{3,2},{4,5},{5,4},{6,7},{7,6},{8,9},{9,8},{10,11... | collective-permute-start | bytes 1544 | tf_op jit(solution)/shard_map/ppermute | solution.py:389
  126.8 4.4 %collective-permute-start.29 = (f32[1,128]{1,0:T(1,128)S(1)}, f32[1,128]{1,0:T(1,128)S(1)}, u32[]{:S(2)}, u32[]{:S(2)}) collective-permute-start(f32[1,128]{1,0:T(1,128)S(1)} %add.38), channel_id=1, source_target_pairs={{0,2},{1,3},{2,0},{3,1},{4,6},{5,7},{6,4},{7,5},{8,10},{9,11},{10,... | collective-permute-start | bytes 1544 | tf_op jit(solution)/shard_map/ppermute | solution.py:389

commit v3 on v2

--- a/solution.py
+++ b/solution.py
@@ -44,21 +44,6 @@
     return result.reshape(samples, 2 * size_x, 2 * size_y, 2 * size_z, -1)
 
 
-def _select_pooled():
-    sel = np.zeros((9, 4, 4, 48), np.float32)
-    for dy, dz, y, z in itertools.product(range(3), range(3), range(4), range(4)):
-        line, k = y + dy, z + dz - 1
-        sel[3 * dy + dz, y, z, 24 + line if k < 0 else 32 + line if k > 3 else line * 4 + k] = 1
-    return sel.reshape(144, 48)
-
-
-def _fine_from_blocks():
-    perm = np.zeros((128, 128), np.float32)
-    for a, y, z in itertools.product(range(2), range(8), range(8)):
-        perm[(a * 8 + y) * 8 + z, (a * 4 + (y % 2) * 2 + z % 2) * 16 + (y // 2) * 4 + z // 2] = 1
-    return perm
-
-
 def _picks(sources, width):
     picks = np.zeros((len(sources), width), np.float32)
     picks[np.arange(len(sources)), sources] = 1
@@ -82,10 +67,7 @@
     return 192 + line if z < 0 else 240 + line if z > 3 else _at_x(s, x, y, z)
 
 
-S2, X2, Y4, Z4 = range(2), range(2), range(4), range(4)
-X4, Y6, Z6 = range(-1, 3), range(-1, 5), range(-1, 5)
-Y_FACES = _picks([_at_y(s, x, y, z) for y in (0, 3) for s in S2 for x in X2 for z in Z4], 64)
-X_EDGES = _picks([e * 16 + (s * 2 + x) * 4 + z for x in (0, 1) for s in S2 for e in range(2) for z in Z4], 32)
+S2, X4, Y6, Z6 = range(2), range(-1, 3), range(-1, 5), range(-1, 5)
 Z_FACES = _picks([_at_x(s, x, y, z) for z in (0, 3) for s in S2 for x in X4 for y in Y6], 192)
 PADDED = _picks([_at_z(s, x, y, z) for s in S2 for x in X4 for y in Y6 for z in Z6], 288)
 
@@ -110,7 +92,7 @@
         in_specs=[pl.BlockSpec(memory_space=pltpu.SMEM)] + [vmem] * (len(args) - 1),
         out_specs=(vmem,) * len(outs),
         scratch_shapes=[pltpu.VMEM(shape, F32) for shape in scratch],
-        compiler_params=pltpu.CompilerParams(vmem_limit_bytes=24 * 1024 * 1024),
+        compiler_params=pltpu.CompilerParams(vmem_limit_bytes=12 * 1024 * 1024),
         cost_estimate=pl.CostEstimate(flops=1_000_000, bytes_accessed=4_000_000, transcendentals=0),
     )(*args)
 
@@ -153,16 +135,40 @@
     return (c == (((r >> 3) & 7) * 6 + y) * 4 + (r >> 6) * 3) & (y < 6)
 
 
-def _pool_kernel(place_ref, act_ref, cot_ref, act_out, cot_out, pooled_ref, here_ref, there_ref):
-    act_out[...] = act_ref[...]
-    cot_out[...] = cot_ref[...]
+def _pool_windows(r, c):
+    u = r >> 4
+    dy = (u * 11) >> 5
+    line, k = ((r >> 2) & 3) + dy, (r & 3) + u - 3 * dy - 1
+    return c == jnp.where(k < 0, 24 + line, jnp.where(k > 3, 32 + line, line * 4 + k))
+
+
+def _fine_from_blocks(r, c):
+    part = (r >> 6) * 4 + ((r >> 3) & 1) * 2 + (r & 1)
+    return c == part * 16 + ((r >> 4) & 3) * 4 + ((r >> 1) & 3)
+
+
+def _blocks_from_fine(r, c):
+    return _fine_from_blocks(c, r)
+
+
+def _y_faces(r, c):
+    return c == (((r >> 2) & 3) * 4 + (r >> 4) * 3) * 4 + (r & 3)
+
+
+def _x_edges(r, c):
+    return c == ((r >> 2) & 1) * 16 + (((r >> 3) & 1) * 2 + (r >> 4)) * 4 + (r & 3)
+
+
+def _pool_kernel(place_ref, both_ref, act_out, cot_out, pooled_ref, here_ref, there_ref):
+    act_out[...] = both_ref[0:512, :]
+    cot_out[...] = both_ref[512:1024, :]
     pool_of = _table(16, 128, _pool_of, 0.125)
-    planes = [_dot(pool_of, act_ref[g * 128 : (g + 1) * 128, :]) for g in range(4)]
+    planes = [_dot(pool_of, both_ref[g * 128 : (g + 1) * 128, :]) for g in range(4)]
     pooled = jnp.concatenate(planes, axis=0).astype(BF16)
     pooled_ref[...] = pooled
 
     def face(x):
-        fine = [ref[s * 256 + x * 192 : s * 256 + x * 192 + 64, :] for ref in (act_ref, cot_ref) for s in range(2)]
+        fine = [both_ref[s * 256 + x * 192 : s * 256 + x * 192 + 64, :] for s in range(4)]
         return jnp.concatenate(fine + [pooled[s * 32 + x * 16 : s * 32 + x * 16 + 16] for s in range(2)], axis=0).astype(F32)
 
     _pack(place_ref[0], face(0), face(1), here_ref, there_ref)
@@ -199,11 +205,11 @@
 
 def _grow_y_kernel(
     place_ref, act_ref, cot_ref, pooled_ref, got_here, got_there,
-    act_out, cot_out, pooled_out, here_ref, there_ref, act_lines,
+    act_out, cot_out, pooled_out, here_ref, there_ref, act_lines, cot_lines,
 ):
     low, high = _sides(place_ref[2], got_here, got_there)
     firsts, lasts = [], []
-    for i, (ref, out) in enumerate(((act_ref, act_lines), (cot_ref, cot_out))):
+    for i, (ref, out) in enumerate(((act_ref, act_lines), (cot_ref, cot_lines))):
         for p in range(12):
             at_face = slice(i * 96 + p * 8, i * 96 + p * 8 + 8)
             out[p * 80 : p * 80 + 8, :] = low[at_face]
@@ -213,6 +219,7 @@
         lasts.append(out[pl.ds(7, 120, 8), :])
     rows = jnp.concatenate([pooled_ref[...], low[192:224].astype(BF16), high[192:224].astype(BF16)], axis=0)
     act_out[...] = act_lines[...].astype(BF16)
+    cot_out[...] = cot_lines[...].astype(BF16)
     grown = _dot(_table(192, 192, _pool_grow_y), rows)
     pooled_out[...] = grown
     faces = _dot(_table(128, 192, _pool_z_faces), grown.astype(BF16))
@@ -236,20 +243,20 @@
     return lax.ppermute(here, axis, first_pairs), lax.ppermute(there, axis, second_pairs)
 
 
-def extended(place, act, cot):
+def extended(place, both):
     rows, f32_rows = lambda n: ((n, 128), BF16), lambda n: ((n, 128), F32)
-    own, cot, pooled, *faces = _call(_pool_kernel, (rows(512), rows(512), rows(64), rows(288), rows(288)), place, act, cot)
+    own, cot, pooled, *faces = _call(_pool_kernel, (rows(512), rows(512), rows(64), rows(288), rows(288)), place, both)
     outs = (f32_rows(768), f32_rows(768), rows(128), rows(224), rows(224))
     act, cot, pooled, *faces = _call(_grow_x_kernel, outs, place, own, cot, pooled, *traded(*faces, "gx"))
-    outs = (rows(960), f32_rows(960), f32_rows(192), rows(304), rows(304))
+    outs = (rows(960), rows(960), f32_rows(192), rows(304), rows(304))
     act, cot, pooled, *faces = _call(
-        _grow_y_kernel, outs, place, act, cot, pooled, *traded(*faces, ("x", "core")), scratch=((960, 128),)
+        _grow_y_kernel, outs, place, act, cot, pooled, *traded(*faces, ("x", "core")), scratch=((960, 128),) * 2
     )
     return own, act, cot, pooled, traded(*faces, "gz")
 
 
 def _gradients_kernel(
-    place_ref, act_ref, cot_ref, pool_ref, got_here, got_there, sel_ref, perm_ref, perm_t_ref, y_faces_ref,
+    place_ref, act_ref, cot_ref, pool_ref, got_here, got_there,
     w_in_hbm, w_back_hbm, w_up_hbm,
     keep_ref, send_ref, coarse_ref, d_act_ref,
     w_in, w_back, w_up, lines, shifted, pooled, spaced, sums, sem_in, sem_out,
@@ -281,7 +288,7 @@
         return copy
 
     low, high = _sides(place_ref[3], got_here, got_there)
-    lines[:, 8:16, :] = cot_ref[...].reshape(120, 8, 128)
+    lines[:, 8:16, :] = cot_ref[...].astype(F32).reshape(120, 8, 128)
     lines[:, 7:8, :] = low[120:240][:, None, :]
     lines[:, 16:17, :] = high[120:240][:, None, :]
     for dz in range(3):
@@ -290,10 +297,11 @@
             u = 8 - 3 * dy - dz
             shifted[:, :, :, u * 128 : (u + 1) * 128] = window[:, :, dy : dy + 8].reshape(2, 6, 64, 128).astype(BF16)
 
+    windows = _table(144, 48, _pool_windows)
     for g in range(8):
         at_face = slice(240 + g * 8, 248 + g * 8)
         plane = [pool_ref[g * 24 : (g + 1) * 24, :], low[at_face], high[at_face], jnp.zeros((8, 128), F32)]
-        picked = _dot(sel_ref[...], jnp.concatenate(plane, axis=0).astype(BF16))
+        picked = _dot(windows, jnp.concatenate(plane, axis=0).astype(BF16))
         for u in range(9):
             pooled[g // 4, g % 4, :, u * 128 : (u + 1) * 128] = picked[u * 16 : (u + 1) * 16].astype(BF16)
     loads[0].wait()
@@ -305,8 +313,9 @@
     bottom = bottom32.astype(BF16)
     loads[1].wait()
     parts = [_dot(bottom, w_up[p * 256 : (p + 1) * 256, :]).astype(BF16) for p in range(8)]
+    perm = _table(128, 128, _fine_from_blocks)
     upward = jnp.concatenate(
-        [_dot(perm_ref[...], jnp.concatenate([p[g * 16 : (g + 1) * 16] for p in parts], axis=0)) for g in range(4)], axis=0
+        [_dot(perm, jnp.concatenate([p[g * 16 : (g + 1) * 16] for p in parts], axis=0)) for g in range(4)], axis=0
     )
 
     loads[2].wait()
@@ -323,7 +332,8 @@
     copies = [ship(0, 4960, 7936)]
 
     d_upward = d_joined[:, 128:].astype(BF16)
-    planes = [_dot(perm_t_ref[...], d_upward[g * 128 : (g + 1) * 128]).astype(BF16) for g in range(4)]
+    perm = _table(128, 128, _blocks_from_fine)
+    planes = [_dot(perm, d_upward[g * 128 : (g + 1) * 128]).astype(BF16) for g in range(4)]
     blocks = [jnp.concatenate([plane[p * 16 : (p + 1) * 16] for plane in planes], axis=0) for p in range(8)]
     d_bottom = jnp.zeros((64, 256), F32)
     for p in range(8):
@@ -334,7 +344,7 @@
     slope = (d_bottom * squash * (1.0 + before * (1.0 - squash))).astype(BF16)
     coarse = jnp.concatenate([bottom, slope], axis=1)
     coarse_ref[...] = coarse
-    faces = _dot(y_faces_ref[...], coarse)
+    faces = _dot(_table(32, 64, _y_faces), coarse)
     for lane in range(4):
         send_ref[7936 + lane * 32 : 7968 + lane * 32, :] = faces[:, lane * 128 : (lane + 1) * 128].astype(BF16)
 
@@ -361,7 +371,7 @@
         out_shape=(
             shape((7936, 128), F32), shape((8064, 128), BF16), shape((64, 512), BF16), shape((512, 128), F32),
         ),
-        in_specs=[pl.BlockSpec(memory_space=pltpu.SMEM)] + [vmem] * 9 + [hbm] * 3,
+        in_specs=[pl.BlockSpec(memory_space=pltpu.SMEM)] + [vmem] * 5 + [hbm] * 3,
         out_specs=(vmem,) * 4,
         scratch_shapes=[
             pltpu.VMEM((3456, 256), BF16), pltpu.VMEM((3456, 256), BF16), pltpu.VMEM((2048, 128), BF16),
@@ -370,12 +380,11 @@
             pltpu.VMEM((2, 7936, 128), F32),
             pltpu.SemaphoreType.DMA((3,)), pltpu.SemaphoreType.DMA((2,)),
         ],
-        compiler_params=pltpu.CompilerParams(vmem_limit_bytes=32 * 1024 * 1024),
+        compiler_params=pltpu.CompilerParams(vmem_limit_bytes=26 * 1024 * 1024),
         cost_estimate=pl.CostEstimate(flops=2_500_000_000, bytes_accessed=16_000_000, transcendentals=16384),
     )(
         place, act, cot, pool, got_here, got_there,
-        jnp.asarray(_select_pooled(), BF16), jnp.asarray(_fine_from_blocks(), BF16), jnp.asarray(_fine_from_blocks().T, BF16),
-        jnp.asarray(Y_FACES, BF16), w_in, w_back, w_up,
+        w_in, w_back, w_up,
     )
 
 
@@ -419,7 +428,7 @@
 
 
 def _second_two_kernel(
-    place_ref, faces_ref, x_edges_ref, two_ref, got_1, got_2, got_3, sides_ref, own, send_1, send_2, send_3, two
+    place_ref, faces_ref, two_ref, got_1, got_2, got_3, sides_ref, own, send_1, send_2, send_3, two
 ):
     x, core = place_ref[1], place_ref[2]
     two[...] = two_ref[...] + (got_1[0:992, :].astype(F32) + got_2[...].astype(F32) + got_3[0:992, :].astype(F32))
@@ -432,7 +441,7 @@
     high = got_3[992:1056, :].astype(F32) * _flag((core == 1) & (x < 3)) + near_first * _flag(core == 0)
     sides = jnp.concatenate([_wide(low, 16).astype(BF16), _wide(high, 16).astype(BF16)], axis=0)
     sides_ref[...] = sides
-    edges = _dot(x_edges_ref[...], sides)
+    edges = _dot(_table(32, 32, _x_edges), sides)
     for lane in range(4):
         send_1[248 + lane * 16 : 264 + lane * 16, :] = edges[16:32, lane * 128 : (lane + 1) * 128]
         send_3[248 + lane * 16 : 264 + lane * 16, :] = edges[0:16, lane * 128 : (lane + 1) * 128]
@@ -510,7 +519,7 @@
     got_one = [turned(sends_one[s - 1], "x", s) for s in (1, 2, 3)]
     outs = (((32, 512), BF16), f32_rows(248), f32_rows(312), f32_rows(248), f32_rows(312))
     sides, two, *sends_two = _call(
-        _second_two_kernel, outs, place, faces, jnp.asarray(X_EDGES, BF16), two, *got_two, scratch=((992, 128),)
+        _second_two_kernel, outs, place, faces, two, *got_two, scratch=((992, 128),)
     )
     got_two = [turned(sends_two[s - 1], "gx", s) for s in (1, 2, 3)]
     outs = (((192, 512), BF16), f32_rows(256), f32_rows(448), rows(192))
@@ -521,34 +530,40 @@
     got = paired(send, "gz", 1)
     other = lax.ppermute(other, "gz", [(i, j) for i in range(8) for j in [((i + 1) ^ 1) - 1] if 0 <= j < 8])
     keep, send = _call(_fourth_kernel, (f32_rows(128),) * 2, place, keep, got, scratch=((2, 128, 128),))
-    pads = _call(_pad_kernel, (((288, 256), BF16),) * 2, place, grown, jnp.asarray(PADDED, BF16), got, other)
-    return keep, send, [p.reshape(2, 4, 6, 6, 256) for p in pads]
+    return keep, send, grown, got, other
 
 
 def local(activation, w_in, w_up, w_out, cotangent):
     place = jnp.stack([lax.axis_index(a) for a in ("gx", "x", "core", "gz")]).astype(jnp.int32)
-    own, act, cot, pooled, faces = extended(place, activation.reshape(512, 128), cotangent.reshape(512, 128))
+    both = jnp.concatenate([activation.reshape(512, 128), cotangent.reshape(512, 128)], axis=0)
+    own, act, cot, pooled, faces = extended(place, both)
     w_back = w_out.reshape(27, 256, 128).transpose(0, 2, 1).reshape(3456, 256)
     keep, send, coarse, d_direct = gradients(place, own, cot, pooled, *faces, w_in, w_back, w_up)
-    keep, send, (bottom_pad, slope_pad) = scattered_sum(place, keep, send, coarse)
-
+    keep, send, grown, got, other = scattered_sum(place, keep, send, coarse)
+
+    send, grown, act = lax.optimization_barrier((send, grown, act))
+    mine = keep + paired(send, "gz", 2)
+    pads = _call(_pad_kernel, (((288, 256), BF16),) * 2, place, grown, jnp.asarray(PADDED, BF16), got, other)
+    bottom_pad, slope_pad = (p.reshape(2, 4, 6, 6, 256) for p in pads)
     (active_pad,) = _call(_grow_z_kernel, (((120, 10, 128), BF16),), place, act, *faces, scratch=((120, 24, 128),))
     upward_pad = up_conv(bottom_pad, w_up).astype(BF16)[:, 1:-1, 1:-1, 1:-1]
     joined_pad = jnp.concatenate([active_pad.reshape(2, 6, 10, 10, 128), upward_pad], axis=4)
-    mine = keep + paired(send, "gz", 2)
     mine, joined_pad, slope_pad = lax.optimization_barrier((mine, joined_pad, slope_pad))
 
-    output = conv_forward(joined_pad, w_out).astype(BF16)
+    output_0 = conv_forward(joined_pad[:1], w_out).astype(BF16)
     mine = mine + paired(mine, "gz", 7)
     total = jnp.sum(mine * mine, axis=0, keepdims=True)
+    total, output_0, joined_pad = lax.optimization_barrier((total, output_0, joined_pad))
     total = total + paired(total, "core", 1)
-    total, output, slope_pad = lax.optimization_barrier((total, output, slope_pad))
-
+    total, joined_pad = lax.optimization_barrier((total, joined_pad))
+    output_1 = conv_forward(joined_pad[1:], w_out).astype(BF16)
+    total = total + paired(total, "gx", 1)
+    total, output_1, slope_pad = lax.optimization_barrier((total, output_1, slope_pad))
     d_pooled = conv_transpose(slope_pad, w_in)
     d_activation = (d_direct.reshape(activation.shape) + spread(d_pooled) * 0.125).astype(BF16)
-    total = total + paired(total, "gx", 1)
     total = total + paired(total, "gx", 3)
     total, d_activation = lax.optimization_barrier((total, d_activation))
+    output = jnp.concatenate([output_0, output_1], axis=0)
     for axis, mask in (("x", 1), ("x", 3), ("gz", 1), ("gz", 2)):
         total = total + paired(total, axis, mask)
     (clipped,) = _call(_clip_kernel, (((62, 128), F32),), place, total, mine)

time: 133 us -> 126 us (0.947)
  waiting for transfers between devices: 36.2 us -> 28.9 us
  local copies, waits for them, and re-layouts: 10.3 us -> 6.27 us
  starting transfers between devices: 60.1 us -> 62.1 us
    ppermute x11, waiting for transfers between devices: 25.5 us -> 17.1 us  [paired(): return lax.ppermute(array, axis, [(i, i ^ bit) for i in range(count)])]
    unnamed x33 -> x14, local copies, waits for them, and re-layouts: 5.83 us -> 2.41 us
    ppermute x11, starting transfers between devices: 16.7 us -> 18.5 us  [paired(): return lax.ppermute(array, axis, [(i, i ^ bit) for i in range(count)])]
    ppermute x1, waiting for transfers between devices: 0.41 us -> 1.84 us  [scattered_sum(): lax.ppermute(other, 'gz', [(i, j) for i in range(8) for j in [(i + 1 ^ 1)...]
    conv_general_dilated x1 -> x2, matrix products: 5.06 us -> 5.82 us  [conv_forward(): lax.conv_general_dilated(padded, kernel, (1, 1, 1), 'VALID', dimension_nu...]
  transfers between devices with their start and end apart: 30 -> 30, of which waited for: 15 -> 14; matrix products, arithmetic and copies ran while one was open for 9% -> 11% of each run, Pallas kernels for 2% -> 2%
where the time goes in v3:
time: 126 us; the launch traced here: 125 us
  starting transfers between devices  62.1 us (49%)
  waiting for transfers between devices  28.9 us (23%)
  Pallas kernels  16.7 us (13%)
  matrix products  7 us (6%)
  local copies, waits for them, and re-layouts  6.27 us (5%)
  other arithmetic  2.76 us (2%)
    ppermute x12, starting transfers between devices, turned(): lax.ppermute(array, axis, [(i, (i + shift) % count) for i in range(count)])  28.6 us
    ppermute x11, starting transfers between devices, paired(): return lax.ppermute(array, axis, [(i, i ^ bit) for i in range(count)])  18.5 us
    ppermute x11, waiting for transfers between devices, paired(): return lax.ppermute(array, axis, [(i, i ^ bit) for i in range(count)])  17.1 us
    pallas_call x11, Pallas kernels, _call(): pl.pallas_call(kernel, out_shape=tuple((jax.ShapeDtypeStruct(shape, kind)...  9.19 us
    pallas_call x1, Pallas kernels, gradients(): pl.pallas_call(_gradients_kernel, out_shape=(shape((7936, 128), F32), sha...  7.53 us
    ppermute x12, waiting for transfers between devices, turned(): lax.ppermute(array, axis, [(i, (i + shift) % count) for i in range(count)])  7.27 us
    ppermute x1, starting transfers between devices, scattered_sum(): lax.ppermute(other, 'gz', [(i, j) for i in range(8) for j in [(i + 1 ^ 1)...  6.03 us
    conv_general_dilated x2, matrix products, conv_forward(): lax.conv_general_dilated(padded, kernel, (1, 1, 1), 'VALID', dimension_nu...  5.82 us
  transfers between devices with their start and end apart: 30, of which 14 were waited for; matrix products, arithmetic and copies ran while one was open for 11% of the time, Pallas kernels for 2%

profile of v3, /device:TPU:32, one launch (start us, length us, event | category | flops | bytes accessed | tf_op | source)
XLA Modules:
  0.0 124.8 jit_solution(9977505948768381591)
XLA Ops:
  0.6 1.0 pad_maximum_fusion.1.both_ref
  1.7 0.7 shard_map.94
  2.4 1.7 %collective-permute-start = (bf16[288,128]{1,0:T(8,128)(2,1)S(1)}, bf16[288,128]{1,0:T(8,128)(2,1)S(1)}, u32[]{:S(2)}, u32[]{:S(2)}) collective-permute-start(bf16[288,128]{1,0:T(8,128)(2,1)S(1)} %get-tuple-element.67), channel_id=1, source_target_pairs={{0,64},{64,0},{128,192},{192,128},{1,65},{65,1},{129,193},{193,129... | collective-permute-start | bytes 221192 | tf_op jit(solution)/shard_map/ppermute | solution.py:243
  4.8 2.1 %collective-permute-done.got_here = bf16[288,128]{1,0:T(8,128)(2,1)S(1)} collective-permute-done((bf16[288,128]{1,0:T(8,128)(2,1)S(1)}, bf16[288,128]{1,0:T(8,128)(2,1)S(1)}, u32[]{:S(2)}, u32[]{:S(2)}) %collective-permute-start) | collective-permute-done | bytes 73760 | tf_op jit(solution)/shard_map/ppermute | solution.py:243
  6.9 0.7 shard_map.95
  8.9 1.0 shard_map.96
  9.9 1.9 %collective-permute-start.4 = (bf16[304,128]{1,0:T(8,128)(2,1)S(1)}, bf16[304,128]{1,0:T(8,128)(2,1)S(1)}, u32[]{:S(2)}, u32[]{:S(2)}) collective-permute-start(bf16[304,128]{1,0:T(8,128)(2,1)S(1)} %get-tuple-element.76), channel_id=1, source_target_pairs={{0,1},{1,0},{2,3},{3,2},{4,5},{5,4},{6,7},{7,6},{8,9},{9,8},{10,11... | collective-permute-start | bytes 233480 | tf_op jit(solution)/shard_map/ppermute | solution.py:243
  11.8 3.9 %collective-permute-start.5 = (bf16[304,128]{1,0:T(8,128)(2,1)S(1)}, bf16[304,128]{1,0:T(8,128)(2,1)S(1)}, u32[]{:S(2)}, u32[]{:S(2)}) collective-permute-start(bf16[304,128]{1,0:T(8,128)(2,1)S(1)} %get-tuple-element.77), channel_id=1, source_target_pairs={{1,2},{2,1},{3,4},{4,3},{5,6},{6,5},{9,10},{10,9},{11,12},{12,11},... | collective-permute-start | bytes 233480 | tf_op jit(solution)/shard_map/ppermute | solution.py:243
  15.7 2.7 %copy.15 = bf16[27,256,128]{1,2,0:T(8,128)(2,1)S(1)} copy(bf16[27,256,128]{2,1,0:T(8,128)(2,1)} %bitcast.37) | data formatting | bytes 3538944 | tf_op jit(solution)/shard_map/reshape | solution.py:540
  18.5 1.5 %copy-done.3 = bf16[3456,256]{1,0:T(8,128)(2,1)S(1)} copy-done((bf16[3456,256]{1,0:T(8,128)(2,1)S(1)}, bf16[3456,256]{1,0:T(8,128)(2,1)}, u32[]{:S(2)}) %copy-start.3) | copy-done | bytes 1769496
  19.9 7.5 %shard_map.97 = (f32[7936,128]{1,0:T(8,128)S(1)}, bf16[8064,128]{1,0:T(8,128)(2,1)S(1)}, bf16[64,512]{1,0:T(8,128)(2,1)S(1)}, f32[512,128]{1,0:T(8,128)S(1)}) custom-call(s32[4]{0:T(128)S(1)} %pad_add_fusion.place_ref, bf16[512,128]{1,0:T(8,128)(2,1)S(1)} %get-tuple-element.64.act_ref, bf16[960,128]{1,0:T(8,128)(2,1)S(1)} %get-tuple-element.74.cot_ref, ...), custom_call_target="tpu_custom_call" | custom-call | flops 2500000000 | bytes 16000000 | tf_op jit(solution)/shard_map/pallas_call | solution.py:369
  27.5 4.6 %collective-permute-start.6 = (bf16[8064,128]{1,0:T(8,128)(2,1)S(1)}, bf16[8064,128]{1,0:T(8,128)(2,1)S(1)}, u32[]{:S(2)}, u32[]{:S(2)}) collective-permute-start(bf16[8064,128]{1,0:T(8,128)(2,1)S(1)} %get-tuple-element.80), channel_id=1, source_target_pairs={{0,8},{8,0},{1,9},{9,1},{2,10},{10,2},{3,11},{11,3},{4,12},{12,4},... | collective-permute-start | bytes 6193160 | tf_op jit(solution)/shard_map/ppermute | solution.py:398
  32.0 3.7 %collective-permute-done.6.got_ref = bf16[8064,128]{1,0:T(8,128)(2,1)S(1)} collective-permute-done((bf16[8064,128]{1,0:T(8,128)(2,1)S(1)}, bf16[8064,128]{1,0:T(8,128)(2,1)S(1)}, u32[]{:S(2)}, u32[]{:S(2)}) %collective-permute-start.6) | collective-permute-done | bytes 2064416 | tf_op jit(solution)/shard_map/ppermute | solution.py:398
  35.8 1.0 shard_map.98
  36.8 3.3 %collective-permute-start.8 = (bf16[992,128]{1,0:T(8,128)(2,1)S(1)}, bf16[992,128]{1,0:T(8,128)(2,1)S(1)}, u32[]{:S(2)}, u32[]{:S(2)}) collective-permute-start(bf16[992,128]{1,0:T(8,128)(2,1)S(1)} %get-tuple-element.84), channel_id=1, source_target_pairs={{0,32},{16,48},{32,0},{48,16},{1,33},{17,49},{33,1},{49,17},{2,34}... | collective-permute-start | bytes 761864 | tf_op jit(solution)/shard_map/ppermute | solution.py:393
  40.6 2.6 %collective-permute-start.9 = (bf16[1056,128]{1,0:T(8,128)(2,1)S(1)}, bf16[1056,128]{1,0:T(8,128)(2,1)S(1)}, u32[]{:S(2)}, u32[]{:S(2)}) collective-permute-start(bf16[1056,128]{1,0:T(8,128)(2,1)S(1)} %get-tuple-element.85), channel_id=1, source_target_pairs={{0,48},{16,0},{32,16},{48,32},{1,49},{17,1},{33,17},{49,33},{2,50}... | collective-permute-start | bytes 811016 | tf_op jit(solution)/shard_map/ppermute | solution.py:393
  43.3 4.3 %collective-permute-start.10 = (bf16[1120,128]{1,0:T(8,128)(2,1)S(1)}, bf16[1120,128]{1,0:T(8,128)(2,1)S(1)}, u32[]{:S(2)}, u32[]{:S(2)}) collective-permute-start(bf16[1120,128]{1,0:T(8,128)(2,1)S(1)} %get-tuple-element.87), channel_id=1, source_target_pairs={{0,64},{64,128},{128,192},{192,0},{1,65},{65,129},{129,193},{193,1... | collective-permute-start | bytes 860168 | tf_op jit(solution)/shard_map/ppermute | solution.py:393
  47.6 6.2 %collective-permute-start.12 = (bf16[992,128]{1,0:T(8,128)(2,1)S(1)}, bf16[992,128]{1,0:T(8,128)(2,1)S(1)}, u32[]{:S(2)}, u32[]{:S(2)}) collective-permute-start(bf16[992,128]{1,0:T(8,128)(2,1)S(1)} %get-tuple-element.90), channel_id=1, source_target_pairs={{0,128},{64,192},{128,0},{192,64},{1,129},{65,193},{129,1},{193,65... | collective-permute-start | bytes 761864 | tf_op jit(solution)/shard_map/ppermute | solution.py:393
  53.7 0.9 shard_map.99
  54.6 5.3 %collective-permute-start.17 = (f32[248,128]{1,0:T(8,128)S(1)}, f32[248,128]{1,0:T(8,128)S(1)}, u32[]{:S(2)}, u32[]{:S(2)}) collective-permute-start(f32[248,128]{1,0:T(8,128)S(1)} %get-tuple-element.97), channel_id=1, source_target_pairs={{0,128},{64,192},{128,0},{192,64},{1,129},{65,193},{129,1},{193,65... | collective-permute-start | bytes 380936 | tf_op jit(solution)/shard_map/ppermute | solution.py:393
  59.9 2.1 %collective-permute-done.12.got_2 = bf16[992,128]{1,0:T(8,128)(2,1)S(1)} collective-permute-done((bf16[992,128]{1,0:T(8,128)(2,1)S(1)}, bf16[992,128]{1,0:T(8,128)(2,1)S(1)}, u32[]{:S(2)}, u32[]{:S(2)}) %collective-permute-start.12) | collective-permute-done | bytes 253984 | tf_op jit(solution)/shard_map/ppermute | solution.py:393
  62.0 3.1 %collective-permute-start.18 = (f32[312,128]{1,0:T(8,128)S(1)}, f32[312,128]{1,0:T(8,128)S(1)}, u32[]{:S(2)}, u32[]{:S(2)}) collective-permute-start(f32[312,128]{1,0:T(8,128)S(1)} %get-tuple-element.98), channel_id=1, source_target_pairs={{0,192},{64,0},{128,64},{192,128},{1,193},{65,1},{129,65},{193,129... | collective-permute-start | bytes 479240 | tf_op jit(solution)/shard_map/ppermute | solution.py:393
  65.1 0.8 shard_map.100
  66.0 2.1 %collective-permute-start.14 = (f32[248,128]{1,0:T(8,128)S(1)}, f32[248,128]{1,0:T(8,128)S(1)}, u32[]{:S(2)}, u32[]{:S(2)}) collective-permute-start(f32[248,128]{1,0:T(8,128)S(1)} %get-tuple-element.93), channel_id=1, source_target_pairs={{0,32},{16,48},{32,0},{48,16},{1,33},{17,49},{33,1},{49,17},{2,34}... | collective-permute-start | bytes 380936 | tf_op jit(solution)/shard_map/ppermute | solution.py:393
  68.1 1.1 collective-permute-start.15
  69.2 4.6 %collective-permute-done.13.one_1 = f32[248,128]{1,0:T(8,128)S(1)} collective-permute-done((f32[248,128]{1,0:T(8,128)S(1)}, f32[248,128]{1,0:T(8,128)S(1)}, u32[]{:S(2)}, u32[]{:S(2)}) %collective-permute-start.13) | collective-permute-done | bytes 127008 | tf_op jit(solution)/shard_map/ppermute | solution.py:393
  74.4 0.7 shard_map.101
  75.2 6.0 %collective-permute-start.21 = (bf16[192,128]{1,0:T(8,128)(2,1)S(1)}, bf16[192,128]{1,0:T(8,128)(2,1)S(1)}, u32[]{:S(2)}, u32[]{:S(2)}) collective-permute-start(bf16[192,128]{1,0:T(8,128)(2,1)S(1)} %get-tuple-element.108), channel_id=1, source_target_pairs={{1,2},{2,1},{3,4},{4,3},{5,6},{6,5},{9,10},{10,9},{11,12},{12,11},... | collective-permute-start | bytes 147464 | tf_op jit(solution)/shard_map/ppermute | solution.py:531
  81.8 1.8 %collective-permute-done.21.other_ref = bf16[192,128]{1,0:T(8,128)(2,1)S(1)} collective-permute-done((bf16[192,128]{1,0:T(8,128)(2,1)S(1)}, bf16[192,128]{1,0:T(8,128)(2,1)S(1)}, u32[]{:S(2)}, u32[]{:S(2)}) %collective-permute-start.21) | collective-permute-done | bytes 49184 | tf_op jit(solution)/shard_map/ppermute | solution.py:531
  83.7 0.9 shard_map.104
  84.6 2.4 %collective-permute-start.20 = (f32[128,128]{1,0:T(8,128)S(1)}, f32[128,128]{1,0:T(8,128)S(1)}, u32[]{:S(2)}, u32[]{:S(2)}) collective-permute-start(f32[128,128]{1,0:T(8,128)S(1)} %get-tuple-element.105), channel_id=1, source_target_pairs={{0,2},{1,3},{2,0},{3,1},{4,6},{5,7},{6,4},{7,5},{8,10},{9,11},{10,... | collective-permute-start | bytes 196616 | tf_op jit(solution)/shard_map/ppermute | solution.py:398
  87.0 0.7 shard_map.103
  90.1 4.7 %collective-permute-start.22 = (f32[128,128]{1,0:T(8,128)S(1)}, f32[128,128]{1,0:T(8,128)S(1)}, u32[]{:S(2)}, u32[]{:S(2)}) collective-permute-start(f32[128,128]{1,0:T(8,128)S(1)} %add.30), channel_id=1, source_target_pairs={{0,7},{1,6},{2,5},{3,4},{4,3},{5,2},{6,1},{7,0},{8,15},{9,14},{10,... | collective-permute-start | bytes 196616 | tf_op jit(solution)/shard_map/ppermute | solution.py:398
  94.8 2.8 %convolution_convert_fusion.2 = bf16[1,4,8,8,128]{4,0,3,2,1:T(2,128)(2,1)S(1)} fusion(bf16[3,3,3,256,128]{4,3,2,1,0:T(8,128)(2,1)S(1)} %bitcast.38, bf16[2,6,10,10,256]{4,0,3,2,1:T(2,128)(2,1)S(1)} %pad_maximum_fusion), kind=kOutput, calls=%fused_computation.3 | convolution fusion | flops 453017600 | bytes 2449408 | tf_op jit(solution)/shard_map/conv_general_dilated | solution.py:18
  97.8 1.1 collective-permute-done.23
  99.3 3.0 %convolution_convert_fusion.1 = bf16[1,4,8,8,128]{4,0,3,2,1:T(2,128)(2,1)S(1)} fusion(bf16[3,3,3,256,128]{4,3,2,1,0:T(8,128)(2,1)S(1)} %bitcast.39, bf16[2,6,10,10,256]{4,0,3,2,1:T(2,128)(2,1)S(1)} %pad_maximum_fusion), kind=kOutput, calls=%fused_computation.2 | convolution fusion | flops 453017600 | bytes 2449408 | tf_op jit(solution)/shard_map/conv_general_dilated | solution.py:18
  102.9 0.8 convolution_multiply_fusion
  103.8 0.7 add_convert_fusion
  104.5 2.7 %collective-permute-done.25 = f32[1,128]{1,0:T(1,128)S(1)} collective-permute-done((f32[1,128]{1,0:T(1,128)S(1)}, f32[1,128]{1,0:T(1,128)S(1)}, u32[]{:S(2)}, u32[]{:S(2)}) %collective-permute-start.25) | collective-permute-done | bytes 544 | tf_op jit(solution)/shard_map/ppermute | solution.py:398
  107.2 1.0 collective-permute-start.26
  108.2 2.6 %collective-permute-done.26 = f32[1,128]{1,0:T(1,128)S(1)} collective-permute-done((f32[1,128]{1,0:T(1,128)S(1)}, f32[1,128]{1,0:T(1,128)S(1)}, u32[]{:S(2)}, u32[]{:S(2)}) %collective-permute-start.26) | collective-permute-done | bytes 544 | tf_op jit(solution)/shard_map/ppermute | solution.py:398
  110.8 2.6 %collective-permute-start.27 = (f32[1,128]{1,0:T(1,128)S(1)}, f32[1,128]{1,0:T(1,128)S(1)}, u32[]{:S(2)}, u32[]{:S(2)}) collective-permute-start(f32[1,128]{1,0:T(1,128)S(1)} %add.36), channel_id=1, source_target_pairs={{0,48},{16,32},{32,16},{48,0},{1,49},{17,33},{33,17},{49,1},{2,50}... | collective-permute-start | bytes 1544 | tf_op jit(solution)/shard_map/ppermute | solution.py:398
  113.4 2.1 %collective-permute-done.27 = f32[1,128]{1,0:T(1,128)S(1)} collective-permute-done((f32[1,128]{1,0:T(1,128)S(1)}, f32[1,128]{1,0:T(1,128)S(1)}, u32[]{:S(2)}, u32[]{:S(2)}) %collective-permute-start.27) | collective-permute-done | bytes 544 | tf_op jit(solution)/shard_map/ppermute | solution.py:398
  115.6 3.4 %collective-permute-done.28 = f32[1,128]{1,0:T(1,128)S(1)} collective-permute-done((f32[1,128]{1,0:T(1,128)S(1)}, f32[1,128]{1,0:T(1,128)S(1)}, u32[]{:S(2)}, u32[]{:S(2)}) %collective-permute-start.28) | collective-permute-done | bytes 544 | tf_op jit(solution)/shard_map/ppermute | solution.py:398
  119.1 2.2 %collective-permute-start.29 = (f32[1,128]{1,0:T(1,128)S(1)}, f32[1,128]{1,0:T(1,128)S(1)}, u32[]{:S(2)}, u32[]{:S(2)}) collective-permute-start(f32[1,128]{1,0:T(1,128)S(1)} %add.38), channel_id=1, source_target_pairs={{0,2},{1,3},{2,0},{3,1},{4,6},{5,7},{6,4},{7,5},{8,10},{9,11},{10,... | collective-permute-start | bytes 1544 | tf_op jit(solution)/shard_map/ppermute | solution.py:398
  121.6 0.7 copy.21
  122.2 1.3 %collective-permute-done.29 = f32[1,128]{1,0:T(1,128)S(1)} collective-permute-done((f32[1,128]{1,0:T(1,128)S(1)}, f32[1,128]{1,0:T(1,128)S(1)}, u32[]{:S(2)}, u32[]{:S(2)}) %collective-permute-start.29) | collective-permute-done | bytes 544 | tf_op jit(solution)/shard_map/ppermute | solution.py:398
  123.5 1.3 %shard_map.105 = f32[62,128]{1,0:T(8,128)} custom-call(s32[4]{0:T(128)S(1)} %pad_add_fusion.place_ref, f32[1,128]{1,0:T(1,128)S(1)} %add.39.total_ref, f32[128,128]{1,0:T(8,128)S(1)} %get-tuple-element.132.both_ref), custom_call_target="tpu_custom_call" | custom-call | flops 1000000 | bytes 4000000 | tf_op jit(solution)/shard_map/pallas_call | solution.py:89
  (64 shorter events, 7.9 us)
Async XLA Ops:
  2.4 4.4 %collective-permute-start = (bf16[288,128]{1,0:T(8,128)(2,1)S(1)}, bf16[288,128]{1,0:T(8,128)(2,1)S(1)}, u32[]{:S(2)}, u32[]{:S(2)}) collective-permute-start(bf16[288,128]{1,0:T(8,128)(2,1)S(1)} %get-tuple-element.67), channel_id=1, source_target_pairs={{0,64},{64,0},{128,192},{192,128},{1,65},{65,1},{129,193},{193,129... | collective-permute-start | bytes 221192 | tf_op jit(solution)/shard_map/ppermute | solution.py:243
  4.1 2.8 %collective-permute-start.1 = (bf16[288,128]{1,0:T(8,128)(2,1)S(1)}, bf16[288,128]{1,0:T(8,128)(2,1)S(1)}, u32[]{:S(2)}, u32[]{:S(2)}) collective-permute-start(bf16[288,128]{1,0:T(8,128)(2,1)S(1)} %get-tuple-element.68), channel_id=1, source_target_pairs={{64,128},{128,64},{65,129},{129,65},{66,130},{130,66},{67,131},{13... | collective-permute-start | bytes 221192 | tf_op jit(solution)/shard_map/ppermute | solution.py:243
  7.6 1.3 %collective-permute-start.2 = (bf16[224,128]{1,0:T(8,128)(2,1)S(1)}, bf16[224,128]{1,0:T(8,128)(2,1)S(1)}, u32[]{:S(2)}, u32[]{:S(2)}) collective-permute-start(bf16[224,128]{1,0:T(8,128)(2,1)S(1)} %get-tuple-element.72), channel_id=1, source_target_pairs={{0,8},{8,0},{16,24},{24,16},{32,40},{40,32},{48,56},{56,48},{1,9},... | collective-permute-start | bytes 172040 | tf_op jit(solution)/shard_map/ppermute | solution.py:243
  7.7 1.2 collective-permute-start.3
  9.9 8.5 %collective-permute-start.4 = (bf16[304,128]{1,0:T(8,128)(2,1)S(1)}, bf16[304,128]{1,0:T(8,128)(2,1)S(1)}, u32[]{:S(2)}, u32[]{:S(2)}) collective-permute-start(bf16[304,128]{1,0:T(8,128)(2,1)S(1)} %get-tuple-element.76), channel_id=1, source_target_pairs={{0,1},{1,0},{2,3},{3,2},{4,5},{5,4},{6,7},{7,6},{8,9},{9,8},{10,11... | collective-permute-start | bytes 233480 | tf_op jit(solution)/shard_map/ppermute | solution.py:243
  11.8 6.6 %collective-permute-start.5 = (bf16[304,128]{1,0:T(8,128)(2,1)S(1)}, bf16[304,128]{1,0:T(8,128)(2,1)S(1)}, u32[]{:S(2)}, u32[]{:S(2)}) collective-permute-start(bf16[304,128]{1,0:T(8,128)(2,1)S(1)} %get-tuple-element.77), channel_id=1, source_target_pairs={{1,2},{2,1},{3,4},{4,3},{5,6},{6,5},{9,10},{10,9},{11,12},{12,11},... | collective-permute-start | bytes 233480 | tf_op jit(solution)/shard_map/ppermute | solution.py:243
  15.7 2.7 %copy-start = (bf16[2048,128]{1,0:T(8,128)(2,1)S(1)}, bf16[2048,128]{1,0:T(8,128)(2,1)}, u32[]{:S(2)}) copy-start(bf16[2048,128]{1,0:T(8,128)(2,1)} %w_up_hbm.1) | copy-start | bytes 1572868
  18.5 1.5 %copy-start.3 = (bf16[3456,256]{1,0:T(8,128)(2,1)S(1)}, bf16[3456,256]{1,0:T(8,128)(2,1)}, u32[]{:S(2)}) copy-start(bf16[3456,256]{1,0:T(8,128)(2,1)} %w_in_hbm.1) | copy-start | bytes 5308420
  27.5 8.3 %collective-permute-start.6 = (bf16[8064,128]{1,0:T(8,128)(2,1)S(1)}, bf16[8064,128]{1,0:T(8,128)(2,1)S(1)}, u32[]{:S(2)}, u32[]{:S(2)}) collective-permute-start(bf16[8064,128]{1,0:T(8,128)(2,1)S(1)} %get-tuple-element.80), channel_id=1, source_target_pairs={{0,8},{8,0},{1,9},{9,1},{2,10},{10,2},{3,11},{11,3},{4,12},{12,4},... | collective-permute-start | bytes 6193160 | tf_op jit(solution)/shard_map/ppermute | solution.py:398
  36.8 37.6 %copy-start.2 = (bf16[96,192]{1,0:T(8,128)(2,1)S(1)}, bf16[96,192]{1,0:T(8,128)(2,1)}, u32[]{:S(2)}) copy-start(bf16[96,192]{1,0:T(8,128)(2,1)} %constant.26.clone.z_faces_ref) | copy-start | bytes 110596
  36.8 10.8 %collective-permute-start.8 = (bf16[992,128]{1,0:T(8,128)(2,1)S(1)}, bf16[992,128]{1,0:T(8,128)(2,1)S(1)}, u32[]{:S(2)}, u32[]{:S(2)}) collective-permute-start(bf16[992,128]{1,0:T(8,128)(2,1)S(1)} %get-tuple-element.84), channel_id=1, source_target_pairs={{0,32},{16,48},{32,0},{48,16},{1,33},{17,49},{33,1},{49,17},{2,34}... | collective-permute-start | bytes 761864 | tf_op jit(solution)/shard_map/ppermute | solution.py:393
  40.0 13.7 %collective-permute-start.7 = (bf16[1056,128]{1,0:T(8,128)(2,1)S(1)}, bf16[1056,128]{1,0:T(8,128)(2,1)S(1)}, u32[]{:S(2)}, u32[]{:S(2)}) collective-permute-start(bf16[1056,128]{1,0:T(8,128)(2,1)S(1)} %get-tuple-element.83), channel_id=1, source_target_pairs={{0,16},{16,32},{32,48},{48,0},{1,17},{17,33},{33,49},{49,1},{2,18}... | collective-permute-start | bytes 811016 | tf_op jit(solution)/shard_map/ppermute | solution.py:393
  40.6 13.1 %collective-permute-start.9 = (bf16[1056,128]{1,0:T(8,128)(2,1)S(1)}, bf16[1056,128]{1,0:T(8,128)(2,1)S(1)}, u32[]{:S(2)}, u32[]{:S(2)}) collective-permute-start(bf16[1056,128]{1,0:T(8,128)(2,1)S(1)} %get-tuple-element.85), channel_id=1, source_target_pairs={{0,48},{16,0},{32,16},{48,32},{1,49},{17,1},{33,17},{49,33},{2,50}... | collective-permute-start | bytes 811016 | tf_op jit(solution)/shard_map/ppermute | solution.py:393
  43.3 21.8 %collective-permute-start.10 = (bf16[1120,128]{1,0:T(8,128)(2,1)S(1)}, bf16[1120,128]{1,0:T(8,128)(2,1)S(1)}, u32[]{:S(2)}, u32[]{:S(2)}) collective-permute-start(bf16[1120,128]{1,0:T(8,128)(2,1)S(1)} %get-tuple-element.87), channel_id=1, source_target_pairs={{0,64},{64,128},{128,192},{192,0},{1,65},{65,129},{129,193},{193,1... | collective-permute-start | bytes 860168 | tf_op jit(solution)/shard_map/ppermute | solution.py:393
  47.6 17.5 %collective-permute-start.11 = (bf16[1120,128]{1,0:T(8,128)(2,1)S(1)}, bf16[1120,128]{1,0:T(8,128)(2,1)S(1)}, u32[]{:S(2)}, u32[]{:S(2)}) collective-permute-start(bf16[1120,128]{1,0:T(8,128)(2,1)S(1)} %get-tuple-element.88), channel_id=1, source_target_pairs={{0,192},{64,0},{128,64},{192,128},{1,193},{65,1},{129,65},{193,129... | collective-permute-start | bytes 860168 | tf_op jit(solution)/shard_map/ppermute | solution.py:393
  47.6 14.4 %collective-permute-start.12 = (bf16[992,128]{1,0:T(8,128)(2,1)S(1)}, bf16[992,128]{1,0:T(8,128)(2,1)S(1)}, u32[]{:S(2)}, u32[]{:S(2)}) collective-permute-start(bf16[992,128]{1,0:T(8,128)(2,1)S(1)} %get-tuple-element.90), channel_id=1, source_target_pairs={{0,128},{64,192},{128,0},{192,64},{1,129},{65,193},{129,1},{193,65... | collective-permute-start | bytes 761864 | tf_op jit(solution)/shard_map/ppermute | solution.py:393
  54.6 29.1 %copy-start.1 = (bf16[288,288]{1,0:T(8,128)(2,1)S(1)}, bf16[288,288]{1,0:T(8,128)(2,1)}, u32[]{:S(2)}) copy-start(bf16[288,288]{1,0:T(8,128)(2,1)} %constant.27.clone.padded_ref) | copy-start | bytes 497668
  54.6 13.5 %collective-permute-start.17 = (f32[248,128]{1,0:T(8,128)S(1)}, f32[248,128]{1,0:T(8,128)S(1)}, u32[]{:S(2)}, u32[]{:S(2)}) collective-permute-start(f32[248,128]{1,0:T(8,128)S(1)} %get-tuple-element.97), channel_id=1, source_target_pairs={{0,128},{64,192},{128,0},{192,64},{1,129},{65,193},{129,1},{193,65... | collective-permute-start | bytes 380936 | tf_op jit(solution)/shard_map/ppermute | solution.py:393
  59.9 14.5 %collective-permute-start.16 = (f32[312,128]{1,0:T(8,128)S(1)}, f32[312,128]{1,0:T(8,128)S(1)}, u32[]{:S(2)}, u32[]{:S(2)}) collective-permute-start(f32[312,128]{1,0:T(8,128)S(1)} %get-tuple-element.96), channel_id=1, source_target_pairs={{0,64},{64,128},{128,192},{192,0},{1,65},{65,129},{129,193},{193,1... | collective-permute-start | bytes 479240 | tf_op jit(solution)/shard_map/ppermute | solution.py:393
  62.0 12.4 %collective-permute-start.18 = (f32[312,128]{1,0:T(8,128)S(1)}, f32[312,128]{1,0:T(8,128)S(1)}, u32[]{:S(2)}, u32[]{:S(2)}) collective-permute-start(f32[312,128]{1,0:T(8,128)S(1)} %get-tuple-element.98), channel_id=1, source_target_pairs={{0,192},{64,0},{128,64},{192,128},{1,193},{65,1},{129,65},{193,129... | collective-permute-start | bytes 479240 | tf_op jit(solution)/shard_map/ppermute | solution.py:393
  65.9 7.9 %collective-permute-start.13 = (f32[248,128]{1,0:T(8,128)S(1)}, f32[248,128]{1,0:T(8,128)S(1)}, u32[]{:S(2)}, u32[]{:S(2)}) collective-permute-start(f32[248,128]{1,0:T(8,128)S(1)} %get-tuple-element.92), channel_id=1, source_target_pairs={{0,16},{16,32},{32,48},{48,0},{1,17},{17,33},{33,49},{49,1},{2,18}... | collective-permute-start | bytes 380936 | tf_op jit(solution)/shard_map/ppermute | solution.py:393
  66.0 7.8 %collective-permute-start.14 = (f32[248,128]{1,0:T(8,128)S(1)}, f32[248,128]{1,0:T(8,128)S(1)}, u32[]{:S(2)}, u32[]{:S(2)}) collective-permute-start(f32[248,128]{1,0:T(8,128)S(1)} %get-tuple-element.93), channel_id=1, source_target_pairs={{0,32},{16,48},{32,0},{48,16},{1,33},{17,49},{33,1},{49,17},{2,34}... | collective-permute-start | bytes 380936 | tf_op jit(solution)/shard_map/ppermute | solution.py:393
  68.1 6.3 %collective-permute-start.15 = (f32[248,128]{1,0:T(8,128)S(1)}, f32[248,128]{1,0:T(8,128)S(1)}, u32[]{:S(2)}, u32[]{:S(2)}) collective-permute-start(f32[248,128]{1,0:T(8,128)S(1)} %get-tuple-element.94), channel_id=1, source_target_pairs={{0,48},{16,0},{32,16},{48,32},{1,49},{17,1},{33,17},{49,33},{2,50}... | collective-permute-start | bytes 380936 | tf_op jit(solution)/shard_map/ppermute | solution.py:393
  75.1 6.1 %collective-permute-start.19 = (f32[448,128]{1,0:T(8,128)S(1)}, f32[448,128]{1,0:T(8,128)S(1)}, u32[]{:S(2)}, u32[]{:S(2)}) collective-permute-start(f32[448,128]{1,0:T(8,128)S(1)} %get-tuple-element.100), channel_id=1, source_target_pairs={{0,1},{1,0},{2,3},{3,2},{4,5},{5,4},{6,7},{7,6},{8,9},{9,8},{10,11... | collective-permute-start | bytes 688136 | tf_op jit(solution)/shard_map/ppermute | solution.py:398
  75.2 8.5 %collective-permute-start.21 = (bf16[192,128]{1,0:T(8,128)(2,1)S(1)}, bf16[192,128]{1,0:T(8,128)(2,1)S(1)}, u32[]{:S(2)}, u32[]{:S(2)}) collective-permute-start(bf16[192,128]{1,0:T(8,128)(2,1)S(1)} %get-tuple-element.108), channel_id=1, source_target_pairs={{1,2},{2,1},{3,4},{4,3},{5,6},{6,5},{9,10},{10,9},{11,12},{12,11},... | collective-permute-start | bytes 147464 | tf_op jit(solution)/shard_map/ppermute | solution.py:531
  84.6 5.5 %collective-permute-start.20 = (f32[128,128]{1,0:T(8,128)S(1)}, f32[128,128]{1,0:T(8,128)S(1)}, u32[]{:S(2)}, u32[]{:S(2)}) collective-permute-start(f32[128,128]{1,0:T(8,128)S(1)} %get-tuple-element.105), channel_id=1, source_target_pairs={{0,2},{1,3},{2,0},{3,1},{4,6},{5,7},{6,4},{7,5},{8,10},{9,11},{10,... | collective-permute-start | bytes 196616 | tf_op jit(solution)/shard_map/ppermute | solution.py:398
  89.0 5.8 %copy-start.5 = (bf16[6912,128]{1,0:T(8,128)(2,1)S(1)}, bf16[6912,128]{1,0:T(8,128)(2,1)}, u32[]{:S(2)}) copy-start(bf16[6912,128]{1,0:T(8,128)(2,1)} %param.10) | copy-start | bytes 5308420
  90.1 7.6 %collective-permute-start.22 = (f32[128,128]{1,0:T(8,128)S(1)}, f32[128,128]{1,0:T(8,128)S(1)}, u32[]{:S(2)}, u32[]{:S(2)}) collective-permute-start(f32[128,128]{1,0:T(8,128)S(1)} %add.30), channel_id=1, source_target_pairs={{0,7},{1,6},{2,5},{3,4},{4,3},{5,2},{6,1},{7,0},{8,15},{9,14},{10,... | collective-permute-start | bytes 196616 | tf_op jit(solution)/shard_map/ppermute | solution.py:398
  97.7 1.2 collective-permute-start.23
  98.9 3.9 %copy-start.4 = (bf16[3456,256]{1,0:T(8,128)(2,1)S(1)}, bf16[3456,256]{1,0:T(8,128)(2,1)}, u32[]{:S(2)}) copy-start(bf16[3456,256]{1,0:T(8,128)(2,1)} %w_in_hbm.1) | copy-start | bytes 5308420
  98.9 3.5 %collective-permute-start.24 = (f32[1,128]{1,0:T(1,128)S(1)}, f32[1,128]{1,0:T(1,128)S(1)}, u32[]{:S(2)}, u32[]{:S(2)}) collective-permute-start(f32[1,128]{1,0:T(1,128)S(1)} %add.32), channel_id=1, source_target_pairs={{0,64},{64,0},{128,192},{192,128},{1,65},{65,1},{129,193},{193,129... | collective-permute-start | bytes 1544 | tf_op jit(solution)/shard_map/ppermute | solution.py:398
  102.5 4.8 %collective-permute-start.25 = (f32[1,128]{1,0:T(1,128)S(1)}, f32[1,128]{1,0:T(1,128)S(1)}, u32[]{:S(2)}, u32[]{:S(2)}) collective-permute-start(f32[1,128]{1,0:T(1,128)S(1)} %add.33), channel_id=1, source_target_pairs={{0,192},{64,128},{128,64},{192,0},{1,193},{65,129},{129,65},{193,1... | collective-permute-start | bytes 1544 | tf_op jit(solution)/shard_map/ppermute | solution.py:398
  107.2 3.5 %collective-permute-start.26 = (f32[1,128]{1,0:T(1,128)S(1)}, f32[1,128]{1,0:T(1,128)S(1)}, u32[]{:S(2)}, u32[]{:S(2)}) collective-permute-start(f32[1,128]{1,0:T(1,128)S(1)} %add.34), channel_id=1, source_target_pairs={{0,16},{16,0},{32,48},{48,32},{1,17},{17,1},{33,49},{49,33},{2,18}... | collective-permute-start | bytes 1544 | tf_op jit(solution)/shard_map/ppermute | solution.py:398
  110.8 4.8 %collective-permute-start.27 = (f32[1,128]{1,0:T(1,128)S(1)}, f32[1,128]{1,0:T(1,128)S(1)}, u32[]{:S(2)}, u32[]{:S(2)}) collective-permute-start(f32[1,128]{1,0:T(1,128)S(1)} %add.36), channel_id=1, source_target_pairs={{0,48},{16,32},{32,16},{48,0},{1,49},{17,33},{33,17},{49,1},{2,50}... | collective-permute-start | bytes 1544 | tf_op jit(solution)/shard_map/ppermute | solution.py:398
  115.5 3.5 %collective-permute-start.28 = (f32[1,128]{1,0:T(1,128)S(1)}, f32[1,128]{1,0:T(1,128)S(1)}, u32[]{:S(2)}, u32[]{:S(2)}) collective-permute-start(f32[1,128]{1,0:T(1,128)S(1)} %add.37), channel_id=1, source_target_pairs={{0,1},{1,0},{2,3},{3,2},{4,5},{5,4},{6,7},{7,6},{8,9},{9,8},{10,11... | collective-permute-start | bytes 1544 | tf_op jit(solution)/shard_map/ppermute | solution.py:398
  119.1 4.4 %collective-permute-start.29 = (f32[1,128]{1,0:T(1,128)S(1)}, f32[1,128]{1,0:T(1,128)S(1)}, u32[]{:S(2)}, u32[]{:S(2)}) collective-permute-start(f32[1,128]{1,0:T(1,128)S(1)} %add.38), channel_id=1, source_target_pairs={{0,2},{1,3},{2,0},{3,1},{4,6},{5,7},{6,4},{7,5},{8,10},{9,11},{10,... | collective-permute-start | bytes 1544 | tf_op jit(solution)/shard_map/ppermute | solution.py:398

commit v4 on v3

--- a/solution.py
+++ b/solution.py
@@ -50,26 +50,9 @@
     return picks
 
 
-def _at_y(s, x, y, z):
-    line = s * 2 + x
-    return 64 + line * 4 + z if y < 0 else 80 + line * 4 + z if y > 3 else (line * 4 + y) * 4 + z
-
-
-def _at_x(s, x, y, z):
-    if 0 <= x <= 1:
-        return _at_y(s, x, y, z)
-    base = 96 if x < 0 else 144
-    return base + (s * 4 + y) * 4 + z if 0 <= y <= 3 else base + 32 + (s * 2 + int(y > 3)) * 4 + z
-
-
-def _at_z(s, x, y, z):
-    line = (s * 4 + x + 1) * 6 + y + 1
-    return 192 + line if z < 0 else 240 + line if z > 3 else _at_x(s, x, y, z)
-
-
-S2, X4, Y6, Z6 = range(2), range(-1, 3), range(-1, 5), range(-1, 5)
-Z_FACES = _picks([_at_x(s, x, y, z) for z in (0, 3) for s in S2 for x in X4 for y in Y6], 192)
-PADDED = _picks([_at_z(s, x, y, z) for s in S2 for x in X4 for y in Y6 for z in Z6], 288)
+LINES = [(s * 4 + x) * 6 + y for s in range(2) for x in range(4) for y in range(6)]
+Z_FACES = _picks([line * 4 + z for z in (0, 3) for line in LINES], 192)
+PADDED = _picks([192 + n if z < 0 else 240 + n if z > 3 else n * 4 + z for n in LINES for z in range(-1, 5)], 288)
 
 
 def _dot(a, b, contract=((1,), (0,))):
@@ -151,12 +134,50 @@
     return _fine_from_blocks(c, r)
 
 
-def _y_faces(r, c):
-    return c == (((r >> 2) & 3) * 4 + (r >> 4) * 3) * 4 + (r & 3)
-
-
-def _x_edges(r, c):
-    return c == ((r >> 2) & 1) * 16 + (((r >> 3) & 1) * 2 + (r >> 4)) * 4 + (r & 3)
+NOWHERE = 9999
+
+
+def _chip_cell(s, x, y, z):
+    return (y >> 2) * 64 + ((s * 2 + x) * 4 + (y & 3)) * 4 + z
+
+
+def _first_faces(core, last):
+    def chosen(r, c):
+        x_face = _chip_cell(r >> 5, last, (r >> 2) & 7, r & 3)
+        y_face = jnp.where(r < 16, _chip_cell((r >> 3) & 1, (r >> 2) & 1, last * 7, r & 3), NOWHERE)
+        return c == x_face * (1 - core) + y_face * core
+
+    return chosen
+
+
+def _second_faces(core, last):
+    def chosen(r, c):
+        s, x, z = r >> 4, ((r >> 2) & 3) - 1, r & 3
+        side = s * 32 + last * 28 + z
+        y_face = jnp.where(x < 0, 128 + side, jnp.where(x > 1, 192 + side, _chip_cell(s, x, last * 7, z)))
+        y_face = jnp.where(r < 32, y_face, NOWHERE)
+        s = jnp.where(r < 24, 0, 1)
+        y, z = ((r - s * 24) >> 2) + 3, r & 3
+        x_face = jnp.where(y > 7, 192 + (s * 2 + last) * 4 + z, _chip_cell(s, last, y, z))
+        return c == y_face * (1 - core) + x_face * core
+
+    return chosen
+
+
+def _grown_cells(core):
+    def chosen(r, c):
+        plane = (r * 2731) >> 16
+        y, z = (r - plane * 24) >> 2, r & 3
+        s, x = plane >> 2, (plane & 3) - 1
+        side = s * 32 + (y - 1) * 4 + z
+        low = jnp.where(x < 0, 128 + side, jnp.where(x > 1, 192 + side, _chip_cell(s, x, y - 1, z)))
+        low = jnp.where(y == 0, 256 + s * 16 + (x + 1) * 4 + z, low)
+        side = s * 24 + y * 4 + z
+        high = jnp.where(y == 5, 192 + (s * 2 + x) * 4 + z, _chip_cell(s, x, y + 3, z))
+        high = jnp.where(x < 0, 256 + side, jnp.where(x > 1, 304 + side, high))
+        return c == low * (1 - core) + high * core
+
+    return chosen
 
 
 def _pool_kernel(place_ref, both_ref, act_out, cot_out, pooled_ref, here_ref, there_ref):
@@ -344,9 +365,8 @@
     slope = (d_bottom * squash * (1.0 + before * (1.0 - squash))).astype(BF16)
     coarse = jnp.concatenate([bottom, slope], axis=1)
     coarse_ref[...] = coarse
-    faces = _dot(_table(32, 64, _y_faces), coarse)
     for lane in range(4):
-        send_ref[7936 + lane * 32 : 7968 + lane * 32, :] = faces[:, lane * 128 : (lane + 1) * 128].astype(BF16)
+        send_ref[7936 + lane * 64 : 8000 + lane * 64, :] = coarse[:, lane * 128 : (lane + 1) * 128]
 
     spaced[...] = jnp.zeros((128, 768), BF16)
     for s in range(2):
@@ -369,7 +389,7 @@
     return pl.pallas_call(
         _gradients_kernel,
         out_shape=(
-            shape((7936, 128), F32), shape((8064, 128), BF16), shape((64, 512), BF16), shape((512, 128), F32),
+            shape((7936, 128), F32), shape((8192, 128), BF16), shape((64, 512), BF16), shape((512, 128), F32),
         ),
         in_specs=[pl.BlockSpec(memory_space=pltpu.SMEM)] + [vmem] * 5 + [hbm] * 3,
         out_specs=(vmem,) * 4,
@@ -388,9 +408,12 @@
     )
 
 
-def turned(array, axis, shift):
-    count = lax.axis_size(axis)
-    return lax.ppermute(array, axis, [(i, (i + shift) % count) for i in range(count)])
+def crossed(array, shift, along_gx):
+    pairs = []
+    for gx, x, core in itertools.product(range(4), range(4), range(2)):
+        to = ((gx + shift) % 4, x) if core == along_gx else (gx, (x + shift) % 4)
+        pairs.append(((gx * 4 + x) * 2 + core, (to[0] * 4 + to[1]) * 2 + core))
+    return lax.ppermute(array, ("gx", "x", "core"), pairs)
 
 
 def paired(array, axis, bit):
@@ -398,62 +421,51 @@
     return lax.ppermute(array, axis, [(i, i ^ bit) for i in range(count)])
 
 
-def _split_kernel(place_ref, keep_ref, got_ref, coarse_ref, one_ref, two_ref, faces_ref, *sends):
-    for s in range(4):
-        rows = [pl.multiple_of(((place_ref[0] + s) % 4 * 4 + j) * 496, 16) for j in range(4)]
-        one = jnp.concatenate([keep_ref[pl.ds(r, 248), :] + got_ref[pl.ds(r, 256), :].astype(F32)[:248] for r in rows], axis=0)
-        rows = [pl.multiple_of((j * 4 + (place_ref[1] + s) % 4) * 496 + 240, 16) for j in range(4)]
-        two = jnp.concatenate([keep_ref[pl.ds(r + 8, 248), :] + got_ref[pl.ds(r, 256), :].astype(F32)[8:] for r in rows], axis=0)
-        if s == 0:
-            one_ref[...] = one
-            two_ref[...] = two
-        else:
-            sends[s - 1][0:992, :] = one.astype(BF16)
-            sends[s + 2][0:992, :] = two.astype(BF16)
-    faces = got_ref[7936:8064, :]
-    faces_ref[...] = faces
+def _put_faces(ref, start, count, faces):
     for lane in range(4):
-        sends[3][992 + lane * 16 : 1008 + lane * 16, :] = faces[lane * 32 + 16 : lane * 32 + 32]
-        sends[5][992 + lane * 16 : 1008 + lane * 16, :] = faces[lane * 32 : lane * 32 + 16]
-        for s in range(2):
-            start, channels = 992 + lane * 32 + s * 16, slice(lane * 128, (lane + 1) * 128)
-            sends[0][start : start + 16, :] = coarse_ref[s * 32 + 16 : s * 32 + 32, channels]
-            sends[2][start : start + 16, :] = coarse_ref[s * 32 : s * 32 + 16, channels]
-
-
-def _second_one_kernel(place_ref, one_ref, got_1, got_2, got_3, own, send_1, send_2, send_3, one):
-    one[...] = one_ref[...] + (got_1[0:992, :].astype(F32) + got_2[...].astype(F32) + got_3[0:992, :].astype(F32))
-    for s, out in enumerate((own, send_1, send_2, send_3)):
-        out[...] = one[pl.ds(pl.multiple_of((place_ref[1] + s) % 4 * 248, 8), 248), :]
-
-
-def _second_two_kernel(
-    place_ref, faces_ref, two_ref, got_1, got_2, got_3, sides_ref, own, send_1, send_2, send_3, two
+        rows = slice(start + lane * count, start + (lane + 1) * count)
+        ref[rows, :] = faces[:, lane * 128 : (lane + 1) * 128].astype(ref.dtype)
+
+
+def _get_faces(ref, start, count, there):
+    return _wide(ref[start : start + 4 * count, :].astype(F32) * there, count).astype(BF16)
+
+
+def _split_kernel(place_ref, keep_ref, got_ref, coarse_ref, own, send_1, send_2, send_3, chip_ref):
+    core = place_ref[2]
+    for shift, ref in enumerate((own, send_1, send_2, send_3)):
+        gx, x = (place_ref[0] + shift) % 4, (place_ref[1] + shift) % 4
+        for j in range(4):
+            block = (gx * 4 + j) * (1 - core) + (j * 4 + x) * core
+            rows = pl.ds(pl.multiple_of(block * 496, 16), 496)
+            ref[j * 496 : (j + 1) * 496, :] = (keep_ref[rows, :] + got_ref[rows, :].astype(F32)).astype(ref.dtype)
+    mine, other = coarse_ref[...].astype(F32), _wide(got_ref[7936:8192, :].astype(F32), 64)
+    zero, one = _flag(core == 0), _flag(core == 1)
+    chip = jnp.concatenate([mine * zero + other * one, mine * one + other * zero], axis=0).astype(BF16)
+    chip_ref[...] = chip
+    _put_faces(send_1, 1984, 64, _dot(_table(64, 128, _first_faces(core, 1)), chip))
+    _put_faces(send_3, 1984, 64, _dot(_table(64, 128, _first_faces(core, 0)), chip))
+
+
+def _second_kernel(place_ref, chip_ref, own_ref, got_1, got_2, got_3, known_ref, own, send_1, send_2, send_3, total):
+    gx, x, core = place_ref[0], place_ref[1], place_ref[2]
+    first, second = gx * (1 - core) + x * core, x * (1 - core) + gx * core
+    total[...] = own_ref[...] + (got_1[0:1984, :].astype(F32) + got_2[...].astype(F32) + got_3[0:1984, :].astype(F32))
+    for shift, ref in enumerate((own, send_1, send_2, send_3)):
+        ref[0:496, :] = total[pl.ds(pl.multiple_of((second + shift) % 4 * 496, 16), 496), :]
+    sides = [_get_faces(got_1, 1984, 64, _flag(first > 0)), _get_faces(got_3, 1984, 64, _flag(first < 3))]
+    known = jnp.concatenate([chip_ref[...]] + sides, axis=0)
+    known_ref[...] = known
+    _put_faces(send_1, 496, 48, _dot(_table(48, 256, _second_faces(core, 1)), known))
+    _put_faces(send_3, 496, 48, _dot(_table(48, 256, _second_faces(core, 0)), known))
+
+
+def _third_kernel(
+    place_ref, known_ref, z_faces_ref, own_ref, got_1, got_2, got_3, grown_out, keep_ref, send_ref, other_ref, rows, chunks
 ):
-    x, core = place_ref[1], place_ref[2]
-    two[...] = two_ref[...] + (got_1[0:992, :].astype(F32) + got_2[...].astype(F32) + got_3[0:992, :].astype(F32))
-    for s, out in enumerate((own, send_1, send_2, send_3)):
-        out[0:248, :] = two[pl.ds(pl.multiple_of((place_ref[0] + s) % 4 * 248, 8), 248), :]
-    near = faces_ref[...].astype(F32)
-    near_first = jnp.concatenate([near[i * 32 : i * 32 + 16] for i in range(4)], axis=0)
-    near_last = jnp.concatenate([near[i * 32 + 16 : i * 32 + 32] for i in range(4)], axis=0)
-    low = got_1[992:1056, :].astype(F32) * _flag((core == 0) & (x > 0)) + near_last * _flag(core == 1)
-    high = got_3[992:1056, :].astype(F32) * _flag((core == 1) & (x < 3)) + near_first * _flag(core == 0)
-    sides = jnp.concatenate([_wide(low, 16).astype(BF16), _wide(high, 16).astype(BF16)], axis=0)
-    sides_ref[...] = sides
-    edges = _dot(_table(32, 32, _x_edges), sides)
-    for lane in range(4):
-        send_1[248 + lane * 16 : 264 + lane * 16, :] = edges[16:32, lane * 128 : (lane + 1) * 128]
-        send_3[248 + lane * 16 : 264 + lane * 16, :] = edges[0:16, lane * 128 : (lane + 1) * 128]
-
-
-def _third_kernel(
-    place_ref, coarse_ref, sides_ref, x_low, x_high, z_faces_ref, one_ref, one_1, one_2, one_3, two_ref, two_1, two_2, two_3,
-    grown_out, keep_ref, send_ref, other_ref, rows, chunks,
-):
-    gx, gz = place_ref[0], place_ref[3]
-    rows[0:248, :] = one_ref[...] + (one_1[...] + one_2[...] + one_3[...])
-    rows[248:496, :] = two_ref[...] + (two_1[0:248, :] + two_2[...] + two_3[0:248, :])
+    gx, x, core, gz = (place_ref[i] for i in range(4))
+    second = x * (1 - core) + gx * core
+    rows[...] = own_ref[...] + (got_1[0:496, :] + got_2[...] + got_3[0:496, :])
     chunks[...] = jnp.zeros((2, 256, 128), F32)
     for r, q, p in itertools.product(range(2), repeat=3):
         chunk, place = 4 * r + 2 * q + p, ((q ^ r) * 2 + r) * 64
@@ -461,19 +473,14 @@
     half = (gz + gz // 4) % 2
     keep_ref[...] = chunks[half]
     send_ref[0:256, :] = chunks[1 - half]
-    grown = [coarse_ref[...], sides_ref[...]]
-    for cells, edges, there in ((x_low, two_1, _flag(gx > 0)), (x_high, two_3, _flag(gx < 3))):
-        grown.append(_wide(cells[992:1120, :].astype(F32) * there, 32).astype(BF16))
-        grown.append(_wide(edges[248:312, :] * there, 16).astype(BF16))
-    grown = jnp.concatenate(grown, axis=0)
+    sides = [_get_faces(got_1, 496, 48, _flag(second > 0)), _get_faces(got_3, 496, 48, _flag(second < 3))]
+    known = jnp.concatenate([known_ref[...]] + sides, axis=0)
+    grown = _dot(_table(192, 352, _grown_cells(core)), known).astype(BF16)
     grown_out[...] = grown
     faces = _dot(z_faces_ref[...], grown)
     even = _flag(gz % 2 == 0)
-    here = faces[48:96] * even + faces[0:48] * (1.0 - even)
-    there = (faces[0:48] * even + faces[48:96] * (1.0 - even)).astype(BF16)
-    for lane in range(4):
-        send_ref[256 + lane * 48 : 304 + lane * 48, :] = here[:, lane * 128 : (lane + 1) * 128]
-        other_ref[lane * 48 : (lane + 1) * 48, :] = there[:, lane * 128 : (lane + 1) * 128]
+    _put_faces(send_ref, 256, 48, faces[48:96] * even + faces[0:48] * (1.0 - even))
+    _put_faces(other_ref, 0, 48, faces[0:48] * even + faces[48:96] * (1.0 - even))
 
 
 def _fourth_kernel(place_ref, keep_ref, got_ref, keep_out, send_out, both):
@@ -510,22 +517,15 @@
         return ((n, 128), BF16)
 
     got = paired(send, "core", 1)
-    outs = (f32_rows(992), f32_rows(992), rows(128), rows(1120), rows(992), rows(1120), rows(1056), rows(992), rows(1056))
-    one, two, faces, *sends = _call(_split_kernel, outs, place, keep, got, coarse)
-    got_one = [turned(sends[s - 1], "gx", s) for s in (1, 2, 3)]
-    got_two = [turned(sends[s + 2], "x", s) for s in (1, 2, 3)]
-    one, *sends_one = _call(_second_one_kernel, (f32_rows(248),) * 4, place, one, *got_one, scratch=((992, 128),))
-    x_low, x_high = got_one[0], got_one[2]
-    got_one = [turned(sends_one[s - 1], "x", s) for s in (1, 2, 3)]
-    outs = (((32, 512), BF16), f32_rows(248), f32_rows(312), f32_rows(248), f32_rows(312))
-    sides, two, *sends_two = _call(
-        _second_two_kernel, outs, place, faces, two, *got_two, scratch=((992, 128),)
-    )
-    got_two = [turned(sends_two[s - 1], "gx", s) for s in (1, 2, 3)]
+    outs = (f32_rows(1984), rows(2240), rows(1984), rows(2240), ((128, 512), BF16))
+    own, *sends, chip = _call(_split_kernel, outs, place, keep, got, coarse)
+    gots = [crossed(sends[s - 1], s, 0) for s in (1, 2, 3)]
+    outs = (((256, 512), BF16), f32_rows(496), f32_rows(688), f32_rows(496), f32_rows(688))
+    known, own, *sends = _call(_second_kernel, outs, place, chip, own, *gots, scratch=((1984, 128),))
+    gots = [crossed(sends[s - 1], s, 1) for s in (1, 2, 3)]
     outs = (((192, 512), BF16), f32_rows(256), f32_rows(448), rows(192))
     grown, keep, send, other = _call(
-        _third_kernel, outs, place, coarse, sides, x_low, x_high, jnp.asarray(Z_FACES, BF16), one, *got_one, two, *got_two,
-        scratch=((496, 128), (2, 256, 128)),
+        _third_kernel, outs, place, known, jnp.asarray(Z_FACES, BF16), own, *gots, scratch=((496, 128), (2, 256, 128))
     )
     got = paired(send, "gz", 1)
     other = lax.ppermute(other, "gz", [(i, j) for i in range(8) for j in [((i + 1) ^ 1) - 1] if 0 <= j < 8])

time: 126 us -> 123 us (0.976)
  starting transfers between devices: 62.1 us -> 48.3 us
  waiting for transfers between devices: 28.9 us -> 40.2 us
    ppermute x12 -> x6, starting transfers between devices: 28.6 us -> 13.7 us  [crossed(): return lax.ppermute(array, ('gx', 'x', 'core'), pairs)]
    ppermute x12 -> x6, waiting for transfers between devices: 7.27 us -> 18.3 us  [crossed(): return lax.ppermute(array, ('gx', 'x', 'core'), pairs)]
    pallas_call x11 -> x10, Pallas kernels: 9.19 us -> 9.36 us  [_call(): pl.pallas_call(kernel, out_shape=tuple((jax.ShapeDtypeStruct(shape, kind)...]
  transfers between devices with their start and end apart: 30 -> 24, of which waited for: 14 -> 13; matrix products, arithmetic and copies ran while one was open for 11% -> 11% of each run, Pallas kernels for 2% -> 1%
where the time goes in v4:
time: 123 us; the launch traced here: 122 us
  starting transfers between devices  48.3 us (39%)
  waiting for transfers between devices  40.2 us (33%)
  Pallas kernels  16.9 us (14%)
  matrix products  7 us (6%)
  local copies, waits for them, and re-layouts  6.27 us (5%)
  other arithmetic  2.76 us (2%)
    ppermute x11, starting transfers between devices, paired(): return lax.ppermute(array, axis, [(i, i ^ bit) for i in range(count)])  19.7 us
    ppermute x6, waiting for transfers between devices, crossed(): return lax.ppermute(array, ('gx', 'x', 'core'), pairs)  18.3 us
    ppermute x11, waiting for transfers between devices, paired(): return lax.ppermute(array, axis, [(i, i ^ bit) for i in range(count)])  17.7 us
    ppermute x6, starting transfers between devices, crossed(): return lax.ppermute(array, ('gx', 'x', 'core'), pairs)  13.7 us
    pallas_call x10, Pallas kernels, _call(): pl.pallas_call(kernel, out_shape=tuple((jax.ShapeDtypeStruct(shape, kind)...  9.36 us
    pallas_call x1, Pallas kernels, gradients(): pl.pallas_call(_gradients_kernel, out_shape=(shape((7936, 128), F32), sha...  7.55 us
    ppermute x1, starting transfers between devices, scattered_sum(): lax.ppermute(other, 'gz', [(i, j) for i in range(8) for j in [(i + 1 ^ 1)...  6.03 us
    conv_general_dilated x2, matrix products, conv_forward(): lax.conv_general_dilated(padded, kernel, (1, 1, 1), 'VALID', dimension_nu...  5.82 us
  transfers between devices with their start and end apart: 24, of which 13 were waited for; matrix products, arithmetic and copies ran while one was open for 11% of the time, Pallas kernels for 1%

profile of v4, /device:TPU:32, one launch (start us, length us, event | category | flops | bytes accessed | tf_op | source)
XLA Modules:
  0.0 122.4 jit_solution(9414111627993356448)
XLA Ops:
  0.6 1.0 pad_maximum_fusion.1.both_ref
  1.7 0.7 shard_map.94
  2.4 1.7 %collective-permute-start = (bf16[288,128]{1,0:T(8,128)(2,1)S(1)}, bf16[288,128]{1,0:T(8,128)(2,1)S(1)}, u32[]{:S(2)}, u32[]{:S(2)}) collective-permute-start(bf16[288,128]{1,0:T(8,128)(2,1)S(1)} %get-tuple-element.59), channel_id=1, source_target_pairs={{0,64},{64,0},{128,192},{192,128},{1,65},{65,1},{129,193},{193,129... | collective-permute-start | bytes 221192 | tf_op jit(solution)/shard_map/ppermute | solution.py:264
  4.8 2.1 %collective-permute-done.got_here = bf16[288,128]{1,0:T(8,128)(2,1)S(1)} collective-permute-done((bf16[288,128]{1,0:T(8,128)(2,1)S(1)}, bf16[288,128]{1,0:T(8,128)(2,1)S(1)}, u32[]{:S(2)}, u32[]{:S(2)}) %collective-permute-start) | collective-permute-done | bytes 73760 | tf_op jit(solution)/shard_map/ppermute | solution.py:264
  6.9 0.7 shard_map.95
  7.7 0.7 collective-permute-start.3
  8.9 1.0 shard_map.96
  9.9 1.9 %collective-permute-start.4 = (bf16[304,128]{1,0:T(8,128)(2,1)S(1)}, bf16[304,128]{1,0:T(8,128)(2,1)S(1)}, u32[]{:S(2)}, u32[]{:S(2)}) collective-permute-start(bf16[304,128]{1,0:T(8,128)(2,1)S(1)} %get-tuple-element.68), channel_id=1, source_target_pairs={{0,1},{1,0},{2,3},{3,2},{4,5},{5,4},{6,7},{7,6},{8,9},{9,8},{10,11... | collective-permute-start | bytes 233480 | tf_op jit(solution)/shard_map/ppermute | solution.py:264
  11.8 3.9 %collective-permute-start.5 = (bf16[304,128]{1,0:T(8,128)(2,1)S(1)}, bf16[304,128]{1,0:T(8,128)(2,1)S(1)}, u32[]{:S(2)}, u32[]{:S(2)}) collective-permute-start(bf16[304,128]{1,0:T(8,128)(2,1)S(1)} %get-tuple-element.69), channel_id=1, source_target_pairs={{1,2},{2,1},{3,4},{4,3},{5,6},{6,5},{9,10},{10,9},{11,12},{12,11},... | collective-permute-start | bytes 233480 | tf_op jit(solution)/shard_map/ppermute | solution.py:264
  15.7 2.7 %copy.15 = bf16[27,256,128]{1,2,0:T(8,128)(2,1)S(1)} copy(bf16[27,256,128]{2,1,0:T(8,128)(2,1)} %bitcast.37) | data formatting | bytes 3538944 | tf_op jit(solution)/shard_map/reshape | solution.py:540
  18.5 1.5 %copy-done.3 = bf16[3456,256]{1,0:T(8,128)(2,1)S(1)} copy-done((bf16[3456,256]{1,0:T(8,128)(2,1)S(1)}, bf16[3456,256]{1,0:T(8,128)(2,1)}, u32[]{:S(2)}) %copy-start.3) | copy-done | bytes 1769496
  19.9 7.6 %shard_map.97 = (f32[7936,128]{1,0:T(8,128)S(1)}, bf16[8192,128]{1,0:T(8,128)(2,1)S(1)}, bf16[64,512]{1,0:T(8,128)(2,1)S(1)}, f32[512,128]{1,0:T(8,128)S(1)}) custom-call(s32[4]{0:T(128)S(1)} %pad_add_fusion.place_ref, bf16[512,128]{1,0:T(8,128)(2,1)S(1)} %get-tuple-element.56.act_ref, bf16[960,128]{1,0:T(8,128)(2,1)S(1)} %get-tuple-element.66.cot_ref, ...), custom_call_target="tpu_custom_call" | custom-call | flops 2500000000 | bytes 16000000 | tf_op jit(solution)/shard_map/pallas_call | solution.py:389
  27.5 4.6 %collective-permute-start.6 = (bf16[8192,128]{1,0:T(8,128)(2,1)S(1)}, bf16[8192,128]{1,0:T(8,128)(2,1)S(1)}, u32[]{:S(2)}, u32[]{:S(2)}) collective-permute-start(bf16[8192,128]{1,0:T(8,128)(2,1)S(1)} %get-tuple-element.71), channel_id=1, source_target_pairs={{0,8},{8,0},{1,9},{9,1},{2,10},{10,2},{3,11},{11,3},{4,12},{12,4},... | collective-permute-start | bytes 6291464 | tf_op jit(solution)/shard_map/ppermute | solution.py:421
  32.1 3.8 %collective-permute-done.6.got_ref = bf16[8192,128]{1,0:T(8,128)(2,1)S(1)} collective-permute-done((bf16[8192,128]{1,0:T(8,128)(2,1)S(1)}, bf16[8192,128]{1,0:T(8,128)(2,1)S(1)}, u32[]{:S(2)}, u32[]{:S(2)}) %collective-permute-start.6) | collective-permute-done | bytes 2097184 | tf_op jit(solution)/shard_map/ppermute | solution.py:421
  35.8 1.2 shard_map.98
  37.0 4.4 %collective-permute-start.7 = (bf16[2240,128]{1,0:T(8,128)(2,1)S(1)}, bf16[2240,128]{1,0:T(8,128)(2,1)S(1)}, u32[]{:S(2)}, u32[]{:S(2)}) collective-permute-start(bf16[2240,128]{1,0:T(8,128)(2,1)S(1)} %get-tuple-element.75), channel_id=1, source_target_pairs={{0,64},{8,24},{16,80},{24,40},{32,96},{40,56},{48,112},{56,8},{64,... | collective-permute-start | bytes 1720328 | tf_op jit(solution)/shard_map/ppermute | solution.py:416
  41.4 4.1 %collective-permute-start.8 = (bf16[1984,128]{1,0:T(8,128)(2,1)S(1)}, bf16[1984,128]{1,0:T(8,128)(2,1)S(1)}, u32[]{:S(2)}, u32[]{:S(2)}) collective-permute-start(bf16[1984,128]{1,0:T(8,128)(2,1)S(1)} %get-tuple-element.76), channel_id=1, source_target_pairs={{0,128},{8,40},{16,144},{24,56},{32,160},{40,8},{48,176},{56,24},{... | collective-permute-start | bytes 1523720 | tf_op jit(solution)/shard_map/ppermute | solution.py:416
  45.5 11.1 %collective-permute-done.8.got_2 = bf16[1984,128]{1,0:T(8,128)(2,1)S(1)} collective-permute-done((bf16[1984,128]{1,0:T(8,128)(2,1)S(1)}, bf16[1984,128]{1,0:T(8,128)(2,1)S(1)}, u32[]{:S(2)}, u32[]{:S(2)}) %collective-permute-start.8) | collective-permute-done | bytes 507936 | tf_op jit(solution)/shard_map/ppermute | solution.py:416
  56.6 1.2 %shard_map.99 = (bf16[256,512]{1,0:T(8,128)(2,1)S(1)}, f32[496,128]{1,0:T(8,128)S(1)}, f32[688,128]{1,0:T(8,128)S(1)}, f32[496,128]{1,0:T(8,128)S(1)}, f32[688,128]{1,0:T(8,128)S(1)}) custom-call(s32[4]{0:T(128)S(1)} %pad_add_fusion.place_ref, bf16[128,512]{1,0:T(8,128)(2,1)S(1)} %get-tuple-element.73.chip_ref, f32[1984,128]{1,0:T(8,128)S(1)} %get-tuple-element.74.own_ref, ...), custom_call_target="tpu_custom_call" | custom-call | flops 1000000 | bytes 4000000 | tf_op jit(solution)/shard_map/pallas_call | solution.py:72
  57.9 1.7 %collective-permute-start.10 = (f32[688,128]{1,0:T(8,128)S(1)}, f32[688,128]{1,0:T(8,128)S(1)}, u32[]{:S(2)}, u32[]{:S(2)}) collective-permute-start(f32[688,128]{1,0:T(8,128)S(1)} %get-tuple-element.80), channel_id=1, source_target_pairs={{0,16},{8,72},{16,32},{24,88},{32,48},{40,104},{48,0},{56,120},{64... | collective-permute-start | bytes 1056776 | tf_op jit(solution)/shard_map/ppermute | solution.py:416
  59.6 1.6 %collective-permute-start.12 = (f32[688,128]{1,0:T(8,128)S(1)}, f32[688,128]{1,0:T(8,128)S(1)}, u32[]{:S(2)}, u32[]{:S(2)}) collective-permute-start(f32[688,128]{1,0:T(8,128)S(1)} %get-tuple-element.82), channel_id=1, source_target_pairs={{0,48},{8,200},{16,0},{24,216},{32,16},{40,232},{48,32},{56,248},{... | collective-permute-start | bytes 1056776 | tf_op jit(solution)/shard_map/ppermute | solution.py:416
  61.2 2.0 %collective-permute-start.11 = (f32[496,128]{1,0:T(8,128)S(1)}, f32[496,128]{1,0:T(8,128)S(1)}, u32[]{:S(2)}, u32[]{:S(2)}) collective-permute-start(f32[496,128]{1,0:T(8,128)S(1)} %get-tuple-element.81), channel_id=1, source_target_pairs={{0,32},{8,136},{16,48},{24,152},{32,0},{40,168},{48,16},{56,184},{... | collective-permute-start | bytes 761864 | tf_op jit(solution)/shard_map/ppermute | solution.py:416
  63.1 7.2 %collective-permute-done.11.got_2 = f32[496,128]{1,0:T(8,128)S(1)} collective-permute-done((f32[496,128]{1,0:T(8,128)S(1)}, f32[496,128]{1,0:T(8,128)S(1)}, u32[]{:S(2)}, u32[]{:S(2)}) %collective-permute-start.11) | collective-permute-done | bytes 253984 | tf_op jit(solution)/shard_map/ppermute | solution.py:416
  70.4 1.1 shard_map.100
  71.6 6.0 %collective-permute-start.15 = (bf16[192,128]{1,0:T(8,128)(2,1)S(1)}, bf16[192,128]{1,0:T(8,128)(2,1)S(1)}, u32[]{:S(2)}, u32[]{:S(2)}) collective-permute-start(bf16[192,128]{1,0:T(8,128)(2,1)S(1)} %get-tuple-element.92), channel_id=1, source_target_pairs={{1,2},{2,1},{3,4},{4,3},{5,6},{6,5},{9,10},{10,9},{11,12},{12,11},... | collective-permute-start | bytes 147464 | tf_op jit(solution)/shard_map/ppermute | solution.py:531
  78.2 1.5 %collective-permute-done.15.other_ref = bf16[192,128]{1,0:T(8,128)(2,1)S(1)} collective-permute-done((bf16[192,128]{1,0:T(8,128)(2,1)S(1)}, bf16[192,128]{1,0:T(8,128)(2,1)S(1)}, u32[]{:S(2)}, u32[]{:S(2)}) %collective-permute-start.15) | collective-permute-done | bytes 49184 | tf_op jit(solution)/shard_map/ppermute | solution.py:531
  79.7 0.9 shard_map.103
  80.6 2.8 %collective-permute-start.14 = (f32[128,128]{1,0:T(8,128)S(1)}, f32[128,128]{1,0:T(8,128)S(1)}, u32[]{:S(2)}, u32[]{:S(2)}) collective-permute-start(f32[128,128]{1,0:T(8,128)S(1)} %get-tuple-element.89), channel_id=1, source_target_pairs={{0,2},{1,3},{2,0},{3,1},{4,6},{5,7},{6,4},{7,5},{8,10},{9,11},{10,... | collective-permute-start | bytes 196616 | tf_op jit(solution)/shard_map/ppermute | solution.py:421
  83.4 0.7 shard_map.102
  86.5 3.8 %collective-permute-start.16 = (f32[128,128]{1,0:T(8,128)S(1)}, f32[128,128]{1,0:T(8,128)S(1)}, u32[]{:S(2)}, u32[]{:S(2)}) collective-permute-start(f32[128,128]{1,0:T(8,128)S(1)} %add.30), channel_id=1, source_target_pairs={{0,7},{1,6},{2,5},{3,4},{4,3},{5,2},{6,1},{7,0},{8,15},{9,14},{10,... | collective-permute-start | bytes 196616 | tf_op jit(solution)/shard_map/ppermute | solution.py:421
  90.3 2.8 %convolution_convert_fusion.2 = bf16[1,4,8,8,128]{4,0,3,2,1:T(2,128)(2,1)S(1)} fusion(bf16[3,3,3,256,128]{4,3,2,1,0:T(8,128)(2,1)S(1)} %bitcast.38, bf16[2,6,10,10,256]{4,0,3,2,1:T(2,128)(2,1)S(1)} %pad_maximum_fusion), kind=kOutput, calls=%fused_computation.3 | convolution fusion | flops 453017600 | bytes 2449408 | tf_op jit(solution)/shard_map/conv_general_dilated | solution.py:18
  93.1 0.7 collective-permute-done.16
  94.0 1.1 collective-permute-done.17
  95.1 2.0 %collective-permute-start.18 = (f32[1,128]{1,0:T(1,128)S(1)}, f32[1,128]{1,0:T(1,128)S(1)}, u32[]{:S(2)}, u32[]{:S(2)}) collective-permute-start(f32[1,128]{1,0:T(1,128)S(1)} %add.32), channel_id=1, source_target_pairs={{0,64},{64,0},{128,192},{192,128},{1,65},{65,1},{129,193},{193,129... | collective-permute-start | bytes 1544 | tf_op jit(solution)/shard_map/ppermute | solution.py:421
  97.0 3.0 %convolution_convert_fusion.1 = bf16[1,4,8,8,128]{4,0,3,2,1:T(2,128)(2,1)S(1)} fusion(bf16[3,3,3,256,128]{4,3,2,1,0:T(8,128)(2,1)S(1)} %bitcast.39, bf16[2,6,10,10,256]{4,0,3,2,1:T(2,128)(2,1)S(1)} %pad_maximum_fusion), kind=kOutput, calls=%fused_computation.2 | convolution fusion | flops 453017600 | bytes 2449408 | tf_op jit(solution)/shard_map/conv_general_dilated | solution.py:18
  100.1 1.2 collective-permute-start.19
  101.2 0.8 convolution_multiply_fusion
  102.2 0.7 add_convert_fusion
  102.9 2.0 %collective-permute-done.19 = f32[1,128]{1,0:T(1,128)S(1)} collective-permute-done((f32[1,128]{1,0:T(1,128)S(1)}, f32[1,128]{1,0:T(1,128)S(1)}, u32[]{:S(2)}, u32[]{:S(2)}) %collective-permute-start.19) | collective-permute-done | bytes 544 | tf_op jit(solution)/shard_map/ppermute | solution.py:421
  104.9 1.4 %collective-permute-start.20 = (f32[1,128]{1,0:T(1,128)S(1)}, f32[1,128]{1,0:T(1,128)S(1)}, u32[]{:S(2)}, u32[]{:S(2)}) collective-permute-start(f32[1,128]{1,0:T(1,128)S(1)} %add.34), channel_id=1, source_target_pairs={{0,16},{16,0},{32,48},{48,32},{1,17},{17,1},{33,49},{49,33},{2,18}... | collective-permute-start | bytes 1544 | tf_op jit(solution)/shard_map/ppermute | solution.py:421
  106.3 2.1 %collective-permute-done.20 = f32[1,128]{1,0:T(1,128)S(1)} collective-permute-done((f32[1,128]{1,0:T(1,128)S(1)}, f32[1,128]{1,0:T(1,128)S(1)}, u32[]{:S(2)}, u32[]{:S(2)}) %collective-permute-start.20) | collective-permute-done | bytes 544 | tf_op jit(solution)/shard_map/ppermute | solution.py:421
  108.5 2.1 %collective-permute-start.21 = (f32[1,128]{1,0:T(1,128)S(1)}, f32[1,128]{1,0:T(1,128)S(1)}, u32[]{:S(2)}, u32[]{:S(2)}) collective-permute-start(f32[1,128]{1,0:T(1,128)S(1)} %add.36), channel_id=1, source_target_pairs={{0,48},{16,32},{32,16},{48,0},{1,49},{17,33},{33,17},{49,1},{2,50}... | collective-permute-start | bytes 1544 | tf_op jit(solution)/shard_map/ppermute | solution.py:421
  110.5 2.7 %collective-permute-done.21 = f32[1,128]{1,0:T(1,128)S(1)} collective-permute-done((f32[1,128]{1,0:T(1,128)S(1)}, f32[1,128]{1,0:T(1,128)S(1)}, u32[]{:S(2)}, u32[]{:S(2)}) %collective-permute-start.21) | collective-permute-done | bytes 544 | tf_op jit(solution)/shard_map/ppermute | solution.py:421
  113.2 3.5 %collective-permute-done.22 = f32[1,128]{1,0:T(1,128)S(1)} collective-permute-done((f32[1,128]{1,0:T(1,128)S(1)}, f32[1,128]{1,0:T(1,128)S(1)}, u32[]{:S(2)}, u32[]{:S(2)}) %collective-permute-start.22) | collective-permute-done | bytes 544 | tf_op jit(solution)/shard_map/ppermute | solution.py:421
  116.8 1.7 %collective-permute-start.23 = (f32[1,128]{1,0:T(1,128)S(1)}, f32[1,128]{1,0:T(1,128)S(1)}, u32[]{:S(2)}, u32[]{:S(2)}) collective-permute-start(f32[1,128]{1,0:T(1,128)S(1)} %add.38), channel_id=1, source_target_pairs={{0,2},{1,3},{2,0},{3,1},{4,6},{5,7},{6,4},{7,5},{8,10},{9,11},{10,... | collective-permute-start | bytes 1544 | tf_op jit(solution)/shard_map/ppermute | solution.py:421
  118.7 0.7 copy.21
  119.4 1.8 %collective-permute-done.23 = f32[1,128]{1,0:T(1,128)S(1)} collective-permute-done((f32[1,128]{1,0:T(1,128)S(1)}, f32[1,128]{1,0:T(1,128)S(1)}, u32[]{:S(2)}, u32[]{:S(2)}) %collective-permute-start.23) | collective-permute-done | bytes 544 | tf_op jit(solution)/shard_map/ppermute | solution.py:421
  121.2 1.3 %shard_map.104 = f32[62,128]{1,0:T(8,128)} custom-call(s32[4]{0:T(128)S(1)} %pad_add_fusion.place_ref, f32[1,128]{1,0:T(1,128)S(1)} %add.39.total_ref, f32[128,128]{1,0:T(8,128)S(1)} %get-tuple-element.116.both_ref), custom_call_target="tpu_custom_call" | custom-call | flops 1000000 | bytes 4000000 | tf_op jit(solution)/shard_map/pallas_call | solution.py:72
  (51 shorter events, 4.9 us)
Async XLA Ops:
  2.4 4.4 %collective-permute-start = (bf16[288,128]{1,0:T(8,128)(2,1)S(1)}, bf16[288,128]{1,0:T(8,128)(2,1)S(1)}, u32[]{:S(2)}, u32[]{:S(2)}) collective-permute-start(bf16[288,128]{1,0:T(8,128)(2,1)S(1)} %get-tuple-element.59), channel_id=1, source_target_pairs={{0,64},{64,0},{128,192},{192,128},{1,65},{65,1},{129,193},{193,129... | collective-permute-start | bytes 221192 | tf_op jit(solution)/shard_map/ppermute | solution.py:264
  4.1 2.8 %collective-permute-start.1 = (bf16[288,128]{1,0:T(8,128)(2,1)S(1)}, bf16[288,128]{1,0:T(8,128)(2,1)S(1)}, u32[]{:S(2)}, u32[]{:S(2)}) collective-permute-start(bf16[288,128]{1,0:T(8,128)(2,1)S(1)} %get-tuple-element.60), channel_id=1, source_target_pairs={{64,128},{128,64},{65,129},{129,65},{66,130},{130,66},{67,131},{13... | collective-permute-start | bytes 221192 | tf_op jit(solution)/shard_map/ppermute | solution.py:264
  7.6 1.3 %collective-permute-start.2 = (bf16[224,128]{1,0:T(8,128)(2,1)S(1)}, bf16[224,128]{1,0:T(8,128)(2,1)S(1)}, u32[]{:S(2)}, u32[]{:S(2)}) collective-permute-start(bf16[224,128]{1,0:T(8,128)(2,1)S(1)} %get-tuple-element.64), channel_id=1, source_target_pairs={{0,8},{8,0},{16,24},{24,16},{32,40},{40,32},{48,56},{56,48},{1,9},... | collective-permute-start | bytes 172040 | tf_op jit(solution)/shard_map/ppermute | solution.py:264
  7.7 1.2 %collective-permute-start.3 = (bf16[224,128]{1,0:T(8,128)(2,1)S(1)}, bf16[224,128]{1,0:T(8,128)(2,1)S(1)}, u32[]{:S(2)}, u32[]{:S(2)}) collective-permute-start(bf16[224,128]{1,0:T(8,128)(2,1)S(1)} %get-tuple-element.65), channel_id=1, source_target_pairs={{8,16},{16,8},{24,32},{32,24},{40,48},{48,40},{9,17},{17,9},{25,33... | collective-permute-start | bytes 172040 | tf_op jit(solution)/shard_map/ppermute | solution.py:264
  9.9 8.5 %collective-permute-start.4 = (bf16[304,128]{1,0:T(8,128)(2,1)S(1)}, bf16[304,128]{1,0:T(8,128)(2,1)S(1)}, u32[]{:S(2)}, u32[]{:S(2)}) collective-permute-start(bf16[304,128]{1,0:T(8,128)(2,1)S(1)} %get-tuple-element.68), channel_id=1, source_target_pairs={{0,1},{1,0},{2,3},{3,2},{4,5},{5,4},{6,7},{7,6},{8,9},{9,8},{10,11... | collective-permute-start | bytes 233480 | tf_op jit(solution)/shard_map/ppermute | solution.py:264
  11.8 6.6 %collective-permute-start.5 = (bf16[304,128]{1,0:T(8,128)(2,1)S(1)}, bf16[304,128]{1,0:T(8,128)(2,1)S(1)}, u32[]{:S(2)}, u32[]{:S(2)}) collective-permute-start(bf16[304,128]{1,0:T(8,128)(2,1)S(1)} %get-tuple-element.69), channel_id=1, source_target_pairs={{1,2},{2,1},{3,4},{4,3},{5,6},{6,5},{9,10},{10,9},{11,12},{12,11},... | collective-permute-start | bytes 233480 | tf_op jit(solution)/shard_map/ppermute | solution.py:264
  15.7 2.7 %copy-start = (bf16[2048,128]{1,0:T(8,128)(2,1)S(1)}, bf16[2048,128]{1,0:T(8,128)(2,1)}, u32[]{:S(2)}) copy-start(bf16[2048,128]{1,0:T(8,128)(2,1)} %w_up_hbm.1) | copy-start | bytes 1572868
  18.5 1.5 %copy-start.3 = (bf16[3456,256]{1,0:T(8,128)(2,1)S(1)}, bf16[3456,256]{1,0:T(8,128)(2,1)}, u32[]{:S(2)}) copy-start(bf16[3456,256]{1,0:T(8,128)(2,1)} %w_in_hbm.1) | copy-start | bytes 5308420
  27.5 8.4 %collective-permute-start.6 = (bf16[8192,128]{1,0:T(8,128)(2,1)S(1)}, bf16[8192,128]{1,0:T(8,128)(2,1)S(1)}, u32[]{:S(2)}, u32[]{:S(2)}) collective-permute-start(bf16[8192,128]{1,0:T(8,128)(2,1)S(1)} %get-tuple-element.71), channel_id=1, source_target_pairs={{0,8},{8,0},{1,9},{9,1},{2,10},{10,2},{3,11},{11,3},{4,12},{12,4},... | collective-permute-start | bytes 6291464 | tf_op jit(solution)/shard_map/ppermute | solution.py:421
  37.0 33.3 %copy-start.2 = (bf16[96,192]{1,0:T(8,128)(2,1)S(1)}, bf16[96,192]{1,0:T(8,128)(2,1)}, u32[]{:S(2)}) copy-start(bf16[96,192]{1,0:T(8,128)(2,1)} %constant.26.clone.z_faces_ref) | copy-start | bytes 110596
  37.0 19.6 %collective-permute-start.7 = (bf16[2240,128]{1,0:T(8,128)(2,1)S(1)}, bf16[2240,128]{1,0:T(8,128)(2,1)S(1)}, u32[]{:S(2)}, u32[]{:S(2)}) collective-permute-start(bf16[2240,128]{1,0:T(8,128)(2,1)S(1)} %get-tuple-element.75), channel_id=1, source_target_pairs={{0,64},{8,24},{16,80},{24,40},{32,96},{40,56},{48,112},{56,8},{64,... | collective-permute-start | bytes 1720328 | tf_op jit(solution)/shard_map/ppermute | solution.py:416
  41.4 15.2 %collective-permute-start.9 = (bf16[2240,128]{1,0:T(8,128)(2,1)S(1)}, bf16[2240,128]{1,0:T(8,128)(2,1)S(1)}, u32[]{:S(2)}, u32[]{:S(2)}) collective-permute-start(bf16[2240,128]{1,0:T(8,128)(2,1)S(1)} %get-tuple-element.77), channel_id=1, source_target_pairs={{0,192},{8,56},{16,208},{24,8},{32,224},{40,24},{48,240},{56,40},{... | collective-permute-start | bytes 1720328 | tf_op jit(solution)/shard_map/ppermute | solution.py:416
  41.4 15.2 %collective-permute-start.8 = (bf16[1984,128]{1,0:T(8,128)(2,1)S(1)}, bf16[1984,128]{1,0:T(8,128)(2,1)S(1)}, u32[]{:S(2)}, u32[]{:S(2)}) collective-permute-start(bf16[1984,128]{1,0:T(8,128)(2,1)S(1)} %get-tuple-element.76), channel_id=1, source_target_pairs={{0,128},{8,40},{16,144},{24,56},{32,160},{40,8},{48,176},{56,24},{... | collective-permute-start | bytes 1523720 | tf_op jit(solution)/shard_map/ppermute | solution.py:416
  56.6 23.1 %copy-start.1 = (bf16[288,288]{1,0:T(8,128)(2,1)S(1)}, bf16[288,288]{1,0:T(8,128)(2,1)}, u32[]{:S(2)}) copy-start(bf16[288,288]{1,0:T(8,128)(2,1)} %constant.27.clone.padded_ref) | copy-start | bytes 497668
  57.9 12.5 %collective-permute-start.10 = (f32[688,128]{1,0:T(8,128)S(1)}, f32[688,128]{1,0:T(8,128)S(1)}, u32[]{:S(2)}, u32[]{:S(2)}) collective-permute-start(f32[688,128]{1,0:T(8,128)S(1)} %get-tuple-element.80), channel_id=1, source_target_pairs={{0,16},{8,72},{16,32},{24,88},{32,48},{40,104},{48,0},{56,120},{64... | collective-permute-start | bytes 1056776 | tf_op jit(solution)/shard_map/ppermute | solution.py:416
  59.6 10.8 %collective-permute-start.12 = (f32[688,128]{1,0:T(8,128)S(1)}, f32[688,128]{1,0:T(8,128)S(1)}, u32[]{:S(2)}, u32[]{:S(2)}) collective-permute-start(f32[688,128]{1,0:T(8,128)S(1)} %get-tuple-element.82), channel_id=1, source_target_pairs={{0,48},{8,200},{16,0},{24,216},{32,16},{40,232},{48,32},{56,248},{... | collective-permute-start | bytes 1056776 | tf_op jit(solution)/shard_map/ppermute | solution.py:416
  61.2 9.2 %collective-permute-start.11 = (f32[496,128]{1,0:T(8,128)S(1)}, f32[496,128]{1,0:T(8,128)S(1)}, u32[]{:S(2)}, u32[]{:S(2)}) collective-permute-start(f32[496,128]{1,0:T(8,128)S(1)} %get-tuple-element.81), channel_id=1, source_target_pairs={{0,32},{8,136},{16,48},{24,152},{32,0},{40,168},{48,16},{56,184},{... | collective-permute-start | bytes 761864 | tf_op jit(solution)/shard_map/ppermute | solution.py:416
  71.5 6.1 %collective-permute-start.13 = (f32[448,128]{1,0:T(8,128)S(1)}, f32[448,128]{1,0:T(8,128)S(1)}, u32[]{:S(2)}, u32[]{:S(2)}) collective-permute-start(f32[448,128]{1,0:T(8,128)S(1)} %get-tuple-element.84), channel_id=1, source_target_pairs={{0,1},{1,0},{2,3},{3,2},{4,5},{5,4},{6,7},{7,6},{8,9},{9,8},{10,11... | collective-permute-start | bytes 688136 | tf_op jit(solution)/shard_map/ppermute | solution.py:421
  71.6 8.1 %collective-permute-start.15 = (bf16[192,128]{1,0:T(8,128)(2,1)S(1)}, bf16[192,128]{1,0:T(8,128)(2,1)S(1)}, u32[]{:S(2)}, u32[]{:S(2)}) collective-permute-start(bf16[192,128]{1,0:T(8,128)(2,1)S(1)} %get-tuple-element.92), channel_id=1, source_target_pairs={{1,2},{2,1},{3,4},{4,3},{5,6},{6,5},{9,10},{10,9},{11,12},{12,11},... | collective-permute-start | bytes 147464 | tf_op jit(solution)/shard_map/ppermute | solution.py:531
  80.6 5.8 %collective-permute-start.14 = (f32[128,128]{1,0:T(8,128)S(1)}, f32[128,128]{1,0:T(8,128)S(1)}, u32[]{:S(2)}, u32[]{:S(2)}) collective-permute-start(f32[128,128]{1,0:T(8,128)S(1)} %get-tuple-element.89), channel_id=1, source_target_pairs={{0,2},{1,3},{2,0},{3,1},{4,6},{5,7},{6,4},{7,5},{8,10},{9,11},{10,... | collective-permute-start | bytes 196616 | tf_op jit(solution)/shard_map/ppermute | solution.py:421
  85.4 4.9 %copy-start.5 = (bf16[6912,128]{1,0:T(8,128)(2,1)S(1)}, bf16[6912,128]{1,0:T(8,128)(2,1)}, u32[]{:S(2)}) copy-start(bf16[6912,128]{1,0:T(8,128)(2,1)} %param.10) | copy-start | bytes 5308420
  86.5 7.4 %collective-permute-start.16 = (f32[128,128]{1,0:T(8,128)S(1)}, f32[128,128]{1,0:T(8,128)S(1)}, u32[]{:S(2)}, u32[]{:S(2)}) collective-permute-start(f32[128,128]{1,0:T(8,128)S(1)} %add.30), channel_id=1, source_target_pairs={{0,7},{1,6},{2,5},{3,4},{4,3},{5,2},{6,1},{7,0},{8,15},{9,14},{10,... | collective-permute-start | bytes 196616 | tf_op jit(solution)/shard_map/ppermute | solution.py:421
  93.9 1.2 collective-permute-start.17
  95.1 6.2 %copy-start.4 = (bf16[3456,256]{1,0:T(8,128)(2,1)S(1)}, bf16[3456,256]{1,0:T(8,128)(2,1)}, u32[]{:S(2)}) copy-start(bf16[3456,256]{1,0:T(8,128)(2,1)} %w_in_hbm.1) | copy-start | bytes 5308420
  95.1 5.0 %collective-permute-start.18 = (f32[1,128]{1,0:T(1,128)S(1)}, f32[1,128]{1,0:T(1,128)S(1)}, u32[]{:S(2)}, u32[]{:S(2)}) collective-permute-start(f32[1,128]{1,0:T(1,128)S(1)} %add.32), channel_id=1, source_target_pairs={{0,64},{64,0},{128,192},{192,128},{1,65},{65,1},{129,193},{193,129... | collective-permute-start | bytes 1544 | tf_op jit(solution)/shard_map/ppermute | solution.py:421
  100.1 4.8 %collective-permute-start.19 = (f32[1,128]{1,0:T(1,128)S(1)}, f32[1,128]{1,0:T(1,128)S(1)}, u32[]{:S(2)}, u32[]{:S(2)}) collective-permute-start(f32[1,128]{1,0:T(1,128)S(1)} %add.33), channel_id=1, source_target_pairs={{0,192},{64,128},{128,64},{192,0},{1,193},{65,129},{129,65},{193,1... | collective-permute-start | bytes 1544 | tf_op jit(solution)/shard_map/ppermute | solution.py:421
  104.9 3.5 %collective-permute-start.20 = (f32[1,128]{1,0:T(1,128)S(1)}, f32[1,128]{1,0:T(1,128)S(1)}, u32[]{:S(2)}, u32[]{:S(2)}) collective-permute-start(f32[1,128]{1,0:T(1,128)S(1)} %add.34), channel_id=1, source_target_pairs={{0,16},{16,0},{32,48},{48,32},{1,17},{17,1},{33,49},{49,33},{2,18}... | collective-permute-start | bytes 1544 | tf_op jit(solution)/shard_map/ppermute | solution.py:421
  108.5 4.8 %collective-permute-start.21 = (f32[1,128]{1,0:T(1,128)S(1)}, f32[1,128]{1,0:T(1,128)S(1)}, u32[]{:S(2)}, u32[]{:S(2)}) collective-permute-start(f32[1,128]{1,0:T(1,128)S(1)} %add.36), channel_id=1, source_target_pairs={{0,48},{16,32},{32,16},{48,0},{1,49},{17,33},{33,17},{49,1},{2,50}... | collective-permute-start | bytes 1544 | tf_op jit(solution)/shard_map/ppermute | solution.py:421
  113.2 3.5 %collective-permute-start.22 = (f32[1,128]{1,0:T(1,128)S(1)}, f32[1,128]{1,0:T(1,128)S(1)}, u32[]{:S(2)}, u32[]{:S(2)}) collective-permute-start(f32[1,128]{1,0:T(1,128)S(1)} %add.37), channel_id=1, source_target_pairs={{0,1},{1,0},{2,3},{3,2},{4,5},{5,4},{6,7},{7,6},{8,9},{9,8},{10,11... | collective-permute-start | bytes 1544 | tf_op jit(solution)/shard_map/ppermute | solution.py:421
  116.8 4.4 %collective-permute-start.23 = (f32[1,128]{1,0:T(1,128)S(1)}, f32[1,128]{1,0:T(1,128)S(1)}, u32[]{:S(2)}, u32[]{:S(2)}) collective-permute-start(f32[1,128]{1,0:T(1,128)S(1)} %add.38), channel_id=1, source_target_pairs={{0,2},{1,3},{2,0},{3,1},{4,6},{5,7},{6,4},{7,5},{8,10},{9,11},{10,... | collective-permute-start | bytes 1544 | tf_op jit(solution)/shard_map/ppermute | solution.py:421

commit v5 on v4

--- a/solution.py
+++ b/solution.py
@@ -279,8 +279,8 @@
 def _gradients_kernel(
     place_ref, act_ref, cot_ref, pool_ref, got_here, got_there,
     w_in_hbm, w_back_hbm, w_up_hbm,
-    keep_ref, send_ref, coarse_ref, d_act_ref,
-    w_in, w_back, w_up, lines, shifted, pooled, spaced, sums, sem_in, sem_out,
+    sums_ref, send_ref, coarse_ref, d_act_ref,
+    w_in, w_back, w_up, lines, shifted, pooled, spaced, sem_in,
 ):
     loads = [
         pltpu.make_async_copy(source, target, sem_in.at[i])
@@ -299,14 +299,11 @@
             here = min(count - done, -((first - 496 * (block + 1)) // stride))
             start = block // 2 * 496 + first % 496
             where = pl.ds(start, here) if stride == 1 else pl.ds(start, here, stride)
-            sums[side[block % 2], where, :] = value[done : done + here]
+            sums_ref[side[block % 2], where, :] = value[done : done + here]
             done += here
 
-    def ship(index, first, last):
-        copy = pltpu.make_async_copy(sums.at[0, pl.ds(first, last - first)], keep_ref.at[pl.ds(first, last - first)], sem_out.at[index])
-        copy.start()
-        send_ref[first:last, :] = sums[1, first:last, :].astype(BF16)
-        return copy
+    def ship(first, last):
+        send_ref[first:last, :] = sums_ref[1, first:last, :].astype(BF16)
 
     low, high = _sides(place_ref[3], got_here, got_there)
     lines[:, 8:16, :] = cot_ref[...].astype(F32).reshape(120, 8, 128)
@@ -350,7 +347,7 @@
         grad = _dot(joined_t, shifted[:, dx : dx + 4].reshape(512, 1152))
         for u in range(9):
             put(8960 + (18 - 9 * dx + u) * 256, grad[:, u * 128 : (u + 1) * 128])
-    copies = [ship(0, 4960, 7936)]
+    ship(4960, 7936)
 
     d_upward = d_joined[:, 128:].astype(BF16)
     perm = _table(128, 128, _blocks_from_fine)
@@ -378,9 +375,7 @@
         for dx in range(3):
             for h in range(2):
                 put((9 * dx + u) * 256 + h, grad[:, dx * 256 + h * 128 : dx * 256 + (h + 1) * 128], 2)
-    copies.append(ship(1, 0, 4960))
-    for copy in copies:
-        copy.wait()
+    ship(0, 4960)
 
 
 def gradients(place, act, cot, pool, got_here, got_there, w_in, w_back, w_up):
@@ -389,7 +384,7 @@
     return pl.pallas_call(
         _gradients_kernel,
         out_shape=(
-            shape((7936, 128), F32), shape((8192, 128), BF16), shape((64, 512), BF16), shape((512, 128), F32),
+            shape((2, 7936, 128), F32), shape((8192, 128), BF16), shape((64, 512), BF16), shape((512, 128), F32),
         ),
         in_specs=[pl.BlockSpec(memory_space=pltpu.SMEM)] + [vmem] * 5 + [hbm] * 3,
         out_specs=(vmem,) * 4,
@@ -397,10 +392,9 @@
             pltpu.VMEM((3456, 256), BF16), pltpu.VMEM((3456, 256), BF16), pltpu.VMEM((2048, 128), BF16),
             pltpu.VMEM((120, 24, 128), F32), pltpu.VMEM((2, 6, 64, 1152), BF16),
             pltpu.VMEM((2, 4, 16, 1152), BF16), pltpu.VMEM((128, 768), BF16),
-            pltpu.VMEM((2, 7936, 128), F32),
-            pltpu.SemaphoreType.DMA((3,)), pltpu.SemaphoreType.DMA((2,)),
+            pltpu.SemaphoreType.DMA((3,)),
         ],
-        compiler_params=pltpu.CompilerParams(vmem_limit_bytes=26 * 1024 * 1024),
+        compiler_params=pltpu.CompilerParams(vmem_limit_bytes=24 * 1024 * 1024),
         cost_estimate=pl.CostEstimate(flops=2_500_000_000, bytes_accessed=16_000_000, transcendentals=16384),
     )(
         place, act, cot, pool, got_here, got_there,
@@ -438,7 +432,7 @@
         for j in range(4):
             block = (gx * 4 + j) * (1 - core) + (j * 4 + x) * core
             rows = pl.ds(pl.multiple_of(block * 496, 16), 496)
-            ref[j * 496 : (j + 1) * 496, :] = (keep_ref[rows, :] + got_ref[rows, :].astype(F32)).astype(ref.dtype)
+            ref[j * 496 : (j + 1) * 496, :] = (keep_ref[0, rows, :] + got_ref[rows, :].astype(F32)).astype(ref.dtype)
     mine, other = coarse_ref[...].astype(F32), _wide(got_ref[7936:8192, :].astype(F32), 64)
     zero, one = _flag(core == 0), _flag(core == 1)
     chip = jnp.concatenate([mine * zero + other * one, mine * one + other * zero], axis=0).astype(BF16)
@@ -447,7 +441,7 @@
     _put_faces(send_3, 1984, 64, _dot(_table(64, 128, _first_faces(core, 0)), chip))
 
 
-def _second_kernel(place_ref, chip_ref, own_ref, got_1, got_2, got_3, known_ref, own, send_1, send_2, send_3, total):
+def _second_kernel(place_ref, chip_ref, own_ref, got_2, got_1, got_3, known_ref, own, send_1, send_2, send_3, total):
     gx, x, core = place_ref[0], place_ref[1], place_ref[2]
     first, second = gx * (1 - core) + x * core, x * (1 - core) + gx * core
     total[...] = own_ref[...] + (got_1[0:1984, :].astype(F32) + got_2[...].astype(F32) + got_3[0:1984, :].astype(F32))
@@ -461,7 +455,7 @@
 
 
 def _third_kernel(
-    place_ref, known_ref, z_faces_ref, own_ref, got_1, got_2, got_3, grown_out, keep_ref, send_ref, other_ref, rows, chunks
+    place_ref, known_ref, z_faces_ref, own_ref, got_2, got_1, got_3, grown_out, keep_ref, send_ref, other_ref, rows, chunks
 ):
     gx, x, core, gz = (place_ref[i] for i in range(4))
     second = x * (1 - core) + gx * core
@@ -519,13 +513,13 @@
     got = paired(send, "core", 1)
     outs = (f32_rows(1984), rows(2240), rows(1984), rows(2240), ((128, 512), BF16))
     own, *sends, chip = _call(_split_kernel, outs, place, keep, got, coarse)
-    gots = [crossed(sends[s - 1], s, 0) for s in (1, 2, 3)]
+    got_2, got_1, got_3 = [crossed(sends[s - 1], s, 0) for s in (2, 1, 3)]
     outs = (((256, 512), BF16), f32_rows(496), f32_rows(688), f32_rows(496), f32_rows(688))
-    known, own, *sends = _call(_second_kernel, outs, place, chip, own, *gots, scratch=((1984, 128),))
-    gots = [crossed(sends[s - 1], s, 1) for s in (1, 2, 3)]
+    known, own, *sends = _call(_second_kernel, outs, place, chip, own, got_2, got_1, got_3, scratch=((1984, 128),))
+    got_2, got_1, got_3 = [crossed(sends[s - 1], s, 1) for s in (2, 1, 3)]
     outs = (((192, 512), BF16), f32_rows(256), f32_rows(448), rows(192))
     grown, keep, send, other = _call(
-        _third_kernel, outs, place, known, jnp.asarray(Z_FACES, BF16), own, *gots, scratch=((496, 128), (2, 256, 128))
+        _third_kernel, outs, place, known, jnp.asarray(Z_FACES, BF16), own, got_2, got_1, got_3, scratch=((496, 128), (2, 256, 128))
     )
     got = paired(send, "gz", 1)
     other = lax.ppermute(other, "gz", [(i, j) for i in range(8) for j in [((i + 1) ^ 1) - 1] if 0 <= j < 8])

time: 123 us -> 122 us (level)
  no operation moved by 1% of the time
where the time goes in v5:
time: 122 us
  starting transfers between devices  48.3 us (40%)
  waiting for transfers between devices  40.2 us (33%)
  Pallas kernels  16 us (13%)
  matrix products  7 us (6%)
  local copies, waits for them, and re-layouts  6.27 us (5%)
  other arithmetic  2.76 us (2%)
    ppermute x11, starting transfers between devices, paired(): return lax.ppermute(array, axis, [(i, i ^ bit) for i in range(count)])  19.7 us
    ppermute x6, waiting for transfers between devices, crossed(): return lax.ppermute(array, ('gx', 'x', 'core'), pairs)  18.3 us
    ppermute x11, waiting for transfers between devices, paired(): return lax.ppermute(array, axis, [(i, i ^ bit) for i in range(count)])  17.7 us
    ppermute x6, starting transfers between devices, crossed(): return lax.ppermute(array, ('gx', 'x', 'core'), pairs)  13.7 us
    pallas_call x10, Pallas kernels, _call(): pl.pallas_call(kernel, out_shape=tuple((jax.ShapeDtypeStruct(shape, kind)...  9.36 us
    pallas_call x1, Pallas kernels, gradients(): pl.pallas_call(_gradients_kernel, out_shape=(shape((2, 7936, 128), F32),...  6.64 us
    ppermute x1, starting transfers between devices, scattered_sum(): lax.ppermute(other, 'gz', [(i, j) for i in range(8) for j in [(i + 1 ^ 1)...  6.03 us
    conv_general_dilated x2, matrix products, conv_forward(): lax.conv_general_dilated(padded, kernel, (1, 1, 1), 'VALID', dimension_nu...  5.82 us
  transfers between devices with their start and end apart: 24, of which 13 were waited for; matrix products, arithmetic and copies ran while one was open for 11% of the time, Pallas kernels for 1%

profile of v5, /device:TPU:32, one launch (start us, length us, event | category | flops | bytes accessed | tf_op | source)
XLA Modules:
  0.0 121.5 jit_solution(2473549780685626591)
XLA Ops:
  0.6 1.0 pad_maximum_fusion.1.both_ref
  1.7 0.7 shard_map.94
  2.4 1.7 %collective-permute-start = (bf16[288,128]{1,0:T(8,128)(2,1)S(1)}, bf16[288,128]{1,0:T(8,128)(2,1)S(1)}, u32[]{:S(2)}, u32[]{:S(2)}) collective-permute-start(bf16[288,128]{1,0:T(8,128)(2,1)S(1)} %get-tuple-element.59), channel_id=1, source_target_pairs={{0,64},{64,0},{128,192},{192,128},{1,65},{65,1},{129,193},{193,129... | collective-permute-start | bytes 221192 | tf_op jit(solution)/shard_map/ppermute | solution.py:264
  4.8 2.1 %collective-permute-done.got_here = bf16[288,128]{1,0:T(8,128)(2,1)S(1)} collective-permute-done((bf16[288,128]{1,0:T(8,128)(2,1)S(1)}, bf16[288,128]{1,0:T(8,128)(2,1)S(1)}, u32[]{:S(2)}, u32[]{:S(2)}) %collective-permute-start) | collective-permute-done | bytes 73760 | tf_op jit(solution)/shard_map/ppermute | solution.py:264
  6.9 0.7 shard_map.95
  7.7 0.7 collective-permute-start.3
  8.9 1.0 shard_map.96
  9.9 1.9 %collective-permute-start.4 = (bf16[304,128]{1,0:T(8,128)(2,1)S(1)}, bf16[304,128]{1,0:T(8,128)(2,1)S(1)}, u32[]{:S(2)}, u32[]{:S(2)}) collective-permute-start(bf16[304,128]{1,0:T(8,128)(2,1)S(1)} %get-tuple-element.68), channel_id=1, source_target_pairs={{0,1},{1,0},{2,3},{3,2},{4,5},{5,4},{6,7},{7,6},{8,9},{9,8},{10,11... | collective-permute-start | bytes 233480 | tf_op jit(solution)/shard_map/ppermute | solution.py:264
  11.8 3.9 %collective-permute-start.5 = (bf16[304,128]{1,0:T(8,128)(2,1)S(1)}, bf16[304,128]{1,0:T(8,128)(2,1)S(1)}, u32[]{:S(2)}, u32[]{:S(2)}) collective-permute-start(bf16[304,128]{1,0:T(8,128)(2,1)S(1)} %get-tuple-element.69), channel_id=1, source_target_pairs={{1,2},{2,1},{3,4},{4,3},{5,6},{6,5},{9,10},{10,9},{11,12},{12,11},... | collective-permute-start | bytes 233480 | tf_op jit(solution)/shard_map/ppermute | solution.py:264
  15.7 2.7 %copy.15 = bf16[27,256,128]{1,2,0:T(8,128)(2,1)S(1)} copy(bf16[27,256,128]{2,1,0:T(8,128)(2,1)} %bitcast.37) | data formatting | bytes 3538944 | tf_op jit(solution)/shard_map/reshape | solution.py:534
  18.5 1.5 %copy-done.3 = bf16[3456,256]{1,0:T(8,128)(2,1)S(1)} copy-done((bf16[3456,256]{1,0:T(8,128)(2,1)S(1)}, bf16[3456,256]{1,0:T(8,128)(2,1)}, u32[]{:S(2)}) %copy-start.3) | copy-done | bytes 1769496
  19.9 6.6 %shard_map.97 = (f32[2,7936,128]{2,1,0:T(8,128)S(1)}, bf16[8192,128]{1,0:T(8,128)(2,1)S(1)}, bf16[64,512]{1,0:T(8,128)(2,1)S(1)}, f32[512,128]{1,0:T(8,128)S(1)}) custom-call(s32[4]{0:T(128)S(1)} %pad_add_fusion.place_ref, bf16[512,128]{1,0:T(8,128)(2,1)S(1)} %get-tuple-element.56.act_ref, bf16[960,128]{1,0:T(8,128)(2,1)S(1)} %get-tuple-element.66.cot_ref, ...), custom_call_target="tpu_custom_call" | custom-call | flops 2500000000 | bytes 16000000 | tf_op jit(solution)/shard_map/pallas_call | solution.py:384
  26.6 4.6 %collective-permute-start.6 = (bf16[8192,128]{1,0:T(8,128)(2,1)S(1)}, bf16[8192,128]{1,0:T(8,128)(2,1)S(1)}, u32[]{:S(2)}, u32[]{:S(2)}) collective-permute-start(bf16[8192,128]{1,0:T(8,128)(2,1)S(1)} %get-tuple-element.71), channel_id=1, source_target_pairs={{0,8},{8,0},{1,9},{9,1},{2,10},{10,2},{3,11},{11,3},{4,12},{12,4},... | collective-permute-start | bytes 6291464 | tf_op jit(solution)/shard_map/ppermute | solution.py:415
  31.1 3.8 %collective-permute-done.6.got_ref = bf16[8192,128]{1,0:T(8,128)(2,1)S(1)} collective-permute-done((bf16[8192,128]{1,0:T(8,128)(2,1)S(1)}, bf16[8192,128]{1,0:T(8,128)(2,1)S(1)}, u32[]{:S(2)}, u32[]{:S(2)}) %collective-permute-start.6) | collective-permute-done | bytes 2097184 | tf_op jit(solution)/shard_map/ppermute | solution.py:415
  34.9 1.2 shard_map.98
  36.1 4.4 %collective-permute-start.8 = (bf16[2240,128]{1,0:T(8,128)(2,1)S(1)}, bf16[2240,128]{1,0:T(8,128)(2,1)S(1)}, u32[]{:S(2)}, u32[]{:S(2)}) collective-permute-start(bf16[2240,128]{1,0:T(8,128)(2,1)S(1)} %get-tuple-element.76), channel_id=1, source_target_pairs={{0,64},{8,24},{16,80},{24,40},{32,96},{40,56},{48,112},{56,8},{64,... | collective-permute-start | bytes 1720328 | tf_op jit(solution)/shard_map/ppermute | solution.py:410
  40.5 4.1 %collective-permute-start.7 = (bf16[1984,128]{1,0:T(8,128)(2,1)S(1)}, bf16[1984,128]{1,0:T(8,128)(2,1)S(1)}, u32[]{:S(2)}, u32[]{:S(2)}) collective-permute-start(bf16[1984,128]{1,0:T(8,128)(2,1)S(1)} %get-tuple-element.75), channel_id=1, source_target_pairs={{0,128},{8,40},{16,144},{24,56},{32,160},{40,8},{48,176},{56,24},{... | collective-permute-start | bytes 1523720 | tf_op jit(solution)/shard_map/ppermute | solution.py:410
  44.6 11.1 %collective-permute-done.7.got_2 = bf16[1984,128]{1,0:T(8,128)(2,1)S(1)} collective-permute-done((bf16[1984,128]{1,0:T(8,128)(2,1)S(1)}, bf16[1984,128]{1,0:T(8,128)(2,1)S(1)}, u32[]{:S(2)}, u32[]{:S(2)}) %collective-permute-start.7) | collective-permute-done | bytes 507936 | tf_op jit(solution)/shard_map/ppermute | solution.py:410
  55.7 1.2 %shard_map.99 = (bf16[256,512]{1,0:T(8,128)(2,1)S(1)}, f32[496,128]{1,0:T(8,128)S(1)}, f32[688,128]{1,0:T(8,128)S(1)}, f32[496,128]{1,0:T(8,128)S(1)}, f32[688,128]{1,0:T(8,128)S(1)}) custom-call(s32[4]{0:T(128)S(1)} %pad_add_fusion.place_ref, bf16[128,512]{1,0:T(8,128)(2,1)S(1)} %get-tuple-element.73.chip_ref, f32[1984,128]{1,0:T(8,128)S(1)} %get-tuple-element.74.own_ref, ...), custom_call_target="tpu_custom_call" | custom-call | flops 1000000 | bytes 4000000 | tf_op jit(solution)/shard_map/pallas_call | solution.py:72
  57.0 1.7 %collective-permute-start.11 = (f32[688,128]{1,0:T(8,128)S(1)}, f32[688,128]{1,0:T(8,128)S(1)}, u32[]{:S(2)}, u32[]{:S(2)}) collective-permute-start(f32[688,128]{1,0:T(8,128)S(1)} %get-tuple-element.81), channel_id=1, source_target_pairs={{0,16},{8,72},{16,32},{24,88},{32,48},{40,104},{48,0},{56,120},{64... | collective-permute-start | bytes 1056776 | tf_op jit(solution)/shard_map/ppermute | solution.py:410
  58.7 1.6 %collective-permute-start.12 = (f32[688,128]{1,0:T(8,128)S(1)}, f32[688,128]{1,0:T(8,128)S(1)}, u32[]{:S(2)}, u32[]{:S(2)}) collective-permute-start(f32[688,128]{1,0:T(8,128)S(1)} %get-tuple-element.82), channel_id=1, source_target_pairs={{0,48},{8,200},{16,0},{24,216},{32,16},{40,232},{48,32},{56,248},{... | collective-permute-start | bytes 1056776 | tf_op jit(solution)/shard_map/ppermute | solution.py:410
  60.3 2.0 %collective-permute-start.10 = (f32[496,128]{1,0:T(8,128)S(1)}, f32[496,128]{1,0:T(8,128)S(1)}, u32[]{:S(2)}, u32[]{:S(2)}) collective-permute-start(f32[496,128]{1,0:T(8,128)S(1)} %get-tuple-element.80), channel_id=1, source_target_pairs={{0,32},{8,136},{16,48},{24,152},{32,0},{40,168},{48,16},{56,184},{... | collective-permute-start | bytes 761864 | tf_op jit(solution)/shard_map/ppermute | solution.py:410
  62.2 7.2 %collective-permute-done.10.got_2 = f32[496,128]{1,0:T(8,128)S(1)} collective-permute-done((f32[496,128]{1,0:T(8,128)S(1)}, f32[496,128]{1,0:T(8,128)S(1)}, u32[]{:S(2)}, u32[]{:S(2)}) %collective-permute-start.10) | collective-permute-done | bytes 253984 | tf_op jit(solution)/shard_map/ppermute | solution.py:410
  69.4 1.1 shard_map.100
  70.7 6.0 %collective-permute-start.15 = (bf16[192,128]{1,0:T(8,128)(2,1)S(1)}, bf16[192,128]{1,0:T(8,128)(2,1)S(1)}, u32[]{:S(2)}, u32[]{:S(2)}) collective-permute-start(bf16[192,128]{1,0:T(8,128)(2,1)S(1)} %get-tuple-element.92), channel_id=1, source_target_pairs={{1,2},{2,1},{3,4},{4,3},{5,6},{6,5},{9,10},{10,9},{11,12},{12,11},... | collective-permute-start | bytes 147464 | tf_op jit(solution)/shard_map/ppermute | solution.py:525
  77.3 1.5 %collective-permute-done.15.other_ref = bf16[192,128]{1,0:T(8,128)(2,1)S(1)} collective-permute-done((bf16[192,128]{1,0:T(8,128)(2,1)S(1)}, bf16[192,128]{1,0:T(8,128)(2,1)S(1)}, u32[]{:S(2)}, u32[]{:S(2)}) %collective-permute-start.15) | collective-permute-done | bytes 49184 | tf_op jit(solution)/shard_map/ppermute | solution.py:525
  78.8 0.9 shard_map.103
  79.7 2.8 %collective-permute-start.14 = (f32[128,128]{1,0:T(8,128)S(1)}, f32[128,128]{1,0:T(8,128)S(1)}, u32[]{:S(2)}, u32[]{:S(2)}) collective-permute-start(f32[128,128]{1,0:T(8,128)S(1)} %get-tuple-element.89), channel_id=1, source_target_pairs={{0,2},{1,3},{2,0},{3,1},{4,6},{5,7},{6,4},{7,5},{8,10},{9,11},{10,... | collective-permute-start | bytes 196616 | tf_op jit(solution)/shard_map/ppermute | solution.py:415
  82.5 0.7 shard_map.102
  85.5 3.8 %collective-permute-start.16 = (f32[128,128]{1,0:T(8,128)S(1)}, f32[128,128]{1,0:T(8,128)S(1)}, u32[]{:S(2)}, u32[]{:S(2)}) collective-permute-start(f32[128,128]{1,0:T(8,128)S(1)} %add.30), channel_id=1, source_target_pairs={{0,7},{1,6},{2,5},{3,4},{4,3},{5,2},{6,1},{7,0},{8,15},{9,14},{10,... | collective-permute-start | bytes 196616 | tf_op jit(solution)/shard_map/ppermute | solution.py:415
  89.4 2.8 %convolution_convert_fusion.2 = bf16[1,4,8,8,128]{4,0,3,2,1:T(2,128)(2,1)S(1)} fusion(bf16[3,3,3,256,128]{4,3,2,1,0:T(8,128)(2,1)S(1)} %bitcast.38, bf16[2,6,10,10,256]{4,0,3,2,1:T(2,128)(2,1)S(1)} %pad_maximum_fusion), kind=kOutput, calls=%fused_computation.3 | convolution fusion | flops 453017600 | bytes 2449408 | tf_op jit(solution)/shard_map/conv_general_dilated | solution.py:18
  92.2 0.7 collective-permute-done.16
  93.0 1.1 collective-permute-done.17
  94.1 2.0 %collective-permute-start.18 = (f32[1,128]{1,0:T(1,128)S(1)}, f32[1,128]{1,0:T(1,128)S(1)}, u32[]{:S(2)}, u32[]{:S(2)}) collective-permute-start(f32[1,128]{1,0:T(1,128)S(1)} %add.32), channel_id=1, source_target_pairs={{0,64},{64,0},{128,192},{192,128},{1,65},{65,1},{129,193},{193,129... | collective-permute-start | bytes 1544 | tf_op jit(solution)/shard_map/ppermute | solution.py:415
  96.1 3.0 %convolution_convert_fusion.1 = bf16[1,4,8,8,128]{4,0,3,2,1:T(2,128)(2,1)S(1)} fusion(bf16[3,3,3,256,128]{4,3,2,1,0:T(8,128)(2,1)S(1)} %bitcast.39, bf16[2,6,10,10,256]{4,0,3,2,1:T(2,128)(2,1)S(1)} %pad_maximum_fusion), kind=kOutput, calls=%fused_computation.2 | convolution fusion | flops 453017600 | bytes 2449408 | tf_op jit(solution)/shard_map/conv_general_dilated | solution.py:18
  99.2 1.2 collective-permute-start.19
  100.3 0.8 convolution_multiply_fusion
  101.3 0.7 add_convert_fusion
  102.0 2.0 %collective-permute-done.19 = f32[1,128]{1,0:T(1,128)S(1)} collective-permute-done((f32[1,128]{1,0:T(1,128)S(1)}, f32[1,128]{1,0:T(1,128)S(1)}, u32[]{:S(2)}, u32[]{:S(2)}) %collective-permute-start.19) | collective-permute-done | bytes 544 | tf_op jit(solution)/shard_map/ppermute | solution.py:415
  104.0 1.4 %collective-permute-start.20 = (f32[1,128]{1,0:T(1,128)S(1)}, f32[1,128]{1,0:T(1,128)S(1)}, u32[]{:S(2)}, u32[]{:S(2)}) collective-permute-start(f32[1,128]{1,0:T(1,128)S(1)} %add.34), channel_id=1, source_target_pairs={{0,16},{16,0},{32,48},{48,32},{1,17},{17,1},{33,49},{49,33},{2,18}... | collective-permute-start | bytes 1544 | tf_op jit(solution)/shard_map/ppermute | solution.py:415
  105.4 2.1 %collective-permute-done.20 = f32[1,128]{1,0:T(1,128)S(1)} collective-permute-done((f32[1,128]{1,0:T(1,128)S(1)}, f32[1,128]{1,0:T(1,128)S(1)}, u32[]{:S(2)}, u32[]{:S(2)}) %collective-permute-start.20) | collective-permute-done | bytes 544 | tf_op jit(solution)/shard_map/ppermute | solution.py:415
  107.5 2.1 %collective-permute-start.21 = (f32[1,128]{1,0:T(1,128)S(1)}, f32[1,128]{1,0:T(1,128)S(1)}, u32[]{:S(2)}, u32[]{:S(2)}) collective-permute-start(f32[1,128]{1,0:T(1,128)S(1)} %add.36), channel_id=1, source_target_pairs={{0,48},{16,32},{32,16},{48,0},{1,49},{17,33},{33,17},{49,1},{2,50}... | collective-permute-start | bytes 1544 | tf_op jit(solution)/shard_map/ppermute | solution.py:415
  109.6 2.7 %collective-permute-done.21 = f32[1,128]{1,0:T(1,128)S(1)} collective-permute-done((f32[1,128]{1,0:T(1,128)S(1)}, f32[1,128]{1,0:T(1,128)S(1)}, u32[]{:S(2)}, u32[]{:S(2)}) %collective-permute-start.21) | collective-permute-done | bytes 544 | tf_op jit(solution)/shard_map/ppermute | solution.py:415
  112.3 3.5 %collective-permute-done.22 = f32[1,128]{1,0:T(1,128)S(1)} collective-permute-done((f32[1,128]{1,0:T(1,128)S(1)}, f32[1,128]{1,0:T(1,128)S(1)}, u32[]{:S(2)}, u32[]{:S(2)}) %collective-permute-start.22) | collective-permute-done | bytes 544 | tf_op jit(solution)/shard_map/ppermute | solution.py:415
  115.8 1.7 %collective-permute-start.23 = (f32[1,128]{1,0:T(1,128)S(1)}, f32[1,128]{1,0:T(1,128)S(1)}, u32[]{:S(2)}, u32[]{:S(2)}) collective-permute-start(f32[1,128]{1,0:T(1,128)S(1)} %add.38), channel_id=1, source_target_pairs={{0,2},{1,3},{2,0},{3,1},{4,6},{5,7},{6,4},{7,5},{8,10},{9,11},{10,... | collective-permute-start | bytes 1544 | tf_op jit(solution)/shard_map/ppermute | solution.py:415
  117.8 0.7 copy.21
  118.5 1.8 %collective-permute-done.23 = f32[1,128]{1,0:T(1,128)S(1)} collective-permute-done((f32[1,128]{1,0:T(1,128)S(1)}, f32[1,128]{1,0:T(1,128)S(1)}, u32[]{:S(2)}, u32[]{:S(2)}) %collective-permute-start.23) | collective-permute-done | bytes 544 | tf_op jit(solution)/shard_map/ppermute | solution.py:415
  120.3 1.3 %shard_map.104 = f32[62,128]{1,0:T(8,128)} custom-call(s32[4]{0:T(128)S(1)} %pad_add_fusion.place_ref, f32[1,128]{1,0:T(1,128)S(1)} %add.39.total_ref, f32[128,128]{1,0:T(8,128)S(1)} %get-tuple-element.116.both_ref), custom_call_target="tpu_custom_call" | custom-call | flops 1000000 | bytes 4000000 | tf_op jit(solution)/shard_map/pallas_call | solution.py:72
  (51 shorter events, 4.9 us)
Async XLA Ops:
  2.4 4.4 %collective-permute-start = (bf16[288,128]{1,0:T(8,128)(2,1)S(1)}, bf16[288,128]{1,0:T(8,128)(2,1)S(1)}, u32[]{:S(2)}, u32[]{:S(2)}) collective-permute-start(bf16[288,128]{1,0:T(8,128)(2,1)S(1)} %get-tuple-element.59), channel_id=1, source_target_pairs={{0,64},{64,0},{128,192},{192,128},{1,65},{65,1},{129,193},{193,129... | collective-permute-start | bytes 221192 | tf_op jit(solution)/shard_map/ppermute | solution.py:264
  4.1 2.8 %collective-permute-start.1 = (bf16[288,128]{1,0:T(8,128)(2,1)S(1)}, bf16[288,128]{1,0:T(8,128)(2,1)S(1)}, u32[]{:S(2)}, u32[]{:S(2)}) collective-permute-start(bf16[288,128]{1,0:T(8,128)(2,1)S(1)} %get-tuple-element.60), channel_id=1, source_target_pairs={{64,128},{128,64},{65,129},{129,65},{66,130},{130,66},{67,131},{13... | collective-permute-start | bytes 221192 | tf_op jit(solution)/shard_map/ppermute | solution.py:264
  7.6 1.3 %collective-permute-start.2 = (bf16[224,128]{1,0:T(8,128)(2,1)S(1)}, bf16[224,128]{1,0:T(8,128)(2,1)S(1)}, u32[]{:S(2)}, u32[]{:S(2)}) collective-permute-start(bf16[224,128]{1,0:T(8,128)(2,1)S(1)} %get-tuple-element.64), channel_id=1, source_target_pairs={{0,8},{8,0},{16,24},{24,16},{32,40},{40,32},{48,56},{56,48},{1,9},... | collective-permute-start | bytes 172040 | tf_op jit(solution)/shard_map/ppermute | solution.py:264
  7.7 1.2 %collective-permute-start.3 = (bf16[224,128]{1,0:T(8,128)(2,1)S(1)}, bf16[224,128]{1,0:T(8,128)(2,1)S(1)}, u32[]{:S(2)}, u32[]{:S(2)}) collective-permute-start(bf16[224,128]{1,0:T(8,128)(2,1)S(1)} %get-tuple-element.65), channel_id=1, source_target_pairs={{8,16},{16,8},{24,32},{32,24},{40,48},{48,40},{9,17},{17,9},{25,33... | collective-permute-start | bytes 172040 | tf_op jit(solution)/shard_map/ppermute | solution.py:264
  9.9 8.5 %collective-permute-start.4 = (bf16[304,128]{1,0:T(8,128)(2,1)S(1)}, bf16[304,128]{1,0:T(8,128)(2,1)S(1)}, u32[]{:S(2)}, u32[]{:S(2)}) collective-permute-start(bf16[304,128]{1,0:T(8,128)(2,1)S(1)} %get-tuple-element.68), channel_id=1, source_target_pairs={{0,1},{1,0},{2,3},{3,2},{4,5},{5,4},{6,7},{7,6},{8,9},{9,8},{10,11... | collective-permute-start | bytes 233480 | tf_op jit(solution)/shard_map/ppermute | solution.py:264
  11.8 6.6 %collective-permute-start.5 = (bf16[304,128]{1,0:T(8,128)(2,1)S(1)}, bf16[304,128]{1,0:T(8,128)(2,1)S(1)}, u32[]{:S(2)}, u32[]{:S(2)}) collective-permute-start(bf16[304,128]{1,0:T(8,128)(2,1)S(1)} %get-tuple-element.69), channel_id=1, source_target_pairs={{1,2},{2,1},{3,4},{4,3},{5,6},{6,5},{9,10},{10,9},{11,12},{12,11},... | collective-permute-start | bytes 233480 | tf_op jit(solution)/shard_map/ppermute | solution.py:264
  15.7 2.7 %copy-start = (bf16[2048,128]{1,0:T(8,128)(2,1)S(1)}, bf16[2048,128]{1,0:T(8,128)(2,1)}, u32[]{:S(2)}) copy-start(bf16[2048,128]{1,0:T(8,128)(2,1)} %w_up_hbm.1) | copy-start | bytes 1572868
  18.5 1.5 %copy-start.3 = (bf16[3456,256]{1,0:T(8,128)(2,1)S(1)}, bf16[3456,256]{1,0:T(8,128)(2,1)}, u32[]{:S(2)}) copy-start(bf16[3456,256]{1,0:T(8,128)(2,1)} %w_in_hbm.1) | copy-start | bytes 5308420
  26.6 8.4 %collective-permute-start.6 = (bf16[8192,128]{1,0:T(8,128)(2,1)S(1)}, bf16[8192,128]{1,0:T(8,128)(2,1)S(1)}, u32[]{:S(2)}, u32[]{:S(2)}) collective-permute-start(bf16[8192,128]{1,0:T(8,128)(2,1)S(1)} %get-tuple-element.71), channel_id=1, source_target_pairs={{0,8},{8,0},{1,9},{9,1},{2,10},{10,2},{3,11},{11,3},{4,12},{12,4},... | collective-permute-start | bytes 6291464 | tf_op jit(solution)/shard_map/ppermute | solution.py:415
  36.1 33.3 %copy-start.2 = (bf16[96,192]{1,0:T(8,128)(2,1)S(1)}, bf16[96,192]{1,0:T(8,128)(2,1)}, u32[]{:S(2)}) copy-start(bf16[96,192]{1,0:T(8,128)(2,1)} %constant.26.clone.z_faces_ref) | copy-start | bytes 110596
  36.1 19.6 %collective-permute-start.8 = (bf16[2240,128]{1,0:T(8,128)(2,1)S(1)}, bf16[2240,128]{1,0:T(8,128)(2,1)S(1)}, u32[]{:S(2)}, u32[]{:S(2)}) collective-permute-start(bf16[2240,128]{1,0:T(8,128)(2,1)S(1)} %get-tuple-element.76), channel_id=1, source_target_pairs={{0,64},{8,24},{16,80},{24,40},{32,96},{40,56},{48,112},{56,8},{64,... | collective-permute-start | bytes 1720328 | tf_op jit(solution)/shard_map/ppermute | solution.py:410
  40.5 15.2 %collective-permute-start.9 = (bf16[2240,128]{1,0:T(8,128)(2,1)S(1)}, bf16[2240,128]{1,0:T(8,128)(2,1)S(1)}, u32[]{:S(2)}, u32[]{:S(2)}) collective-permute-start(bf16[2240,128]{1,0:T(8,128)(2,1)S(1)} %get-tuple-element.77), channel_id=1, source_target_pairs={{0,192},{8,56},{16,208},{24,8},{32,224},{40,24},{48,240},{56,40},{... | collective-permute-start | bytes 1720328 | tf_op jit(solution)/shard_map/ppermute | solution.py:410
  40.5 15.2 %collective-permute-start.7 = (bf16[1984,128]{1,0:T(8,128)(2,1)S(1)}, bf16[1984,128]{1,0:T(8,128)(2,1)S(1)}, u32[]{:S(2)}, u32[]{:S(2)}) collective-permute-start(bf16[1984,128]{1,0:T(8,128)(2,1)S(1)} %get-tuple-element.75), channel_id=1, source_target_pairs={{0,128},{8,40},{16,144},{24,56},{32,160},{40,8},{48,176},{56,24},{... | collective-permute-start | bytes 1523720 | tf_op jit(solution)/shard_map/ppermute | solution.py:410
  55.7 23.0 %copy-start.1 = (bf16[288,288]{1,0:T(8,128)(2,1)S(1)}, bf16[288,288]{1,0:T(8,128)(2,1)}, u32[]{:S(2)}) copy-start(bf16[288,288]{1,0:T(8,128)(2,1)} %constant.27.clone.padded_ref) | copy-start | bytes 497668
  57.0 12.5 %collective-permute-start.11 = (f32[688,128]{1,0:T(8,128)S(1)}, f32[688,128]{1,0:T(8,128)S(1)}, u32[]{:S(2)}, u32[]{:S(2)}) collective-permute-start(f32[688,128]{1,0:T(8,128)S(1)} %get-tuple-element.81), channel_id=1, source_target_pairs={{0,16},{8,72},{16,32},{24,88},{32,48},{40,104},{48,0},{56,120},{64... | collective-permute-start | bytes 1056776 | tf_op jit(solution)/shard_map/ppermute | solution.py:410
  58.7 10.8 %collective-permute-start.12 = (f32[688,128]{1,0:T(8,128)S(1)}, f32[688,128]{1,0:T(8,128)S(1)}, u32[]{:S(2)}, u32[]{:S(2)}) collective-permute-start(f32[688,128]{1,0:T(8,128)S(1)} %get-tuple-element.82), channel_id=1, source_target_pairs={{0,48},{8,200},{16,0},{24,216},{32,16},{40,232},{48,32},{56,248},{... | collective-permute-start | bytes 1056776 | tf_op jit(solution)/shard_map/ppermute | solution.py:410
  60.3 9.2 %collective-permute-start.10 = (f32[496,128]{1,0:T(8,128)S(1)}, f32[496,128]{1,0:T(8,128)S(1)}, u32[]{:S(2)}, u32[]{:S(2)}) collective-permute-start(f32[496,128]{1,0:T(8,128)S(1)} %get-tuple-element.80), channel_id=1, source_target_pairs={{0,32},{8,136},{16,48},{24,152},{32,0},{40,168},{48,16},{56,184},{... | collective-permute-start | bytes 761864 | tf_op jit(solution)/shard_map/ppermute | solution.py:410
  70.6 6.1 %collective-permute-start.13 = (f32[448,128]{1,0:T(8,128)S(1)}, f32[448,128]{1,0:T(8,128)S(1)}, u32[]{:S(2)}, u32[]{:S(2)}) collective-permute-start(f32[448,128]{1,0:T(8,128)S(1)} %get-tuple-element.84), channel_id=1, source_target_pairs={{0,1},{1,0},{2,3},{3,2},{4,5},{5,4},{6,7},{7,6},{8,9},{9,8},{10,11... | collective-permute-start | bytes 688136 | tf_op jit(solution)/shard_map/ppermute | solution.py:415
  70.7 8.1 %collective-permute-start.15 = (bf16[192,128]{1,0:T(8,128)(2,1)S(1)}, bf16[192,128]{1,0:T(8,128)(2,1)S(1)}, u32[]{:S(2)}, u32[]{:S(2)}) collective-permute-start(bf16[192,128]{1,0:T(8,128)(2,1)S(1)} %get-tuple-element.92), channel_id=1, source_target_pairs={{1,2},{2,1},{3,4},{4,3},{5,6},{6,5},{9,10},{10,9},{11,12},{12,11},... | collective-permute-start | bytes 147464 | tf_op jit(solution)/shard_map/ppermute | solution.py:525
  79.7 5.8 %collective-permute-start.14 = (f32[128,128]{1,0:T(8,128)S(1)}, f32[128,128]{1,0:T(8,128)S(1)}, u32[]{:S(2)}, u32[]{:S(2)}) collective-permute-start(f32[128,128]{1,0:T(8,128)S(1)} %get-tuple-element.89), channel_id=1, source_target_pairs={{0,2},{1,3},{2,0},{3,1},{4,6},{5,7},{6,4},{7,5},{8,10},{9,11},{10,... | collective-permute-start | bytes 196616 | tf_op jit(solution)/shard_map/ppermute | solution.py:415
  84.5 4.9 %copy-start.5 = (bf16[6912,128]{1,0:T(8,128)(2,1)S(1)}, bf16[6912,128]{1,0:T(8,128)(2,1)}, u32[]{:S(2)}) copy-start(bf16[6912,128]{1,0:T(8,128)(2,1)} %param.10) | copy-start | bytes 5308420
  85.5 7.4 %collective-permute-start.16 = (f32[128,128]{1,0:T(8,128)S(1)}, f32[128,128]{1,0:T(8,128)S(1)}, u32[]{:S(2)}, u32[]{:S(2)}) collective-permute-start(f32[128,128]{1,0:T(8,128)S(1)} %add.30), channel_id=1, source_target_pairs={{0,7},{1,6},{2,5},{3,4},{4,3},{5,2},{6,1},{7,0},{8,15},{9,14},{10,... | collective-permute-start | bytes 196616 | tf_op jit(solution)/shard_map/ppermute | solution.py:415
  92.9 1.2 collective-permute-start.17
  94.1 6.2 %copy-start.4 = (bf16[3456,256]{1,0:T(8,128)(2,1)S(1)}, bf16[3456,256]{1,0:T(8,128)(2,1)}, u32[]{:S(2)}) copy-start(bf16[3456,256]{1,0:T(8,128)(2,1)} %w_in_hbm.1) | copy-start | bytes 5308420
  94.1 5.0 %collective-permute-start.18 = (f32[1,128]{1,0:T(1,128)S(1)}, f32[1,128]{1,0:T(1,128)S(1)}, u32[]{:S(2)}, u32[]{:S(2)}) collective-permute-start(f32[1,128]{1,0:T(1,128)S(1)} %add.32), channel_id=1, source_target_pairs={{0,64},{64,0},{128,192},{192,128},{1,65},{65,1},{129,193},{193,129... | collective-permute-start | bytes 1544 | tf_op jit(solution)/shard_map/ppermute | solution.py:415
  99.2 4.8 %collective-permute-start.19 = (f32[1,128]{1,0:T(1,128)S(1)}, f32[1,128]{1,0:T(1,128)S(1)}, u32[]{:S(2)}, u32[]{:S(2)}) collective-permute-start(f32[1,128]{1,0:T(1,128)S(1)} %add.33), channel_id=1, source_target_pairs={{0,192},{64,128},{128,64},{192,0},{1,193},{65,129},{129,65},{193,1... | collective-permute-start | bytes 1544 | tf_op jit(solution)/shard_map/ppermute | solution.py:415
  104.0 3.5 %collective-permute-start.20 = (f32[1,128]{1,0:T(1,128)S(1)}, f32[1,128]{1,0:T(1,128)S(1)}, u32[]{:S(2)}, u32[]{:S(2)}) collective-permute-start(f32[1,128]{1,0:T(1,128)S(1)} %add.34), channel_id=1, source_target_pairs={{0,16},{16,0},{32,48},{48,32},{1,17},{17,1},{33,49},{49,33},{2,18}... | collective-permute-start | bytes 1544 | tf_op jit(solution)/shard_map/ppermute | solution.py:415
  107.5 4.8 %collective-permute-start.21 = (f32[1,128]{1,0:T(1,128)S(1)}, f32[1,128]{1,0:T(1,128)S(1)}, u32[]{:S(2)}, u32[]{:S(2)}) collective-permute-start(f32[1,128]{1,0:T(1,128)S(1)} %add.36), channel_id=1, source_target_pairs={{0,48},{16,32},{32,16},{48,0},{1,49},{17,33},{33,17},{49,1},{2,50}... | collective-permute-start | bytes 1544 | tf_op jit(solution)/shard_map/ppermute | solution.py:415
  112.3 3.5 %collective-permute-start.22 = (f32[1,128]{1,0:T(1,128)S(1)}, f32[1,128]{1,0:T(1,128)S(1)}, u32[]{:S(2)}, u32[]{:S(2)}) collective-permute-start(f32[1,128]{1,0:T(1,128)S(1)} %add.37), channel_id=1, source_target_pairs={{0,1},{1,0},{2,3},{3,2},{4,5},{5,4},{6,7},{7,6},{8,9},{9,8},{10,11... | collective-permute-start | bytes 1544 | tf_op jit(solution)/shard_map/ppermute | solution.py:415
  115.8 4.4 %collective-permute-start.23 = (f32[1,128]{1,0:T(1,128)S(1)}, f32[1,128]{1,0:T(1,128)S(1)}, u32[]{:S(2)}, u32[]{:S(2)}) collective-permute-start(f32[1,128]{1,0:T(1,128)S(1)} %add.38), channel_id=1, source_target_pairs={{0,2},{1,3},{2,0},{3,1},{4,6},{5,7},{6,4},{7,5},{8,10},{9,11},{10,... | collective-permute-start | bytes 1544 | tf_op jit(solution)/shard_map/ppermute | solution.py:415

commit v6 on v5

--- a/solution.py
+++ b/solution.py
@@ -550,15 +550,18 @@
     total, output_0, joined_pad = lax.optimization_barrier((total, output_0, joined_pad))
     total = total + paired(total, "core", 1)
     total, joined_pad = lax.optimization_barrier((total, joined_pad))
-    output_1 = conv_forward(joined_pad[1:], w_out).astype(BF16)
+    output_1 = conv_forward(joined_pad[1:, :4], w_out).astype(BF16)
     total = total + paired(total, "gx", 1)
-    total, output_1, slope_pad = lax.optimization_barrier((total, output_1, slope_pad))
+    total, output_1, joined_pad = lax.optimization_barrier((total, output_1, joined_pad))
+    output_2 = conv_forward(joined_pad[1:, 2:], w_out).astype(BF16)
+    total = total + paired(total, "gx", 3)
+    total, output_2, slope_pad = lax.optimization_barrier((total, output_2, slope_pad))
     d_pooled = conv_transpose(slope_pad, w_in)
     d_activation = (d_direct.reshape(activation.shape) + spread(d_pooled) * 0.125).astype(BF16)
-    total = total + paired(total, "gx", 3)
+    total = total + paired(total, "x", 1)
     total, d_activation = lax.optimization_barrier((total, d_activation))
-    output = jnp.concatenate([output_0, output_1], axis=0)
-    for axis, mask in (("x", 1), ("x", 3), ("gz", 1), ("gz", 2)):
+    output = jnp.concatenate([output_0, jnp.concatenate([output_1, output_2], axis=1)], axis=0)
+    for axis, mask in (("x", 3), ("gz", 1), ("gz", 2)):
         total = total + paired(total, axis, mask)
     (clipped,) = _call(_clip_kernel, (((62, 128), F32),), place, total, mine)
     return (output, d_activation, clipped.reshape(-1))

time: 122 us -> 121 us (level)
  waiting for transfers between devices: 40.2 us -> 37.4 us
  starting transfers between devices: 48.3 us -> 49.6 us
    ppermute x11, waiting for transfers between devices: 17.7 us -> 14.9 us  [paired(): return lax.ppermute(array, axis, [(i, i ^ bit) for i in range(count)])]
    ppermute x11, starting transfers between devices: 19.7 us -> 21 us  [paired(): return lax.ppermute(array, axis, [(i, i ^ bit) for i in range(count)])]
    conv_general_dilated x2 -> x3, matrix products: 5.82 us -> 6.24 us  [conv_forward(): lax.conv_general_dilated(padded, kernel, (1, 1, 1), 'VALID', dimension_nu...]
where the time goes in v6:
time: 121 us; the launch traced here: 120 us
  starting transfers between devices  49.6 us (41%)
  waiting for transfers between devices  37.4 us (31%)
  Pallas kernels  16 us (13%)
  matrix products  7.42 us (6%)
  local copies, waits for them, and re-layouts  6.27 us (5%)
  other arithmetic  2.76 us (2%)
    ppermute x11, starting transfers between devices, paired(): return lax.ppermute(array, axis, [(i, i ^ bit) for i in range(count)])  21 us
    ppermute x6, waiting for transfers between devices, crossed(): return lax.ppermute(array, ('gx', 'x', 'core'), pairs)  18.3 us
    ppermute x11, waiting for transfers between devices, paired(): return lax.ppermute(array, axis, [(i, i ^ bit) for i in range(count)])  14.9 us
    ppermute x6, starting transfers between devices, crossed(): return lax.ppermute(array, ('gx', 'x', 'core'), pairs)  13.7 us
    pallas_call x10, Pallas kernels, _call(): pl.pallas_call(kernel, out_shape=tuple((jax.ShapeDtypeStruct(shape, kind)...  9.36 us
    pallas_call x1, Pallas kernels, gradients(): pl.pallas_call(_gradients_kernel, out_shape=(shape((2, 7936, 128), F32),...  6.64 us
    conv_general_dilated x3, matrix products, conv_forward(): lax.conv_general_dilated(padded, kernel, (1, 1, 1), 'VALID', dimension_nu...  6.24 us
    ppermute x1, starting transfers between devices, scattered_sum(): lax.ppermute(other, 'gz', [(i, j) for i in range(8) for j in [(i + 1 ^ 1)...  6.03 us
  transfers between devices with their start and end apart: 24, of which 13 were waited for; matrix products, arithmetic and copies ran while one was open for 11% of the time, Pallas kernels for 1%

profile of v6, /device:TPU:32, one launch (start us, length us, event | category | flops | bytes accessed | tf_op | source)
XLA Modules:
  0.0 120.5 jit_solution(12973316748377396655)
XLA Ops:
  0.6 1.0 pad_maximum_fusion.1.both_ref
  1.7 0.7 shard_map.94
  2.4 1.7 %collective-permute-start = (bf16[288,128]{1,0:T(8,128)(2,1)S(1)}, bf16[288,128]{1,0:T(8,128)(2,1)S(1)}, u32[]{:S(2)}, u32[]{:S(2)}) collective-permute-start(bf16[288,128]{1,0:T(8,128)(2,1)S(1)} %get-tuple-element.62), channel_id=1, source_target_pairs={{0,64},{64,0},{128,192},{192,128},{1,65},{65,1},{129,193},{193,129... | collective-permute-start | bytes 221192 | tf_op jit(solution)/shard_map/ppermute | solution.py:264
  4.8 2.1 %collective-permute-done.got_here = bf16[288,128]{1,0:T(8,128)(2,1)S(1)} collective-permute-done((bf16[288,128]{1,0:T(8,128)(2,1)S(1)}, bf16[288,128]{1,0:T(8,128)(2,1)S(1)}, u32[]{:S(2)}, u32[]{:S(2)}) %collective-permute-start) | collective-permute-done | bytes 73760 | tf_op jit(solution)/shard_map/ppermute | solution.py:264
  6.9 0.7 shard_map.95
  7.7 0.7 collective-permute-start.3
  8.9 1.0 shard_map.96
  9.9 1.9 %collective-permute-start.4 = (bf16[304,128]{1,0:T(8,128)(2,1)S(1)}, bf16[304,128]{1,0:T(8,128)(2,1)S(1)}, u32[]{:S(2)}, u32[]{:S(2)}) collective-permute-start(bf16[304,128]{1,0:T(8,128)(2,1)S(1)} %get-tuple-element.71), channel_id=1, source_target_pairs={{0,1},{1,0},{2,3},{3,2},{4,5},{5,4},{6,7},{7,6},{8,9},{9,8},{10,11... | collective-permute-start | bytes 233480 | tf_op jit(solution)/shard_map/ppermute | solution.py:264
  11.8 3.9 %collective-permute-start.5 = (bf16[304,128]{1,0:T(8,128)(2,1)S(1)}, bf16[304,128]{1,0:T(8,128)(2,1)S(1)}, u32[]{:S(2)}, u32[]{:S(2)}) collective-permute-start(bf16[304,128]{1,0:T(8,128)(2,1)S(1)} %get-tuple-element.72), channel_id=1, source_target_pairs={{1,2},{2,1},{3,4},{4,3},{5,6},{6,5},{9,10},{10,9},{11,12},{12,11},... | collective-permute-start | bytes 233480 | tf_op jit(solution)/shard_map/ppermute | solution.py:264
  15.7 2.7 %copy.15 = bf16[27,256,128]{1,2,0:T(8,128)(2,1)S(1)} copy(bf16[27,256,128]{2,1,0:T(8,128)(2,1)} %bitcast.38) | data formatting | bytes 3538944 | tf_op jit(solution)/shard_map/reshape | solution.py:534
  18.5 1.5 %copy-done.3 = bf16[3456,256]{1,0:T(8,128)(2,1)S(1)} copy-done((bf16[3456,256]{1,0:T(8,128)(2,1)S(1)}, bf16[3456,256]{1,0:T(8,128)(2,1)}, u32[]{:S(2)}) %copy-start.3) | copy-done | bytes 1769496
  19.9 6.6 %shard_map.97 = (f32[2,7936,128]{2,1,0:T(8,128)S(1)}, bf16[8192,128]{1,0:T(8,128)(2,1)S(1)}, bf16[64,512]{1,0:T(8,128)(2,1)S(1)}, f32[512,128]{1,0:T(8,128)S(1)}) custom-call(s32[4]{0:T(128)S(1)} %pad_add_fusion.place_ref, bf16[512,128]{1,0:T(8,128)(2,1)S(1)} %get-tuple-element.59.act_ref, bf16[960,128]{1,0:T(8,128)(2,1)S(1)} %get-tuple-element.69.cot_ref, ...), custom_call_target="tpu_custom_call" | custom-call | flops 2500000000 | bytes 16000000 | tf_op jit(solution)/shard_map/pallas_call | solution.py:384
  26.6 4.6 %collective-permute-start.6 = (bf16[8192,128]{1,0:T(8,128)(2,1)S(1)}, bf16[8192,128]{1,0:T(8,128)(2,1)S(1)}, u32[]{:S(2)}, u32[]{:S(2)}) collective-permute-start(bf16[8192,128]{1,0:T(8,128)(2,1)S(1)} %get-tuple-element.74), channel_id=1, source_target_pairs={{0,8},{8,0},{1,9},{9,1},{2,10},{10,2},{3,11},{11,3},{4,12},{12,4},... | collective-permute-start | bytes 6291464 | tf_op jit(solution)/shard_map/ppermute | solution.py:415
  31.1 3.8 %collective-permute-done.6.got_ref = bf16[8192,128]{1,0:T(8,128)(2,1)S(1)} collective-permute-done((bf16[8192,128]{1,0:T(8,128)(2,1)S(1)}, bf16[8192,128]{1,0:T(8,128)(2,1)S(1)}, u32[]{:S(2)}, u32[]{:S(2)}) %collective-permute-start.6) | collective-permute-done | bytes 2097184 | tf_op jit(solution)/shard_map/ppermute | solution.py:415
  34.9 1.2 shard_map.98
  36.1 4.4 %collective-permute-start.8 = (bf16[2240,128]{1,0:T(8,128)(2,1)S(1)}, bf16[2240,128]{1,0:T(8,128)(2,1)S(1)}, u32[]{:S(2)}, u32[]{:S(2)}) collective-permute-start(bf16[2240,128]{1,0:T(8,128)(2,1)S(1)} %get-tuple-element.79), channel_id=1, source_target_pairs={{0,64},{8,24},{16,80},{24,40},{32,96},{40,56},{48,112},{56,8},{64,... | collective-permute-start | bytes 1720328 | tf_op jit(solution)/shard_map/ppermute | solution.py:410
  40.5 4.1 %collective-permute-start.7 = (bf16[1984,128]{1,0:T(8,128)(2,1)S(1)}, bf16[1984,128]{1,0:T(8,128)(2,1)S(1)}, u32[]{:S(2)}, u32[]{:S(2)}) collective-permute-start(bf16[1984,128]{1,0:T(8,128)(2,1)S(1)} %get-tuple-element.78), channel_id=1, source_target_pairs={{0,128},{8,40},{16,144},{24,56},{32,160},{40,8},{48,176},{56,24},{... | collective-permute-start | bytes 1523720 | tf_op jit(solution)/shard_map/ppermute | solution.py:410
  44.6 11.1 %collective-permute-done.7.got_2 = bf16[1984,128]{1,0:T(8,128)(2,1)S(1)} collective-permute-done((bf16[1984,128]{1,0:T(8,128)(2,1)S(1)}, bf16[1984,128]{1,0:T(8,128)(2,1)S(1)}, u32[]{:S(2)}, u32[]{:S(2)}) %collective-permute-start.7) | collective-permute-done | bytes 507936 | tf_op jit(solution)/shard_map/ppermute | solution.py:410
  55.7 1.2 %shard_map.99 = (bf16[256,512]{1,0:T(8,128)(2,1)S(1)}, f32[496,128]{1,0:T(8,128)S(1)}, f32[688,128]{1,0:T(8,128)S(1)}, f32[496,128]{1,0:T(8,128)S(1)}, f32[688,128]{1,0:T(8,128)S(1)}) custom-call(s32[4]{0:T(128)S(1)} %pad_add_fusion.place_ref, bf16[128,512]{1,0:T(8,128)(2,1)S(1)} %get-tuple-element.76.chip_ref, f32[1984,128]{1,0:T(8,128)S(1)} %get-tuple-element.77.own_ref, ...), custom_call_target="tpu_custom_call" | custom-call | flops 1000000 | bytes 4000000 | tf_op jit(solution)/shard_map/pallas_call | solution.py:72
  57.0 1.7 %collective-permute-start.11 = (f32[688,128]{1,0:T(8,128)S(1)}, f32[688,128]{1,0:T(8,128)S(1)}, u32[]{:S(2)}, u32[]{:S(2)}) collective-permute-start(f32[688,128]{1,0:T(8,128)S(1)} %get-tuple-element.84), channel_id=1, source_target_pairs={{0,16},{8,72},{16,32},{24,88},{32,48},{40,104},{48,0},{56,120},{64... | collective-permute-start | bytes 1056776 | tf_op jit(solution)/shard_map/ppermute | solution.py:410
  58.7 1.6 %collective-permute-start.12 = (f32[688,128]{1,0:T(8,128)S(1)}, f32[688,128]{1,0:T(8,128)S(1)}, u32[]{:S(2)}, u32[]{:S(2)}) collective-permute-start(f32[688,128]{1,0:T(8,128)S(1)} %get-tuple-element.85), channel_id=1, source_target_pairs={{0,48},{8,200},{16,0},{24,216},{32,16},{40,232},{48,32},{56,248},{... | collective-permute-start | bytes 1056776 | tf_op jit(solution)/shard_map/ppermute | solution.py:410
  60.3 2.0 %collective-permute-start.10 = (f32[496,128]{1,0:T(8,128)S(1)}, f32[496,128]{1,0:T(8,128)S(1)}, u32[]{:S(2)}, u32[]{:S(2)}) collective-permute-start(f32[496,128]{1,0:T(8,128)S(1)} %get-tuple-element.83), channel_id=1, source_target_pairs={{0,32},{8,136},{16,48},{24,152},{32,0},{40,168},{48,16},{56,184},{... | collective-permute-start | bytes 761864 | tf_op jit(solution)/shard_map/ppermute | solution.py:410
  62.2 7.2 %collective-permute-done.10.got_2 = f32[496,128]{1,0:T(8,128)S(1)} collective-permute-done((f32[496,128]{1,0:T(8,128)S(1)}, f32[496,128]{1,0:T(8,128)S(1)}, u32[]{:S(2)}, u32[]{:S(2)}) %collective-permute-start.10) | collective-permute-done | bytes 253984 | tf_op jit(solution)/shard_map/ppermute | solution.py:410
  69.4 1.1 shard_map.100
  70.7 6.0 %collective-permute-start.15 = (bf16[192,128]{1,0:T(8,128)(2,1)S(1)}, bf16[192,128]{1,0:T(8,128)(2,1)S(1)}, u32[]{:S(2)}, u32[]{:S(2)}) collective-permute-start(bf16[192,128]{1,0:T(8,128)(2,1)S(1)} %get-tuple-element.95), channel_id=1, source_target_pairs={{1,2},{2,1},{3,4},{4,3},{5,6},{6,5},{9,10},{10,9},{11,12},{12,11},... | collective-permute-start | bytes 147464 | tf_op jit(solution)/shard_map/ppermute | solution.py:525
  77.3 1.5 %collective-permute-done.15.other_ref = bf16[192,128]{1,0:T(8,128)(2,1)S(1)} collective-permute-done((bf16[192,128]{1,0:T(8,128)(2,1)S(1)}, bf16[192,128]{1,0:T(8,128)(2,1)S(1)}, u32[]{:S(2)}, u32[]{:S(2)}) %collective-permute-start.15) | collective-permute-done | bytes 49184 | tf_op jit(solution)/shard_map/ppermute | solution.py:525
  78.8 0.9 shard_map.103
  79.7 2.8 %collective-permute-start.14 = (f32[128,128]{1,0:T(8,128)S(1)}, f32[128,128]{1,0:T(8,128)S(1)}, u32[]{:S(2)}, u32[]{:S(2)}) collective-permute-start(f32[128,128]{1,0:T(8,128)S(1)} %get-tuple-element.92), channel_id=1, source_target_pairs={{0,2},{1,3},{2,0},{3,1},{4,6},{5,7},{6,4},{7,5},{8,10},{9,11},{10,... | collective-permute-start | bytes 196616 | tf_op jit(solution)/shard_map/ppermute | solution.py:415
  82.5 0.7 shard_map.102
  85.5 3.8 %collective-permute-start.16 = (f32[128,128]{1,0:T(8,128)S(1)}, f32[128,128]{1,0:T(8,128)S(1)}, u32[]{:S(2)}, u32[]{:S(2)}) collective-permute-start(f32[128,128]{1,0:T(8,128)S(1)} %add.30), channel_id=1, source_target_pairs={{0,7},{1,6},{2,5},{3,4},{4,3},{5,2},{6,1},{7,0},{8,15},{9,14},{10,... | collective-permute-start | bytes 196616 | tf_op jit(solution)/shard_map/ppermute | solution.py:415
  89.4 2.8 %convolution_convert_fusion.1 = bf16[1,4,8,8,128]{4,0,3,2,1:T(2,128)(2,1)S(1)} fusion(bf16[3,3,3,256,128]{4,3,2,1,0:T(8,128)(2,1)S(1)} %bitcast.39, bf16[2,6,10,10,256]{4,0,3,2,1:T(2,128)(2,1)S(1)} %pad_maximum_fusion), kind=kOutput, calls=%fused_computation.2 | convolution fusion | flops 453017600 | bytes 2449408 | tf_op jit(solution)/shard_map/conv_general_dilated | solution.py:18
  92.2 0.7 collective-permute-done.16
  93.0 1.1 collective-permute-done.17
  94.1 2.0 %collective-permute-start.18 = (f32[1,128]{1,0:T(1,128)S(1)}, f32[1,128]{1,0:T(1,128)S(1)}, u32[]{:S(2)}, u32[]{:S(2)}) collective-permute-start(f32[1,128]{1,0:T(1,128)S(1)} %add.32), channel_id=1, source_target_pairs={{0,64},{64,0},{128,192},{192,128},{1,65},{65,1},{129,193},{193,129... | collective-permute-start | bytes 1544 | tf_op jit(solution)/shard_map/ppermute | solution.py:415
  96.1 1.7 %convolution_convert_fusion.3 = bf16[1,2,8,8,128]{4,0,3,2,1:T(2,128)(2,1)S(1)} fusion(bf16[3,3,3,256,128]{4,3,2,1,0:T(8,128)(2,1)S(1)} %bitcast.40, bf16[2,6,10,10,256]{4,0,3,2,1:T(2,128)(2,1)S(1)} %pad_maximum_fusion), kind=kOutput, calls=%fused_computation.4 | convolution fusion | flops 226508800 | bytes 2211840 | tf_op jit(solution)/shard_map/conv_general_dilated | solution.py:18
  97.9 2.5 %collective-permute-start.19 = (f32[1,128]{1,0:T(1,128)S(1)}, f32[1,128]{1,0:T(1,128)S(1)}, u32[]{:S(2)}, u32[]{:S(2)}) collective-permute-start(f32[1,128]{1,0:T(1,128)S(1)} %add.33), channel_id=1, source_target_pairs={{0,192},{64,128},{128,64},{192,0},{1,193},{65,129},{129,65},{193,1... | collective-permute-start | bytes 1544 | tf_op jit(solution)/shard_map/ppermute | solution.py:415
  100.3 1.7 %convolution_convert_fusion.2 = bf16[1,2,8,8,128]{4,0,3,2,1:T(2,128)(2,1)S(1)} fusion(bf16[3,3,3,256,128]{4,3,2,1,0:T(8,128)(2,1)S(1)} %bitcast.41, bf16[2,6,10,10,256]{4,0,3,2,1:T(2,128)(2,1)S(1)} %pad_maximum_fusion), kind=kOutput, calls=%fused_computation.3 | convolution fusion | flops 226508800 | bytes 2211840 | tf_op jit(solution)/shard_map/conv_general_dilated | solution.py:18
  102.0 0.9 collective-permute-done.19
  102.9 1.4 %collective-permute-start.20 = (f32[1,128]{1,0:T(1,128)S(1)}, f32[1,128]{1,0:T(1,128)S(1)}, u32[]{:S(2)}, u32[]{:S(2)}) collective-permute-start(f32[1,128]{1,0:T(1,128)S(1)} %add.34), channel_id=1, source_target_pairs={{0,16},{16,0},{32,48},{48,32},{1,17},{17,1},{33,49},{49,33},{2,18}... | collective-permute-start | bytes 1544 | tf_op jit(solution)/shard_map/ppermute | solution.py:415
  104.4 0.8 convolution_multiply_fusion
  105.3 0.7 add_convert_fusion
  106.5 2.1 %collective-permute-start.21 = (f32[1,128]{1,0:T(1,128)S(1)}, f32[1,128]{1,0:T(1,128)S(1)}, u32[]{:S(2)}, u32[]{:S(2)}) collective-permute-start(f32[1,128]{1,0:T(1,128)S(1)} %add.35), channel_id=1, source_target_pairs={{0,48},{16,32},{32,16},{48,0},{1,49},{17,33},{33,17},{49,1},{2,50}... | collective-permute-start | bytes 1544 | tf_op jit(solution)/shard_map/ppermute | solution.py:415
  108.6 2.7 %collective-permute-done.21 = f32[1,128]{1,0:T(1,128)S(1)} collective-permute-done((f32[1,128]{1,0:T(1,128)S(1)}, f32[1,128]{1,0:T(1,128)S(1)}, u32[]{:S(2)}, u32[]{:S(2)}) %collective-permute-start.21) | collective-permute-done | bytes 544 | tf_op jit(solution)/shard_map/ppermute | solution.py:415
  111.2 3.5 %collective-permute-done.22 = f32[1,128]{1,0:T(1,128)S(1)} collective-permute-done((f32[1,128]{1,0:T(1,128)S(1)}, f32[1,128]{1,0:T(1,128)S(1)}, u32[]{:S(2)}, u32[]{:S(2)}) %collective-permute-start.22) | collective-permute-done | bytes 544 | tf_op jit(solution)/shard_map/ppermute | solution.py:415
  114.8 1.7 %collective-permute-start.23 = (f32[1,128]{1,0:T(1,128)S(1)}, f32[1,128]{1,0:T(1,128)S(1)}, u32[]{:S(2)}, u32[]{:S(2)}) collective-permute-start(f32[1,128]{1,0:T(1,128)S(1)} %add.38), channel_id=1, source_target_pairs={{0,2},{1,3},{2,0},{3,1},{4,6},{5,7},{6,4},{7,5},{8,10},{9,11},{10,... | collective-permute-start | bytes 1544 | tf_op jit(solution)/shard_map/ppermute | solution.py:415
  116.7 0.7 copy.21
  117.4 1.8 %collective-permute-done.23 = f32[1,128]{1,0:T(1,128)S(1)} collective-permute-done((f32[1,128]{1,0:T(1,128)S(1)}, f32[1,128]{1,0:T(1,128)S(1)}, u32[]{:S(2)}, u32[]{:S(2)}) %collective-permute-start.23) | collective-permute-done | bytes 544 | tf_op jit(solution)/shard_map/ppermute | solution.py:415
  119.2 1.3 %shard_map.104 = f32[62,128]{1,0:T(8,128)} custom-call(s32[4]{0:T(128)S(1)} %pad_add_fusion.place_ref, f32[1,128]{1,0:T(1,128)S(1)} %add.39.total_ref, f32[128,128]{1,0:T(8,128)S(1)} %get-tuple-element.122.both_ref), custom_call_target="tpu_custom_call" | custom-call | flops 1000000 | bytes 4000000 | tf_op jit(solution)/shard_map/pallas_call | solution.py:72
  (52 shorter events, 5.4 us)
Async XLA Ops:
  2.4 4.4 %collective-permute-start = (bf16[288,128]{1,0:T(8,128)(2,1)S(1)}, bf16[288,128]{1,0:T(8,128)(2,1)S(1)}, u32[]{:S(2)}, u32[]{:S(2)}) collective-permute-start(bf16[288,128]{1,0:T(8,128)(2,1)S(1)} %get-tuple-element.62), channel_id=1, source_target_pairs={{0,64},{64,0},{128,192},{192,128},{1,65},{65,1},{129,193},{193,129... | collective-permute-start | bytes 221192 | tf_op jit(solution)/shard_map/ppermute | solution.py:264
  4.1 2.8 %collective-permute-start.1 = (bf16[288,128]{1,0:T(8,128)(2,1)S(1)}, bf16[288,128]{1,0:T(8,128)(2,1)S(1)}, u32[]{:S(2)}, u32[]{:S(2)}) collective-permute-start(bf16[288,128]{1,0:T(8,128)(2,1)S(1)} %get-tuple-element.63), channel_id=1, source_target_pairs={{64,128},{128,64},{65,129},{129,65},{66,130},{130,66},{67,131},{13... | collective-permute-start | bytes 221192 | tf_op jit(solution)/shard_map/ppermute | solution.py:264
  7.6 1.3 %collective-permute-start.2 = (bf16[224,128]{1,0:T(8,128)(2,1)S(1)}, bf16[224,128]{1,0:T(8,128)(2,1)S(1)}, u32[]{:S(2)}, u32[]{:S(2)}) collective-permute-start(bf16[224,128]{1,0:T(8,128)(2,1)S(1)} %get-tuple-element.67), channel_id=1, source_target_pairs={{0,8},{8,0},{16,24},{24,16},{32,40},{40,32},{48,56},{56,48},{1,9},... | collective-permute-start | bytes 172040 | tf_op jit(solution)/shard_map/ppermute | solution.py:264
  7.7 1.2 %collective-permute-start.3 = (bf16[224,128]{1,0:T(8,128)(2,1)S(1)}, bf16[224,128]{1,0:T(8,128)(2,1)S(1)}, u32[]{:S(2)}, u32[]{:S(2)}) collective-permute-start(bf16[224,128]{1,0:T(8,128)(2,1)S(1)} %get-tuple-element.68), channel_id=1, source_target_pairs={{8,16},{16,8},{24,32},{32,24},{40,48},{48,40},{9,17},{17,9},{25,33... | collective-permute-start | bytes 172040 | tf_op jit(solution)/shard_map/ppermute | solution.py:264
  9.9 8.5 %collective-permute-start.4 = (bf16[304,128]{1,0:T(8,128)(2,1)S(1)}, bf16[304,128]{1,0:T(8,128)(2,1)S(1)}, u32[]{:S(2)}, u32[]{:S(2)}) collective-permute-start(bf16[304,128]{1,0:T(8,128)(2,1)S(1)} %get-tuple-element.71), channel_id=1, source_target_pairs={{0,1},{1,0},{2,3},{3,2},{4,5},{5,4},{6,7},{7,6},{8,9},{9,8},{10,11... | collective-permute-start | bytes 233480 | tf_op jit(solution)/shard_map/ppermute | solution.py:264
  11.8 6.6 %collective-permute-start.5 = (bf16[304,128]{1,0:T(8,128)(2,1)S(1)}, bf16[304,128]{1,0:T(8,128)(2,1)S(1)}, u32[]{:S(2)}, u32[]{:S(2)}) collective-permute-start(bf16[304,128]{1,0:T(8,128)(2,1)S(1)} %get-tuple-element.72), channel_id=1, source_target_pairs={{1,2},{2,1},{3,4},{4,3},{5,6},{6,5},{9,10},{10,9},{11,12},{12,11},... | collective-permute-start | bytes 233480 | tf_op jit(solution)/shard_map/ppermute | solution.py:264
  15.7 2.7 %copy-start = (bf16[2048,128]{1,0:T(8,128)(2,1)S(1)}, bf16[2048,128]{1,0:T(8,128)(2,1)}, u32[]{:S(2)}) copy-start(bf16[2048,128]{1,0:T(8,128)(2,1)} %w_up_hbm.1) | copy-start | bytes 1572868
  18.5 1.5 %copy-start.3 = (bf16[3456,256]{1,0:T(8,128)(2,1)S(1)}, bf16[3456,256]{1,0:T(8,128)(2,1)}, u32[]{:S(2)}) copy-start(bf16[3456,256]{1,0:T(8,128)(2,1)} %w_in_hbm.1) | copy-start | bytes 5308420
  26.6 8.4 %collective-permute-start.6 = (bf16[8192,128]{1,0:T(8,128)(2,1)S(1)}, bf16[8192,128]{1,0:T(8,128)(2,1)S(1)}, u32[]{:S(2)}, u32[]{:S(2)}) collective-permute-start(bf16[8192,128]{1,0:T(8,128)(2,1)S(1)} %get-tuple-element.74), channel_id=1, source_target_pairs={{0,8},{8,0},{1,9},{9,1},{2,10},{10,2},{3,11},{11,3},{4,12},{12,4},... | collective-permute-start | bytes 6291464 | tf_op jit(solution)/shard_map/ppermute | solution.py:415
  36.1 33.3 %copy-start.2 = (bf16[96,192]{1,0:T(8,128)(2,1)S(1)}, bf16[96,192]{1,0:T(8,128)(2,1)}, u32[]{:S(2)}) copy-start(bf16[96,192]{1,0:T(8,128)(2,1)} %constant.26.clone.z_faces_ref) | copy-start | bytes 110596
  36.1 19.6 %collective-permute-start.8 = (bf16[2240,128]{1,0:T(8,128)(2,1)S(1)}, bf16[2240,128]{1,0:T(8,128)(2,1)S(1)}, u32[]{:S(2)}, u32[]{:S(2)}) collective-permute-start(bf16[2240,128]{1,0:T(8,128)(2,1)S(1)} %get-tuple-element.79), channel_id=1, source_target_pairs={{0,64},{8,24},{16,80},{24,40},{32,96},{40,56},{48,112},{56,8},{64,... | collective-permute-start | bytes 1720328 | tf_op jit(solution)/shard_map/ppermute | solution.py:410
  40.5 15.2 %collective-permute-start.9 = (bf16[2240,128]{1,0:T(8,128)(2,1)S(1)}, bf16[2240,128]{1,0:T(8,128)(2,1)S(1)}, u32[]{:S(2)}, u32[]{:S(2)}) collective-permute-start(bf16[2240,128]{1,0:T(8,128)(2,1)S(1)} %get-tuple-element.80), channel_id=1, source_target_pairs={{0,192},{8,56},{16,208},{24,8},{32,224},{40,24},{48,240},{56,40},{... | collective-permute-start | bytes 1720328 | tf_op jit(solution)/shard_map/ppermute | solution.py:410
  40.5 15.2 %collective-permute-start.7 = (bf16[1984,128]{1,0:T(8,128)(2,1)S(1)}, bf16[1984,128]{1,0:T(8,128)(2,1)S(1)}, u32[]{:S(2)}, u32[]{:S(2)}) collective-permute-start(bf16[1984,128]{1,0:T(8,128)(2,1)S(1)} %get-tuple-element.78), channel_id=1, source_target_pairs={{0,128},{8,40},{16,144},{24,56},{32,160},{40,8},{48,176},{56,24},{... | collective-permute-start | bytes 1523720 | tf_op jit(solution)/shard_map/ppermute | solution.py:410
  55.7 23.0 %copy-start.1 = (bf16[288,288]{1,0:T(8,128)(2,1)S(1)}, bf16[288,288]{1,0:T(8,128)(2,1)}, u32[]{:S(2)}) copy-start(bf16[288,288]{1,0:T(8,128)(2,1)} %constant.27.clone.padded_ref) | copy-start | bytes 497668
  57.0 12.5 %collective-permute-start.11 = (f32[688,128]{1,0:T(8,128)S(1)}, f32[688,128]{1,0:T(8,128)S(1)}, u32[]{:S(2)}, u32[]{:S(2)}) collective-permute-start(f32[688,128]{1,0:T(8,128)S(1)} %get-tuple-element.84), channel_id=1, source_target_pairs={{0,16},{8,72},{16,32},{24,88},{32,48},{40,104},{48,0},{56,120},{64... | collective-permute-start | bytes 1056776 | tf_op jit(solution)/shard_map/ppermute | solution.py:410
  58.7 10.8 %collective-permute-start.12 = (f32[688,128]{1,0:T(8,128)S(1)}, f32[688,128]{1,0:T(8,128)S(1)}, u32[]{:S(2)}, u32[]{:S(2)}) collective-permute-start(f32[688,128]{1,0:T(8,128)S(1)} %get-tuple-element.85), channel_id=1, source_target_pairs={{0,48},{8,200},{16,0},{24,216},{32,16},{40,232},{48,32},{56,248},{... | collective-permute-start | bytes 1056776 | tf_op jit(solution)/shard_map/ppermute | solution.py:410
  60.3 9.2 %collective-permute-start.10 = (f32[496,128]{1,0:T(8,128)S(1)}, f32[496,128]{1,0:T(8,128)S(1)}, u32[]{:S(2)}, u32[]{:S(2)}) collective-permute-start(f32[496,128]{1,0:T(8,128)S(1)} %get-tuple-element.83), channel_id=1, source_target_pairs={{0,32},{8,136},{16,48},{24,152},{32,0},{40,168},{48,16},{56,184},{... | collective-permute-start | bytes 761864 | tf_op jit(solution)/shard_map/ppermute | solution.py:410
  70.6 6.1 %collective-permute-start.13 = (f32[448,128]{1,0:T(8,128)S(1)}, f32[448,128]{1,0:T(8,128)S(1)}, u32[]{:S(2)}, u32[]{:S(2)}) collective-permute-start(f32[448,128]{1,0:T(8,128)S(1)} %get-tuple-element.87), channel_id=1, source_target_pairs={{0,1},{1,0},{2,3},{3,2},{4,5},{5,4},{6,7},{7,6},{8,9},{9,8},{10,11... | collective-permute-start | bytes 688136 | tf_op jit(solution)/shard_map/ppermute | solution.py:415
  70.7 8.1 %collective-permute-start.15 = (bf16[192,128]{1,0:T(8,128)(2,1)S(1)}, bf16[192,128]{1,0:T(8,128)(2,1)S(1)}, u32[]{:S(2)}, u32[]{:S(2)}) collective-permute-start(bf16[192,128]{1,0:T(8,128)(2,1)S(1)} %get-tuple-element.95), channel_id=1, source_target_pairs={{1,2},{2,1},{3,4},{4,3},{5,6},{6,5},{9,10},{10,9},{11,12},{12,11},... | collective-permute-start | bytes 147464 | tf_op jit(solution)/shard_map/ppermute | solution.py:525
  79.7 5.8 %collective-permute-start.14 = (f32[128,128]{1,0:T(8,128)S(1)}, f32[128,128]{1,0:T(8,128)S(1)}, u32[]{:S(2)}, u32[]{:S(2)}) collective-permute-start(f32[128,128]{1,0:T(8,128)S(1)} %get-tuple-element.92), channel_id=1, source_target_pairs={{0,2},{1,3},{2,0},{3,1},{4,6},{5,7},{6,4},{7,5},{8,10},{9,11},{10,... | collective-permute-start | bytes 196616 | tf_op jit(solution)/shard_map/ppermute | solution.py:415
  84.5 4.9 %copy-start.5 = (bf16[6912,128]{1,0:T(8,128)(2,1)S(1)}, bf16[6912,128]{1,0:T(8,128)(2,1)}, u32[]{:S(2)}) copy-start(bf16[6912,128]{1,0:T(8,128)(2,1)} %param.10) | copy-start | bytes 5308420
  85.5 7.4 %collective-permute-start.16 = (f32[128,128]{1,0:T(8,128)S(1)}, f32[128,128]{1,0:T(8,128)S(1)}, u32[]{:S(2)}, u32[]{:S(2)}) collective-permute-start(f32[128,128]{1,0:T(8,128)S(1)} %add.30), channel_id=1, source_target_pairs={{0,7},{1,6},{2,5},{3,4},{4,3},{5,2},{6,1},{7,0},{8,15},{9,14},{10,... | collective-permute-start | bytes 196616 | tf_op jit(solution)/shard_map/ppermute | solution.py:415
  92.9 1.2 collective-permute-start.17
  94.1 3.7 %collective-permute-start.18 = (f32[1,128]{1,0:T(1,128)S(1)}, f32[1,128]{1,0:T(1,128)S(1)}, u32[]{:S(2)}, u32[]{:S(2)}) collective-permute-start(f32[1,128]{1,0:T(1,128)S(1)} %add.32), channel_id=1, source_target_pairs={{0,64},{64,0},{128,192},{192,128},{1,65},{65,1},{129,193},{193,129... | collective-permute-start | bytes 1544 | tf_op jit(solution)/shard_map/ppermute | solution.py:415
  97.9 6.5 %copy-start.4 = (bf16[3456,256]{1,0:T(8,128)(2,1)S(1)}, bf16[3456,256]{1,0:T(8,128)(2,1)}, u32[]{:S(2)}) copy-start(bf16[3456,256]{1,0:T(8,128)(2,1)} %w_in_hbm.1) | copy-start | bytes 5308420
  97.9 5.1 %collective-permute-start.19 = (f32[1,128]{1,0:T(1,128)S(1)}, f32[1,128]{1,0:T(1,128)S(1)}, u32[]{:S(2)}, u32[]{:S(2)}) collective-permute-start(f32[1,128]{1,0:T(1,128)S(1)} %add.33), channel_id=1, source_target_pairs={{0,192},{64,128},{128,64},{192,0},{1,193},{65,129},{129,65},{193,1... | collective-permute-start | bytes 1544 | tf_op jit(solution)/shard_map/ppermute | solution.py:415
  102.9 3.5 %collective-permute-start.20 = (f32[1,128]{1,0:T(1,128)S(1)}, f32[1,128]{1,0:T(1,128)S(1)}, u32[]{:S(2)}, u32[]{:S(2)}) collective-permute-start(f32[1,128]{1,0:T(1,128)S(1)} %add.34), channel_id=1, source_target_pairs={{0,16},{16,0},{32,48},{48,32},{1,17},{17,1},{33,49},{49,33},{2,18}... | collective-permute-start | bytes 1544 | tf_op jit(solution)/shard_map/ppermute | solution.py:415
  106.5 4.8 %collective-permute-start.21 = (f32[1,128]{1,0:T(1,128)S(1)}, f32[1,128]{1,0:T(1,128)S(1)}, u32[]{:S(2)}, u32[]{:S(2)}) collective-permute-start(f32[1,128]{1,0:T(1,128)S(1)} %add.35), channel_id=1, source_target_pairs={{0,48},{16,32},{32,16},{48,0},{1,49},{17,33},{33,17},{49,1},{2,50}... | collective-permute-start | bytes 1544 | tf_op jit(solution)/shard_map/ppermute | solution.py:415
  111.2 3.5 %collective-permute-start.22 = (f32[1,128]{1,0:T(1,128)S(1)}, f32[1,128]{1,0:T(1,128)S(1)}, u32[]{:S(2)}, u32[]{:S(2)}) collective-permute-start(f32[1,128]{1,0:T(1,128)S(1)} %add.37), channel_id=1, source_target_pairs={{0,1},{1,0},{2,3},{3,2},{4,5},{5,4},{6,7},{7,6},{8,9},{9,8},{10,11... | collective-permute-start | bytes 1544 | tf_op jit(solution)/shard_map/ppermute | solution.py:415
  114.8 4.4 %collective-permute-start.23 = (f32[1,128]{1,0:T(1,128)S(1)}, f32[1,128]{1,0:T(1,128)S(1)}, u32[]{:S(2)}, u32[]{:S(2)}) collective-permute-start(f32[1,128]{1,0:T(1,128)S(1)} %add.38), channel_id=1, source_target_pairs={{0,2},{1,3},{2,0},{3,1},{4,6},{5,7},{6,4},{7,5},{8,10},{9,11},{10,... | collective-permute-start | bytes 1544 | tf_op jit(solution)/shard_map/ppermute | solution.py:415

commit v7 on v6

--- a/solution.py
+++ b/solution.py
@@ -537,9 +537,10 @@
 
     send, grown, act = lax.optimization_barrier((send, grown, act))
     mine = keep + paired(send, "gz", 2)
+    (active_pad,) = _call(_grow_z_kernel, (((120, 10, 128), BF16),), place, act, *faces, scratch=((120, 24, 128),))
+    active_pad, grown = lax.optimization_barrier((active_pad, grown))
     pads = _call(_pad_kernel, (((288, 256), BF16),) * 2, place, grown, jnp.asarray(PADDED, BF16), got, other)
     bottom_pad, slope_pad = (p.reshape(2, 4, 6, 6, 256) for p in pads)
-    (active_pad,) = _call(_grow_z_kernel, (((120, 10, 128), BF16),), place, act, *faces, scratch=((120, 24, 128),))
     upward_pad = up_conv(bottom_pad, w_up).astype(BF16)[:, 1:-1, 1:-1, 1:-1]
     joined_pad = jnp.concatenate([active_pad.reshape(2, 6, 10, 10, 128), upward_pad], axis=4)
     mine, joined_pad, slope_pad = lax.optimization_barrier((mine, joined_pad, slope_pad))

time: 121 us -> 120 us (level)
    ppermute x11, waiting for transfers between devices: 14.9 us -> 16.5 us  [paired(): return lax.ppermute(array, axis, [(i, i ^ bit) for i in range(count)])]
    ppermute x1, waiting for transfers between devices: 1.47 us -> 0.01 us  [scattered_sum(): lax.ppermute(other, 'gz', [(i, j) for i in range(8) for j in [(i + 1 ^ 1)...]
  transfers between devices with their start and end apart: 24 -> 24, of which waited for: 13 -> 12; matrix products, arithmetic and copies ran while one was open for 11% -> 12% of each run, Pallas kernels for 1% -> 2%
where the time goes in v7:
time: 120 us
  starting transfers between devices  49 us (41%)
  waiting for transfers between devices  37.5 us (31%)
  Pallas kernels  16 us (13%)
  matrix products  7.42 us (6%)
  local copies, waits for them, and re-layouts  6.27 us (5%)
  other arithmetic  2.76 us (2%)
    ppermute x11, starting transfers between devices, paired(): return lax.ppermute(array, axis, [(i, i ^ bit) for i in range(count)])  20.3 us
    ppermute x6, waiting for transfers between devices, crossed(): return lax.ppermute(array, ('gx', 'x', 'core'), pairs)  18.3 us
    ppermute x11, waiting for transfers between devices, paired(): return lax.ppermute(array, axis, [(i, i ^ bit) for i in range(count)])  16.5 us
    ppermute x6, starting transfers between devices, crossed(): return lax.ppermute(array, ('gx', 'x', 'core'), pairs)  13.7 us
    pallas_call x10, Pallas kernels, _call(): pl.pallas_call(kernel, out_shape=tuple((jax.ShapeDtypeStruct(shape, kind)...  9.36 us
    pallas_call x1, Pallas kernels, gradients(): pl.pallas_call(_gradients_kernel, out_shape=(shape((2, 7936, 128), F32),...  6.64 us
    conv_general_dilated x3, matrix products, conv_forward(): lax.conv_general_dilated(padded, kernel, (1, 1, 1), 'VALID', dimension_nu...  6.24 us
    ppermute x1, starting transfers between devices, scattered_sum(): lax.ppermute(other, 'gz', [(i, j) for i in range(8) for j in [(i + 1 ^ 1)...  6.03 us
  transfers between devices with their start and end apart: 24, of which 12 were waited for; matrix products, arithmetic and copies ran while one was open for 12% of the time, Pallas kernels for 2%

profile of v7, /device:TPU:32, one launch (start us, length us, event | category | flops | bytes accessed | tf_op | source)
XLA Modules:
  0.0 119.9 jit_solution(10900220266322069645)
XLA Ops:
  0.6 1.0 pad_maximum_fusion.1.both_ref
  1.7 0.7 shard_map.94
  2.4 1.7 %collective-permute-start = (bf16[288,128]{1,0:T(8,128)(2,1)S(1)}, bf16[288,128]{1,0:T(8,128)(2,1)S(1)}, u32[]{:S(2)}, u32[]{:S(2)}) collective-permute-start(bf16[288,128]{1,0:T(8,128)(2,1)S(1)} %get-tuple-element.64), channel_id=1, source_target_pairs={{0,64},{64,0},{128,192},{192,128},{1,65},{65,1},{129,193},{193,129... | collective-permute-start | bytes 221192 | tf_op jit(solution)/shard_map/ppermute | solution.py:264
  4.1 0.7 collective-permute-start.1
  4.8 2.1 %collective-permute-done.got_here = bf16[288,128]{1,0:T(8,128)(2,1)S(1)} collective-permute-done((bf16[288,128]{1,0:T(8,128)(2,1)S(1)}, bf16[288,128]{1,0:T(8,128)(2,1)S(1)}, u32[]{:S(2)}, u32[]{:S(2)}) %collective-permute-start) | collective-permute-done | bytes 73760 | tf_op jit(solution)/shard_map/ppermute | solution.py:264
  6.9 0.7 shard_map.95
  7.7 0.7 collective-permute-start.3
  8.9 1.0 shard_map.96
  9.9 1.9 %collective-permute-start.4 = (bf16[304,128]{1,0:T(8,128)(2,1)S(1)}, bf16[304,128]{1,0:T(8,128)(2,1)S(1)}, u32[]{:S(2)}, u32[]{:S(2)}) collective-permute-start(bf16[304,128]{1,0:T(8,128)(2,1)S(1)} %get-tuple-element.73), channel_id=1, source_target_pairs={{0,1},{1,0},{2,3},{3,2},{4,5},{5,4},{6,7},{7,6},{8,9},{9,8},{10,11... | collective-permute-start | bytes 233480 | tf_op jit(solution)/shard_map/ppermute | solution.py:264
  11.8 3.9 %collective-permute-start.5 = (bf16[304,128]{1,0:T(8,128)(2,1)S(1)}, bf16[304,128]{1,0:T(8,128)(2,1)S(1)}, u32[]{:S(2)}, u32[]{:S(2)}) collective-permute-start(bf16[304,128]{1,0:T(8,128)(2,1)S(1)} %get-tuple-element.74), channel_id=1, source_target_pairs={{1,2},{2,1},{3,4},{4,3},{5,6},{6,5},{9,10},{10,9},{11,12},{12,11},... | collective-permute-start | bytes 233480 | tf_op jit(solution)/shard_map/ppermute | solution.py:264
  15.7 2.7 %copy.15 = bf16[27,256,128]{1,2,0:T(8,128)(2,1)S(1)} copy(bf16[27,256,128]{2,1,0:T(8,128)(2,1)} %bitcast.38) | data formatting | bytes 3538944 | tf_op jit(solution)/shard_map/reshape | solution.py:534
  18.5 1.5 %copy-done.3 = bf16[3456,256]{1,0:T(8,128)(2,1)S(1)} copy-done((bf16[3456,256]{1,0:T(8,128)(2,1)S(1)}, bf16[3456,256]{1,0:T(8,128)(2,1)}, u32[]{:S(2)}) %copy-start.3) | copy-done | bytes 1769496
  19.9 6.6 %shard_map.97 = (f32[2,7936,128]{2,1,0:T(8,128)S(1)}, bf16[8192,128]{1,0:T(8,128)(2,1)S(1)}, bf16[64,512]{1,0:T(8,128)(2,1)S(1)}, f32[512,128]{1,0:T(8,128)S(1)}) custom-call(s32[4]{0:T(128)S(1)} %pad_add_fusion.place_ref, bf16[512,128]{1,0:T(8,128)(2,1)S(1)} %get-tuple-element.61.act_ref, bf16[960,128]{1,0:T(8,128)(2,1)S(1)} %get-tuple-element.71.cot_ref, ...), custom_call_target="tpu_custom_call" | custom-call | flops 2500000000 | bytes 16000000 | tf_op jit(solution)/shard_map/pallas_call | solution.py:384
  26.6 4.6 %collective-permute-start.6 = (bf16[8192,128]{1,0:T(8,128)(2,1)S(1)}, bf16[8192,128]{1,0:T(8,128)(2,1)S(1)}, u32[]{:S(2)}, u32[]{:S(2)}) collective-permute-start(bf16[8192,128]{1,0:T(8,128)(2,1)S(1)} %get-tuple-element.76), channel_id=1, source_target_pairs={{0,8},{8,0},{1,9},{9,1},{2,10},{10,2},{3,11},{11,3},{4,12},{12,4},... | collective-permute-start | bytes 6291464 | tf_op jit(solution)/shard_map/ppermute | solution.py:415
  31.1 3.8 %collective-permute-done.6.got_ref = bf16[8192,128]{1,0:T(8,128)(2,1)S(1)} collective-permute-done((bf16[8192,128]{1,0:T(8,128)(2,1)S(1)}, bf16[8192,128]{1,0:T(8,128)(2,1)S(1)}, u32[]{:S(2)}, u32[]{:S(2)}) %collective-permute-start.6) | collective-permute-done | bytes 2097184 | tf_op jit(solution)/shard_map/ppermute | solution.py:415
  34.9 1.2 shard_map.98
  36.1 4.4 %collective-permute-start.8 = (bf16[2240,128]{1,0:T(8,128)(2,1)S(1)}, bf16[2240,128]{1,0:T(8,128)(2,1)S(1)}, u32[]{:S(2)}, u32[]{:S(2)}) collective-permute-start(bf16[2240,128]{1,0:T(8,128)(2,1)S(1)} %get-tuple-element.81), channel_id=1, source_target_pairs={{0,64},{8,24},{16,80},{24,40},{32,96},{40,56},{48,112},{56,8},{64,... | collective-permute-start | bytes 1720328 | tf_op jit(solution)/shard_map/ppermute | solution.py:410
  40.5 4.1 %collective-permute-start.7 = (bf16[1984,128]{1,0:T(8,128)(2,1)S(1)}, bf16[1984,128]{1,0:T(8,128)(2,1)S(1)}, u32[]{:S(2)}, u32[]{:S(2)}) collective-permute-start(bf16[1984,128]{1,0:T(8,128)(2,1)S(1)} %get-tuple-element.80), channel_id=1, source_target_pairs={{0,128},{8,40},{16,144},{24,56},{32,160},{40,8},{48,176},{56,24},{... | collective-permute-start | bytes 1523720 | tf_op jit(solution)/shard_map/ppermute | solution.py:410
  44.6 11.1 %collective-permute-done.7.got_2 = bf16[1984,128]{1,0:T(8,128)(2,1)S(1)} collective-permute-done((bf16[1984,128]{1,0:T(8,128)(2,1)S(1)}, bf16[1984,128]{1,0:T(8,128)(2,1)S(1)}, u32[]{:S(2)}, u32[]{:S(2)}) %collective-permute-start.7) | collective-permute-done | bytes 507936 | tf_op jit(solution)/shard_map/ppermute | solution.py:410
  55.7 1.2 %shard_map.99 = (bf16[256,512]{1,0:T(8,128)(2,1)S(1)}, f32[496,128]{1,0:T(8,128)S(1)}, f32[688,128]{1,0:T(8,128)S(1)}, f32[496,128]{1,0:T(8,128)S(1)}, f32[688,128]{1,0:T(8,128)S(1)}) custom-call(s32[4]{0:T(128)S(1)} %pad_add_fusion.place_ref, bf16[128,512]{1,0:T(8,128)(2,1)S(1)} %get-tuple-element.78.chip_ref, f32[1984,128]{1,0:T(8,128)S(1)} %get-tuple-element.79.own_ref, ...), custom_call_target="tpu_custom_call" | custom-call | flops 1000000 | bytes 4000000 | tf_op jit(solution)/shard_map/pallas_call | solution.py:72
  57.0 1.7 %collective-permute-start.11 = (f32[688,128]{1,0:T(8,128)S(1)}, f32[688,128]{1,0:T(8,128)S(1)}, u32[]{:S(2)}, u32[]{:S(2)}) collective-permute-start(f32[688,128]{1,0:T(8,128)S(1)} %get-tuple-element.86), channel_id=1, source_target_pairs={{0,16},{8,72},{16,32},{24,88},{32,48},{40,104},{48,0},{56,120},{64... | collective-permute-start | bytes 1056776 | tf_op jit(solution)/shard_map/ppermute | solution.py:410
  58.7 1.6 %collective-permute-start.12 = (f32[688,128]{1,0:T(8,128)S(1)}, f32[688,128]{1,0:T(8,128)S(1)}, u32[]{:S(2)}, u32[]{:S(2)}) collective-permute-start(f32[688,128]{1,0:T(8,128)S(1)} %get-tuple-element.87), channel_id=1, source_target_pairs={{0,48},{8,200},{16,0},{24,216},{32,16},{40,232},{48,32},{56,248},{... | collective-permute-start | bytes 1056776 | tf_op jit(solution)/shard_map/ppermute | solution.py:410
  60.3 2.0 %collective-permute-start.10 = (f32[496,128]{1,0:T(8,128)S(1)}, f32[496,128]{1,0:T(8,128)S(1)}, u32[]{:S(2)}, u32[]{:S(2)}) collective-permute-start(f32[496,128]{1,0:T(8,128)S(1)} %get-tuple-element.85), channel_id=1, source_target_pairs={{0,32},{8,136},{16,48},{24,152},{32,0},{40,168},{48,16},{56,184},{... | collective-permute-start | bytes 761864 | tf_op jit(solution)/shard_map/ppermute | solution.py:410
  62.2 7.2 %collective-permute-done.10.got_2 = f32[496,128]{1,0:T(8,128)S(1)} collective-permute-done((f32[496,128]{1,0:T(8,128)S(1)}, f32[496,128]{1,0:T(8,128)S(1)}, u32[]{:S(2)}, u32[]{:S(2)}) %collective-permute-start.10) | collective-permute-done | bytes 253984 | tf_op jit(solution)/shard_map/ppermute | solution.py:410
  69.5 1.1 shard_map.100
  70.7 6.0 %collective-permute-start.15 = (bf16[192,128]{1,0:T(8,128)(2,1)S(1)}, bf16[192,128]{1,0:T(8,128)(2,1)S(1)}, u32[]{:S(2)}, u32[]{:S(2)}) collective-permute-start(bf16[192,128]{1,0:T(8,128)(2,1)S(1)} %get-tuple-element.99), channel_id=1, source_target_pairs={{1,2},{2,1},{3,4},{4,3},{5,6},{6,5},{9,10},{10,9},{11,12},{12,11},... | collective-permute-start | bytes 147464 | tf_op jit(solution)/shard_map/ppermute | solution.py:525
  77.3 3.6 %collective-permute-start.14 = (f32[128,128]{1,0:T(8,128)S(1)}, f32[128,128]{1,0:T(8,128)S(1)}, u32[]{:S(2)}, u32[]{:S(2)}) collective-permute-start(f32[128,128]{1,0:T(8,128)S(1)} %get-tuple-element.94), channel_id=1, source_target_pairs={{0,2},{1,3},{2,0},{3,1},{4,6},{5,7},{6,4},{7,5},{8,10},{9,11},{10,... | collective-permute-start | bytes 196616 | tf_op jit(solution)/shard_map/ppermute | solution.py:415
  80.9 0.7 shard_map.102
  82.0 0.9 shard_map.103
  84.3 0.7 pad_maximum_fusion
  85.0 3.9 %collective-permute-start.16 = (f32[128,128]{1,0:T(8,128)S(1)}, f32[128,128]{1,0:T(8,128)S(1)}, u32[]{:S(2)}, u32[]{:S(2)}) collective-permute-start(f32[128,128]{1,0:T(8,128)S(1)} %add.30), channel_id=1, source_target_pairs={{0,7},{1,6},{2,5},{3,4},{4,3},{5,2},{6,1},{7,0},{8,15},{9,14},{10,... | collective-permute-start | bytes 196616 | tf_op jit(solution)/shard_map/ppermute | solution.py:415
  88.8 2.8 %convolution_convert_fusion.1 = bf16[1,4,8,8,128]{4,0,3,2,1:T(2,128)(2,1)S(1)} fusion(bf16[3,3,3,256,128]{4,3,2,1,0:T(8,128)(2,1)S(1)} %bitcast.39, bf16[2,6,10,10,256]{4,0,3,2,1:T(2,128)(2,1)S(1)} %pad_maximum_fusion), kind=kOutput, calls=%fused_computation.2 | convolution fusion | flops 453017600 | bytes 2449408 | tf_op jit(solution)/shard_map/conv_general_dilated | solution.py:18
  91.6 0.7 collective-permute-done.16
  92.4 1.1 collective-permute-done.17
  93.6 2.0 %collective-permute-start.18 = (f32[1,128]{1,0:T(1,128)S(1)}, f32[1,128]{1,0:T(1,128)S(1)}, u32[]{:S(2)}, u32[]{:S(2)}) collective-permute-start(f32[1,128]{1,0:T(1,128)S(1)} %add.32), channel_id=1, source_target_pairs={{0,64},{64,0},{128,192},{192,128},{1,65},{65,1},{129,193},{193,129... | collective-permute-start | bytes 1544 | tf_op jit(solution)/shard_map/ppermute | solution.py:415
  95.5 1.7 %convolution_convert_fusion.3 = bf16[1,2,8,8,128]{4,0,3,2,1:T(2,128)(2,1)S(1)} fusion(bf16[3,3,3,256,128]{4,3,2,1,0:T(8,128)(2,1)S(1)} %bitcast.40, bf16[2,6,10,10,256]{4,0,3,2,1:T(2,128)(2,1)S(1)} %pad_maximum_fusion), kind=kOutput, calls=%fused_computation.4 | convolution fusion | flops 226508800 | bytes 2211840 | tf_op jit(solution)/shard_map/conv_general_dilated | solution.py:18
  97.3 2.5 %collective-permute-start.19 = (f32[1,128]{1,0:T(1,128)S(1)}, f32[1,128]{1,0:T(1,128)S(1)}, u32[]{:S(2)}, u32[]{:S(2)}) collective-permute-start(f32[1,128]{1,0:T(1,128)S(1)} %add.33), channel_id=1, source_target_pairs={{0,192},{64,128},{128,64},{192,0},{1,193},{65,129},{129,65},{193,1... | collective-permute-start | bytes 1544 | tf_op jit(solution)/shard_map/ppermute | solution.py:415
  99.7 1.7 %convolution_convert_fusion.2 = bf16[1,2,8,8,128]{4,0,3,2,1:T(2,128)(2,1)S(1)} fusion(bf16[3,3,3,256,128]{4,3,2,1,0:T(8,128)(2,1)S(1)} %bitcast.41, bf16[2,6,10,10,256]{4,0,3,2,1:T(2,128)(2,1)S(1)} %pad_maximum_fusion), kind=kOutput, calls=%fused_computation.3 | convolution fusion | flops 226508800 | bytes 2211840 | tf_op jit(solution)/shard_map/conv_general_dilated | solution.py:18
  101.5 0.9 collective-permute-done.19
  102.4 1.4 %collective-permute-start.20 = (f32[1,128]{1,0:T(1,128)S(1)}, f32[1,128]{1,0:T(1,128)S(1)}, u32[]{:S(2)}, u32[]{:S(2)}) collective-permute-start(f32[1,128]{1,0:T(1,128)S(1)} %add.34), channel_id=1, source_target_pairs={{0,16},{16,0},{32,48},{48,32},{1,17},{17,1},{33,49},{49,33},{2,18}... | collective-permute-start | bytes 1544 | tf_op jit(solution)/shard_map/ppermute | solution.py:415
  103.8 0.8 convolution_multiply_fusion
  104.7 0.7 add_convert_fusion
  105.9 2.1 %collective-permute-start.21 = (f32[1,128]{1,0:T(1,128)S(1)}, f32[1,128]{1,0:T(1,128)S(1)}, u32[]{:S(2)}, u32[]{:S(2)}) collective-permute-start(f32[1,128]{1,0:T(1,128)S(1)} %add.35), channel_id=1, source_target_pairs={{0,48},{16,32},{32,16},{48,0},{1,49},{17,33},{33,17},{49,1},{2,50}... | collective-permute-start | bytes 1544 | tf_op jit(solution)/shard_map/ppermute | solution.py:415
  108.0 2.7 %collective-permute-done.21 = f32[1,128]{1,0:T(1,128)S(1)} collective-permute-done((f32[1,128]{1,0:T(1,128)S(1)}, f32[1,128]{1,0:T(1,128)S(1)}, u32[]{:S(2)}, u32[]{:S(2)}) %collective-permute-start.21) | collective-permute-done | bytes 544 | tf_op jit(solution)/shard_map/ppermute | solution.py:415
  110.7 3.5 %collective-permute-done.22 = f32[1,128]{1,0:T(1,128)S(1)} collective-permute-done((f32[1,128]{1,0:T(1,128)S(1)}, f32[1,128]{1,0:T(1,128)S(1)}, u32[]{:S(2)}, u32[]{:S(2)}) %collective-permute-start.22) | collective-permute-done | bytes 544 | tf_op jit(solution)/shard_map/ppermute | solution.py:415
  114.7 0.7 copy.21
  115.3 3.3 %collective-permute-done.23 = f32[1,128]{1,0:T(1,128)S(1)} collective-permute-done((f32[1,128]{1,0:T(1,128)S(1)}, f32[1,128]{1,0:T(1,128)S(1)}, u32[]{:S(2)}, u32[]{:S(2)}) %collective-permute-start.23) | collective-permute-done | bytes 544 | tf_op jit(solution)/shard_map/ppermute | solution.py:415
  118.6 1.3 %shard_map.104 = f32[62,128]{1,0:T(8,128)} custom-call(s32[4]{0:T(128)S(1)} %pad_add_fusion.place_ref, f32[1,128]{1,0:T(1,128)S(1)} %add.39.total_ref, f32[128,128]{1,0:T(8,128)S(1)} %get-tuple-element.126.both_ref), custom_call_target="tpu_custom_call" | custom-call | flops 1000000 | bytes 4000000 | tf_op jit(solution)/shard_map/pallas_call | solution.py:72
  (52 shorter events, 4.3 us)
Async XLA Ops:
  2.4 4.4 %collective-permute-start = (bf16[288,128]{1,0:T(8,128)(2,1)S(1)}, bf16[288,128]{1,0:T(8,128)(2,1)S(1)}, u32[]{:S(2)}, u32[]{:S(2)}) collective-permute-start(bf16[288,128]{1,0:T(8,128)(2,1)S(1)} %get-tuple-element.64), channel_id=1, source_target_pairs={{0,64},{64,0},{128,192},{192,128},{1,65},{65,1},{129,193},{193,129... | collective-permute-start | bytes 221192 | tf_op jit(solution)/shard_map/ppermute | solution.py:264
  4.1 2.8 %collective-permute-start.1 = (bf16[288,128]{1,0:T(8,128)(2,1)S(1)}, bf16[288,128]{1,0:T(8,128)(2,1)S(1)}, u32[]{:S(2)}, u32[]{:S(2)}) collective-permute-start(bf16[288,128]{1,0:T(8,128)(2,1)S(1)} %get-tuple-element.65), channel_id=1, source_target_pairs={{64,128},{128,64},{65,129},{129,65},{66,130},{130,66},{67,131},{13... | collective-permute-start | bytes 221192 | tf_op jit(solution)/shard_map/ppermute | solution.py:264
  7.6 1.3 %collective-permute-start.2 = (bf16[224,128]{1,0:T(8,128)(2,1)S(1)}, bf16[224,128]{1,0:T(8,128)(2,1)S(1)}, u32[]{:S(2)}, u32[]{:S(2)}) collective-permute-start(bf16[224,128]{1,0:T(8,128)(2,1)S(1)} %get-tuple-element.69), channel_id=1, source_target_pairs={{0,8},{8,0},{16,24},{24,16},{32,40},{40,32},{48,56},{56,48},{1,9},... | collective-permute-start | bytes 172040 | tf_op jit(solution)/shard_map/ppermute | solution.py:264
  7.7 1.2 %collective-permute-start.3 = (bf16[224,128]{1,0:T(8,128)(2,1)S(1)}, bf16[224,128]{1,0:T(8,128)(2,1)S(1)}, u32[]{:S(2)}, u32[]{:S(2)}) collective-permute-start(bf16[224,128]{1,0:T(8,128)(2,1)S(1)} %get-tuple-element.70), channel_id=1, source_target_pairs={{8,16},{16,8},{24,32},{32,24},{40,48},{48,40},{9,17},{17,9},{25,33... | collective-permute-start | bytes 172040 | tf_op jit(solution)/shard_map/ppermute | solution.py:264
  9.9 8.5 %collective-permute-start.4 = (bf16[304,128]{1,0:T(8,128)(2,1)S(1)}, bf16[304,128]{1,0:T(8,128)(2,1)S(1)}, u32[]{:S(2)}, u32[]{:S(2)}) collective-permute-start(bf16[304,128]{1,0:T(8,128)(2,1)S(1)} %get-tuple-element.73), channel_id=1, source_target_pairs={{0,1},{1,0},{2,3},{3,2},{4,5},{5,4},{6,7},{7,6},{8,9},{9,8},{10,11... | collective-permute-start | bytes 233480 | tf_op jit(solution)/shard_map/ppermute | solution.py:264
  11.8 6.6 %collective-permute-start.5 = (bf16[304,128]{1,0:T(8,128)(2,1)S(1)}, bf16[304,128]{1,0:T(8,128)(2,1)S(1)}, u32[]{:S(2)}, u32[]{:S(2)}) collective-permute-start(bf16[304,128]{1,0:T(8,128)(2,1)S(1)} %get-tuple-element.74), channel_id=1, source_target_pairs={{1,2},{2,1},{3,4},{4,3},{5,6},{6,5},{9,10},{10,9},{11,12},{12,11},... | collective-permute-start | bytes 233480 | tf_op jit(solution)/shard_map/ppermute | solution.py:264
  15.7 2.7 %copy-start = (bf16[2048,128]{1,0:T(8,128)(2,1)S(1)}, bf16[2048,128]{1,0:T(8,128)(2,1)}, u32[]{:S(2)}) copy-start(bf16[2048,128]{1,0:T(8,128)(2,1)} %w_up_hbm.1) | copy-start | bytes 1572868
  18.5 1.5 %copy-start.3 = (bf16[3456,256]{1,0:T(8,128)(2,1)S(1)}, bf16[3456,256]{1,0:T(8,128)(2,1)}, u32[]{:S(2)}) copy-start(bf16[3456,256]{1,0:T(8,128)(2,1)} %w_in_hbm.1) | copy-start | bytes 5308420
  26.6 8.4 %collective-permute-start.6 = (bf16[8192,128]{1,0:T(8,128)(2,1)S(1)}, bf16[8192,128]{1,0:T(8,128)(2,1)S(1)}, u32[]{:S(2)}, u32[]{:S(2)}) collective-permute-start(bf16[8192,128]{1,0:T(8,128)(2,1)S(1)} %get-tuple-element.76), channel_id=1, source_target_pairs={{0,8},{8,0},{1,9},{9,1},{2,10},{10,2},{3,11},{11,3},{4,12},{12,4},... | collective-permute-start | bytes 6291464 | tf_op jit(solution)/shard_map/ppermute | solution.py:415
  36.1 33.3 %copy-start.2 = (bf16[96,192]{1,0:T(8,128)(2,1)S(1)}, bf16[96,192]{1,0:T(8,128)(2,1)}, u32[]{:S(2)}) copy-start(bf16[96,192]{1,0:T(8,128)(2,1)} %constant.26.clone.z_faces_ref) | copy-start | bytes 110596
  36.1 19.6 %collective-permute-start.8 = (bf16[2240,128]{1,0:T(8,128)(2,1)S(1)}, bf16[2240,128]{1,0:T(8,128)(2,1)S(1)}, u32[]{:S(2)}, u32[]{:S(2)}) collective-permute-start(bf16[2240,128]{1,0:T(8,128)(2,1)S(1)} %get-tuple-element.81), channel_id=1, source_target_pairs={{0,64},{8,24},{16,80},{24,40},{32,96},{40,56},{48,112},{56,8},{64,... | collective-permute-start | bytes 1720328 | tf_op jit(solution)/shard_map/ppermute | solution.py:410
  40.5 15.2 %collective-permute-start.9 = (bf16[2240,128]{1,0:T(8,128)(2,1)S(1)}, bf16[2240,128]{1,0:T(8,128)(2,1)S(1)}, u32[]{:S(2)}, u32[]{:S(2)}) collective-permute-start(bf16[2240,128]{1,0:T(8,128)(2,1)S(1)} %get-tuple-element.82), channel_id=1, source_target_pairs={{0,192},{8,56},{16,208},{24,8},{32,224},{40,24},{48,240},{56,40},{... | collective-permute-start | bytes 1720328 | tf_op jit(solution)/shard_map/ppermute | solution.py:410
  40.5 15.2 %collective-permute-start.7 = (bf16[1984,128]{1,0:T(8,128)(2,1)S(1)}, bf16[1984,128]{1,0:T(8,128)(2,1)S(1)}, u32[]{:S(2)}, u32[]{:S(2)}) collective-permute-start(bf16[1984,128]{1,0:T(8,128)(2,1)S(1)} %get-tuple-element.80), channel_id=1, source_target_pairs={{0,128},{8,40},{16,144},{24,56},{32,160},{40,8},{48,176},{56,24},{... | collective-permute-start | bytes 1523720 | tf_op jit(solution)/shard_map/ppermute | solution.py:410
  57.0 12.5 %collective-permute-start.11 = (f32[688,128]{1,0:T(8,128)S(1)}, f32[688,128]{1,0:T(8,128)S(1)}, u32[]{:S(2)}, u32[]{:S(2)}) collective-permute-start(f32[688,128]{1,0:T(8,128)S(1)} %get-tuple-element.86), channel_id=1, source_target_pairs={{0,16},{8,72},{16,32},{24,88},{32,48},{40,104},{48,0},{56,120},{64... | collective-permute-start | bytes 1056776 | tf_op jit(solution)/shard_map/ppermute | solution.py:410
  58.7 10.8 %collective-permute-start.12 = (f32[688,128]{1,0:T(8,128)S(1)}, f32[688,128]{1,0:T(8,128)S(1)}, u32[]{:S(2)}, u32[]{:S(2)}) collective-permute-start(f32[688,128]{1,0:T(8,128)S(1)} %get-tuple-element.87), channel_id=1, source_target_pairs={{0,48},{8,200},{16,0},{24,216},{32,16},{40,232},{48,32},{56,248},{... | collective-permute-start | bytes 1056776 | tf_op jit(solution)/shard_map/ppermute | solution.py:410
  60.3 9.2 %collective-permute-start.10 = (f32[496,128]{1,0:T(8,128)S(1)}, f32[496,128]{1,0:T(8,128)S(1)}, u32[]{:S(2)}, u32[]{:S(2)}) collective-permute-start(f32[496,128]{1,0:T(8,128)S(1)} %get-tuple-element.85), channel_id=1, source_target_pairs={{0,32},{8,136},{16,48},{24,152},{32,0},{40,168},{48,16},{56,184},{... | collective-permute-start | bytes 761864 | tf_op jit(solution)/shard_map/ppermute | solution.py:410
  69.4 12.5 %copy-start.1 = (bf16[288,288]{1,0:T(8,128)(2,1)S(1)}, bf16[288,288]{1,0:T(8,128)(2,1)}, u32[]{:S(2)}) copy-start(bf16[288,288]{1,0:T(8,128)(2,1)} %constant.27.clone.padded_ref) | copy-start | bytes 497668
  70.6 6.1 %collective-permute-start.13 = (f32[448,128]{1,0:T(8,128)S(1)}, f32[448,128]{1,0:T(8,128)S(1)}, u32[]{:S(2)}, u32[]{:S(2)}) collective-permute-start(f32[448,128]{1,0:T(8,128)S(1)} %get-tuple-element.89), channel_id=1, source_target_pairs={{0,1},{1,0},{2,3},{3,2},{4,5},{5,4},{6,7},{7,6},{8,9},{9,8},{10,11... | collective-permute-start | bytes 688136 | tf_op jit(solution)/shard_map/ppermute | solution.py:415
  70.7 11.3 %collective-permute-start.15 = (bf16[192,128]{1,0:T(8,128)(2,1)S(1)}, bf16[192,128]{1,0:T(8,128)(2,1)S(1)}, u32[]{:S(2)}, u32[]{:S(2)}) collective-permute-start(bf16[192,128]{1,0:T(8,128)(2,1)S(1)} %get-tuple-element.99), channel_id=1, source_target_pairs={{1,2},{2,1},{3,4},{4,3},{5,6},{6,5},{9,10},{10,9},{11,12},{12,11},... | collective-permute-start | bytes 147464 | tf_op jit(solution)/shard_map/ppermute | solution.py:525
  77.3 7.6 %collective-permute-start.14 = (f32[128,128]{1,0:T(8,128)S(1)}, f32[128,128]{1,0:T(8,128)S(1)}, u32[]{:S(2)}, u32[]{:S(2)}) collective-permute-start(f32[128,128]{1,0:T(8,128)S(1)} %get-tuple-element.94), channel_id=1, source_target_pairs={{0,2},{1,3},{2,0},{3,1},{4,6},{5,7},{6,4},{7,5},{8,10},{9,11},{10,... | collective-permute-start | bytes 196616 | tf_op jit(solution)/shard_map/ppermute | solution.py:415
  83.9 4.9 %copy-start.5 = (bf16[6912,128]{1,0:T(8,128)(2,1)S(1)}, bf16[6912,128]{1,0:T(8,128)(2,1)}, u32[]{:S(2)}) copy-start(bf16[6912,128]{1,0:T(8,128)(2,1)} %param.10) | copy-start | bytes 5308420
  85.0 7.4 %collective-permute-start.16 = (f32[128,128]{1,0:T(8,128)S(1)}, f32[128,128]{1,0:T(8,128)S(1)}, u32[]{:S(2)}, u32[]{:S(2)}) collective-permute-start(f32[128,128]{1,0:T(8,128)S(1)} %add.30), channel_id=1, source_target_pairs={{0,7},{1,6},{2,5},{3,4},{4,3},{5,2},{6,1},{7,0},{8,15},{9,14},{10,... | collective-permute-start | bytes 196616 | tf_op jit(solution)/shard_map/ppermute | solution.py:415
  92.4 1.2 collective-permute-start.17
  93.6 3.7 %collective-permute-start.18 = (f32[1,128]{1,0:T(1,128)S(1)}, f32[1,128]{1,0:T(1,128)S(1)}, u32[]{:S(2)}, u32[]{:S(2)}) collective-permute-start(f32[1,128]{1,0:T(1,128)S(1)} %add.32), channel_id=1, source_target_pairs={{0,64},{64,0},{128,192},{192,128},{1,65},{65,1},{129,193},{193,129... | collective-permute-start | bytes 1544 | tf_op jit(solution)/shard_map/ppermute | solution.py:415
  97.3 6.5 %copy-start.4 = (bf16[3456,256]{1,0:T(8,128)(2,1)S(1)}, bf16[3456,256]{1,0:T(8,128)(2,1)}, u32[]{:S(2)}) copy-start(bf16[3456,256]{1,0:T(8,128)(2,1)} %w_in_hbm.1) | copy-start | bytes 5308420
  97.3 5.1 %collective-permute-start.19 = (f32[1,128]{1,0:T(1,128)S(1)}, f32[1,128]{1,0:T(1,128)S(1)}, u32[]{:S(2)}, u32[]{:S(2)}) collective-permute-start(f32[1,128]{1,0:T(1,128)S(1)} %add.33), channel_id=1, source_target_pairs={{0,192},{64,128},{128,64},{192,0},{1,193},{65,129},{129,65},{193,1... | collective-permute-start | bytes 1544 | tf_op jit(solution)/shard_map/ppermute | solution.py:415
  102.4 3.5 %collective-permute-start.20 = (f32[1,128]{1,0:T(1,128)S(1)}, f32[1,128]{1,0:T(1,128)S(1)}, u32[]{:S(2)}, u32[]{:S(2)}) collective-permute-start(f32[1,128]{1,0:T(1,128)S(1)} %add.34), channel_id=1, source_target_pairs={{0,16},{16,0},{32,48},{48,32},{1,17},{17,1},{33,49},{49,33},{2,18}... | collective-permute-start | bytes 1544 | tf_op jit(solution)/shard_map/ppermute | solution.py:415
  105.9 4.8 %collective-permute-start.21 = (f32[1,128]{1,0:T(1,128)S(1)}, f32[1,128]{1,0:T(1,128)S(1)}, u32[]{:S(2)}, u32[]{:S(2)}) collective-permute-start(f32[1,128]{1,0:T(1,128)S(1)} %add.35), channel_id=1, source_target_pairs={{0,48},{16,32},{32,16},{48,0},{1,49},{17,33},{33,17},{49,1},{2,50}... | collective-permute-start | bytes 1544 | tf_op jit(solution)/shard_map/ppermute | solution.py:415
  110.7 3.5 %collective-permute-start.22 = (f32[1,128]{1,0:T(1,128)S(1)}, f32[1,128]{1,0:T(1,128)S(1)}, u32[]{:S(2)}, u32[]{:S(2)}) collective-permute-start(f32[1,128]{1,0:T(1,128)S(1)} %add.37), channel_id=1, source_target_pairs={{0,1},{1,0},{2,3},{3,2},{4,5},{5,4},{6,7},{7,6},{8,9},{9,8},{10,11... | collective-permute-start | bytes 1544 | tf_op jit(solution)/shard_map/ppermute | solution.py:415
  114.2 4.4 %collective-permute-start.23 = (f32[1,128]{1,0:T(1,128)S(1)}, f32[1,128]{1,0:T(1,128)S(1)}, u32[]{:S(2)}, u32[]{:S(2)}) collective-permute-start(f32[1,128]{1,0:T(1,128)S(1)} %add.38), channel_id=1, source_target_pairs={{0,2},{1,3},{2,0},{3,1},{4,6},{5,7},{6,4},{7,5},{8,10},{9,11},{10,... | collective-permute-start | bytes 1544 | tf_op jit(solution)/shard_map/ppermute | solution.py:415

commit v8 on v7

--- a/solution.py
+++ b/solution.py
@@ -75,7 +75,7 @@
         in_specs=[pl.BlockSpec(memory_space=pltpu.SMEM)] + [vmem] * (len(args) - 1),
         out_specs=(vmem,) * len(outs),
         scratch_shapes=[pltpu.VMEM(shape, F32) for shape in scratch],
-        compiler_params=pltpu.CompilerParams(vmem_limit_bytes=12 * 1024 * 1024),
+        compiler_params=pltpu.CompilerParams(vmem_limit_bytes=6 * 1024 * 1024),
         cost_estimate=pl.CostEstimate(flops=1_000_000, bytes_accessed=4_000_000, transcendentals=0),
     )(*args)
 
@@ -394,7 +394,7 @@
             pltpu.VMEM((2, 4, 16, 1152), BF16), pltpu.VMEM((128, 768), BF16),
             pltpu.SemaphoreType.DMA((3,)),
         ],
-        compiler_params=pltpu.CompilerParams(vmem_limit_bytes=24 * 1024 * 1024),
+        compiler_params=pltpu.CompilerParams(vmem_limit_bytes=18 * 1024 * 1024),
         cost_estimate=pl.CostEstimate(flops=2_500_000_000, bytes_accessed=16_000_000, transcendentals=16384),
     )(
         place, act, cot, pool, got_here, got_there,

time: 120 us -> 120 us (level)
  no operation moved by 1% of the time
where the time goes in v8:
time: 120 us
  starting transfers between devices  49 us (41%)
  waiting for transfers between devices  37.5 us (31%)
  Pallas kernels  16 us (13%)
  matrix products  7.42 us (6%)
  local copies, waits for them, and re-layouts  6.27 us (5%)
  other arithmetic  2.76 us (2%)
    ppermute x11, starting transfers between devices, paired(): return lax.ppermute(array, axis, [(i, i ^ bit) for i in range(count)])  20.3 us
    ppermute x6, waiting for transfers between devices, crossed(): return lax.ppermute(array, ('gx', 'x', 'core'), pairs)  18.3 us
    ppermute x11, waiting for transfers between devices, paired(): return lax.ppermute(array, axis, [(i, i ^ bit) for i in range(count)])  16.5 us
    ppermute x6, starting transfers between devices, crossed(): return lax.ppermute(array, ('gx', 'x', 'core'), pairs)  13.7 us
    pallas_call x10, Pallas kernels, _call(): pl.pallas_call(kernel, out_shape=tuple((jax.ShapeDtypeStruct(shape, kind)...  9.36 us
    pallas_call x1, Pallas kernels, gradients(): pl.pallas_call(_gradients_kernel, out_shape=(shape((2, 7936, 128), F32),...  6.64 us
    conv_general_dilated x3, matrix products, conv_forward(): lax.conv_general_dilated(padded, kernel, (1, 1, 1), 'VALID', dimension_nu...  6.24 us
    ppermute x1, starting transfers between devices, scattered_sum(): lax.ppermute(other, 'gz', [(i, j) for i in range(8) for j in [(i + 1 ^ 1)...  6.03 us
  transfers between devices with their start and end apart: 24, of which 12 were waited for; matrix products, arithmetic and copies ran while one was open for 12% of the time, Pallas kernels for 2%

profile of v8, /device:TPU:32, one launch (start us, length us, event | category | flops | bytes accessed | tf_op | source)
XLA Modules:
  0.0 119.9 jit_solution(17051237621661714097)
XLA Ops:
  0.6 1.0 pad_maximum_fusion.1.both_ref
  1.7 0.7 shard_map.94
  2.4 1.7 %collective-permute-start = (bf16[288,128]{1,0:T(8,128)(2,1)S(1)}, bf16[288,128]{1,0:T(8,128)(2,1)S(1)}, u32[]{:S(2)}, u32[]{:S(2)}) collective-permute-start(bf16[288,128]{1,0:T(8,128)(2,1)S(1)} %get-tuple-element.64), channel_id=1, source_target_pairs={{0,64},{64,0},{128,192},{192,128},{1,65},{65,1},{129,193},{193,129... | collective-permute-start | bytes 221192 | tf_op jit(solution)/shard_map/ppermute | solution.py:264
  4.1 0.7 collective-permute-start.1
  4.8 2.1 %collective-permute-done.got_here = bf16[288,128]{1,0:T(8,128)(2,1)S(1)} collective-permute-done((bf16[288,128]{1,0:T(8,128)(2,1)S(1)}, bf16[288,128]{1,0:T(8,128)(2,1)S(1)}, u32[]{:S(2)}, u32[]{:S(2)}) %collective-permute-start) | collective-permute-done | bytes 73760 | tf_op jit(solution)/shard_map/ppermute | solution.py:264
  6.9 0.7 shard_map.95
  7.7 0.7 collective-permute-start.3
  8.9 1.0 shard_map.96
  9.9 1.9 %collective-permute-start.4 = (bf16[304,128]{1,0:T(8,128)(2,1)S(1)}, bf16[304,128]{1,0:T(8,128)(2,1)S(1)}, u32[]{:S(2)}, u32[]{:S(2)}) collective-permute-start(bf16[304,128]{1,0:T(8,128)(2,1)S(1)} %get-tuple-element.73), channel_id=1, source_target_pairs={{0,1},{1,0},{2,3},{3,2},{4,5},{5,4},{6,7},{7,6},{8,9},{9,8},{10,11... | collective-permute-start | bytes 233480 | tf_op jit(solution)/shard_map/ppermute | solution.py:264
  11.8 3.9 %collective-permute-start.5 = (bf16[304,128]{1,0:T(8,128)(2,1)S(1)}, bf16[304,128]{1,0:T(8,128)(2,1)S(1)}, u32[]{:S(2)}, u32[]{:S(2)}) collective-permute-start(bf16[304,128]{1,0:T(8,128)(2,1)S(1)} %get-tuple-element.74), channel_id=1, source_target_pairs={{1,2},{2,1},{3,4},{4,3},{5,6},{6,5},{9,10},{10,9},{11,12},{12,11},... | collective-permute-start | bytes 233480 | tf_op jit(solution)/shard_map/ppermute | solution.py:264
  15.7 2.7 %copy.15 = bf16[27,256,128]{1,2,0:T(8,128)(2,1)S(1)} copy(bf16[27,256,128]{2,1,0:T(8,128)(2,1)} %bitcast.38) | data formatting | bytes 3538944 | tf_op jit(solution)/shard_map/reshape | solution.py:534
  18.5 1.5 %copy-done.3 = bf16[3456,256]{1,0:T(8,128)(2,1)S(1)} copy-done((bf16[3456,256]{1,0:T(8,128)(2,1)S(1)}, bf16[3456,256]{1,0:T(8,128)(2,1)}, u32[]{:S(2)}) %copy-start.3) | copy-done | bytes 1769496
  19.9 6.6 %shard_map.97 = (f32[2,7936,128]{2,1,0:T(8,128)S(1)}, bf16[8192,128]{1,0:T(8,128)(2,1)S(1)}, bf16[64,512]{1,0:T(8,128)(2,1)S(1)}, f32[512,128]{1,0:T(8,128)S(1)}) custom-call(s32[4]{0:T(128)S(1)} %pad_add_fusion.place_ref, bf16[512,128]{1,0:T(8,128)(2,1)S(1)} %get-tuple-element.61.act_ref, bf16[960,128]{1,0:T(8,128)(2,1)S(1)} %get-tuple-element.71.cot_ref, ...), custom_call_target="tpu_custom_call" | custom-call | flops 2500000000 | bytes 16000000 | tf_op jit(solution)/shard_map/pallas_call | solution.py:384
  26.6 4.6 %collective-permute-start.6 = (bf16[8192,128]{1,0:T(8,128)(2,1)S(1)}, bf16[8192,128]{1,0:T(8,128)(2,1)S(1)}, u32[]{:S(2)}, u32[]{:S(2)}) collective-permute-start(bf16[8192,128]{1,0:T(8,128)(2,1)S(1)} %get-tuple-element.76), channel_id=1, source_target_pairs={{0,8},{8,0},{1,9},{9,1},{2,10},{10,2},{3,11},{11,3},{4,12},{12,4},... | collective-permute-start | bytes 6291464 | tf_op jit(solution)/shard_map/ppermute | solution.py:415
  31.1 3.8 %collective-permute-done.6.got_ref = bf16[8192,128]{1,0:T(8,128)(2,1)S(1)} collective-permute-done((bf16[8192,128]{1,0:T(8,128)(2,1)S(1)}, bf16[8192,128]{1,0:T(8,128)(2,1)S(1)}, u32[]{:S(2)}, u32[]{:S(2)}) %collective-permute-start.6) | collective-permute-done | bytes 2097184 | tf_op jit(solution)/shard_map/ppermute | solution.py:415
  34.9 1.2 shard_map.98
  36.1 4.4 %collective-permute-start.8 = (bf16[2240,128]{1,0:T(8,128)(2,1)S(1)}, bf16[2240,128]{1,0:T(8,128)(2,1)S(1)}, u32[]{:S(2)}, u32[]{:S(2)}) collective-permute-start(bf16[2240,128]{1,0:T(8,128)(2,1)S(1)} %get-tuple-element.81), channel_id=1, source_target_pairs={{0,64},{8,24},{16,80},{24,40},{32,96},{40,56},{48,112},{56,8},{64,... | collective-permute-start | bytes 1720328 | tf_op jit(solution)/shard_map/ppermute | solution.py:410
  40.5 4.1 %collective-permute-start.7 = (bf16[1984,128]{1,0:T(8,128)(2,1)S(1)}, bf16[1984,128]{1,0:T(8,128)(2,1)S(1)}, u32[]{:S(2)}, u32[]{:S(2)}) collective-permute-start(bf16[1984,128]{1,0:T(8,128)(2,1)S(1)} %get-tuple-element.80), channel_id=1, source_target_pairs={{0,128},{8,40},{16,144},{24,56},{32,160},{40,8},{48,176},{56,24},{... | collective-permute-start | bytes 1523720 | tf_op jit(solution)/shard_map/ppermute | solution.py:410
  44.6 11.1 %collective-permute-done.7.got_2 = bf16[1984,128]{1,0:T(8,128)(2,1)S(1)} collective-permute-done((bf16[1984,128]{1,0:T(8,128)(2,1)S(1)}, bf16[1984,128]{1,0:T(8,128)(2,1)S(1)}, u32[]{:S(2)}, u32[]{:S(2)}) %collective-permute-start.7) | collective-permute-done | bytes 507936 | tf_op jit(solution)/shard_map/ppermute | solution.py:410
  55.7 1.2 %shard_map.99 = (bf16[256,512]{1,0:T(8,128)(2,1)S(1)}, f32[496,128]{1,0:T(8,128)S(1)}, f32[688,128]{1,0:T(8,128)S(1)}, f32[496,128]{1,0:T(8,128)S(1)}, f32[688,128]{1,0:T(8,128)S(1)}) custom-call(s32[4]{0:T(128)S(1)} %pad_add_fusion.place_ref, bf16[128,512]{1,0:T(8,128)(2,1)S(1)} %get-tuple-element.78.chip_ref, f32[1984,128]{1,0:T(8,128)S(1)} %get-tuple-element.79.own_ref, ...), custom_call_target="tpu_custom_call" | custom-call | flops 1000000 | bytes 4000000 | tf_op jit(solution)/shard_map/pallas_call | solution.py:72
  57.0 1.7 %collective-permute-start.11 = (f32[688,128]{1,0:T(8,128)S(1)}, f32[688,128]{1,0:T(8,128)S(1)}, u32[]{:S(2)}, u32[]{:S(2)}) collective-permute-start(f32[688,128]{1,0:T(8,128)S(1)} %get-tuple-element.86), channel_id=1, source_target_pairs={{0,16},{8,72},{16,32},{24,88},{32,48},{40,104},{48,0},{56,120},{64... | collective-permute-start | bytes 1056776 | tf_op jit(solution)/shard_map/ppermute | solution.py:410
  58.7 1.6 %collective-permute-start.12 = (f32[688,128]{1,0:T(8,128)S(1)}, f32[688,128]{1,0:T(8,128)S(1)}, u32[]{:S(2)}, u32[]{:S(2)}) collective-permute-start(f32[688,128]{1,0:T(8,128)S(1)} %get-tuple-element.87), channel_id=1, source_target_pairs={{0,48},{8,200},{16,0},{24,216},{32,16},{40,232},{48,32},{56,248},{... | collective-permute-start | bytes 1056776 | tf_op jit(solution)/shard_map/ppermute | solution.py:410
  60.3 2.0 %collective-permute-start.10 = (f32[496,128]{1,0:T(8,128)S(1)}, f32[496,128]{1,0:T(8,128)S(1)}, u32[]{:S(2)}, u32[]{:S(2)}) collective-permute-start(f32[496,128]{1,0:T(8,128)S(1)} %get-tuple-element.85), channel_id=1, source_target_pairs={{0,32},{8,136},{16,48},{24,152},{32,0},{40,168},{48,16},{56,184},{... | collective-permute-start | bytes 761864 | tf_op jit(solution)/shard_map/ppermute | solution.py:410
  62.2 7.2 %collective-permute-done.10.got_2 = f32[496,128]{1,0:T(8,128)S(1)} collective-permute-done((f32[496,128]{1,0:T(8,128)S(1)}, f32[496,128]{1,0:T(8,128)S(1)}, u32[]{:S(2)}, u32[]{:S(2)}) %collective-permute-start.10) | collective-permute-done | bytes 253984 | tf_op jit(solution)/shard_map/ppermute | solution.py:410
  69.5 1.1 shard_map.100
  70.7 6.0 %collective-permute-start.15 = (bf16[192,128]{1,0:T(8,128)(2,1)S(1)}, bf16[192,128]{1,0:T(8,128)(2,1)S(1)}, u32[]{:S(2)}, u32[]{:S(2)}) collective-permute-start(bf16[192,128]{1,0:T(8,128)(2,1)S(1)} %get-tuple-element.99), channel_id=1, source_target_pairs={{1,2},{2,1},{3,4},{4,3},{5,6},{6,5},{9,10},{10,9},{11,12},{12,11},... | collective-permute-start | bytes 147464 | tf_op jit(solution)/shard_map/ppermute | solution.py:525
  77.3 3.6 %collective-permute-start.14 = (f32[128,128]{1,0:T(8,128)S(1)}, f32[128,128]{1,0:T(8,128)S(1)}, u32[]{:S(2)}, u32[]{:S(2)}) collective-permute-start(f32[128,128]{1,0:T(8,128)S(1)} %get-tuple-element.94), channel_id=1, source_target_pairs={{0,2},{1,3},{2,0},{3,1},{4,6},{5,7},{6,4},{7,5},{8,10},{9,11},{10,... | collective-permute-start | bytes 196616 | tf_op jit(solution)/shard_map/ppermute | solution.py:415
  80.9 0.7 shard_map.102
  82.0 0.9 shard_map.103
  84.3 0.7 pad_maximum_fusion
  85.0 3.8 %collective-permute-start.16 = (f32[128,128]{1,0:T(8,128)S(1)}, f32[128,128]{1,0:T(8,128)S(1)}, u32[]{:S(2)}, u32[]{:S(2)}) collective-permute-start(f32[128,128]{1,0:T(8,128)S(1)} %add.30), channel_id=1, source_target_pairs={{0,7},{1,6},{2,5},{3,4},{4,3},{5,2},{6,1},{7,0},{8,15},{9,14},{10,... | collective-permute-start | bytes 196616 | tf_op jit(solution)/shard_map/ppermute | solution.py:415
  88.8 2.8 %convolution_convert_fusion.1 = bf16[1,4,8,8,128]{4,0,3,2,1:T(2,128)(2,1)S(1)} fusion(bf16[3,3,3,256,128]{4,3,2,1,0:T(8,128)(2,1)S(1)} %bitcast.39, bf16[2,6,10,10,256]{4,0,3,2,1:T(2,128)(2,1)S(1)} %pad_maximum_fusion), kind=kOutput, calls=%fused_computation.2 | convolution fusion | flops 453017600 | bytes 2449408 | tf_op jit(solution)/shard_map/conv_general_dilated | solution.py:18
  91.6 0.7 collective-permute-done.16
  92.5 1.1 collective-permute-done.17
  93.6 2.0 %collective-permute-start.18 = (f32[1,128]{1,0:T(1,128)S(1)}, f32[1,128]{1,0:T(1,128)S(1)}, u32[]{:S(2)}, u32[]{:S(2)}) collective-permute-start(f32[1,128]{1,0:T(1,128)S(1)} %add.32), channel_id=1, source_target_pairs={{0,64},{64,0},{128,192},{192,128},{1,65},{65,1},{129,193},{193,129... | collective-permute-start | bytes 1544 | tf_op jit(solution)/shard_map/ppermute | solution.py:415
  95.5 1.7 %convolution_convert_fusion.3 = bf16[1,2,8,8,128]{4,0,3,2,1:T(2,128)(2,1)S(1)} fusion(bf16[3,3,3,256,128]{4,3,2,1,0:T(8,128)(2,1)S(1)} %bitcast.40, bf16[2,6,10,10,256]{4,0,3,2,1:T(2,128)(2,1)S(1)} %pad_maximum_fusion), kind=kOutput, calls=%fused_computation.4 | convolution fusion | flops 226508800 | bytes 2211840 | tf_op jit(solution)/shard_map/conv_general_dilated | solution.py:18
  97.3 2.5 %collective-permute-start.19 = (f32[1,128]{1,0:T(1,128)S(1)}, f32[1,128]{1,0:T(1,128)S(1)}, u32[]{:S(2)}, u32[]{:S(2)}) collective-permute-start(f32[1,128]{1,0:T(1,128)S(1)} %add.33), channel_id=1, source_target_pairs={{0,192},{64,128},{128,64},{192,0},{1,193},{65,129},{129,65},{193,1... | collective-permute-start | bytes 1544 | tf_op jit(solution)/shard_map/ppermute | solution.py:415
  99.7 1.7 %convolution_convert_fusion.2 = bf16[1,2,8,8,128]{4,0,3,2,1:T(2,128)(2,1)S(1)} fusion(bf16[3,3,3,256,128]{4,3,2,1,0:T(8,128)(2,1)S(1)} %bitcast.41, bf16[2,6,10,10,256]{4,0,3,2,1:T(2,128)(2,1)S(1)} %pad_maximum_fusion), kind=kOutput, calls=%fused_computation.3 | convolution fusion | flops 226508800 | bytes 2211840 | tf_op jit(solution)/shard_map/conv_general_dilated | solution.py:18
  101.5 0.9 collective-permute-done.19
  102.4 1.4 %collective-permute-start.20 = (f32[1,128]{1,0:T(1,128)S(1)}, f32[1,128]{1,0:T(1,128)S(1)}, u32[]{:S(2)}, u32[]{:S(2)}) collective-permute-start(f32[1,128]{1,0:T(1,128)S(1)} %add.34), channel_id=1, source_target_pairs={{0,16},{16,0},{32,48},{48,32},{1,17},{17,1},{33,49},{49,33},{2,18}... | collective-permute-start | bytes 1544 | tf_op jit(solution)/shard_map/ppermute | solution.py:415
  103.8 0.8 convolution_multiply_fusion
  104.7 0.7 add_convert_fusion
  105.9 2.1 %collective-permute-start.21 = (f32[1,128]{1,0:T(1,128)S(1)}, f32[1,128]{1,0:T(1,128)S(1)}, u32[]{:S(2)}, u32[]{:S(2)}) collective-permute-start(f32[1,128]{1,0:T(1,128)S(1)} %add.35), channel_id=1, source_target_pairs={{0,48},{16,32},{32,16},{48,0},{1,49},{17,33},{33,17},{49,1},{2,50}... | collective-permute-start | bytes 1544 | tf_op jit(solution)/shard_map/ppermute | solution.py:415
  108.0 2.7 %collective-permute-done.21 = f32[1,128]{1,0:T(1,128)S(1)} collective-permute-done((f32[1,128]{1,0:T(1,128)S(1)}, f32[1,128]{1,0:T(1,128)S(1)}, u32[]{:S(2)}, u32[]{:S(2)}) %collective-permute-start.21) | collective-permute-done | bytes 544 | tf_op jit(solution)/shard_map/ppermute | solution.py:415
  110.7 3.5 %collective-permute-done.22 = f32[1,128]{1,0:T(1,128)S(1)} collective-permute-done((f32[1,128]{1,0:T(1,128)S(1)}, f32[1,128]{1,0:T(1,128)S(1)}, u32[]{:S(2)}, u32[]{:S(2)}) %collective-permute-start.22) | collective-permute-done | bytes 544 | tf_op jit(solution)/shard_map/ppermute | solution.py:415
  114.7 0.7 copy.21
  115.3 3.3 %collective-permute-done.23 = f32[1,128]{1,0:T(1,128)S(1)} collective-permute-done((f32[1,128]{1,0:T(1,128)S(1)}, f32[1,128]{1,0:T(1,128)S(1)}, u32[]{:S(2)}, u32[]{:S(2)}) %collective-permute-start.23) | collective-permute-done | bytes 544 | tf_op jit(solution)/shard_map/ppermute | solution.py:415
  118.6 1.3 %shard_map.104 = f32[62,128]{1,0:T(8,128)} custom-call(s32[4]{0:T(128)S(1)} %pad_add_fusion.place_ref, f32[1,128]{1,0:T(1,128)S(1)} %add.39.total_ref, f32[128,128]{1,0:T(8,128)S(1)} %get-tuple-element.126.both_ref), custom_call_target="tpu_custom_call" | custom-call | flops 1000000 | bytes 4000000 | tf_op jit(solution)/shard_map/pallas_call | solution.py:72
  (52 shorter events, 4.3 us)
Async XLA Ops:
  2.4 4.4 %collective-permute-start = (bf16[288,128]{1,0:T(8,128)(2,1)S(1)}, bf16[288,128]{1,0:T(8,128)(2,1)S(1)}, u32[]{:S(2)}, u32[]{:S(2)}) collective-permute-start(bf16[288,128]{1,0:T(8,128)(2,1)S(1)} %get-tuple-element.64), channel_id=1, source_target_pairs={{0,64},{64,0},{128,192},{192,128},{1,65},{65,1},{129,193},{193,129... | collective-permute-start | bytes 221192 | tf_op jit(solution)/shard_map/ppermute | solution.py:264
  4.1 2.8 %collective-permute-start.1 = (bf16[288,128]{1,0:T(8,128)(2,1)S(1)}, bf16[288,128]{1,0:T(8,128)(2,1)S(1)}, u32[]{:S(2)}, u32[]{:S(2)}) collective-permute-start(bf16[288,128]{1,0:T(8,128)(2,1)S(1)} %get-tuple-element.65), channel_id=1, source_target_pairs={{64,128},{128,64},{65,129},{129,65},{66,130},{130,66},{67,131},{13... | collective-permute-start | bytes 221192 | tf_op jit(solution)/shard_map/ppermute | solution.py:264
  7.6 1.3 %collective-permute-start.2 = (bf16[224,128]{1,0:T(8,128)(2,1)S(1)}, bf16[224,128]{1,0:T(8,128)(2,1)S(1)}, u32[]{:S(2)}, u32[]{:S(2)}) collective-permute-start(bf16[224,128]{1,0:T(8,128)(2,1)S(1)} %get-tuple-element.69), channel_id=1, source_target_pairs={{0,8},{8,0},{16,24},{24,16},{32,40},{40,32},{48,56},{56,48},{1,9},... | collective-permute-start | bytes 172040 | tf_op jit(solution)/shard_map/ppermute | solution.py:264
  7.7 1.2 %collective-permute-start.3 = (bf16[224,128]{1,0:T(8,128)(2,1)S(1)}, bf16[224,128]{1,0:T(8,128)(2,1)S(1)}, u32[]{:S(2)}, u32[]{:S(2)}) collective-permute-start(bf16[224,128]{1,0:T(8,128)(2,1)S(1)} %get-tuple-element.70), channel_id=1, source_target_pairs={{8,16},{16,8},{24,32},{32,24},{40,48},{48,40},{9,17},{17,9},{25,33... | collective-permute-start | bytes 172040 | tf_op jit(solution)/shard_map/ppermute | solution.py:264
  9.9 8.5 %collective-permute-start.4 = (bf16[304,128]{1,0:T(8,128)(2,1)S(1)}, bf16[304,128]{1,0:T(8,128)(2,1)S(1)}, u32[]{:S(2)}, u32[]{:S(2)}) collective-permute-start(bf16[304,128]{1,0:T(8,128)(2,1)S(1)} %get-tuple-element.73), channel_id=1, source_target_pairs={{0,1},{1,0},{2,3},{3,2},{4,5},{5,4},{6,7},{7,6},{8,9},{9,8},{10,11... | collective-permute-start | bytes 233480 | tf_op jit(solution)/shard_map/ppermute | solution.py:264
  11.8 6.6 %collective-permute-start.5 = (bf16[304,128]{1,0:T(8,128)(2,1)S(1)}, bf16[304,128]{1,0:T(8,128)(2,1)S(1)}, u32[]{:S(2)}, u32[]{:S(2)}) collective-permute-start(bf16[304,128]{1,0:T(8,128)(2,1)S(1)} %get-tuple-element.74), channel_id=1, source_target_pairs={{1,2},{2,1},{3,4},{4,3},{5,6},{6,5},{9,10},{10,9},{11,12},{12,11},... | collective-permute-start | bytes 233480 | tf_op jit(solution)/shard_map/ppermute | solution.py:264
  15.7 2.7 %copy-start = (bf16[2048,128]{1,0:T(8,128)(2,1)S(1)}, bf16[2048,128]{1,0:T(8,128)(2,1)}, u32[]{:S(2)}) copy-start(bf16[2048,128]{1,0:T(8,128)(2,1)} %w_up_hbm.1) | copy-start | bytes 1572868
  18.5 1.5 %copy-start.3 = (bf16[3456,256]{1,0:T(8,128)(2,1)S(1)}, bf16[3456,256]{1,0:T(8,128)(2,1)}, u32[]{:S(2)}) copy-start(bf16[3456,256]{1,0:T(8,128)(2,1)} %w_in_hbm.1) | copy-start | bytes 5308420
  26.6 8.4 %collective-permute-start.6 = (bf16[8192,128]{1,0:T(8,128)(2,1)S(1)}, bf16[8192,128]{1,0:T(8,128)(2,1)S(1)}, u32[]{:S(2)}, u32[]{:S(2)}) collective-permute-start(bf16[8192,128]{1,0:T(8,128)(2,1)S(1)} %get-tuple-element.76), channel_id=1, source_target_pairs={{0,8},{8,0},{1,9},{9,1},{2,10},{10,2},{3,11},{11,3},{4,12},{12,4},... | collective-permute-start | bytes 6291464 | tf_op jit(solution)/shard_map/ppermute | solution.py:415
  36.1 33.3 %copy-start.2 = (bf16[96,192]{1,0:T(8,128)(2,1)S(1)}, bf16[96,192]{1,0:T(8,128)(2,1)}, u32[]{:S(2)}) copy-start(bf16[96,192]{1,0:T(8,128)(2,1)} %constant.26.clone.z_faces_ref) | copy-start | bytes 110596
  36.1 19.6 %collective-permute-start.8 = (bf16[2240,128]{1,0:T(8,128)(2,1)S(1)}, bf16[2240,128]{1,0:T(8,128)(2,1)S(1)}, u32[]{:S(2)}, u32[]{:S(2)}) collective-permute-start(bf16[2240,128]{1,0:T(8,128)(2,1)S(1)} %get-tuple-element.81), channel_id=1, source_target_pairs={{0,64},{8,24},{16,80},{24,40},{32,96},{40,56},{48,112},{56,8},{64,... | collective-permute-start | bytes 1720328 | tf_op jit(solution)/shard_map/ppermute | solution.py:410
  40.5 15.2 %collective-permute-start.9 = (bf16[2240,128]{1,0:T(8,128)(2,1)S(1)}, bf16[2240,128]{1,0:T(8,128)(2,1)S(1)}, u32[]{:S(2)}, u32[]{:S(2)}) collective-permute-start(bf16[2240,128]{1,0:T(8,128)(2,1)S(1)} %get-tuple-element.82), channel_id=1, source_target_pairs={{0,192},{8,56},{16,208},{24,8},{32,224},{40,24},{48,240},{56,40},{... | collective-permute-start | bytes 1720328 | tf_op jit(solution)/shard_map/ppermute | solution.py:410
  40.5 15.2 %collective-permute-start.7 = (bf16[1984,128]{1,0:T(8,128)(2,1)S(1)}, bf16[1984,128]{1,0:T(8,128)(2,1)S(1)}, u32[]{:S(2)}, u32[]{:S(2)}) collective-permute-start(bf16[1984,128]{1,0:T(8,128)(2,1)S(1)} %get-tuple-element.80), channel_id=1, source_target_pairs={{0,128},{8,40},{16,144},{24,56},{32,160},{40,8},{48,176},{56,24},{... | collective-permute-start | bytes 1523720 | tf_op jit(solution)/shard_map/ppermute | solution.py:410
  57.0 12.5 %collective-permute-start.11 = (f32[688,128]{1,0:T(8,128)S(1)}, f32[688,128]{1,0:T(8,128)S(1)}, u32[]{:S(2)}, u32[]{:S(2)}) collective-permute-start(f32[688,128]{1,0:T(8,128)S(1)} %get-tuple-element.86), channel_id=1, source_target_pairs={{0,16},{8,72},{16,32},{24,88},{32,48},{40,104},{48,0},{56,120},{64... | collective-permute-start | bytes 1056776 | tf_op jit(solution)/shard_map/ppermute | solution.py:410
  58.7 10.8 %collective-permute-start.12 = (f32[688,128]{1,0:T(8,128)S(1)}, f32[688,128]{1,0:T(8,128)S(1)}, u32[]{:S(2)}, u32[]{:S(2)}) collective-permute-start(f32[688,128]{1,0:T(8,128)S(1)} %get-tuple-element.87), channel_id=1, source_target_pairs={{0,48},{8,200},{16,0},{24,216},{32,16},{40,232},{48,32},{56,248},{... | collective-permute-start | bytes 1056776 | tf_op jit(solution)/shard_map/ppermute | solution.py:410
  60.3 9.2 %collective-permute-start.10 = (f32[496,128]{1,0:T(8,128)S(1)}, f32[496,128]{1,0:T(8,128)S(1)}, u32[]{:S(2)}, u32[]{:S(2)}) collective-permute-start(f32[496,128]{1,0:T(8,128)S(1)} %get-tuple-element.85), channel_id=1, source_target_pairs={{0,32},{8,136},{16,48},{24,152},{32,0},{40,168},{48,16},{56,184},{... | collective-permute-start | bytes 761864 | tf_op jit(solution)/shard_map/ppermute | solution.py:410
  69.4 12.6 %copy-start.1 = (bf16[288,288]{1,0:T(8,128)(2,1)S(1)}, bf16[288,288]{1,0:T(8,128)(2,1)}, u32[]{:S(2)}) copy-start(bf16[288,288]{1,0:T(8,128)(2,1)} %constant.27.clone.padded_ref) | copy-start | bytes 497668
  70.6 6.1 %collective-permute-start.13 = (f32[448,128]{1,0:T(8,128)S(1)}, f32[448,128]{1,0:T(8,128)S(1)}, u32[]{:S(2)}, u32[]{:S(2)}) collective-permute-start(f32[448,128]{1,0:T(8,128)S(1)} %get-tuple-element.89), channel_id=1, source_target_pairs={{0,1},{1,0},{2,3},{3,2},{4,5},{5,4},{6,7},{7,6},{8,9},{9,8},{10,11... | collective-permute-start | bytes 688136 | tf_op jit(solution)/shard_map/ppermute | solution.py:415
  70.7 11.3 %collective-permute-start.15 = (bf16[192,128]{1,0:T(8,128)(2,1)S(1)}, bf16[192,128]{1,0:T(8,128)(2,1)S(1)}, u32[]{:S(2)}, u32[]{:S(2)}) collective-permute-start(bf16[192,128]{1,0:T(8,128)(2,1)S(1)} %get-tuple-element.99), channel_id=1, source_target_pairs={{1,2},{2,1},{3,4},{4,3},{5,6},{6,5},{9,10},{10,9},{11,12},{12,11},... | collective-permute-start | bytes 147464 | tf_op jit(solution)/shard_map/ppermute | solution.py:525
  77.3 7.6 %collective-permute-start.14 = (f32[128,128]{1,0:T(8,128)S(1)}, f32[128,128]{1,0:T(8,128)S(1)}, u32[]{:S(2)}, u32[]{:S(2)}) collective-permute-start(f32[128,128]{1,0:T(8,128)S(1)} %get-tuple-element.94), channel_id=1, source_target_pairs={{0,2},{1,3},{2,0},{3,1},{4,6},{5,7},{6,4},{7,5},{8,10},{9,11},{10,... | collective-permute-start | bytes 196616 | tf_op jit(solution)/shard_map/ppermute | solution.py:415
  83.9 4.9 %copy-start.5 = (bf16[6912,128]{1,0:T(8,128)(2,1)S(1)}, bf16[6912,128]{1,0:T(8,128)(2,1)}, u32[]{:S(2)}) copy-start(bf16[6912,128]{1,0:T(8,128)(2,1)} %param.10) | copy-start | bytes 5308420
  85.0 7.4 %collective-permute-start.16 = (f32[128,128]{1,0:T(8,128)S(1)}, f32[128,128]{1,0:T(8,128)S(1)}, u32[]{:S(2)}, u32[]{:S(2)}) collective-permute-start(f32[128,128]{1,0:T(8,128)S(1)} %add.30), channel_id=1, source_target_pairs={{0,7},{1,6},{2,5},{3,4},{4,3},{5,2},{6,1},{7,0},{8,15},{9,14},{10,... | collective-permute-start | bytes 196616 | tf_op jit(solution)/shard_map/ppermute | solution.py:415
  92.4 1.2 collective-permute-start.17
  93.6 3.7 %collective-permute-start.18 = (f32[1,128]{1,0:T(1,128)S(1)}, f32[1,128]{1,0:T(1,128)S(1)}, u32[]{:S(2)}, u32[]{:S(2)}) collective-permute-start(f32[1,128]{1,0:T(1,128)S(1)} %add.32), channel_id=1, source_target_pairs={{0,64},{64,0},{128,192},{192,128},{1,65},{65,1},{129,193},{193,129... | collective-permute-start | bytes 1544 | tf_op jit(solution)/shard_map/ppermute | solution.py:415
  97.3 6.5 %copy-start.4 = (bf16[3456,256]{1,0:T(8,128)(2,1)S(1)}, bf16[3456,256]{1,0:T(8,128)(2,1)}, u32[]{:S(2)}) copy-start(bf16[3456,256]{1,0:T(8,128)(2,1)} %w_in_hbm.1) | copy-start | bytes 5308420
  97.3 5.1 %collective-permute-start.19 = (f32[1,128]{1,0:T(1,128)S(1)}, f32[1,128]{1,0:T(1,128)S(1)}, u32[]{:S(2)}, u32[]{:S(2)}) collective-permute-start(f32[1,128]{1,0:T(1,128)S(1)} %add.33), channel_id=1, source_target_pairs={{0,192},{64,128},{128,64},{192,0},{1,193},{65,129},{129,65},{193,1... | collective-permute-start | bytes 1544 | tf_op jit(solution)/shard_map/ppermute | solution.py:415
  102.4 3.5 %collective-permute-start.20 = (f32[1,128]{1,0:T(1,128)S(1)}, f32[1,128]{1,0:T(1,128)S(1)}, u32[]{:S(2)}, u32[]{:S(2)}) collective-permute-start(f32[1,128]{1,0:T(1,128)S(1)} %add.34), channel_id=1, source_target_pairs={{0,16},{16,0},{32,48},{48,32},{1,17},{17,1},{33,49},{49,33},{2,18}... | collective-permute-start | bytes 1544 | tf_op jit(solution)/shard_map/ppermute | solution.py:415
  105.9 4.8 %collective-permute-start.21 = (f32[1,128]{1,0:T(1,128)S(1)}, f32[1,128]{1,0:T(1,128)S(1)}, u32[]{:S(2)}, u32[]{:S(2)}) collective-permute-start(f32[1,128]{1,0:T(1,128)S(1)} %add.35), channel_id=1, source_target_pairs={{0,48},{16,32},{32,16},{48,0},{1,49},{17,33},{33,17},{49,1},{2,50}... | collective-permute-start | bytes 1544 | tf_op jit(solution)/shard_map/ppermute | solution.py:415
  110.7 3.5 %collective-permute-start.22 = (f32[1,128]{1,0:T(1,128)S(1)}, f32[1,128]{1,0:T(1,128)S(1)}, u32[]{:S(2)}, u32[]{:S(2)}) collective-permute-start(f32[1,128]{1,0:T(1,128)S(1)} %add.37), channel_id=1, source_target_pairs={{0,1},{1,0},{2,3},{3,2},{4,5},{5,4},{6,7},{7,6},{8,9},{9,8},{10,11... | collective-permute-start | bytes 1544 | tf_op jit(solution)/shard_map/ppermute | solution.py:415
  114.2 4.4 %collective-permute-start.23 = (f32[1,128]{1,0:T(1,128)S(1)}, f32[1,128]{1,0:T(1,128)S(1)}, u32[]{:S(2)}, u32[]{:S(2)}) collective-permute-start(f32[1,128]{1,0:T(1,128)S(1)} %add.38), channel_id=1, source_target_pairs={{0,2},{1,3},{2,0},{3,1},{4,6},{5,7},{6,4},{7,5},{8,10},{9,11},{10,... | collective-permute-start | bytes 1544 | tf_op jit(solution)/shard_map/ppermute | solution.py:415
